TPU v7x, 32 devices: a whole 2x2x4 slice. The times are simulated.
32 devices in a mesh: dp: 16 (over z, y, core), tensor: 2 (over x).
Axes of the slice: x: 2, y: 2, z: 4, core: 2. Of those that a mesh axis runs over, the one named last changes fastest.
Arguments:
- block_in: bfloat16 [65536, 512], P(('dp', 'tensor')), may hold values from -6 to 6
- out_cotangent: bfloat16 [65536, 512], P(('dp', 'tensor')), may hold values from -6 to 6
- seq_lengths: int32 [16, 8], P('dp'), may hold values from 0 to 2048, as said below
- premix_gain: bfloat16 [512], replicated, may hold values from 0.5 to 1.5
- forget_weight: bfloat16 [512, 1024], P(None, 'tensor'), may hold values from -0.25 to 0.25
- admit_weight: bfloat16 [512, 1024], P(None, 'tensor'), may hold values from -0.25 to 0.25
- value_weight: bfloat16 [512, 1024], P(None, 'tensor'), may hold values from -0.25 to 0.25
- admit_bias: bfloat16 [1024], P('tensor'), may hold values from -6 to 1
- output_weight: bfloat16 [1024, 512], P('tensor'), may hold values from -0.5 to 0.5
- dense_gain: bfloat16 [512], replicated, may hold values from 0.5 to 1.5
- upper_weight: bfloat16 [512, 2048], P(None, ('dp', 'tensor')), may hold values from -0.25 to 0.25
- lower_weight: bfloat16 [2048, 512], P(('dp', 'tensor')), may hold values from -0.125 to 0.125
Outputs:
- block_out: bfloat16 [65536, 512], P(('dp', 'tensor'))
- input_slope: float32 [65536, 512], P(('dp', 'tensor'))
- premix_slope: float32 [512], P(('dp', 'tensor'))
- forget_slope: float32 [512, 1024], P(None, 'tensor')
- admit_slope: float32 [512, 1024], P(None, 'tensor')
- value_slope: float32 [512, 1024], P(None, 'tensor')
- bias_slope: float32 [1024], P('tensor')
- output_slope: float32 [1024, 512], P('tensor')
- dense_slope: float32 [512], P(('dp', 'tensor'))
- upper_slope: float32 [512, 2048], P(None, ('dp', 'tensor'))
- lower_slope: float32 [2048, 512], P(('dp', 'tensor'))
Inputs may be any that keep to these rules, and one draw needn't show every extreme that they name: `seq_lengths`: row g lists the sequences of group g in order: either 4096 // 2048 entries 2048 followed by zeros, or 8 entries 512; exactly 8 rows are of the first kind, which ones drawn from the seed.
All inputs are finite; a program needn't handle non-finite values.
Results may differ from a plain program's by a relative error of at most 0.02.
Values may be sent and summed in bfloat16 or wider, within the bound.
No kernel may reach another device: no remote copies, remote signals or barrier semaphores. Data moves between devices by JAX's collectives and lax.ppermute only.
A program may use at most 320 MiB of HBM per device.

v0:
```python
import jax
import jax.numpy as jnp
from jax import lax
from jax.sharding import PartitionSpec as P

BLOCK = 32


EPSILON = 1e-06


def gate_terms(forget_logit, admit_logit, value_logit):
    log_forget = -jax.nn.softplus(-forget_logit)
    log_admit = -jax.nn.softplus(-admit_logit)
    margin = log_forget - log_admit
    return (-jax.nn.softplus(-margin), jnp.exp(-jax.nn.softplus(margin)) * value_logit)


def block_local(pair):
    keep_log, inflow = pair
    summed = jnp.cumsum(keep_log, axis=2)
    width = keep_log.shape[2]
    lower = jnp.arange(width)[:, None] >= jnp.arange(width)[None, :]
    spread = summed[:, :, :, None, :] - summed[:, :, None, :, :]
    weights = jnp.exp(jnp.where(lower[None, None, :, :, None], spread, -jnp.inf))
    return (summed, jnp.sum(weights * inflow[:, :, None, :, :], axis=3))


def pair_combine(earlier, later):
    return (earlier[0] * later[0], later[0] * earlier[1] + later[1])


def local_pass(keep_log, inflow, resets, width):
    total, channels = keep_log.shape
    blocks = total // width
    per_turn = min(16, blocks)

    def shaped(values):
        return values.reshape(blocks // per_turn, 1, per_turn, width, channels)

    summed, local = lax.map(jax.checkpoint(block_local), (shaped(keep_log), shaped(inflow)))
    summed = summed.reshape(blocks, width, channels)
    local = local.reshape(blocks, width, channels)
    keep_mask = (1.0 - resets)[:, None]
    gains, ends = lax.associative_scan(
        pair_combine, (jnp.exp(summed[:, -1]) * keep_mask, local[:, -1])
    )
    return (summed, local, gains, ends)


def finish_states(summed, local, gains, ends, resets, incoming):
    blocks, width, channels = local.shape
    keep_mask = (1.0 - resets)[:, None]
    reached = ends[:-1] + gains[:-1] * incoming[None, :]
    previous = jnp.concatenate([incoming[None, :], reached], 0) * keep_mask
    states = local + jnp.exp(summed) * previous[:, None, :]
    return states.reshape(blocks * width, channels)


def block_resets(seq_lengths, total, width):
    ends = jnp.cumsum(seq_lengths, axis=-1, dtype=jnp.int32)
    begins = ends - seq_lengths
    positions = jnp.arange(total // width, dtype=jnp.int32) * width
    hits = (positions[:, None] == begins[..., None, :]) & (seq_lengths[..., None, :] > 0)
    return jnp.any(hits, -1).astype(jnp.float32)


def contract(left, right, left_dim, right_dim):
    return lax.dot_general(
        left, right, (((left_dim,), (right_dim,)), ((), ())), preferred_element_type=jnp.float32
    )


def gelu_tanh(values):
    return jax.nn.gelu(values, approximate=True)


def norm_back(values, scale, gain, delta):
    scaled = delta * gain
    inner = jnp.mean(scaled * values, -1, keepdims=True)
    return (scale * (scaled - values * scale * scale * inner), jnp.sum(delta * values * scale, 0))


def on_device(
    block_in,
    out_cotangent,
    seq_lengths,
    premix_gain,
    forget_weight,
    admit_weight,
    value_weight,
    admit_bias,
    output_weight,
    dense_gain,
    upper_weight,
    lower_weight,
):
    channels = forget_weight.shape[1]
    own_rows = block_in.astype(jnp.float32)
    premix = premix_gain.astype(jnp.float32)
    dense_weight_gain = dense_gain.astype(jnp.float32)
    own_scale = lax.rsqrt(jnp.mean(own_rows * own_rows, -1, keepdims=True) + EPSILON)
    gathered = lax.all_gather(block_in, "tensor", axis=0, tiled=True)
    wide = gathered.astype(jnp.float32)
    wide_scale = lax.rsqrt(jnp.mean(wide * wide, -1, keepdims=True) + EPSILON)
    normed = (wide * wide_scale * premix).astype(jnp.bfloat16)
    joined = jnp.concatenate([forget_weight, admit_weight, value_weight], 1)
    logits = jnp.dot(normed, joined, preferred_element_type=jnp.float32)
    forget_logit = logits[:, :channels]
    admit_logit = logits[:, channels : 2 * channels] + admit_bias.astype(jnp.float32)
    value_logit = logits[:, 2 * channels :]
    resets = block_resets(seq_lengths, gathered.shape[0], BLOCK)[0]
    zeros_row = jnp.zeros((channels,), jnp.float32)

    def mixer_states(forget_part, admit_part, value_part):
        keep_log, inflow = gate_terms(forget_part, admit_part, value_part)
        pieces = local_pass(keep_log, inflow, resets, BLOCK)
        return finish_states(pieces[0], pieces[1], pieces[2], pieces[3], resets, zeros_row)

    states = mixer_states(forget_logit, admit_logit, value_logit)
    state_low = states.astype(jnp.bfloat16)
    part = state_low
    mixed = lax.psum_scatter(
        jnp.dot(part, output_weight, preferred_element_type=jnp.float32).astype(jnp.bfloat16),
        "tensor",
        scatter_dimension=0,
        tiled=True,
    ).astype(jnp.float32)
    middle = own_rows + mixed
    dense_scale = lax.rsqrt(jnp.mean(middle * middle, -1, keepdims=True) + EPSILON)
    dense_in = (middle * dense_scale * dense_weight_gain).astype(jnp.bfloat16)
    upper_all, lower_all = (
        lax.all_gather(upper_weight, ("dp", "tensor"), axis=1, tiled=True),
        lax.all_gather(lower_weight, ("dp", "tensor"), axis=0, tiled=True),
    )
    upper = jnp.dot(dense_in, upper_all, preferred_element_type=jnp.float32)
    active = gelu_tanh(upper).astype(jnp.bfloat16)
    block_out = (middle + jnp.dot(active, lower_all, preferred_element_type=jnp.float32)).astype(
        jnp.bfloat16
    )
    upper_all, lower_all = (
        lax.all_gather(upper_weight, ("dp", "tensor"), axis=1, tiled=True),
        lax.all_gather(lower_weight, ("dp", "tensor"), axis=0, tiled=True),
    )
    active_delta = contract(out_cotangent, lower_all, 1, 1)
    lower_part = contract(active, out_cotangent, 0, 0)
    _, gelu_pull = jax.vjp(gelu_tanh, upper)
    upper_delta = gelu_pull(active_delta)[0].astype(jnp.bfloat16)
    upper_part = contract(dense_in, upper_delta, 0, 0)
    dense_delta = contract(upper_delta, upper_all, 1, 1)
    middle_back, dense_part = norm_back(middle, dense_scale, dense_weight_gain, dense_delta)
    middle_delta = out_cotangent.astype(jnp.float32) + middle_back
    mixed_delta = middle_delta.astype(jnp.bfloat16)
    delta_all = lax.all_gather(mixed_delta, "tensor", axis=0, tiled=True)
    output_part = contract(state_low, delta_all, 0, 0)
    state_delta = contract(delta_all, output_weight, 1, 1)
    _, state_pull = jax.vjp(mixer_states, forget_logit, admit_logit, value_logit)
    logit_deltas = state_pull(state_delta)
    logit_delta = jnp.concatenate(logit_deltas, 1).astype(jnp.bfloat16)
    weight_whole = contract(normed, logit_delta, 0, 0)
    forget_part = weight_whole[:, :channels]
    admit_part = weight_whole[:, channels : 2 * channels]
    value_part = weight_whole[:, 2 * channels :]
    bias_part = jnp.sum(logit_delta[:, channels : 2 * channels].astype(jnp.float32), 0)
    part = logit_delta
    normed_delta = lax.psum_scatter(
        contract(part, joined, 1, 1).astype(jnp.bfloat16), "tensor", scatter_dimension=0, tiled=True
    ).astype(jnp.float32)
    input_delta, premix_part = norm_back(own_rows, own_scale, premix, normed_delta)
    input_slope = middle_delta + input_delta
    forget_slope, admit_slope, value_slope, bias_slope, output_slope = (
        lax.psum(forget_part.astype(jnp.bfloat16), "dp").astype(jnp.float32),
        lax.psum(admit_part.astype(jnp.bfloat16), "dp").astype(jnp.float32),
        lax.psum(value_part.astype(jnp.bfloat16), "dp").astype(jnp.float32),
        lax.psum(bias_part.astype(jnp.bfloat16), "dp").astype(jnp.float32),
        lax.psum(output_part.astype(jnp.bfloat16), "dp").astype(jnp.float32),
    )
    upper_slope, lower_slope, premix_slope, dense_slope = (
        lax.psum_scatter(upper_part, ("dp", "tensor"), scatter_dimension=1, tiled=True),
        lax.psum_scatter(lower_part, ("dp", "tensor"), scatter_dimension=0, tiled=True),
        lax.psum_scatter(premix_part, ("dp", "tensor"), scatter_dimension=0, tiled=True),
        lax.psum_scatter(dense_part, ("dp", "tensor"), scatter_dimension=0, tiled=True),
    )
    return (
        block_out,
        input_slope,
        premix_slope,
        forget_slope,
        admit_slope,
        value_slope,
        bias_slope,
        output_slope,
        dense_slope,
        upper_slope,
        lower_slope,
    )


def solution(mesh):
    placed = (
        P(("dp", "tensor"), None),
        P(("dp", "tensor"), None),
        P("dp", None),
        P(),
        P(None, "tensor"),
        P(None, "tensor"),
        P(None, "tensor"),
        P("tensor"),
        P("tensor", None),
        P(),
        P(None, ("dp", "tensor")),
        P(("dp", "tensor"), None),
    )
    return jax.shard_map(
        on_device,
        mesh=mesh,
        in_specs=placed,
        out_specs=(
            P(("dp", "tensor"), None),
            P(("dp", "tensor"), None),
            P(("dp", "tensor")),
            P(None, "tensor"),
            P(None, "tensor"),
            P(None, "tensor"),
            P("tensor"),
            P("tensor", None),
            P(("dp", "tensor")),
            P(None, ("dp", "tensor")),
            P(("dp", "tensor"), None),
        ),
        check_vma=False,
    )
```

profile of v0, /device:TPU:1, one launch (start us, length us, event | category | flops | bytes accessed | tf_op | source)
XLA Modules:
  0.0 1397.1 jit_solution(5065158116202797372)
XLA Ops:
  15.7 53.6 %all-gather.5.cloned.1.call-done = bf16[4096,512]{1,0:T(8,128)(2,1)} async-done(((bf16[2048,512]{1,0:T(8,128)(2,1)}), bf16[4096,512]{1,0:T(8,128)(2,1)}) %all-gather.5.cloned.1.call-update) | async-done | bytes 4194320 | tf_op jit(solution)/shard_map/all_gather | solution.py:103
  73.0 14.2 %fusion.65 = f32[4096,1536]{1,0:T(8,128)} fusion(bf16[512,1536]{1,0:T(8,128)(2,1)S(1)} %constant_dynamic-update-slice_fusion.1, bf16[4096,512]{1,0:T(8,128)(2,1)} %all-gather.5.cloned.1.call-done, f32[512]{0:T(512)S(1)} %convert_element_type.87, f32[4096]{0:T(1024)S(1)} %add_rsqrt_fusion), kind=kOutput, calls=%fused_computation.130 | convolution fusion | flops 6450839552 | bytes 30951424 | tf_op jit(solution)/shard_map/dot_general | solution.py:108
  87.1 20.7 %fusion.51 = (f32[4096,512]{1,0:T(8,128)}, f32[4096,512]{1,0:T(8,128)S(1)}) fusion(f32[4096,1536]{1,0:T(8,128)} %fusion.65, f32[512]{0:T(512)S(1)} %convert_element_type.89), kind=kLoop, calls=%fused_computation.100 | loop fusion | flops 54525952 | bytes 41945088 | tf_op jit(solution)/shard_map/mul | solution.py:16
  112.8 8.1 copy.109
  129.6 125.9 %while.42 = (s32[]{:T(128)}, f32[8,1,16,32,512]{4,3,2,0,1:T(8,128)}, f32[8,1,16,32,512]{4,3,2,1,0:T(8,128)}, f32[8,1,16,32,512]{4,2,3,1,0:T(8,128)}, f32[8,1,16,32,512]{4,3,2,1,0:T(8,128)}, /*index=5*/s32[]{:T(128)}) while((s32[]{:T(128)}, f32[8,1,16,32,512]{4,3,2,0,1:T(8,128)}, f32[8,1,16,32,512]{4,3,2,1,0:T(8,128)}, ...), condition=%wide.region_4.5_spmd, body=%wide.region_1.4_spmd.sunk | while | flops 41419776 | bytes 13633629 | solution.py:41
  133.2 9.8 multiply_reduce_fusion.9
  148.9 9.8 multiply_reduce_fusion.9
  164.6 9.8 multiply_reduce_fusion.9
  180.2 9.8 multiply_reduce_fusion.9
  196.0 9.8 multiply_reduce_fusion.9
  211.6 9.8 multiply_reduce_fusion.9
  227.3 9.8 multiply_reduce_fusion.9
  243.0 9.8 multiply_reduce_fusion.9
  257.9 8.2 copy.112
  267.8 8.5 exp.103
  277.6 10.3 fusion.50
  295.9 53.7 %reduce-scatter.5.cloned.1.call-done = bf16[2048,512]{1,0:T(8,128)(2,1)} async-done(((bf16[4096,512]{1,0:T(8,128)(2,1)}), bf16[2048,512]{1,0:T(8,128)(2,1)}) %reduce-scatter.5.cloned.1.call-update) | async-done | bytes 2097168 | tf_op jit(solution)/shard_map/reduce_scatter | solution.py:123
  351.9 26.1 %all-gather.7.cloned.1.call-done = bf16[512,2048]{0,1:T(8,128)(2,1)} async-done(((bf16[512,64]{0,1:T(8,128)(2,1)}), bf16[512,2048]{0,1:T(8,128)(2,1)}) %all-gather.7.cloned.1.call-update) | async-done | bytes 2097168 | tf_op jit(solution)/shard_map/all_gather | solution.py:133
  378.0 14.1 %multiply_convert_fusion = (bf16[2048,2048]{1,0:T(8,128)(2,1)}, f32[2048,2048]{1,0:T(8,128)}) fusion(bf16[512,2048]{0,1:T(8,128)(2,1)} %all-gather.7.cloned.1.call-done, bf16[2048,512]{1,0:T(8,128)(2,1)} %reduce-scatter.5.cloned.1.call-done, bf16[2048,512]{1,0:T(8,128)(2,1)S(1)} %copy-done.5, f32[512]{0:T(512)S(1)} %convert_element_type.94, ...), kind=kOutput, calls=%fused_computation.60 | convolution fusion | flops 4339007488 | bytes 31467520 | tf_op jit(solution)/shard_map/dot_general | solution.py:136
  392.1 44.8 %all-gather.9.cloned.1.call-done = bf16[2048,512]{1,0:T(8,128)(2,1)} async-done(((bf16[64,512]{1,0:T(8,128)(2,1)}), bf16[2048,512]{1,0:T(8,128)(2,1)}) %all-gather.9.cloned.1.call-update) | async-done | bytes 2097168 | tf_op jit(solution)/shard_map/all_gather | solution.py:134
  436.9 20.2 %fusion.23 = bf16[2048,2048]{1,0:T(8,128)(2,1)} fusion(f32[2048,2048]{1,0:T(8,128)} %get-tuple-element.553, bf16[2048,512]{1,0:T(8,128)(2,1)} %param.20, bf16[2048,512]{1,0:T(8,128)(2,1)} %all-gather.9.cloned.1.call-done), kind=kOutput, calls=%fused_computation.59 | convolution fusion | flops 4378853376 | bytes 29360128 | tf_op jit(solution)/shard_map/dot_general | solution.py:69
  457.2 8.6 multiply_reduce_fusion.4
  474.9 131.4 %while.44 = (s32[]{:T(128)}, f32[8,1,16,32,512]{4,3,2,0,1:T(8,128)}, f32[8,1,16,32,512]{4,2,0,3,1:T(8,128)}, f32[8,1,16,32,512]{4,2,3,1,0:T(8,128)}, f32[8,1,16,...) while((s32[]{:T(128)}, f32[8,1,16,32,512]{4,3,2,0,1:T(8,128)}, ...), condition=%wide.region_14.16_spmd.clone, body=%wide.region_11.15_spmd.clone.sunk | while | flops 41418752 | bytes 13632613 | solution.py:41
  478.9 9.8 multiply_reduce_fusion.10
  495.2 9.8 multiply_reduce_fusion.10
  511.5 9.8 multiply_reduce_fusion.10
  527.9 9.8 multiply_reduce_fusion.10
  544.3 9.8 multiply_reduce_fusion.10
  560.6 9.8 multiply_reduce_fusion.10
  577.0 9.8 multiply_reduce_fusion.10
  593.2 9.8 multiply_reduce_fusion.10
  613.9 11.2 multiply_reduce_fusion.3
  643.0 19.9 %pad_add_fusion = (f32[128,32,512]{2,0,1:T(8,128)}, f32[128,32,512]{2,0,1:T(8,128)}) fusion(f32[128,1,512]{2,0,1:T(8,128)S(1)} %add_bitcast_fusion, f32[128,32,512]{2,1,0:T(8,128)} %bitcast.176, f32[128,1,512]{2,0,1:T(8,128)S(1)} %get-tuple-element.551, f32[128,32,512]{2,1,0:T(8,128)} %bitcast.177, f32[128,512]{1,0:T(8,128)S(1)} %get-tuple-element.550), kind=kLoop, calls=%fused_computation.96 | loop fusion | flops 8388608 | bytes 34340864 | tf_op jit(solution)/shard_map/transpose(jvp())/add_any | solution.py:46
  671.7 287.5 %while.43 = (s32[]{:T(128)}, f32[8,1,16,32,512]{4,2,3,1,0:T(8,128)}, f32[8,1,16,32,512]{4,3,2,1,0:T(8,128)}, f32[8,1,16,32,512]{4,2,3,1,0:T(8,128)}, f32[8,1,16,...) while((s32[]{:T(128)}, ...), condition=%wide.region_22.24_spmd, body=%wide.region_16.23_spmd.sunk | while | flops 91751424 | bytes 31459452 | solution.py:41
  677.6 8.0 fusion.151
  686.2 18.2 %fusion.152 = (f32[16,32,512]{2,1,0:T(8,128)S(1)}, f32[16,32,512]{2,1,0:T(8,128)S(1)}, f32[16,32,512]{2,1,0:T(8,128)S(1)}) fusion(f32[16,32,512]{2,1,0:T(8,128)S(1)} %copy.308, f32[16,32,512]{2,1,0:T(8,128)S(1)} %bitcast.184, f32[16,32,512]{2,1,0:T(8,128)S(1)} %bitcast.186, pred[32,32]{1,0:T(8,128)(4,1)S(1)} %iota_compare_fusion.6), kind=kLoop, calls=%fused_computation.14.clone.1 | loop fusion | flops 74711040 | bytes 6292480 | tf_op jit(solution)/shard_map/transpose(jvp())/while/body/eval_jaxpr/checkpoint/reduce_sum | solution.py:24
  713.5 8.0 fusion.151
  722.1 18.2 %fusion.152 = (f32[16,32,512]{2,1,0:T(8,128)S(1)}, f32[16,32,512]{2,1,0:T(8,128)S(1)}, f32[16,32,512]{2,1,0:T(8,128)S(1)}) fusion(f32[16,32,512]{2,1,0:T(8,128)S(1)} %copy.308, f32[16,32,512]{2,1,0:T(8,128)S(1)} %bitcast.184, f32[16,32,512]{2,1,0:T(8,128)S(1)} %bitcast.186, pred[32,32]{1,0:T(8,128)(4,1)S(1)} %iota_compare_fusion.6), kind=kLoop, calls=%fused_computation.14.clone.1 | loop fusion | flops 74711040 | bytes 6292480 | tf_op jit(solution)/shard_map/transpose(jvp())/while/body/eval_jaxpr/checkpoint/reduce_sum | solution.py:24
  749.3 8.0 fusion.151
  757.9 18.2 %fusion.152 = (f32[16,32,512]{2,1,0:T(8,128)S(1)}, f32[16,32,512]{2,1,0:T(8,128)S(1)}, f32[16,32,512]{2,1,0:T(8,128)S(1)}) fusion(f32[16,32,512]{2,1,0:T(8,128)S(1)} %copy.308, f32[16,32,512]{2,1,0:T(8,128)S(1)} %bitcast.184, f32[16,32,512]{2,1,0:T(8,128)S(1)} %bitcast.186, pred[32,32]{1,0:T(8,128)(4,1)S(1)} %iota_compare_fusion.6), kind=kLoop, calls=%fused_computation.14.clone.1 | loop fusion | flops 74711040 | bytes 6292480 | tf_op jit(solution)/shard_map/transpose(jvp())/while/body/eval_jaxpr/checkpoint/reduce_sum | solution.py:24
  785.2 8.0 fusion.151
  793.8 18.2 %fusion.152 = (f32[16,32,512]{2,1,0:T(8,128)S(1)}, f32[16,32,512]{2,1,0:T(8,128)S(1)}, f32[16,32,512]{2,1,0:T(8,128)S(1)}) fusion(f32[16,32,512]{2,1,0:T(8,128)S(1)} %copy.308, f32[16,32,512]{2,1,0:T(8,128)S(1)} %bitcast.184, f32[16,32,512]{2,1,0:T(8,128)S(1)} %bitcast.186, pred[32,32]{1,0:T(8,128)(4,1)S(1)} %iota_compare_fusion.6), kind=kLoop, calls=%fused_computation.14.clone.1 | loop fusion | flops 74711040 | bytes 6292480 | tf_op jit(solution)/shard_map/transpose(jvp())/while/body/eval_jaxpr/checkpoint/reduce_sum | solution.py:24
  821.1 8.0 fusion.151
  829.7 18.2 %fusion.152 = (f32[16,32,512]{2,1,0:T(8,128)S(1)}, f32[16,32,512]{2,1,0:T(8,128)S(1)}, f32[16,32,512]{2,1,0:T(8,128)S(1)}) fusion(f32[16,32,512]{2,1,0:T(8,128)S(1)} %copy.308, f32[16,32,512]{2,1,0:T(8,128)S(1)} %bitcast.184, f32[16,32,512]{2,1,0:T(8,128)S(1)} %bitcast.186, pred[32,32]{1,0:T(8,128)(4,1)S(1)} %iota_compare_fusion.6), kind=kLoop, calls=%fused_computation.14.clone.1 | loop fusion | flops 74711040 | bytes 6292480 | tf_op jit(solution)/shard_map/transpose(jvp())/while/body/eval_jaxpr/checkpoint/reduce_sum | solution.py:24
  856.9 8.0 fusion.151
  865.5 18.2 %fusion.152 = (f32[16,32,512]{2,1,0:T(8,128)S(1)}, f32[16,32,512]{2,1,0:T(8,128)S(1)}, f32[16,32,512]{2,1,0:T(8,128)S(1)}) fusion(f32[16,32,512]{2,1,0:T(8,128)S(1)} %copy.308, f32[16,32,512]{2,1,0:T(8,128)S(1)} %bitcast.184, f32[16,32,512]{2,1,0:T(8,128)S(1)} %bitcast.186, pred[32,32]{1,0:T(8,128)(4,1)S(1)} %iota_compare_fusion.6), kind=kLoop, calls=%fused_computation.14.clone.1 | loop fusion | flops 74711040 | bytes 6292480 | tf_op jit(solution)/shard_map/transpose(jvp())/while/body/eval_jaxpr/checkpoint/reduce_sum | solution.py:24
  892.8 8.0 fusion.151
  901.4 18.2 %fusion.152 = (f32[16,32,512]{2,1,0:T(8,128)S(1)}, f32[16,32,512]{2,1,0:T(8,128)S(1)}, f32[16,32,512]{2,1,0:T(8,128)S(1)}) fusion(f32[16,32,512]{2,1,0:T(8,128)S(1)} %copy.308, f32[16,32,512]{2,1,0:T(8,128)S(1)} %bitcast.184, f32[16,32,512]{2,1,0:T(8,128)S(1)} %bitcast.186, pred[32,32]{1,0:T(8,128)(4,1)S(1)} %iota_compare_fusion.6), kind=kLoop, calls=%fused_computation.14.clone.1 | loop fusion | flops 74711040 | bytes 6292480 | tf_op jit(solution)/shard_map/transpose(jvp())/while/body/eval_jaxpr/checkpoint/reduce_sum | solution.py:24
  928.7 8.0 fusion.151
  937.3 18.2 %fusion.152 = (f32[16,32,512]{2,1,0:T(8,128)S(1)}, f32[16,32,512]{2,1,0:T(8,128)S(1)}, f32[16,32,512]{2,1,0:T(8,128)S(1)}) fusion(f32[16,32,512]{2,1,0:T(8,128)S(1)} %copy.308, f32[16,32,512]{2,1,0:T(8,128)S(1)} %bitcast.184, f32[16,32,512]{2,1,0:T(8,128)S(1)} %bitcast.186, pred[32,32]{1,0:T(8,128)(4,1)S(1)} %iota_compare_fusion.6), kind=kLoop, calls=%fused_computation.14.clone.1 | loop fusion | flops 74711040 | bytes 6292480 | tf_op jit(solution)/shard_map/transpose(jvp())/while/body/eval_jaxpr/checkpoint/reduce_sum | solution.py:24
  959.2 8.8 neg.99
  968.0 11.8 copy.130
  985.9 28.6 %fusion.95 = (bf16[512]{0:T(512)(128)(2,1)S(1)}, bf16[4096,512]{1,0:T(8,128)(2,1)}, f32[4096,512]{1,0:T(8,128)}) fusion(f32[512]{0:T(512)S(1)} %copy-done.54, f32[4096,1536]{1,0:T(8,128)} %fusion.65, f32[4096,512]{1,0:T(8,128)S(1)} %bitcast.173, f32[8,1,16,32,512]{4,3,2,0,1:T(8,128)} %copy.130, f32[8,1,16,32,512]{4,3,2,1,0:T(8,128)S(1)} %bitcast.180), kind=kLoop, calls=%fused_computation.321 | loop fusion | flops 100662784 | bytes 54529024 | tf_op jit(solution)/shard_map/reduce_sum | solution.py:164
  1014.5 11.3 fusion.31
  1039.6 11.1 convolution_convert_fusion
  1050.9 10.8 fusion.121
  1062.0 11.3 fusion.92
  1073.3 11.0 add_convert_fusion
  1084.4 29.1 %psum.38 = bf16[512]{0:T(512)(128)(2,1)S(1)} all-reduce(bf16[512]{0:T(512)(128)(2,1)S(1)} %get-tuple-element.400), channel_id=1, replica_groups=mesh['dp'=16,'tensor'=2] {'dp'}, use_global_device_ids=true, to_apply=%region_31.33 | all-reduce | flops 512 | bytes 2048 | tf_op jit(solution)/shard_map/psum | solution.py:175
  1114.1 22.0 %all-reduce.132.cloned.1.call-done = (bf16[512,512]{1,0:T(8,128)(2,1)}, bf16[512,512]{1,0:T(8,128)(2,1)}, bf16[512,512]{1,0:T(8,128)(2,1)}, bf16[512,512]{1,0:T(8,128)(2,1)}) async-done(((bf16[512,512]{1,0:T(8,128)(2,1)}, bf16[512,512]{1,0:T(8,128)(2,1)}, bf16[512,512]{1,0:T(8,128)(2,1)}, bf16[512,512]{1,0:T(8,128)(2,1)}), (bf16[512,512]{1,0:T(8,128)(2,1)}, bf16[512,512]{1,0:T(8,128)(2,1)}, ...) | async-done | bytes 2097168 | tf_op jit(solution)/shard_map/psum | solution.py:172
  1147.9 41.2 %all-reduce.128 = (f32[512]{0:T(512)S(1)}, f32[512]{0:T(512)S(1)}) all-reduce(f32[512]{0:T(512)S(1)} %get-tuple-element.355, f32[512]{0:T(512)S(1)} %copy-done.60), channel_id=4, replica_groups=mesh['dp'=16,'tensor'=2] {'dp','tensor'}, use_global_device_ids=true, to_apply=%region_26.28.clone | all-reduce | flops 1024 | bytes 8192
  1190.2 8.3 fusion.56
  1198.5 48.9 %reduce-scatter.11.cloned.1.call-done = f32[64,512]{1,0:T(8,128)} async-done(((f32[2048,512]{1,0:T(8,128)}), f32[64,512]{1,0:T(8,128)}) %reduce-scatter.11.cloned.1.call-update) | async-done | bytes 131088 | tf_op jit(solution)/shard_map/reduce_scatter | solution.py:180
  1247.4 141.7 %reduce-scatter.9.cloned.1.call-done = f32[512,64]{0,1:T(8,128)} async-done(((f32[512,2048]{0,1:T(8,128)}), f32[512,64]{0,1:T(8,128)}) %reduce-scatter.9.cloned.1.call-update) | async-done | bytes 131088 | tf_op jit(solution)/shard_map/reduce_scatter | solution.py:179
  (703 shorter events, 292.2 us)
Async XLA Ops:
  8.0 279.9 %copy-start = (bf16[512,512]{1,0:T(8,128)(2,1)S(1)}, bf16[512,512]{1,0:T(8,128)(2,1)}, u32[]{:S(2)}) copy-start(bf16[512,512]{1,0:T(8,128)(2,1)} %param.27) | copy-start | bytes 1572868
  8.0 61.2 %all-gather.5.cloned.1.call-start = ((), (), s32[]{:S(2)}) async-start(), calls=%async_computation.4 | async-start | bytes 6291456 | tf_op jit(solution)/shard_map/all_gather | solution.py:103
  8.8 340.8 %reduce-scatter.5.cloned.1.call-start = ((), (), s32[]{:S(2)}) async-start(), calls=%async_computation.5 | async-start | bytes 6291456 | tf_op jit(solution)/shard_map/reduce_scatter | solution.py:123
  10.3 76.8 %copy-start.49 = (f32[512]{0:T(512)}, f32[512]{0:T(512)S(1)}, u32[]{:S(2)}) copy-start(f32[512]{0:T(512)S(1)} %convert_element_type.87) | copy-start | bytes 6148
  11.0 76.1 %copy-start.53 = (f32[512]{0:T(512)}, f32[512]{0:T(512)S(1)}, u32[]{:S(2)}) copy-start(f32[512]{0:T(512)S(1)} %convert_element_type.89) | copy-start | bytes 6148
  15.7 71.5 %copy-start.22 = (bf16[512,1536]{1,0:T(8,128)(2,1)}, bf16[512,1536]{1,0:T(8,128)(2,1)S(1)}, u32[]{:S(2)}) copy-start(bf16[512,1536]{1,0:T(8,128)(2,1)S(1)} %constant_dynamic-update-slice_fusion.1) | copy-start | bytes 4718596
  15.7 609.9 %copy-start.57 = (f32[128]{0:T(128)}, f32[128]{0:T(128)S(1)}, u32[]{:S(2)}) copy-start(f32[128]{0:T(128)S(1)} %convert_subtract_fusion) | copy-start | bytes 1540
  107.9 4.9 copy-start.2
  257.5 8.7 copy-start.15
  267.7 9.5 slice-start.4
  287.9 8.0 copy-start.61
  287.9 61.7 %copy-start.5 = (bf16[2048,512]{1,0:T(8,128)(2,1)S(1)}, bf16[2048,512]{1,0:T(8,128)(2,1)}, u32[]{:S(2)}) copy-start(bf16[2048,512]{1,0:T(8,128)(2,1)} %param.19) | copy-start | bytes 6291460
  294.6 83.4 %all-gather.7.cloned.1.call-start = ((), (), s32[]{:S(2)}) async-start(), calls=%async_computation.6 | async-start | bytes 2162688 | tf_op jit(solution)/shard_map/all_gather | solution.py:133
  295.2 141.8 %all-gather.9.cloned.1.call-start = ((), (), s32[]{:S(2)}) async-start(), calls=%async_computation.7 | async-start | bytes 2162688 | tf_op jit(solution)/shard_map/all_gather | solution.py:134
  295.7 313.3 %all-gather.11.cloned.1.call-start = ((), (), s32[]{:S(2)}) async-start(), calls=%async_computation.8 | async-start | bytes 6291456 | tf_op jit(solution)/shard_map/all_gather | solution.py:154
  295.9 169.9 %copy-start.51 = (f32[512]{0:T(512)}, f32[512]{0:T(512)S(1)}, u32[]{:S(2)}) copy-start(f32[512]{0:T(512)S(1)} %convert_element_type.94) | copy-start | bytes 6148
  351.9 113.9 %copy-start.35 = (f32[2048]{0:T(1024)}, f32[2048]{0:T(1024)S(1)}, u32[]{:S(2)}) copy-start(f32[2048]{0:T(1024)S(1)} %add_rsqrt_fusion.2) | copy-start | bytes 24580
  436.9 20.2 %copy-start.7 = (bf16[2048,512]{1,0:T(8,128)(2,1)S(1)}, bf16[2048,512]{1,0:T(8,128)(2,1)}, u32[]{:S(2)}) copy-start(bf16[2048,512]{1,0:T(8,128)(2,1)} %reduce-scatter.5.cloned.1.call-done) | copy-start | bytes 6291460
  436.9 20.2 %copy-start.62 = (bf16[512,2048]{0,1:T(8,128)(2,1)S(1)}, bf16[512,2048]{0,1:T(8,128)(2,1)}, u32[]{:S(2)}) copy-start(bf16[512,2048]{0,1:T(8,128)(2,1)} %all-gather.7.cloned.1.call-done) | copy-start | bytes 6291460
  457.2 10.7 copy-start.9
  465.8 2.0 copy-start.8
  465.8 2.0 copy-start.37
  470.5 665.6 %all-reduce.132.cloned.1.call-start = ((), (), s32[]{:S(2)}) async-start(), calls=%async_computation.12 | async-start | bytes 4194304 | tf_op jit(solution)/shard_map/psum | solution.py:172
  609.0 4.9 copy-start.4
  613.9 11.3 copy-start.3
  625.4 6.2 copy-start.16
  625.5 6.2 copy-start.17
  628.2 2.7 copy-start.24
  628.2 2.7 copy-start.25
  628.2 2.7 copy-start.26
  628.3 2.6 copy-start.27
  628.4 2.2 copy-start.33
  628.4 1.4 copy-start.34
  628.5 1.4 copy-start.40
  628.5 2.1 copy-start.41
  628.6 1.5 copy-start.42
  628.6 1.4 copy-start.43
  629.2 1.8 copy-start.28
  631.4 10.5 copy-start.58
  631.6 10.3 slice-start.5
  631.8 10.1 slice-start.6
  959.2 20.7 %slice-start = ((s8[8388608]{0:T(1024)(128)(4,1)}), s8[4194304]{0:T(1024)(128)(4,1)S(1)}, s32[]{:S(2)}) async-start(s8[8388608]{0:T(1024)(128)(4,1)} %bitcast.172), calls=%async_computation.13 | async-start | bytes 8388608
  959.2 20.7 %slice-start.2 = ((s8[8388608]{0:T(1024)(128)(4,1)}), s8[4194304]{0:T(1024)(128)(4,1)S(1)}, s32[]{:S(2)}) async-start(s8[8388608]{0:T(1024)(128)(4,1)} %bitcast.179), calls=%async_computation.15 | async-start | bytes 8388608
  968.0 11.8 slice-start.1
  968.0 11.8 slice-start.3
  979.9 6.0 copy-start.54
  985.8 39.9 %copy-start.11 = (bf16[4096,512]{1,0:T(8,128)(2,1)}, bf16[4096,512]{1,0:T(8,128)(2,1)S(1)}, u32[]{:S(2)}) copy-start(bf16[4096,512]{1,0:T(8,128)(2,1)S(1)} %fusion.48) | copy-start | bytes 12582916
  1014.4 11.3 copy-start.12
  1014.4 11.3 copy-start.14
  1014.5 11.3 copy-start.50
  1014.5 11.3 copy-start.56
  1025.7 7.1 copy-start.13
  1025.8 8.3 copy-start.10
  1034.1 5.5 copy-start.23
  1039.5 105.2 %reduce-scatter.7.cloned.1.call-start = ((), (), s32[]{:S(2)}) async-start(), calls=%async_computation.9 | async-start | bytes 6291456 | tf_op jit(solution)/shard_map/reduce_scatter | solution.py:166
  1050.8 196.6 %reduce-scatter.11.cloned.1.call-start = ((), (), s32[]{:S(2)}) async-start(), calls=%async_computation.11 | async-start | bytes 4325376 | tf_op jit(solution)/shard_map/reduce_scatter | solution.py:180
  1050.8 11.2 copy-start.6
  1050.8 11.2 copy-start.36
  1050.8 11.2 copy-start.52
  1061.7 11.6 copy-start.59
  1061.7 327.4 %reduce-scatter.9.cloned.1.call-start = ((), (), s32[]{:S(2)}) async-start(), calls=%async_computation.10 | async-start | bytes 4325376 | tf_op jit(solution)/shard_map/reduce_scatter | solution.py:179
  1084.4 63.5 %copy-start.60 = (f32[512]{0:T(512)S(1)}, f32[512]{0:T(512)}, u32[]{:S(2)}) copy-start(f32[512]{0:T(512)} %get-tuple-element.353) | copy-start | bytes 6148
  1084.4 105.8 %copy-start.38 = (f32[2048]{0:T(1024)S(1)}, f32[2048]{0:T(1024)}, u32[]{:S(2)}) copy-start(f32[2048]{0:T(1024)} %copy-done.37) | copy-start | bytes 24580
  1190.2 198.9 %copy-start.1 = (bf16[512,512]{1,0:T(8,128)(2,1)S(1)}, bf16[512,512]{1,0:T(8,128)(2,1)}, u32[]{:S(2)}) copy-start(bf16[512,512]{1,0:T(8,128)(2,1)} %param.27) | copy-start | bytes 1572868
  (15 other events, 11.4 us)
Sparse Core Ops, SparseCore 0:
  10.4 58.8 all-gather.4
  294.7 54.8 reduce-scatter.4
  470.6 55.1 all-gather.10
  1050.9 52.5 reduce-scatter.6
  1106.3 141.0 reduce-scatter.10
  1250.2 138.8 reduce-scatter.8
Sparse Core Ops, SparseCore 1:
  298.1 79.8 all-gather.6
  381.4 55.4 all-gather.8
  1039.6 96.4 all-reduce.131
where the time goes:
time: 1410 us; the launch traced here: 1400 us
  other arithmetic  572 us (41%)
  waiting for transfers between devices  393 us (28%)
  local copies, waits for them, and re-layouts  216 us (15%)
  matrix products  125 us (9%)
  blocking collectives  70.3 us (5%)
  between operations  18.7 us (1%)
    reduce_sum x16, other arithmetic, block_local(): return (summed, jnp.sum(weights * inflow[:, :, None, :, :], axis=3))  157 us
    reduce_sum x8, other arithmetic, block_local(): spread = summed[:, :, :, None, :] - summed[:, :, None, :, :]  145 us
    reduce_scatter x1, waiting for transfers between devices, on_device(): lax.psum_scatter(upper_part, ('dp', 'tensor'), scatter_dimension=1, tiled...  142 us
    another operation x40, other arithmetic, block_local(): summed = jnp.cumsum(keep_log, axis=2)  103 us
    dot_general x8, matrix products, contract(): lax.dot_general(left, right, (((left_dim,), (right_dim,)), ((), ())), pre...  79.5 us
    dynamic_update_slice x40, local copies, waits for them, and re-layouts, local_pass(): lax.map(jax.checkpoint(block_local), (shaped(keep_log), shaped(inflow)))  56.5 us
    reduce_scatter x1, waiting for transfers between devices, on_device(): lax.psum_scatter(jnp.dot(part, output_weight, preferred_element_type=jnp....  53.7 us
    all_gather x1, waiting for transfers between devices, on_device(): gathered = lax.all_gather(block_in, 'tensor', axis=0, tiled=True)  53.6 us
  transfers between devices with their start and end apart: 9, of which 7 were waited for; matrix products, arithmetic and copies ran while one was open for 16% of the time, Pallas kernels for 0%

commit v1 on v0

v1 whole, which is shorter than its diff:
```python
import functools

import jax
import jax.numpy as jnp
from jax import lax
from jax.experimental import pallas as pl
from jax.experimental.pallas import tpu as pltpu
from jax.sharding import PartitionSpec as P

EPSILON = 1e-06
LONGEST = 2048
SEGMENTS = 8
PLACES = 16
STEPS = 32
BLOCK = SEGMENTS * STEPS
GELU_SLOPE = 0.7978845608028654
GELU_CUBE = 0.044715
VMEM_BYTES = 56 * 1024 * 1024
F32 = jnp.float32
BF16 = jnp.bfloat16


def dot_nn(left, right):
    return lax.dot_general(left, right, (((1,), (0,)), ((), ())), preferred_element_type=F32)


def dot_nt(left, right):
    return lax.dot_general(left, right, (((1,), (1,)), ((), ())), preferred_element_type=F32)


def row_scale(rows):
    return lax.rsqrt(jnp.mean(rows * rows, -1, keepdims=True) + EPSILON)


def fold_rows(values):
    return jnp.sum(values.reshape(-1, 8, values.shape[-1]), 0)


def put_blocks(values, out, me, first):
    tall = values.shape[0] // PLACES
    for block in range(PLACES):
        there = pl.multiple_of((block ^ me) * tall, tall)
        out[pl.ds(there, tall), first : first + values.shape[1]] = values[block * tall : (block + 1) * tall].astype(out.dtype)


def interleave(block, scratch):
    lanes = scratch.shape[0]
    for lane in range(lanes):
        for run in range(SEGMENTS):
            part = block[run, :, lane * 128 : (lane + 1) * 128]
            scratch[lane, pl.ds(run, block.shape[1], stride=SEGMENTS), :] = part.astype(F32)
    return jnp.concatenate([scratch[lane] for lane in range(lanes)], -1)


def separate(values, scratch, out):
    lanes = scratch.shape[0]
    for lane in range(lanes):
        scratch[lane] = values[:, lane * 128 : (lane + 1) * 128]
    for run in range(SEGMENTS):
        parts = [scratch[lane, pl.ds(run, out.shape[1], stride=SEGMENTS), :] for lane in range(lanes)]
        out[run] = jnp.concatenate(parts, -1).astype(out.dtype)


def gates(forget_logit, admit_logit):
    top = jnp.maximum(jnp.maximum(-admit_logit, -forget_logit), 0.0)
    one = jnp.exp(-top)
    admit_exp = jnp.exp(-admit_logit - top)
    forget_exp = jnp.exp(-forget_logit - top)
    keep_part = one + admit_exp
    admit_part = one + forget_exp
    total = keep_part + admit_part
    inverse = pl.reciprocal(total, approx=True)
    inverse = inverse * (2.0 - total * inverse)
    keep = keep_part * inverse
    admit = admit_part * inverse
    return keep, admit, keep * (forget_exp * inverse), -admit * (admit_exp * inverse)


def product_of_runs(values):
    result = values[0:1]
    for run in range(1, SEGMENTS):
        result = result * values[run : run + 1]
    return result


def chain_runs(ends, gains, mask, carry, out):
    entering = mask[0:1] * carry
    out[0:1] = entering
    for run in range(1, SEGMENTS):
        entering = mask[run : run + 1] * (ends[run - 1 : run] + gains[run - 1 : run] * entering)
        out[run : run + 1] = entering


def mixer_kernel(first, *refs):
    if first:
        x_ref, gain_ref, *refs = refs
    else:
        normed_in, *refs = refs
    wf, wa, wv, bias, mask, carry, *refs = refs
    if first:
        x_out, normed_out, *refs = refs
    keep_out, admit_out, state_out, forget_fac, admit_fac, ends_out, *refs = refs
    logits, hs, ps, vs, fs, as_, enter, *refs = refs
    phase, block = pl.program_id(0), pl.program_id(1)
    channels = wf.shape[1]
    start = pl.multiple_of(block * BLOCK, BLOCK)

    @pl.when((phase == 0) & (block == 0))
    def _():
        hs[0:8, :] = jnp.zeros((8, channels), F32)
        ps[0:8, :] = jnp.ones((8, channels), F32)

    @pl.when(phase == 0)
    def _():
        if first:
            rows = interleave(x_ref[...], refs[0])
            x_out[...] = rows.astype(BF16)
            normed = (rows * row_scale(rows) * gain_ref[...]).astype(BF16)
            normed_out[...] = normed
        else:
            normed = normed_in[...]
        logits[:, :channels] = dot_nn(normed, wf[...])
        logits[:, channels : 2 * channels] = dot_nn(normed, wa[...])
        logits[:, 2 * channels :] = dot_nn(normed, wv[...])

        def some_rows(group, _):
            here = pl.multiple_of(group * 64, 64)
            there = pl.multiple_of(start + here, 64)
            for lane in range(0, channels, 128):
                cols = pl.ds(lane, 128)
                forget_logit = logits[pl.ds(here, 64), pl.ds(lane, 128)]
                admit_logit = logits[pl.ds(here, 64), pl.ds(channels + lane, 128)] + bias[:, lane : lane + 128]
                value = logits[pl.ds(here, 64), pl.ds(2 * channels + lane, 128)]
                keep, admit, forget_side, admit_side = gates(forget_logit, admit_logit)
                keep_out[pl.ds(here, 64), cols] = keep
                admit_out[pl.ds(here, 64), cols] = admit.astype(BF16)
                vs[pl.ds(there, 64), cols] = value
                fs[pl.ds(there, 64), cols] = forget_side
                as_[pl.ds(there, 64), cols] = admit_side
                inflow = admit * value
                state = hs[pl.ds(there, 8), cols]
                gain = ps[pl.ds(there, 8), cols]
                for step in range(8):
                    rows8 = slice(step * 8, step * 8 + 8)
                    state = keep[rows8] * state + inflow[rows8]
                    gain = gain * keep[rows8]
                    hs[pl.ds(there + 8 + step * 8, 8), cols] = state
                    ps[pl.ds(there + 8 + step * 8, 8), cols] = gain
            return 0

        lax.fori_loop(0, BLOCK // 64, some_rows, 0)

    @pl.when((phase == 1) & (block == 0))
    def _():
        total = hs.shape[0]
        ends, gains = hs[total - 8 : total, :], ps[total - 8 : total, :]
        chain_runs(ends, gains, mask, carry[...], enter)
        ends_out[0:1, :] = ends[7:8] + gains[7:8] * enter[7:8, :]
        ends_out[1:2, :] = product_of_runs(gains * mask[...])
        ends_out[2:8, :] = jnp.zeros((6, channels), F32)

    @pl.when(phase == 1)
    def _():
        def some_rows(group, _):
            here = pl.multiple_of(group * 64, 64)
            there = pl.multiple_of(start + here, 64)
            for lane in range(0, channels, 128):
                cols = pl.ds(lane, 128)
                entering = enter[:, lane : lane + 128]
                states = hs[pl.ds(there, 72), cols].reshape(9, 8, 128) + ps[pl.ds(there, 72), cols].reshape(9, 8, 128) * entering
                states = states.reshape(72, 128)
                state_out[pl.ds(here, 64), cols] = states[8:].astype(BF16)
                change = states[:64] - vs[pl.ds(there, 64), cols]
                forget_fac[pl.ds(here, 64), cols] = (change * fs[pl.ds(there, 64), cols]).astype(BF16)
                admit_fac[pl.ds(here, 64), cols] = (change * as_[pl.ds(there, 64), cols]).astype(BF16)
            return 0

        lax.fori_loop(0, BLOCK // 64, some_rows, 0)


def mixer_forward(first, rows_in, gain, weights, bias, mask, carry):
    width = rows_in.shape[-1]
    rows = rows_in.size // width
    channels = weights[0].shape[1]
    blocks = rows // BLOCK
    early = lambda phase, block: (jnp.where(phase == 0, block, blocks - 1), 0)
    late = lambda phase, block: (jnp.where(phase == 0, 0, block), 0)
    whole = lambda phase, block: (0, 0)
    if first:
        in_specs = [
            pl.BlockSpec((SEGMENTS, STEPS, width), lambda phase, block: (0, jnp.where(phase == 0, block, blocks - 1), 0)),
            pl.BlockSpec((1, width), whole),
        ]
        operands = [rows_in.reshape(SEGMENTS, rows // SEGMENTS, width), gain]
        out_specs = [pl.BlockSpec((BLOCK, width), early)] * 2
        out_shape = [jax.ShapeDtypeStruct((rows, width), BF16)] * 2
    else:
        in_specs, operands = [pl.BlockSpec((BLOCK, width), early)], [rows_in]
        out_specs, out_shape = [], []
    in_specs += [pl.BlockSpec((width, channels), whole)] * 3
    in_specs += [pl.BlockSpec((1, channels), whole), pl.BlockSpec((8, channels), whole), pl.BlockSpec((1, channels), whole)]
    out_specs += [pl.BlockSpec((BLOCK, channels), early)] * 2 + [pl.BlockSpec((BLOCK, channels), late)] * 3
    out_specs += [pl.BlockSpec((8, channels), whole)]
    out_shape += [jax.ShapeDtypeStruct((rows, channels), d) for d in (F32, BF16, BF16, BF16, BF16)]
    out_shape += [jax.ShapeDtypeStruct((8, channels), F32)]
    scratch = [pltpu.VMEM((BLOCK, 3 * channels), F32)]
    scratch += [pltpu.VMEM((rows + 8, channels), F32)] * 2
    scratch += [pltpu.VMEM((rows, channels), F32)] * 3
    scratch += [pltpu.VMEM((8, channels), F32)]
    if first:
        scratch += [pltpu.VMEM((width // 128, BLOCK, 128), F32)]
    return pl.pallas_call(
        functools.partial(mixer_kernel, first),
        grid=(2, blocks),
        in_specs=in_specs,
        out_specs=out_specs,
        out_shape=out_shape,
        scratch_shapes=scratch,
        compiler_params=pltpu.CompilerParams(vmem_limit_bytes=VMEM_BYTES, dimension_semantics=("arbitrary", "arbitrary")),
        cost_estimate=pl.CostEstimate(flops=2 * rows * width * 3 * channels, bytes_accessed=rows * channels * 16, transcendentals=4 * rows * channels),
        name="mixer_forward",
    )(*operands, *weights, bias, mask, carry)


def dense_kernel(sets, hidden_chunk, *refs):
    x_ref, c_ref, *refs = refs
    states, refs = refs[:sets], refs[sets:]
    outs_w, refs = refs[:sets], refs[sets:]
    gain_ref, w_ref, me_ref, *refs = refs
    out_ref, mixed_ref, grads_ref, slope_ref, *refs = refs
    outputs_ref, refs = refs[:sets], refs[sets:]
    upper_acc, lower_acc, output_acc, cotangent_s, out_s = refs
    step = pl.program_id(0)
    rows, width = x_ref.shape
    shards, both, _ = w_ref.shape
    half = both // 2
    per = hidden_chunk // half

    @pl.when(step == 0)
    def _():
        upper_acc[...] = jnp.zeros_like(upper_acc)
        lower_acc[...] = jnp.zeros_like(lower_acc)
        output_acc[...] = jnp.zeros_like(output_acc)
        slope_ref[...] = jnp.zeros_like(slope_ref)

    middle = x_ref[...].astype(F32)
    for state, weight in zip(states, outs_w):
        middle = middle + dot_nn(state[...], weight[...])
    scale = row_scale(middle)
    gain = gain_ref[...]
    dense_in = (middle * scale * gain).astype(BF16)
    dense_t = dense_in.T
    cotangent = interleave(c_ref[...], cotangent_s).astype(BF16)
    cotangent_t = cotangent.T
    fed, delta = None, None
    for chunk in range(shards // per):
        here = slice(chunk * per, chunk * per + per)
        cols = slice(chunk * hidden_chunk, (chunk + 1) * hidden_chunk)
        upper_w = w_ref[here, :half, :].reshape(hidden_chunk, width)
        lower_w = w_ref[here, half:, :].reshape(hidden_chunk, width)
        upper = dot_nt(dense_in, upper_w)
        square = upper * upper
        bell = 0.5 + 0.5 * jnp.tanh(upper * (GELU_SLOPE + GELU_SLOPE * GELU_CUBE * square))
        active = upper * bell
        slope = bell + active * (1.0 - bell) * (2.0 * GELU_SLOPE + 6.0 * GELU_SLOPE * GELU_CUBE * square)
        active = active.astype(BF16)
        part = dot_nn(active, lower_w)
        fed = part if fed is None else fed + part
        upper_delta = (slope * dot_nt(cotangent, lower_w)).astype(BF16)
        part = dot_nn(upper_delta, upper_w)
        delta = part if delta is None else delta + part
        lower_acc[:, cols] += dot_nn(cotangent_t, active)
        upper_acc[:, cols] += dot_nn(dense_t, upper_delta)
    separate(middle + fed, out_s, out_ref)
    slope_ref[...] += fold_rows(delta * middle * scale)
    scaled = delta * gain
    inner = jnp.mean(scaled * middle, -1, keepdims=True)
    mixed = (cotangent.astype(F32) + scale * (scaled - middle * (scale * scale * inner))).astype(BF16)
    mixed_ref[...] = mixed
    mixed_t = mixed.T
    channels = states[0].shape[1]
    for index, state in enumerate(states):
        output_acc[:, index * channels : (index + 1) * channels] += dot_nn(mixed_t, state[...])

    @pl.when(step == pl.num_programs(0) - 1)
    def _():
        for shard in range(0, shards, 2):
            cols = slice(shard * half, (shard + 2) * half)
            grads_ref[shard : shard + 2, :half, :] = upper_acc[:, cols].T.astype(BF16).reshape(2, half, width)
            grads_ref[shard : shard + 2, half:, :] = lower_acc[:, cols].T.astype(BF16).reshape(2, half, width)
        for index, output in enumerate(outputs_ref):
            put_blocks(output_acc[:, index * channels : (index + 1) * channels], output, me_ref[0], 0)


def dense_both(x_rows, cotangent, states, output_weights, gain, gathered, me):
    rows, width = x_rows.shape
    shards, both, _ = gathered.shape
    hidden = shards * both // 2
    channels = states[0].shape[1]
    sets = len(states)
    tall = min(rows, 512)
    by_rows = lambda block: (block, 0)
    by_runs = lambda block: (0, block, 0)
    whole = lambda block: (0, 0)
    runs_spec = pl.BlockSpec((SEGMENTS, tall // SEGMENTS, width), by_runs)
    in_specs = [pl.BlockSpec((tall, width), by_rows), runs_spec]
    in_specs += [pl.BlockSpec((tall, channels), by_rows)] * sets
    in_specs += [pl.BlockSpec((channels, width), whole)] * sets
    in_specs += [pl.BlockSpec((1, width), whole), pl.BlockSpec((shards, both, width), lambda block: (0, 0, 0))]
    in_specs += [pl.BlockSpec(memory_space=pltpu.SMEM)]
    return pl.pallas_call(
        functools.partial(dense_kernel, sets, 512),
        grid=(rows // tall,),
        in_specs=in_specs,
        out_specs=[
            runs_spec,
            pl.BlockSpec((tall, width), by_rows),
            pl.BlockSpec((shards, both, width), lambda block: (0, 0, 0)),
            pl.BlockSpec((8, width), whole),
        ]
        + [pl.BlockSpec((width, channels), whole)] * sets,
        out_shape=[
            jax.ShapeDtypeStruct((SEGMENTS, rows // SEGMENTS, width), BF16),
            jax.ShapeDtypeStruct((rows, width), BF16),
            jax.ShapeDtypeStruct((shards, both, width), BF16),
            jax.ShapeDtypeStruct((8, width), F32),
        ]
        + [jax.ShapeDtypeStruct((width, channels), BF16)] * sets,
        scratch_shapes=[
            pltpu.VMEM((width, hidden), F32),
            pltpu.VMEM((width, hidden), F32),
            pltpu.VMEM((width, sets * channels), F32),
            pltpu.VMEM((width // 128, tall, 128), F32),
            pltpu.VMEM((width // 128, tall, 128), F32),
        ],
        compiler_params=pltpu.CompilerParams(vmem_limit_bytes=VMEM_BYTES, dimension_semantics=("arbitrary",)),
        cost_estimate=pl.CostEstimate(flops=12 * rows * width * hidden, bytes_accessed=rows * width * 12, transcendentals=rows * hidden),
        name="dense_both",
    )(x_rows, cotangent.reshape(SEGMENTS, rows // SEGMENTS, width), *states, *output_weights, gain, gathered, me)


def mixer_back_kernel(mixed_ref, normed_ref, weight, keep_ref, admit_ref, forget_fac, admit_fac, mask, carry, output_grads, me_ref, *refs):
    delta_out, slopes_out, bias_out, ends_out, *refs = refs
    cs, ps, state_delta, slopes_acc, last, enter = refs
    phase, block = pl.program_id(0), pl.program_id(1)
    blocks = pl.num_programs(1)
    channels = keep_ref.shape[1]
    place = jnp.where(phase == 0, blocks - 1 - block, block)
    start = pl.multiple_of(place * BLOCK, BLOCK)

    @pl.when((phase == 0) & (block == 0))
    def _():
        last[0:8, :] = jnp.zeros((8, channels), F32)
        last[8:16, :] = jnp.ones((8, channels), F32)

    @pl.when(phase == 0)
    def _():
        state_delta[...] = dot_nt(mixed_ref[...], weight[...])

        def some_rows(turn, _):
            here = pl.multiple_of((BLOCK // 64 - 1 - turn) * 64, 64)
            there = pl.multiple_of(start + here, 64)
            for lane in range(0, channels, 128):
                cols = pl.ds(lane, 128)
                keep = keep_ref[pl.ds(here, 64), cols]
                fresh = state_delta[pl.ds(here, 64), cols]
                kept = last[0:8, cols]
                gain = last[8:16, cols]
                for step in range(7, -1, -1):
                    rows8 = slice(step * 8, step * 8 + 8)
                    carried = fresh[rows8] + kept
                    cs[pl.ds(there + step * 8, 8), cols] = carried
                    ps[pl.ds(there + step * 8, 8), cols] = gain
                    kept = keep[rows8] * carried
                    gain = gain * keep[rows8]
                last[0:8, cols] = kept
                last[8:16, cols] = gain
            return 0

        lax.fori_loop(0, BLOCK // 64, some_rows, 0)

    @pl.when((phase == 1) & (block == 0))
    def _():
        kept, gain = last[0:8, :], last[8:16, :]
        entering = carry[...]
        enter[7:8, :] = entering
        for run in range(SEGMENTS - 1, 0, -1):
            entering = mask[run : run + 1, :] * (kept[run : run + 1] + gain[run : run + 1] * entering)
            enter[run - 1 : run, :] = entering
        ends_out[0:1, :] = mask[0:1, :] * (kept[0:1] + gain[0:1] * entering)
        ends_out[1:2, :] = product_of_runs(gain * mask[...])
        ends_out[2:8, :] = jnp.zeros((6, channels), F32)
        slopes_acc[...] = jnp.zeros_like(slopes_acc)
        bias_out[...] = jnp.zeros_like(bias_out)

    @pl.when(phase == 1)
    def _():
        def some_rows(group, _):
            here = pl.multiple_of(group * 64, 64)
            there = pl.multiple_of(start + here, 64)
            for lane in range(0, channels, 128):
                cols = pl.ds(lane, 128)
                entering = enter[:, lane : lane + 128]
                carried = cs[pl.ds(there, 64), cols].reshape(8, 8, 128) + ps[pl.ds(there, 64), cols].reshape(8, 8, 128) * entering
                carried = carried.reshape(64, 128)
                admit_delta = (carried * admit_fac[pl.ds(here, 64), cols].astype(F32)).astype(BF16)
                delta_out[pl.ds(here, 64), pl.ds(lane, 128)] = (carried * forget_fac[pl.ds(here, 64), cols].astype(F32)).astype(BF16)
                delta_out[pl.ds(here, 64), pl.ds(channels + lane, 128)] = admit_delta
                delta_out[pl.ds(here, 64), pl.ds(2 * channels + lane, 128)] = (carried * admit_ref[pl.ds(here, 64), cols].astype(F32)).astype(BF16)
                bias_out[:, cols] += fold_rows(admit_delta.astype(F32))
            return 0

        lax.fori_loop(0, BLOCK // 64, some_rows, 0)
        normed_t = normed_ref[...].T
        for part in range(3):
            cols = slice(part * channels, (part + 1) * channels)
            slopes_acc[:, cols] += dot_nn(normed_t, delta_out[:, cols])

    @pl.when((phase == 1) & (block == blocks - 1))
    def _():
        for part in range(3):
            cols = slice(part * channels, (part + 1) * channels)
            put_blocks(slopes_acc[:, cols], slopes_out, me_ref[0], part * channels)
        slopes_out[:, 3 * channels :] = output_grads[...]


def mixer_backward(mixed, normed, weight, keep, admit, forget_fac, admit_fac, mask, carry, output_grads, me):
    rows, width = mixed.shape
    channels = keep.shape[1]
    blocks = rows // BLOCK
    back = lambda phase, block: (jnp.where(phase == 0, blocks - 1 - block, 0), 0)
    late = lambda phase, block: (jnp.where(phase == 0, 0, block), 0)
    whole = lambda phase, block: (0, 0)
    return pl.pallas_call(
        mixer_back_kernel,
        grid=(2, blocks),
        in_specs=[
            pl.BlockSpec((BLOCK, width), back),
            pl.BlockSpec((BLOCK, width), late),
            pl.BlockSpec((channels, width), whole),
            pl.BlockSpec((BLOCK, channels), back),
            pl.BlockSpec((BLOCK, channels), late),
            pl.BlockSpec((BLOCK, channels), late),
            pl.BlockSpec((BLOCK, channels), late),
            pl.BlockSpec((8, channels), whole),
            pl.BlockSpec((1, channels), whole),
            pl.BlockSpec((width, channels), whole),
            pl.BlockSpec(memory_space=pltpu.SMEM),
        ],
        out_specs=[
            pl.BlockSpec((BLOCK, 3 * channels), late),
            pl.BlockSpec((width, 4 * channels), whole),
            pl.BlockSpec((8, channels), whole),
            pl.BlockSpec((8, channels), whole),
        ],
        out_shape=[
            jax.ShapeDtypeStruct((rows, 3 * channels), BF16),
            jax.ShapeDtypeStruct((width, 4 * channels), BF16),
            jax.ShapeDtypeStruct((8, channels), F32),
            jax.ShapeDtypeStruct((8, channels), F32),
        ],
        scratch_shapes=[
            pltpu.VMEM((rows, channels), F32),
            pltpu.VMEM((rows, channels), F32),
            pltpu.VMEM((BLOCK, channels), F32),
            pltpu.VMEM((width, 3 * channels), F32),
            pltpu.VMEM((16, channels), F32),
            pltpu.VMEM((8, channels), F32),
        ],
        compiler_params=pltpu.CompilerParams(vmem_limit_bytes=VMEM_BYTES, dimension_semantics=("arbitrary", "arbitrary")),
        cost_estimate=pl.CostEstimate(flops=2 * rows * width * 4 * channels, bytes_accessed=rows * channels * 16, transcendentals=0),
        name="mixer_backward",
    )(mixed, normed, weight, keep, admit, forget_fac, admit_fac, mask, carry, output_grads, me)


def input_kernel(sets, *refs):
    x_ref, mixed_ref, gain_ref, *refs = refs
    deltas, refs = refs[:sets], refs[sets:]
    weights, refs = refs[: 3 * sets], refs[3 * sets :]
    out_ref, slope_ref, out_s = refs
    channels = weights[0].shape[1]

    @pl.when(pl.program_id(0) == 0)
    def _():
        slope_ref[...] = jnp.zeros_like(slope_ref)

    normed_delta = None
    for index in range(sets):
        for part in range(3):
            cols = slice(part * channels, (part + 1) * channels)
            term = dot_nt(deltas[index][:, cols], weights[3 * index + part][...])
            normed_delta = term if normed_delta is None else normed_delta + term
    rows = x_ref[...].astype(F32)
    scale = row_scale(rows)
    slope_ref[...] += fold_rows(normed_delta * rows * scale)
    scaled = normed_delta * gain_ref[...]
    inner = jnp.mean(scaled * rows, -1, keepdims=True)
    result = mixed_ref[...].astype(F32) + scale * (scaled - rows * (scale * scale * inner))
    separate(result, out_s, out_ref)


def input_backward(x_rows, mixed, gain, deltas, weights):
    rows, width = x_rows.shape
    sets = len(deltas)
    channels = weights[0].shape[1]
    by_rows = lambda block: (block, 0)
    whole = lambda block: (0, 0)
    return pl.pallas_call(
        functools.partial(input_kernel, sets),
        grid=(rows // BLOCK,),
        in_specs=[pl.BlockSpec((BLOCK, width), by_rows)] * 2
        + [pl.BlockSpec((1, width), whole)]
        + [pl.BlockSpec((BLOCK, 3 * channels), by_rows)] * sets
        + [pl.BlockSpec((width, channels), whole)] * (3 * sets),
        out_specs=[pl.BlockSpec((SEGMENTS, STEPS, width), lambda block: (0, block, 0)), pl.BlockSpec((8, width), whole)],
        out_shape=[jax.ShapeDtypeStruct((SEGMENTS, rows // SEGMENTS, width), F32), jax.ShapeDtypeStruct((8, width), F32)],
        scratch_shapes=[pltpu.VMEM((width // 128, BLOCK, 128), F32)],
        compiler_params=pltpu.CompilerParams(vmem_limit_bytes=VMEM_BYTES, dimension_semantics=("arbitrary",)),
        cost_estimate=pl.CostEstimate(flops=2 * rows * width * 3 * channels * sets, bytes_accessed=rows * channels * 6 * sets, transcendentals=0),
        name="input_backward",
    )(x_rows, mixed, gain, *deltas, *weights)


def finish_kernel(channels, sums_ref, me_ref, forget_out, admit_out, value_out, output_out, scratch):
    tall = sums_ref.shape[0] // PLACES
    for place in range(PLACES):
        there = pl.multiple_of((place ^ me_ref[0]) * tall, tall)
        here = slice(place * tall, (place + 1) * tall)
        for part, out in enumerate((forget_out, admit_out, value_out, scratch)):
            out[pl.ds(there, tall), :] = sums_ref[here, part * channels : (part + 1) * channels].astype(F32)
    output_out[...] = scratch[...].T


def finish_slopes(sums, me):
    width, channels = sums.shape[0], sums.shape[1] // 4
    return pl.pallas_call(
        functools.partial(finish_kernel, channels),
        in_specs=[pl.BlockSpec(memory_space=pltpu.VMEM), pl.BlockSpec(memory_space=pltpu.SMEM)],
        out_shape=[jax.ShapeDtypeStruct((width, channels), F32)] * 3 + [jax.ShapeDtypeStruct((channels, width), F32)],
        scratch_shapes=[pltpu.VMEM((width, channels), F32)],
        compiler_params=pltpu.CompilerParams(vmem_limit_bytes=VMEM_BYTES),
        name="finish_slopes",
    )(sums, me)


def run_masks(seq_lengths, rows, shift, channels):
    ends = jnp.cumsum(seq_lengths[0])
    begins = ends - seq_lengths[0]
    places = shift + jnp.arange(SEGMENTS, dtype=jnp.int32) * (rows // SEGMENTS)
    fresh = jnp.any((places[:, None] == begins[None, :]) & (seq_lengths[0] > 0)[None, :], -1)
    return jnp.broadcast_to(jnp.where(fresh, 0.0, 1.0).astype(F32)[:, None], (SEGMENTS, channels))


def regroup(stacked, half):
    count, both, width = stacked.shape
    if both == 2 * half:
        return stacked
    arrays = jnp.moveaxis(stacked.reshape(count, 2, both // 2, width), 1, 0).reshape(2, -1, half, width)
    return jnp.moveaxis(arrays, 0, 1).reshape(-1, 2 * half, width)


def added(mine, theirs):
    return (mine.astype(F32) + theirs.astype(F32)).astype(mine.dtype)


class Exchange:
    def __init__(self, count):
        self.count = count

    def swap(self, values, bit):
        pairs = [(device, device ^ bit) for device in range(self.count)]
        return lax.ppermute(values, ("dp", "tensor"), pairs)

    def grow(self, values, bit):
        return jnp.concatenate([values, self.swap(values, bit)], 0)

    def halve(self, values, bit):
        half = values.shape[0] // 2
        return added(values[:half], self.swap(values[half:], bit))


class Links:
    TENSOR, CORE, NEAR, Z_NEAR, Z_FAR = 1, 2, 4, 8, 16

    def __init__(self):
        self.exchange = Exchange(32)
        core = lax.axis_index("dp") % 2
        dp = lax.axis_index("dp")
        self.core = core
        self.me = (core * 8 + (dp // 2 % 2) * 4 + (dp // 4 % 2) * 2 + dp // 8).astype(jnp.int32)

    def weights(self, own_weights):
        parts = []
        for group in (own_weights[:3], own_weights[3:]):
            half = group[0].shape[0] // 2
            mine = jnp.stack([lax.dynamic_slice_in_dim(w, self.core * half, half) for w in group])
            got = self.exchange.swap(mine, self.TENSOR)
            rest = self.exchange.swap(got, self.CORE)
            first = self.core == 0
            whole = jnp.concatenate([jnp.where(first, got, rest), jnp.where(first, rest, got)], 1)
            parts += [whole[index] for index in range(len(group))]
        return own_weights, parts

    def bias(self, own_bias):
        return own_bias, self.exchange.swap(own_bias, self.TENSOR)

    def dense(self, shard):
        held = shard[None]
        for bit in (self.Z_NEAR, self.Z_FAR, self.NEAR, self.TENSOR, self.CORE):
            held = self.exchange.grow(held, bit)
        return held

    def dense_sums(self, grads):
        for bit in (self.CORE, self.TENSOR, self.NEAR, self.Z_FAR, self.Z_NEAR):
            grads = self.exchange.halve(grads, bit)
        return grads[0]

    def mixer_sums(self, own_grads, other_grads):
        sums = self.exchange.halve(own_grads, self.CORE)
        other = self.exchange.halve(other_grads, self.CORE)
        sums = added(sums, self.exchange.swap(other, self.TENSOR))
        for bit in (self.NEAR, self.Z_NEAR, self.Z_FAR):
            sums = self.exchange.halve(sums, bit)
        for bit in (self.Z_FAR, self.Z_NEAR, self.NEAR, self.CORE):
            sums = self.exchange.grow(sums, bit)
        return sums

    def small_sums(self, values):
        for bit in (self.CORE, self.TENSOR, self.NEAR, self.Z_NEAR, self.Z_FAR):
            values = values + self.exchange.swap(values, bit)
        return values


class Plain:
    def __init__(self, n_tensor, own):
        self.n_tensor, self.own = n_tensor, own
        self.me = jnp.int32(0)

    def halves(self, whole):
        middle = whole.shape[1] // 2
        return whole[:, :middle], whole[:, middle:]

    def weights(self, own_weights):
        pairs = [self.halves(lax.all_gather(w, "tensor", axis=1, tiled=True)) for w in own_weights[:3]]
        last = lax.all_gather(own_weights[3], "tensor", axis=0, tiled=True)
        pairs.append(tuple(jnp.split(last, 2, 0)))
        return [p[0] for p in pairs], [p[1] for p in pairs]

    def bias(self, own_bias):
        return tuple(jnp.split(lax.all_gather(own_bias, "tensor", axis=0, tiled=True), 2))

    def dense(self, shard):
        return regroup(lax.all_gather(shard, ("dp", "tensor"), axis=0), 64)

    def dense_sums(self, grads):
        count = lax.axis_size("dp") * self.n_tensor
        half = grads.shape[0] * grads.shape[1] // (2 * count)
        return lax.psum_scatter(regroup(grads, half), ("dp", "tensor"), scatter_dimension=0, tiled=True)[0]

    def mixer_sums(self, low_grads, high_grads):
        width = low_grads.shape[0]
        whole = jnp.concatenate([low_grads.reshape(width, 4, -1), high_grads.reshape(width, 4, -1)], 2)
        part = lax.psum_scatter(whole, "tensor", scatter_dimension=2, tiled=True)
        return lax.psum(part, "dp").reshape(width, 4 * self.own)

    def small_sums(self, values):
        return lax.psum(values, ("dp", "tensor"))


def on_device(
    block_in,
    out_cotangent,
    seq_lengths,
    premix_gain,
    forget_weight,
    admit_weight,
    value_weight,
    admit_bias,
    output_weight,
    dense_gain,
    upper_weight,
    lower_weight,
):
    n_dp, n_tensor = lax.axis_size("dp"), lax.axis_size("tensor")
    rows, width = block_in.shape
    place = lax.axis_index("tensor")
    own = forget_weight.shape[1]
    premix = premix_gain.astype(F32)[None]
    dense = dense_gain.astype(F32)[None]
    paired = (n_dp, n_tensor) == (16, 2)
    links = Links() if paired else Plain(n_tensor, own)
    me = links.me.reshape(1)

    weights = links.weights([forget_weight, admit_weight, value_weight, output_weight])
    biases = [b.astype(F32)[None] for b in links.bias(admit_bias)]
    gathered = links.dense(jnp.concatenate([upper_weight.T, lower_weight], 0))
    channels = weights[0][0].shape[1]

    mask = run_masks(seq_lengths, rows, place * rows, channels)
    crossing = rows % LONGEST != 0

    def chained(ends, backwards):
        every = lax.all_gather(ends, "tensor", axis=0)
        entering = jnp.zeros_like(ends[0:1])
        mine = entering
        order = range(n_tensor - 1, -1, -1) if backwards else range(n_tensor)
        for index in order:
            mine = jnp.where(place == index, entering, mine)
            entering = every[index, 0:1] + every[index, 1:2] * entering
        return mine

    nothing = jnp.zeros((1, channels), F32)

    def forward(first, rows_in, index):
        carry = nothing
        if crossing:
            ends = mixer_forward(first, rows_in, premix, weights[index][:3], biases[index], mask, carry)[-1]
            carry = chained(ends, False)
        return mixer_forward(first, rows_in, premix, weights[index][:3], biases[index], mask, carry)

    x_rows, normed, *kept_0 = forward(True, block_in, 0)
    kept_1 = forward(False, normed, 1)
    kept = [kept_0, kept_1]
    outputs = [w[3] for w in weights]
    block_out, mixed, dense_grads, dense_part, *output_grads = dense_both(
        x_rows, out_cotangent, [k[2] for k in kept], outputs, dense, gathered, me
    )

    def backward(index):
        keep, admit, _, forget_fac, admit_fac, _ = kept[index]
        args = (mixed, normed, outputs[index], keep, admit, forget_fac, admit_fac, mask)
        carry = nothing
        if crossing:
            carry = chained(mixer_backward(*args, carry, output_grads[index], me)[-1], True)
        return mixer_backward(*args, carry, output_grads[index], me)

    back_1 = backward(1)
    back_0 = backward(0)
    input_slope, premix_part = input_backward(x_rows, mixed, premix, [back_0[0], back_1[0]], weights[0][:3] + weights[1][:3])

    dense_sum = links.dense_sums(dense_grads).astype(F32)
    hidden = upper_weight.shape[1]
    upper_slope, lower_slope = dense_sum[:hidden].T, dense_sum[hidden:]
    sums = links.mixer_sums(back_0[1], back_1[1])
    forget_slope, admit_slope, value_slope, output_slope = finish_slopes(sums, me)
    bias_parts = [jnp.sum(b[2], 0) for b in (back_0, back_1)]
    if paired:
        bias_parts = [jnp.where(place == 0, bias_parts[0], bias_parts[1]), jnp.where(place == 0, bias_parts[1], bias_parts[0])]
    small = links.small_sums(jnp.concatenate([jnp.sum(premix_part, 0), jnp.sum(dense_part, 0)] + bias_parts, 0))
    shard = width // (n_dp * n_tensor)
    at = (lax.axis_index("dp") * n_tensor + place) * shard
    premix_slope = lax.dynamic_slice(small, (at,), (shard,))
    dense_slope = lax.dynamic_slice(small, (width + at,), (shard,))
    bias_slope = lax.dynamic_slice(small, (2 * width + place * own,), (own,))
    return (
        block_out.reshape(rows, width),
        input_slope.reshape(rows, width),
        premix_slope,
        forget_slope,
        admit_slope,
        value_slope,
        bias_slope,
        output_slope,
        dense_slope,
        upper_slope,
        lower_slope,
    )


def solution(mesh):
    placed = (
        P(("dp", "tensor"), None),
        P(("dp", "tensor"), None),
        P("dp", None),
        P(),
        P(None, "tensor"),
        P(None, "tensor"),
        P(None, "tensor"),
        P("tensor"),
        P("tensor", None),
        P(),
        P(None, ("dp", "tensor")),
        P(("dp", "tensor"), None),
    )
    return jax.shard_map(
        on_device,
        mesh=mesh,
        in_specs=placed,
        out_specs=(
            P(("dp", "tensor"), None),
            P(("dp", "tensor"), None),
            P(("dp", "tensor")),
            P(None, "tensor"),
            P(None, "tensor"),
            P(None, "tensor"),
            P("tensor"),
            P("tensor", None),
            P(("dp", "tensor")),
            P(None, ("dp", "tensor")),
            P(("dp", "tensor"), None),
        ),
        check_vma=False,
    )
```

time: 1410 us -> 353 us (0.25)
  other arithmetic: 572 us -> 16.3 us
  waiting for transfers between devices: 393 us -> 122 us
  local copies, waits for them, and re-layouts: 216 us -> 16.9 us
  Pallas kernels: 0 us -> 142 us
  matrix products: 125 us -> 0 us
  blocking collectives: 70.3 us -> 0 us
  starting transfers between devices: 0.58 us -> 49.7 us
  between operations: 18.7 us -> 1.05 us
    reduce_sum x29 -> x4, other arithmetic: 350 us -> 0.79 us  [the longest x1 0.73 us: on_device(): jnp.sum(premix_part, 0)]
    reduce_scatter x4 -> x0, waiting for transfers between devices: 244 us -> none  [the longest x1 142 us: on_device(): lax.psum_scatter(upper_part, ('dp', 'tensor'), scatter_dimension=1, tiled...]
    pallas_call x0 -> x7, Pallas kernels: none -> 142 us  [the longest x1 45.1 us: dense_both(): pl.pallas_call(functools.partial(dense_kernel, sets, 512), grid=(rows //...]
    dot_general x12 -> x0, matrix products: 125 us -> none  [the longest x8 79.5 us: contract(): lax.dot_general(left, right, (((left_dim,), (right_dim,)), ((), ())), pre...]
    all_gather x4 -> x0, waiting for transfers between devices: 124 us -> none  [the longest x1 53.6 us: on_device(): gathered = lax.all_gather(block_in, 'tensor', axis=0, tiled=True)]
    ppermute x0 -> x30, waiting for transfers between devices: none -> 122 us  [swap(): return lax.ppermute(values, ('dp', 'tensor'), pairs)]
    another operation x44 -> x2, other arithmetic: 121 us -> 1.65 us  [the longest x1 0.97 us: weights(): jnp.stack([lax.dynamic_slice_in_dim(w, self.core * half, half) for w in g...]
    dynamic_update_slice x40 -> x0, local copies, waits for them, and re-layouts: 56.5 us -> none  [local_pass(): lax.map(jax.checkpoint(block_local), (shaped(keep_log), shaped(inflow)))]
  transfers between devices with their start and end apart: 9 -> 30, of which waited for: 7 -> 17; matrix products, arithmetic and copies ran while one was open for 16% -> 8% of each run, Pallas kernels for 0% -> 21%
where the time goes in v1:
time: 353 us; the launch traced here: 348 us
  Pallas kernels  142 us (40%)
  waiting for transfers between devices  122 us (35%)
  starting transfers between devices  49.7 us (14%)
  local copies, waits for them, and re-layouts  16.9 us (5%)
  other arithmetic  16.3 us (5%)
    ppermute x30, waiting for transfers between devices, swap(): return lax.ppermute(values, ('dp', 'tensor'), pairs)  122 us
    ppermute x30, starting transfers between devices, swap(): return lax.ppermute(values, ('dp', 'tensor'), pairs)  49.7 us
    pallas_call x1, Pallas kernels, dense_both(): pl.pallas_call(functools.partial(dense_kernel, sets, 512), grid=(rows //...  45.1 us
    pallas_call x2, Pallas kernels, mixer_backward(): pl.pallas_call(mixer_back_kernel, grid=(2, blocks), in_specs=[pl.BlockSpe...  38.9 us
    pallas_call x2, Pallas kernels, mixer_forward(): pl.pallas_call(functools.partial(mixer_kernel, first), grid=(2, blocks),...  38.4 us
    pallas_call x1, Pallas kernels, input_backward(): pl.pallas_call(functools.partial(input_kernel, sets), grid=(rows // BLOCK...  15 us
  transfers between devices with their start and end apart: 30, of which 17 were waited for; matrix products, arithmetic and copies ran while one was open for 8% of the time, Pallas kernels for 21%

profile of v1, /device:TPU:1, one launch (start us, length us, event | category | flops | bytes accessed | tf_op | source)
XLA Modules:
  0.0 347.5 jit_solution(5352187255703483003)
XLA Ops:
  0.6 0.9 maximum_bitcast_fusion.1
  1.5 2.2 collective-permute-start.5
  3.7 3.2 collective-permute-done.5
  7.0 2.2 collective-permute-start.6
  9.2 11.7 %collective-permute-done.6 = bf16[2,128,512]{2,1,0:T(8,128)(2,1)S(1)} collective-permute-done((bf16[2,128,512]{2,1,0:T(8,128)(2,1)S(1)}, bf16[2,128,512]{2,1,0:T(8,128)(2,1)S(1)}, u32[]{:S(2)}, u32[]{:S(2)}) %collective-permute-start.6) | collective-permute-done | bytes 262176 | tf_op jit(solution)/shard_map/ppermute | solution.py:572
  20.9 1.0 collective-permute-start.7
  21.9 1.1 dynamic-slice_bitcast_fusion.1
  23.0 10.0 %collective-permute-done.7 = bf16[4,128,512]{2,1,0:T(8,128)(2,1)S(1)} collective-permute-done((bf16[4,128,512]{2,1,0:T(8,128)(2,1)S(1)}, bf16[4,128,512]{2,1,0:T(8,128)(2,1)S(1)}, u32[]{:S(2)}, u32[]{:S(2)}) %collective-permute-start.7) | collective-permute-done | bytes 524320 | tf_op jit(solution)/shard_map/ppermute | solution.py:572
  33.1 0.8 collective-permute-start.8
  33.9 1.0 pad_maximum_fusion.2
  34.9 0.7 collective-permute-start
  35.6 0.7 collective-permute-start.2
  36.4 0.8 collective-permute-start.3
  37.9 1.5 constant_dynamic-update-slice_fusion.4
  40.1 0.7 constant_dynamic-update-slice_fusion.2
  40.8 0.9 constant_dynamic-update-slice_fusion.1
  41.7 13.8 %collective-permute-done.8 = bf16[8,128,512]{2,1,0:T(8,128)(2,1)S(1)} collective-permute-done((bf16[8,128,512]{2,1,0:T(8,128)(2,1)S(1)}, bf16[8,128,512]{2,1,0:T(8,128)(2,1)S(1)}, u32[]{:S(2)}, u32[]{:S(2)}) %collective-permute-start.8) | collective-permute-done | bytes 1048608 | tf_op jit(solution)/shard_map/ppermute | solution.py:572
  55.5 1.1 constant_dynamic-update-slice_fusion
  56.6 6.1 %collective-permute-start.9 = (bf16[16,128,512]{2,1,0:T(8,128)(2,1)}, bf16[16,128,512]{2,1,0:T(8,128)(2,1)S(1)}, u32[]{:S(2)}, u32[]{:S(2)}) collective-permute-start(bf16[16,128,512]{2,1,0:T(8,128)(2,1)} %get-tuple-element.78), channel_id=1, source_target_pairs={{0,2},{1,3},{2,0},{3,1},{4,6},{5,7},{6,4},{7,5},{8,10},{9,11},{10,... | collective-permute-start | bytes 6291464 | tf_op jit(solution)/shard_map/ppermute | solution.py:572
  62.9 9.5 %collective-permute-done = bf16[3,256,512]{2,1,0:T(8,128)(2,1)} collective-permute-done((bf16[3,256,512]{2,1,0:T(8,128)(2,1)}, bf16[3,256,512]{2,1,0:T(8,128)(2,1)}, u32[]{:S(2)}, u32[]{:S(2)}) %collective-permute-start) | collective-permute-done | bytes 786464 | tf_op jit(solution)/shard_map/ppermute | solution.py:572
  72.4 6.1 %collective-permute-start.1 = (bf16[3,256,512]{2,1,0:T(8,128)(2,1)}, bf16[3,256,512]{2,1,0:T(8,128)(2,1)S(1)}, u32[]{:S(2)}, u32[]{:S(2)}) collective-permute-start(bf16[3,256,512]{2,1,0:T(8,128)(2,1)} %collective-permute-done), channel_id=1, source_target_pairs={{0,2},{1,3},{2,0},{3,1},{4,6},{5,7},{6,4},{7,5},{8,10},{9,11},{10,... | collective-permute-start | bytes 2359304 | tf_op jit(solution)/shard_map/ppermute | solution.py:572
  79.7 1.5 collective-permute-start.4
  82.5 19.7 %mixer_forward.2 = (bf16[2048,512]{1,0:T(8,128)(2,1)}, bf16[2048,512]{1,0:T(8,128)(2,1)}, f32[2048,512]{1,0:T(8,128)}, bf16[2048,512]{1,0:T(8,128)(2,1)}, bf16[2...) custom-call(bf16[8,256,512]{2,1,0:T(8,128)(2,1)} %bitcast.49, ...), custom_call_target="tpu_custom_call" | custom-call | flops 3221225472 | bytes 16777216 | tf_op jit(solution)/shard_map/mixer_forward/pallas_call | solution.py:212
  103.5 0.8 maximum_bitcast_fusion.refs_5_.weight
  104.3 1.2 broadcast_select_fusion
  105.6 1.2 fusion.4
  106.7 18.6 %mixer_forward.3 = (f32[2048,512]{1,0:T(8,128)}, bf16[2048,512]{1,0:T(8,128)(2,1)}, bf16[2048,512]{1,0:T(8,128)(2,1)}, bf16[2048,512]{1,0:T(8,128)(2,1)}, bf16[2048,512]{1,0:T(8,128)(2,1)}, /*index=5*/f32[8,512]{1,0:T(8,128)}) custom-call(bf16[2048,512]{1,0:T(8,128)(2,1)} %get-tuple-element.43.refs_0_.normed_ref, ...), custom_call_target="tpu_custom_call" | custom-call | flops 3221225472 | bytes 16777216 | tf_op jit(solution)/shard_map/mixer_forward/pallas_call | solution.py:212
  125.6 1.9 copy-done.12
  127.5 45.1 %dense_both.1 = (bf16[8,256,512]{2,1,0:T(8,128)(2,1)}, bf16[2048,512]{1,0:T(8,128)(2,1)}, bf16[32,128,512]{2,1,0:T(8,128)(2,1)}, f32[8,512]{1,0:T(8,128)}, bf16[...) custom-call(bf16[2048,512]{1,0:T(8,128)(2,1)} %get-tuple-element.41.refs_0_, bf16[8,256,512]{2,1,0:T(8,128)(2,1)} %bitcast.50, ...), custom_call_target="tpu_custom_call" | custom-call | flops 25769803776 | bytes 12582912 | tf_op jit(solution)/shard_map/dense_both/pallas_call | solution.py:311
  172.7 19.5 %mixer_backward.3 = (bf16[2048,1536]{1,0:T(8,128)(2,1)}, bf16[512,2048]{1,0:T(8,128)(2,1)}, f32[8,512]{1,0:T(8,128)}, f32[8,512]{1,0:T(8,128)}) custom-call(bf16[2048,512]{1,0:T(8,128)(2,1)} %get-tuple-element.46.mixed_ref.refs_1_, bf16[2048,512]{1,0:T(8,128)(2,1)} %get-tuple-element.43.refs_0_.normed_ref, ...), custom_call_target="tpu_custom_call" | custom-call | flops 4294967296 | bytes 16777216 | tf_op jit(solution)/shard_map/mixer_backward/pallas_call | solution.py:434
  192.2 1.3 slice.87
  193.6 19.3 %mixer_backward.2 = (bf16[2048,1536]{1,0:T(8,128)(2,1)}, bf16[512,2048]{1,0:T(8,128)(2,1)}, f32[8,512]{1,0:T(8,128)}, f32[8,512]{1,0:T(8,128)}) custom-call(bf16[2048,512]{1,0:T(8,128)(2,1)} %get-tuple-element.46.mixed_ref.refs_1_, bf16[2048,512]{1,0:T(8,128)(2,1)} %get-tuple-element.43.refs_0_.normed_ref, bf16[512,512]{1,0:T(8,128)(2,1)} %weight.1, ...), custom_call_target="tpu_custom_call" | custom-call | flops 4294967296 | bytes 16777216 | tf_op jit(solution)/shard_map/mixer_backward/pallas_call | solution.py:434
  213.0 1.4 slice.85
  215.4 0.8 collective-permute-start.17
  216.2 1.0 collective-permute-done.15
  217.3 22.6 %collective-permute-done.17 = bf16[256,2048]{1,0:T(8,128)(2,1)S(1)} collective-permute-done((bf16[256,2048]{1,0:T(8,128)(2,1)S(1)}, bf16[256,2048]{1,0:T(8,128)(2,1)S(1)}, u32[]{:S(2)}, u32[]{:S(2)}) %collective-permute-start.17) | collective-permute-done | bytes 1048608 | tf_op jit(solution)/shard_map/ppermute | solution.py:572
  240.4 0.8 collective-permute-start.18
  241.3 1.6 slice.95
  242.8 1.5 collective-permute-start.25
  244.3 8.4 %collective-permute-done.18 = bf16[128,2048]{1,0:T(8,128)(2,1)S(1)} collective-permute-done((bf16[128,2048]{1,0:T(8,128)(2,1)S(1)}, bf16[128,2048]{1,0:T(8,128)(2,1)S(1)}, u32[]{:S(2)}, u32[]{:S(2)}) %collective-permute-start.18) | collective-permute-done | bytes 524320 | tf_op jit(solution)/shard_map/ppermute | solution.py:572
  252.9 2.2 collective-permute-start.19
  255.1 15.0 %input_backward.1 = (f32[8,256,512]{2,1,0:T(8,128)}, f32[8,512]{1,0:T(8,128)}) custom-call(bf16[2048,512]{1,0:T(8,128)(2,1)} %get-tuple-element.41.refs_0_, bf16[2048,512]{1,0:T(8,128)(2,1)} %get-tuple-element.46.mixed_ref.refs_1_, f32[1,512]{1,0:T(1,128)} %bitcast.45, bf16[2048,1536]{1,0:T(8,128)(2,1)} %get-tuple-element.52.refs_3_, ...), custom_call_target="tpu_custom_call" | custom-call | flops 6442450944 | bytes 12582912 | tf_op jit(solution)/shard_map/input_backward/pallas_call | solution.py:508
  270.2 0.7 reduce_sum.36
  271.1 3.2 collective-permute-start.20
  274.3 2.9 add_convert_fusion
  277.2 1.1 slice.119
  278.3 1.2 collective-permute-start.26
  279.5 3.0 collective-permute-start.10
  283.6 17.1 %collective-permute-done.11 = f32[2048]{0:T(1024)S(1)} collective-permute-done((f32[2048]{0:T(1024)S(1)}, f32[2048]{0:T(1024)S(1)}, u32[]{:S(2)}, u32[]{:S(2)}) %collective-permute-start.11) | collective-permute-done | bytes 8224 | tf_op jit(solution)/shard_map/ppermute | solution.py:572
  300.7 1.2 collective-permute-start.12
  301.9 1.6 collective-permute-done.12
  303.8 2.2 collective-permute-done.13
  306.3 3.1 collective-permute-done.14
  310.2 1.3 collective-permute-start.27
  311.5 3.2 collective-permute-done.22
  314.7 1.3 collective-permute-start.23
  317.3 1.0 collective-permute-done.27
  318.6 9.6 %collective-permute-done.23 = bf16[128,2048]{1,0:T(8,128)(2,1)S(1)} collective-permute-done((bf16[128,2048]{1,0:T(8,128)(2,1)S(1)}, bf16[128,2048]{1,0:T(8,128)(2,1)S(1)}, u32[]{:S(2)}, u32[]{:S(2)}) %collective-permute-start.23) | collective-permute-done | bytes 524320 | tf_op jit(solution)/shard_map/ppermute | solution.py:572
  328.3 7.7 %collective-permute-start.24 = (bf16[256,2048]{1,0:T(8,128)(2,1)S(1)}, bf16[256,2048]{1,0:T(8,128)(2,1)S(1)}, u32[]{:S(2)}, u32[]{:S(2)}) collective-permute-start(bf16[256,2048]{1,0:T(8,128)(2,1)S(1)} %pad_maximum_fusion.1), channel_id=1, source_target_pairs={{0,2},{1,3},{2,0},{3,1},{4,6},{5,7},{6,4},{7,5},{8,10},{9,11},{10,... | collective-permute-start | bytes 3145736 | tf_op jit(solution)/shard_map/ppermute | solution.py:572
  336.1 1.2 collective-permute-start.29
  337.3 3.9 %collective-permute-done.29 = bf16[1,128,512]{2,1,0:T(8,128)(2,1)S(1)} collective-permute-done((bf16[1,128,512]{2,1,0:T(8,128)(2,1)S(1)}, bf16[1,128,512]{2,1,0:T(8,128)(2,1)S(1)}, u32[]{:S(2)}, u32[]{:S(2)}) %collective-permute-start.29) | collective-permute-done | bytes 131104 | tf_op jit(solution)/shard_map/ppermute | solution.py:572
  341.3 0.7 slice_bitcast_fusion
  342.1 1.3 copy-done.2
  343.4 4.1 %finish_slopes.1 = (f32[512,512]{1,0:T(8,128)}, f32[512,512]{1,0:T(8,128)}, f32[512,512]{1,0:T(8,128)}, f32[512,512]{1,0:T(8,128)}) custom-call(bf16[512,2048]{1,0:T(8,128)(2,1)} %copy-done.2, s32[1]{0:T(128)} %bitcast.18.refs_8_.me_ref), custom_call_target="tpu_custom_call" | custom-call | tf_op jit(solution)/shard_map/finish_slopes/pallas_call | solution.py:536
  (110 shorter events, 12.0 us)
Async XLA Ops:
  1.5 5.4 %collective-permute-start.5 = (bf16[1,128,512]{2,1,0:T(8,128)(2,1)S(1)}, bf16[1,128,512]{2,1,0:T(8,128)(2,1)S(1)}, u32[]{:S(2)}, u32[]{:S(2)}) collective-permute-start(bf16[1,128,512]{2,1,0:T(8,128)(2,1)S(1)} %maximum_bitcast_fusion.1), channel_id=1, source_target_pairs={{0,8},{1,9},{2,10},{3,11},{4,12},{5,13},{6,14},{7,15},{8,0},{9,1},... | collective-permute-start | bytes 393224 | tf_op jit(solution)/shard_map/ppermute | solution.py:572
  7.0 26.9 %copy-start.6 = (bf16[512,512]{1,0:T(8,128)(2,1)S(1)}, bf16[512,512]{1,0:T(8,128)(2,1)}, u32[]{:S(2)}) copy-start(bf16[512,512]{1,0:T(8,128)(2,1)} %refs_5_.1) | copy-start | bytes 1572868
  7.0 13.9 %collective-permute-start.6 = (bf16[2,128,512]{2,1,0:T(8,128)(2,1)S(1)}, bf16[2,128,512]{2,1,0:T(8,128)(2,1)S(1)}, u32[]{:S(2)}, u32[]{:S(2)}) collective-permute-start(bf16[2,128,512]{2,1,0:T(8,128)(2,1)S(1)} %pad_maximum_fusion.6), channel_id=1, source_target_pairs={{0,16},{1,17},{2,18},{3,19},{4,20},{5,21},{6,22},{7,23},{8,24},{9,... | collective-permute-start | bytes 786440 | tf_op jit(solution)/shard_map/ppermute | solution.py:572
  20.9 12.1 %collective-permute-start.7 = (bf16[4,128,512]{2,1,0:T(8,128)(2,1)S(1)}, bf16[4,128,512]{2,1,0:T(8,128)(2,1)S(1)}, u32[]{:S(2)}, u32[]{:S(2)}) collective-permute-start(bf16[4,128,512]{2,1,0:T(8,128)(2,1)S(1)} %pad_maximum_fusion.4), channel_id=1, source_target_pairs={{0,4},{1,5},{2,6},{3,7},{4,0},{5,1},{6,2},{7,3},{8,12},{9,13},{10,... | collective-permute-start | bytes 1572872 | tf_op jit(solution)/shard_map/ppermute | solution.py:572
  23.0 12.6 %copy-start.15 = (bf16[512]{0:T(512)(128)(2,1)S(1)}, bf16[512]{0:T(512)(128)(2,1)}, u32[]{:S(2)}) copy-start(bf16[512]{0:T(512)(128)(2,1)} %param.19) | copy-start | bytes 3076
  23.0 13.4 %copy-start.5 = (bf16[512,512]{1,0:T(8,128)(2,1)S(1)}, bf16[512,512]{1,0:T(8,128)(2,1)}, u32[]{:S(2)}) copy-start(bf16[512,512]{1,0:T(8,128)(2,1)} %weight.1) | copy-start | bytes 1572868
  23.0 14.2 %copy-start.16 = (s32[1,8]{1,0:T(1,128)S(1)}, s32[1,8]{1,0:T(1,128)}, u32[]{:S(2)}) copy-start(s32[1,8]{1,0:T(1,128)} %param.14) | copy-start | bytes 100
  33.1 22.4 %collective-permute-start.8 = (bf16[8,128,512]{2,1,0:T(8,128)(2,1)S(1)}, bf16[8,128,512]{2,1,0:T(8,128)(2,1)S(1)}, u32[]{:S(2)}, u32[]{:S(2)}) collective-permute-start(bf16[8,128,512]{2,1,0:T(8,128)(2,1)S(1)} %pad_maximum_fusion), channel_id=1, source_target_pairs={{0,1},{1,0},{2,3},{3,2},{4,5},{5,4},{6,7},{7,6},{8,9},{9,8},{10,11... | collective-permute-start | bytes 3145736 | tf_op jit(solution)/shard_map/ppermute | solution.py:572
  34.9 37.5 %collective-permute-start = (bf16[3,256,512]{2,1,0:T(8,128)(2,1)}, bf16[3,256,512]{2,1,0:T(8,128)(2,1)}, u32[]{:S(2)}, u32[]{:S(2)}) collective-permute-start(bf16[3,256,512]{2,1,0:T(8,128)(2,1)} %pad_maximum_fusion.2), channel_id=1, source_target_pairs={{0,1},{1,0},{2,3},{3,2},{4,5},{5,4},{6,7},{7,6},{8,9},{9,8},{10,11... | collective-permute-start | bytes 2359304 | tf_op jit(solution)/shard_map/ppermute | solution.py:572
  35.6 67.2 %collective-permute-start.2 = (bf16[512]{0:T(512)(128)(2,1)S(1)}, bf16[512]{0:T(512)(128)(2,1)S(1)}, u32[]{:S(2)}, u32[]{:S(2)}) collective-permute-start(bf16[512]{0:T(512)(128)(2,1)S(1)} %copy-done.15), channel_id=1, source_target_pairs={{0,1},{1,0},{2,3},{3,2},{4,5},{5,4},{6,7},{7,6},{8,9},{9,8},{10,11... | collective-permute-start | bytes 3080 | tf_op jit(solution)/shard_map/ppermute | solution.py:572
  36.4 43.3 %collective-permute-start.3 = (bf16[1,256,512]{2,1,0:T(8,128)(2,1)S(1)}, bf16[1,256,512]{2,1,0:T(8,128)(2,1)S(1)}, u32[]{:S(2)}, u32[]{:S(2)}) collective-permute-start(bf16[1,256,512]{2,1,0:T(8,128)(2,1)S(1)} %dynamic-slice_bitcast_fusion), channel_id=1, source_target_pairs={{0,1},{1,0},{2,3},{3,2},{4,5},{5,4},{6,7},{7,6},{8,9},{9,8},{10,11... | collective-permute-start | bytes 786440 | tf_op jit(solution)/shard_map/ppermute | solution.py:572
  40.8 21.9 %copy-start.17 = (s32[1,8]{1,0:T(1,128)S(1)}, s32[1,8]{1,0:T(1,128)}, u32[]{:S(2)}) copy-start(s32[1,8]{1,0:T(1,128)} %reduce-window_clone.1) | copy-start | bytes 100
  40.8 38.3 %copy-start.13 = (bf16[512]{0:T(512)(128)(2,1)S(1)}, bf16[512]{0:T(512)(128)(2,1)}, u32[]{:S(2)}) copy-start(bf16[512]{0:T(512)(128)(2,1)} %param.15) | copy-start | bytes 3076
  56.6 6.3 %copy-start.10 = (bf16[32,128,512]{2,1,0:T(8,128)(2,1)}, bf16[32,128,512]{2,1,0:T(8,128)(2,1)S(1)}, u32[]{:S(2)}) copy-start(bf16[32,128,512]{2,1,0:T(8,128)(2,1)S(1)} %get-tuple-element.79) | copy-start | bytes 12582916
  56.6 68.8 %collective-permute-start.9 = (bf16[16,128,512]{2,1,0:T(8,128)(2,1)}, bf16[16,128,512]{2,1,0:T(8,128)(2,1)S(1)}, u32[]{:S(2)}, u32[]{:S(2)}) collective-permute-start(bf16[16,128,512]{2,1,0:T(8,128)(2,1)} %get-tuple-element.78), channel_id=1, source_target_pairs={{0,2},{1,3},{2,0},{3,1},{4,6},{5,7},{6,4},{7,5},{8,10},{9,11},{10,... | collective-permute-start | bytes 6291464 | tf_op jit(solution)/shard_map/ppermute | solution.py:572
  72.4 31.9 %collective-permute-start.1 = (bf16[3,256,512]{2,1,0:T(8,128)(2,1)}, bf16[3,256,512]{2,1,0:T(8,128)(2,1)S(1)}, u32[]{:S(2)}, u32[]{:S(2)}) collective-permute-start(bf16[3,256,512]{2,1,0:T(8,128)(2,1)} %collective-permute-done), channel_id=1, source_target_pairs={{0,2},{1,3},{2,0},{3,1},{4,6},{5,7},{6,4},{7,5},{8,10},{9,11},{10,... | collective-permute-start | bytes 2359304 | tf_op jit(solution)/shard_map/ppermute | solution.py:572
  79.7 23.8 %collective-permute-start.4 = (bf16[1,256,512]{2,1,0:T(8,128)(2,1)S(1)}, bf16[1,256,512]{2,1,0:T(8,128)(2,1)S(1)}, u32[]{:S(2)}, u32[]{:S(2)}) collective-permute-start(bf16[1,256,512]{2,1,0:T(8,128)(2,1)S(1)} %collective-permute-done.3), channel_id=1, source_target_pairs={{0,2},{1,3},{2,0},{3,1},{4,6},{5,7},{6,4},{7,5},{8,10},{9,11},{10,... | collective-permute-start | bytes 786440 | tf_op jit(solution)/shard_map/ppermute | solution.py:572
  82.5 19.8 %copy-start.14 = (bf16[512]{0:T(512)(128)(2,1)S(1)}, bf16[512]{0:T(512)(128)(2,1)}, u32[]{:S(2)}) copy-start(bf16[512]{0:T(512)(128)(2,1)} %param.21) | copy-start | bytes 3076
  106.7 18.6 %copy-start.11 = (bf16[32,128,512]{2,1,0:T(8,128)(2,1)S(1)}, bf16[32,128,512]{2,1,0:T(8,128)(2,1)}, u32[]{:S(2)}) copy-start(bf16[32,128,512]{2,1,0:T(8,128)(2,1)} %copy-done.10) | copy-start | bytes 12582916
  125.6 2.0 copy-start.12
  193.6 21.4 %collective-permute-start.16 = (bf16[256,2048]{1,0:T(8,128)(2,1)S(1)}, bf16[256,2048]{1,0:T(8,128)(2,1)S(1)}, u32[]{:S(2)}, u32[]{:S(2)}) collective-permute-start(bf16[256,2048]{1,0:T(8,128)(2,1)S(1)} %slice.87), channel_id=1, source_target_pairs={{0,2},{1,3},{2,0},{3,1},{4,6},{5,7},{6,4},{7,5},{8,10},{9,11},{10,... | collective-permute-start | bytes 3145736 | tf_op jit(solution)/shard_map/ppermute | solution.py:572
  213.0 2.0 copy-start.3
  214.4 25.4 %copy-start.4 = (bf16[512,2048]{1,0:T(8,128)(2,1)S(1)}, bf16[512,2048]{1,0:T(8,128)(2,1)}, u32[]{:S(2)}) copy-start(bf16[512,2048]{1,0:T(8,128)(2,1)} %get-tuple-element.64) | copy-start | bytes 6291460
  214.4 2.8 collective-permute-start.15
  215.4 25.9 %copy-start = (bf16[32,128,512]{2,1,0:T(8,128)(2,1)S(1)}, bf16[32,128,512]{2,1,0:T(8,128)(2,1)}, u32[]{:S(2)}) copy-start(bf16[32,128,512]{2,1,0:T(8,128)(2,1)} %get-tuple-element.70) | copy-start | bytes 12582916
  215.4 24.4 %collective-permute-start.17 = (bf16[256,2048]{1,0:T(8,128)(2,1)S(1)}, bf16[256,2048]{1,0:T(8,128)(2,1)S(1)}, u32[]{:S(2)}, u32[]{:S(2)}) collective-permute-start(bf16[256,2048]{1,0:T(8,128)(2,1)S(1)} %add_convert_fusion.3), channel_id=1, source_target_pairs={{0,1},{1,0},{2,3},{3,2},{4,5},{5,4},{6,7},{7,6},{8,9},{9,8},{10,11... | collective-permute-start | bytes 3145736 | tf_op jit(solution)/shard_map/ppermute | solution.py:572
  240.4 12.3 %collective-permute-start.18 = (bf16[128,2048]{1,0:T(8,128)(2,1)S(1)}, bf16[128,2048]{1,0:T(8,128)(2,1)S(1)}, u32[]{:S(2)}, u32[]{:S(2)}) collective-permute-start(bf16[128,2048]{1,0:T(8,128)(2,1)S(1)} %slice.113), channel_id=1, source_target_pairs={{0,4},{1,5},{2,6},{3,7},{4,0},{5,1},{6,2},{7,3},{8,12},{9,13},{10,... | collective-permute-start | bytes 1572872 | tf_op jit(solution)/shard_map/ppermute | solution.py:572
  242.8 31.5 %collective-permute-start.25 = (bf16[16,128,512]{2,1,0:T(8,128)(2,1)}, bf16[16,128,512]{2,1,0:T(8,128)(2,1)}, u32[]{:S(2)}, u32[]{:S(2)}) collective-permute-start(bf16[16,128,512]{2,1,0:T(8,128)(2,1)} %slice.95), channel_id=1, source_target_pairs={{0,2},{1,3},{2,0},{3,1},{4,6},{5,7},{6,4},{7,5},{8,10},{9,11},{10,... | collective-permute-start | bytes 6291464 | tf_op jit(solution)/shard_map/ppermute | solution.py:572
  252.9 18.1 %collective-permute-start.19 = (bf16[64,2048]{1,0:T(8,128)(2,1)S(1)}, bf16[64,2048]{1,0:T(8,128)(2,1)S(1)}, u32[]{:S(2)}, u32[]{:S(2)}) collective-permute-start(bf16[64,2048]{1,0:T(8,128)(2,1)S(1)} %slice.115), channel_id=1, source_target_pairs={{0,8},{1,9},{2,10},{3,11},{4,12},{5,13},{6,14},{7,15},{8,0},{9,1},... | collective-permute-start | bytes 786440 | tf_op jit(solution)/shard_map/ppermute | solution.py:572
  255.1 15.1 %copy-start.8 = (f32[8,512]{1,0:T(8,128)S(1)}, f32[8,512]{1,0:T(8,128)}, u32[]{:S(2)}) copy-start(f32[8,512]{1,0:T(8,128)} %get-tuple-element.63) | copy-start | bytes 49156
  255.1 15.1 %copy-start.9 = (f32[8,512]{1,0:T(8,128)S(1)}, f32[8,512]{1,0:T(8,128)}, u32[]{:S(2)}) copy-start(f32[8,512]{1,0:T(8,128)} %get-tuple-element.62) | copy-start | bytes 49156
  255.1 15.8 %copy-start.7 = (f32[8,512]{1,0:T(8,128)S(1)}, f32[8,512]{1,0:T(8,128)}, u32[]{:S(2)}) copy-start(f32[8,512]{1,0:T(8,128)} %get-tuple-element.61) | copy-start | bytes 49156
  271.1 11.3 %collective-permute-start.20 = (bf16[32,2048]{1,0:T(8,128)(2,1)S(1)}, bf16[32,2048]{1,0:T(8,128)(2,1)S(1)}, u32[]{:S(2)}, u32[]{:S(2)}) collective-permute-start(bf16[32,2048]{1,0:T(8,128)(2,1)S(1)} %slice.117), channel_id=1, source_target_pairs={{0,16},{1,17},{2,18},{3,19},{4,20},{5,21},{6,22},{7,23},{8,24},{9,... | collective-permute-start | bytes 393224 | tf_op jit(solution)/shard_map/ppermute | solution.py:572
  278.3 31.6 %collective-permute-start.26 = (bf16[8,128,512]{2,1,0:T(8,128)(2,1)}, bf16[8,128,512]{2,1,0:T(8,128)(2,1)S(1)}, u32[]{:S(2)}, u32[]{:S(2)}) collective-permute-start(bf16[8,128,512]{2,1,0:T(8,128)(2,1)} %slice.119), channel_id=1, source_target_pairs={{0,1},{1,0},{2,3},{3,2},{4,5},{5,4},{6,7},{7,6},{8,9},{9,8},{10,11... | collective-permute-start | bytes 3145736 | tf_op jit(solution)/shard_map/ppermute | solution.py:572
  279.5 3.8 %collective-permute-start.10 = (f32[2048]{0:T(1024)S(1)}, f32[2048]{0:T(1024)S(1)}, u32[]{:S(2)}, u32[]{:S(2)}) collective-permute-start(f32[2048]{0:T(1024)S(1)} %pad_maximum_fusion.8), channel_id=1, source_target_pairs={{0,2},{1,3},{2,0},{3,1},{4,6},{5,7},{6,4},{7,5},{8,10},{9,11},{10,... | collective-permute-start | bytes 24584 | tf_op jit(solution)/shard_map/ppermute | solution.py:572
  283.1 26.3 %collective-permute-start.21 = (bf16[32,2048]{1,0:T(8,128)(2,1)S(1)}, bf16[32,2048]{1,0:T(8,128)(2,1)S(1)}, u32[]{:S(2)}, u32[]{:S(2)}) collective-permute-start(bf16[32,2048]{1,0:T(8,128)(2,1)S(1)} %get-tuple-element.72), channel_id=1, source_target_pairs={{0,16},{1,17},{2,18},{3,19},{4,20},{5,21},{6,22},{7,23},{8,24},{9,... | collective-permute-start | bytes 393224 | tf_op jit(solution)/shard_map/ppermute | solution.py:572
  283.3 17.4 %collective-permute-start.11 = (f32[2048]{0:T(1024)S(1)}, f32[2048]{0:T(1024)S(1)}, u32[]{:S(2)}, u32[]{:S(2)}) collective-permute-start(f32[2048]{0:T(1024)S(1)} %fusion.6), channel_id=1, source_target_pairs={{0,1},{1,0},{2,3},{3,2},{4,5},{5,4},{6,7},{7,6},{8,9},{9,8},{10,11... | collective-permute-start | bytes 24584 | tf_op jit(solution)/shard_map/ppermute | solution.py:572
  300.7 2.8 collective-permute-start.12
  303.5 2.5 collective-permute-start.13
  306.0 3.4 collective-permute-start.14
  309.4 7.9 %copy-start.1 = (bf16[512,2048]{1,0:T(8,128)(2,1)S(1)}, bf16[512,2048]{1,0:T(8,128)(2,1)}, u32[]{:S(2)}) copy-start(bf16[512,2048]{1,0:T(8,128)(2,1)} %get-tuple-element.71) | copy-start | bytes 6291460
  309.4 5.3 %collective-permute-start.22 = (bf16[64,2048]{1,0:T(8,128)(2,1)S(1)}, bf16[64,2048]{1,0:T(8,128)(2,1)S(1)}, u32[]{:S(2)}, u32[]{:S(2)}) collective-permute-start(bf16[64,2048]{1,0:T(8,128)(2,1)S(1)} %pad_maximum_fusion.7), channel_id=1, source_target_pairs={{0,8},{1,9},{2,10},{3,11},{4,12},{5,13},{6,14},{7,15},{8,0},{9,1},... | collective-permute-start | bytes 786440 | tf_op jit(solution)/shard_map/ppermute | solution.py:572
  310.2 8.1 %collective-permute-start.27 = (bf16[4,128,512]{2,1,0:T(8,128)(2,1)S(1)}, bf16[4,128,512]{2,1,0:T(8,128)(2,1)S(1)}, u32[]{:S(2)}, u32[]{:S(2)}) collective-permute-start(bf16[4,128,512]{2,1,0:T(8,128)(2,1)S(1)} %slice.121), channel_id=1, source_target_pairs={{0,4},{1,5},{2,6},{3,7},{4,0},{5,1},{6,2},{7,3},{8,12},{9,13},{10,... | collective-permute-start | bytes 1572872 | tf_op jit(solution)/shard_map/ppermute | solution.py:572
  314.7 13.5 %collective-permute-start.23 = (bf16[128,2048]{1,0:T(8,128)(2,1)S(1)}, bf16[128,2048]{1,0:T(8,128)(2,1)S(1)}, u32[]{:S(2)}, u32[]{:S(2)}) collective-permute-start(bf16[128,2048]{1,0:T(8,128)(2,1)S(1)} %pad_maximum_fusion.5), channel_id=1, source_target_pairs={{0,4},{1,5},{2,6},{3,7},{4,0},{5,1},{6,2},{7,3},{8,12},{9,13},{10,... | collective-permute-start | bytes 1572872 | tf_op jit(solution)/shard_map/ppermute | solution.py:572
  318.5 17.6 %collective-permute-start.28 = (bf16[2,128,512]{2,1,0:T(8,128)(2,1)S(1)}, bf16[2,128,512]{2,1,0:T(8,128)(2,1)S(1)}, u32[]{:S(2)}, u32[]{:S(2)}) collective-permute-start(bf16[2,128,512]{2,1,0:T(8,128)(2,1)S(1)} %slice.123), channel_id=1, source_target_pairs={{0,16},{1,17},{2,18},{3,19},{4,20},{5,21},{6,22},{7,23},{8,24},{9,... | collective-permute-start | bytes 786440 | tf_op jit(solution)/shard_map/ppermute | solution.py:572
  328.3 13.7 %collective-permute-start.24 = (bf16[256,2048]{1,0:T(8,128)(2,1)S(1)}, bf16[256,2048]{1,0:T(8,128)(2,1)S(1)}, u32[]{:S(2)}, u32[]{:S(2)}) collective-permute-start(bf16[256,2048]{1,0:T(8,128)(2,1)S(1)} %pad_maximum_fusion.1), channel_id=1, source_target_pairs={{0,2},{1,3},{2,0},{3,1},{4,6},{5,7},{6,4},{7,5},{8,10},{9,11},{10,... | collective-permute-start | bytes 3145736 | tf_op jit(solution)/shard_map/ppermute | solution.py:572
  336.1 5.1 %collective-permute-start.29 = (bf16[1,128,512]{2,1,0:T(8,128)(2,1)S(1)}, bf16[1,128,512]{2,1,0:T(8,128)(2,1)S(1)}, u32[]{:S(2)}, u32[]{:S(2)}) collective-permute-start(bf16[1,128,512]{2,1,0:T(8,128)(2,1)S(1)} %slice.125), channel_id=1, source_target_pairs={{0,8},{1,9},{2,10},{3,11},{4,12},{5,13},{6,14},{7,15},{8,0},{9,1},... | collective-permute-start | bytes 393224 | tf_op jit(solution)/shard_map/ppermute | solution.py:572
  342.1 1.3 copy-start.2

commit v2 on v1

v2 whole, which is shorter than its diff:
```python
import functools

import jax
import jax.numpy as jnp
from jax import lax
from jax.experimental import pallas as pl
from jax.experimental.pallas import tpu as pltpu
from jax.sharding import PartitionSpec as P

EPSILON = 1e-06
LONGEST = 2048
SEGMENTS = 8
PLACES = 16
STEPS = 64
BLOCK = SEGMENTS * STEPS
GROUP = 32
GELU_SLOPE = 0.7978845608028654
GELU_CUBE = 0.044715
VMEM_BYTES = 56 * 1024 * 1024
F32 = jnp.float32
BF16 = jnp.bfloat16


def dot_nn(left, right):
    return lax.dot_general(left, right, (((1,), (0,)), ((), ())), preferred_element_type=F32)


def dot_nt(left, right):
    return lax.dot_general(left, right, (((1,), (1,)), ((), ())), preferred_element_type=F32)


def row_scale(rows):
    return lax.rsqrt(jnp.mean(rows * rows, -1, keepdims=True) + EPSILON)


def fold_rows(values):
    return jnp.sum(values.reshape(-1, 8, values.shape[-1]), 0)


def put_blocks(values, halves, me, first):
    tall = values.shape[0] // PLACES
    for place in range(PLACES):
        block = pl.multiple_of((place ^ me) * tall, tall)
        there = (place % (PLACES // 2)) * tall
        out = halves[place // (PLACES // 2)]
        out[there : there + tall, first : first + values.shape[1]] = values[pl.ds(block, tall), :].astype(out.dtype)


def interleave(block, scratch):
    lanes = scratch.shape[0]
    for lane in range(lanes):
        for run in range(SEGMENTS):
            part = block[run, :, lane * 128 : (lane + 1) * 128]
            scratch[lane, pl.ds(run, block.shape[1], stride=SEGMENTS), :] = part.astype(F32)
    return jnp.concatenate([scratch[lane] for lane in range(lanes)], -1)


def separate(values, scratch, out):
    lanes = scratch.shape[0]
    for lane in range(lanes):
        scratch[lane] = values[:, lane * 128 : (lane + 1) * 128]
    for run in range(SEGMENTS):
        parts = [scratch[lane, pl.ds(run, out.shape[1], stride=SEGMENTS), :] for lane in range(lanes)]
        out[run] = jnp.concatenate(parts, -1).astype(out.dtype)


def gates(forget_logit, admit_logit):
    top = jnp.maximum(jnp.maximum(-admit_logit, -forget_logit), 0.0)
    one = jnp.exp(-top)
    admit_exp = jnp.exp(-admit_logit - top)
    forget_exp = jnp.exp(-forget_logit - top)
    keep_part = one + admit_exp
    admit_part = one + forget_exp
    total = keep_part + admit_part
    inverse = pl.reciprocal(total, approx=True)
    inverse = inverse * (2.0 - total * inverse)
    keep = keep_part * inverse
    admit = admit_part * inverse
    return keep, admit, keep * (forget_exp * inverse), -admit * (admit_exp * inverse)


def product_of_runs(values):
    result = values[0:1]
    for run in range(1, SEGMENTS):
        result = result * values[run : run + 1]
    return result


def chain_runs(ends, gains, mask, carry, out):
    entering = mask[0:1] * carry
    out[0:1] = entering
    for run in range(1, SEGMENTS):
        entering = mask[run : run + 1] * (ends[run - 1 : run] + gains[run - 1 : run] * entering)
        out[run : run + 1] = entering


def mixer_kernel(first, *refs):
    if first:
        x_ref, gain_ref, *refs = refs
    else:
        normed_in, *refs = refs
    wf, wa, wv, bias, mask, carry, *refs = refs
    if first:
        x_out, normed_out, *refs = refs
    admit_out, state_out, forget_fac, admit_fac, ends_out, *refs = refs
    logits, hs, ps, vs, fs, as_, enter, *refs = refs
    phase, block = pl.program_id(0), pl.program_id(1)
    channels = wf.shape[1]
    start = pl.multiple_of(block * BLOCK, BLOCK)

    @pl.when((phase == 0) & (block == 0))
    def _():
        hs[0:8, :] = jnp.zeros((8, channels), F32)
        ps[0:8, :] = jnp.ones((8, channels), F32)

    @pl.when(phase == 0)
    def _():
        if first:
            rows = interleave(x_ref[...], refs[0])
            x_out[...] = rows.astype(BF16)
            normed = (rows * row_scale(rows) * gain_ref[...]).astype(BF16)
            normed_out[...] = normed
        else:
            normed = normed_in[...]
        wide = min(channels, 256)
        for chunk in range(channels // wide):
            cols = slice(chunk * wide, (chunk + 1) * wide)
            for part, weight in enumerate((wf, wa, wv)):
                logits[chunk, part] = dot_nn(normed, weight[:, cols])
        for chunk in range(channels // wide):
            for lane in range(0, wide, 128):
                inner, cols = slice(lane, lane + 128), slice(chunk * wide + lane, chunk * wide + lane + 128)
                state, gain = hs[pl.ds(start, 8), cols], ps[pl.ds(start, 8), cols]
                for here in range(0, BLOCK, GROUP):
                    rows = slice(here, here + GROUP)
                    there = pl.ds(start + here, GROUP)
                    value = logits[chunk, 2, rows, inner]
                    keep, admit, forget_side, admit_side = gates(
                        logits[chunk, 0, rows, inner], logits[chunk, 1, rows, inner] + bias[:, cols]
                    )
                    admit_out[rows, cols] = admit.astype(BF16)
                    vs[there, cols] = value
                    fs[there, cols] = forget_side
                    as_[there, cols] = admit_side
                    inflow = admit * value
                    for step in range(0, GROUP, 8):
                        state = keep[step : step + 8] * state + inflow[step : step + 8]
                        gain = gain * keep[step : step + 8]
                        hs[pl.ds(start + here + step + 8, 8), cols] = state
                        ps[pl.ds(start + here + step + 8, 8), cols] = gain

    @pl.when((phase == 1) & (block == 0))
    def _():
        total = hs.shape[0]
        ends, gains = hs[total - 8 : total, :], ps[total - 8 : total, :]
        chain_runs(ends, gains, mask, carry[...], enter)
        ends_out[0:1, :] = ends[7:8] + gains[7:8] * enter[7:8, :]
        ends_out[1:2, :] = product_of_runs(gains * mask[...])
        ends_out[2:8, :] = jnp.zeros((6, channels), F32)

    @pl.when(phase == 1)
    def _():
        def some_rows(group, _):
            here = pl.multiple_of(group * 64, 64)
            there = pl.multiple_of(start + here, 64)
            for lane in range(0, channels, 128):
                cols = pl.ds(lane, 128)
                entering = enter[:, lane : lane + 128]
                states = hs[pl.ds(there, 72), cols].reshape(9, 8, 128) + ps[pl.ds(there, 72), cols].reshape(9, 8, 128) * entering
                states = states.reshape(72, 128)
                state_out[pl.ds(here, 64), cols] = states[8:].astype(BF16)
                change = states[:64] - vs[pl.ds(there, 64), cols]
                forget_fac[pl.ds(here, 64), cols] = (change * fs[pl.ds(there, 64), cols]).astype(BF16)
                admit_fac[pl.ds(here, 64), cols] = (change * as_[pl.ds(there, 64), cols]).astype(BF16)
            return 0

        lax.fori_loop(0, BLOCK // 64, some_rows, 0)


def mixer_forward(first, rows_in, gain, weights, bias, mask, carry):
    width = rows_in.shape[-1]
    rows = rows_in.size // width
    channels = weights[0].shape[1]
    blocks = rows // BLOCK
    early = lambda phase, block: (jnp.where(phase == 0, block, blocks - 1), 0)
    late = lambda phase, block: (jnp.where(phase == 0, 0, block), 0)
    whole = lambda phase, block: (0, 0)
    if first:
        in_specs = [
            pl.BlockSpec((SEGMENTS, STEPS, width), lambda phase, block: (0, jnp.where(phase == 0, block, blocks - 1), 0)),
            pl.BlockSpec((1, width), whole),
        ]
        operands = [rows_in.reshape(SEGMENTS, rows // SEGMENTS, width), gain]
        out_specs = [pl.BlockSpec((BLOCK, width), early)] * 2
        out_shape = [jax.ShapeDtypeStruct((rows, width), BF16)] * 2
    else:
        in_specs, operands = [pl.BlockSpec((BLOCK, width), early)], [rows_in]
        out_specs, out_shape = [], []
    in_specs += [pl.BlockSpec((width, channels), whole)] * 3
    in_specs += [pl.BlockSpec((1, channels), whole), pl.BlockSpec((8, channels), whole), pl.BlockSpec((1, channels), whole)]
    out_specs += [pl.BlockSpec((BLOCK, channels), early)] + [pl.BlockSpec((BLOCK, channels), late)] * 3
    out_specs += [pl.BlockSpec((8, channels), whole)]
    out_shape += [jax.ShapeDtypeStruct((rows, channels), BF16)] * 4
    out_shape += [jax.ShapeDtypeStruct((8, channels), F32)]
    wide = min(channels, 256)
    scratch = [pltpu.VMEM((channels // wide, 3, BLOCK, wide), F32)]
    scratch += [pltpu.VMEM((rows + 8, channels), F32)] * 2
    scratch += [pltpu.VMEM((rows, channels), F32)] * 3
    scratch += [pltpu.VMEM((8, channels), F32)]
    if first:
        scratch += [pltpu.VMEM((width // 128, BLOCK, 128), F32)]
    return pl.pallas_call(
        functools.partial(mixer_kernel, first),
        grid=(2, blocks),
        in_specs=in_specs,
        out_specs=out_specs,
        out_shape=out_shape,
        scratch_shapes=scratch,
        compiler_params=pltpu.CompilerParams(vmem_limit_bytes=VMEM_BYTES, dimension_semantics=("arbitrary", "arbitrary")),
        cost_estimate=pl.CostEstimate(flops=2 * rows * width * 3 * channels, bytes_accessed=rows * channels * 16, transcendentals=4 * rows * channels),
        name="mixer_forward",
    )(*operands, *weights, bias, mask, carry)


def dense_kernel(sets, hidden_chunk, *refs):
    x_ref, c_ref, *refs = refs
    states, refs = refs[:sets], refs[sets:]
    outs_w, refs = refs[:sets], refs[sets:]
    gain_ref, w_ref, me_ref, *refs = refs
    out_ref, mixed_ref, upper_keep, upper_send, lower_keep, lower_send, slope_ref, *refs = refs
    outputs_ref, refs = refs[:sets], refs[sets:]
    upper_acc, lower_acc, output_acc, cotangent_s, out_s = refs
    step = pl.program_id(0)
    rows, width = x_ref.shape
    shards, both, _ = w_ref.shape
    half = both // 2
    per = hidden_chunk // half

    @pl.when(step == 0)
    def _():
        upper_acc[...] = jnp.zeros_like(upper_acc)
        lower_acc[...] = jnp.zeros_like(lower_acc)
        output_acc[...] = jnp.zeros_like(output_acc)
        slope_ref[...] = jnp.zeros_like(slope_ref)

    middle = x_ref[...].astype(F32)
    for state, weight in zip(states, outs_w):
        middle = middle + dot_nn(state[...], weight[...])
    scale = row_scale(middle)
    gain = gain_ref[...]
    dense_in = (middle * scale * gain).astype(BF16)
    dense_t = dense_in.T
    cotangent = interleave(c_ref[...], cotangent_s).astype(BF16)
    cotangent_t = cotangent.T
    fed, delta = None, None
    for chunk in range(shards // per):
        here = slice(chunk * per, chunk * per + per)
        cols = slice(chunk * hidden_chunk, (chunk + 1) * hidden_chunk)
        upper_w = w_ref[here, :half, :].reshape(hidden_chunk, width)
        lower_w = w_ref[here, half:, :].reshape(hidden_chunk, width)
        upper = dot_nt(dense_in, upper_w)
        square = upper * upper
        bell = 0.5 + 0.5 * jnp.tanh(upper * (GELU_SLOPE + GELU_SLOPE * GELU_CUBE * square))
        active = upper * bell
        slope = bell + active * (1.0 - bell) * (2.0 * GELU_SLOPE + 6.0 * GELU_SLOPE * GELU_CUBE * square)
        active = active.astype(BF16)
        part = dot_nn(active, lower_w)
        fed = part if fed is None else fed + part
        upper_delta = (slope * dot_nt(cotangent, lower_w)).astype(BF16)
        part = dot_nn(upper_delta, upper_w)
        delta = part if delta is None else delta + part
        lower_acc[:, cols] += dot_nn(cotangent_t, active)
        upper_acc[:, cols] += dot_nn(dense_t, upper_delta)
    separate(middle + fed, out_s, out_ref)
    slope_ref[...] += fold_rows(delta * middle * scale)
    scaled = delta * gain
    inner = jnp.mean(scaled * middle, -1, keepdims=True)
    mixed = (cotangent.astype(F32) + scale * (scaled - middle * (scale * scale * inner))).astype(BF16)
    mixed_ref[...] = mixed
    mixed_t = mixed.T
    channels = states[0].shape[1]
    for index, state in enumerate(states):
        output_acc[:, index * channels : (index + 1) * channels] += dot_nn(mixed_t, state[...])

    @pl.when(step == pl.num_programs(0) - 1)
    def _():
        for shard in range(0, shards, 2):
            cols = slice(shard * half, (shard + 2) * half)
            upper_ref, lower_ref = (upper_keep, lower_keep) if shard < shards // 2 else (upper_send, lower_send)
            there = shard % (shards // 2)
            upper_ref[there : there + 2] = upper_acc[:, cols].T.astype(BF16).reshape(2, half, width)
            lower_ref[there : there + 2] = lower_acc[:, cols].T.astype(BF16).reshape(2, half, width)
        for index, output in enumerate(outputs_ref):
            tall = output_acc.shape[0] // PLACES
            for place in range(PLACES):
                there = pl.multiple_of((place ^ me_ref[1]) * tall, tall)
                output[place * tall : (place + 1) * tall, :] = output_acc[pl.ds(there, tall), index * channels : (index + 1) * channels].astype(BF16)


def dense_both(x_rows, cotangent, states, output_weights, gain, gathered, me):
    rows, width = x_rows.shape
    shards, both, _ = gathered.shape
    hidden = shards * both // 2
    channels = states[0].shape[1]
    sets = len(states)
    tall = min(rows, 512)
    by_rows = lambda block: (block, 0)
    by_runs = lambda block: (0, block, 0)
    whole = lambda block: (0, 0)
    runs_spec = pl.BlockSpec((SEGMENTS, tall // SEGMENTS, width), by_runs)
    in_specs = [pl.BlockSpec((tall, width), by_rows), runs_spec]
    in_specs += [pl.BlockSpec((tall, channels), by_rows)] * sets
    in_specs += [pl.BlockSpec((channels, width), whole)] * sets
    in_specs += [pl.BlockSpec((1, width), whole), pl.BlockSpec((shards, both, width), lambda block: (0, 0, 0))]
    in_specs += [pl.BlockSpec(memory_space=pltpu.SMEM)]
    return pl.pallas_call(
        functools.partial(dense_kernel, sets, 512),
        grid=(rows // tall,),
        in_specs=in_specs,
        out_specs=[
            runs_spec,
            pl.BlockSpec((tall, width), by_rows),
        ]
        + [pl.BlockSpec((shards // 2, both // 2, width), lambda block: (0, 0, 0))] * 4
        + [pl.BlockSpec((8, width), whole)]
        + [pl.BlockSpec((width, channels), whole)] * sets,
        out_shape=[
            jax.ShapeDtypeStruct((SEGMENTS, rows // SEGMENTS, width), BF16),
            jax.ShapeDtypeStruct((rows, width), BF16),
        ]
        + [jax.ShapeDtypeStruct((shards // 2, both // 2, width), BF16)] * 4
        + [jax.ShapeDtypeStruct((8, width), F32)]
        + [jax.ShapeDtypeStruct((width, channels), BF16)] * sets,
        scratch_shapes=[
            pltpu.VMEM((width, hidden), F32),
            pltpu.VMEM((width, hidden), F32),
            pltpu.VMEM((width, sets * channels), F32),
            pltpu.VMEM((width // 128, tall, 128), F32),
            pltpu.VMEM((width // 128, tall, 128), F32),
        ],
        compiler_params=pltpu.CompilerParams(vmem_limit_bytes=VMEM_BYTES, dimension_semantics=("arbitrary",)),
        cost_estimate=pl.CostEstimate(flops=12 * rows * width * hidden, bytes_accessed=rows * width * 12, transcendentals=rows * hidden),
        name="dense_both",
    )(x_rows, cotangent.reshape(SEGMENTS, rows // SEGMENTS, width), *states, *output_weights, gain, gathered, me)


def mixer_back_kernel(sets, mixed_ref, normed_ref, mask, me_ref, *refs):
    per_set = [refs[index * 6 : index * 6 + 6] for index in range(sets)]
    refs = refs[6 * sets :]
    carried_out, refs = refs[:sets], refs[sets:]
    first_out, second_out, refs = refs[:2], refs[2:4], refs[4:]
    bias_out, ends_out, *refs = refs
    cs, ps, state_delta, admits, deltas, slopes_acc, last, enter = refs
    phase, block = pl.program_id(0), pl.program_id(1)
    blocks = pl.num_programs(1)
    channels = mask.shape[1]
    place = jnp.where(phase == 0, blocks - 1 - block, block)
    start = pl.multiple_of(place * BLOCK, BLOCK)

    @pl.when((phase == 0) & (block == 0))
    def _():
        last[:, 0:8, :] = jnp.zeros((sets, 8, channels), F32)
        last[:, 8:16, :] = jnp.ones((sets, 8, channels), F32)

    @pl.when(phase == 0)
    def _():
        for index in range(sets):
            state_delta[index] = dot_nt(mixed_ref[...], per_set[index][0][...])
        for index in range(sets):
            admit_ref = per_set[index][1]
            admits[index, pl.ds(start, BLOCK), :] = admit_ref[...]
            for lane in range(0, channels, 128):
                cols = slice(lane, lane + 128)
                kept, gain = last[index, 0:8, cols], last[index, 8:16, cols]
                for here in range(BLOCK - 16, -1, -16):
                    keep = 1.0 - admit_ref[here : here + 16, cols].astype(F32)
                    for step in (8, 0):
                        carried = state_delta[index, here + step : here + step + 8, cols] + kept
                        cs[index, pl.ds(start + here + step, 8), cols] = carried
                        ps[index, pl.ds(start + here + step, 8), cols] = gain
                        kept = keep[step : step + 8] * carried
                        gain = keep[step : step + 8] * gain
                last[index, 0:8, cols] = kept
                last[index, 8:16, cols] = gain

    @pl.when((phase == 1) & (block == 0))
    def _():
        for index in range(sets):
            kept, gain = last[index, 0:8, :], last[index, 8:16, :]
            entering = per_set[index][4][...]
            enter[index, 7:8, :] = entering
            for run in range(SEGMENTS - 1, 0, -1):
                entering = mask[run : run + 1, :] * (kept[run : run + 1] + gain[run : run + 1] * entering)
                enter[index, run - 1 : run, :] = entering
            ends_out[index, 0:1, :] = mask[0:1, :] * (kept[0:1] + gain[0:1] * entering)
            ends_out[index, 1:2, :] = product_of_runs(gain * mask[...])
            ends_out[index, 2:8, :] = jnp.zeros((6, channels), F32)
        bias_out[...] = jnp.zeros_like(bias_out)
        slopes_acc[...] = jnp.zeros_like(slopes_acc)

    @pl.when(phase == 1)
    def _():
        normed_t = normed_ref[...].T
        wide = min(channels, 256)
        for index in range(sets):
            _, _, forget_fac, admit_fac, _, output_grads = per_set[index]
            for first in range(0, channels, wide):
                for lane in range(first, first + wide, 128):
                    cols = slice(lane, lane + 128)
                    entering = enter[index, :, cols]
                    bias = jnp.zeros((8, 128), F32)
                    for here in range(0, BLOCK, GROUP):
                        rows, there = slice(here, here + GROUP), pl.ds(start + here, GROUP)
                        gains = ps[index, there, cols].reshape(GROUP // 8, 8, 128)
                        carried = (cs[index, there, cols].reshape(GROUP // 8, 8, 128) + gains * entering).reshape(GROUP, 128)
                        carried_out[index][rows, cols] = carried.astype(BF16)
                        admit_delta = (carried * admit_fac[rows, cols].astype(F32)).astype(BF16)
                        deltas[index, 0, rows, cols] = (carried * forget_fac[rows, cols].astype(F32)).astype(BF16)
                        deltas[index, 1, rows, cols] = admit_delta
                        deltas[index, 2, rows, cols] = (carried * admits[index, there, cols].astype(F32)).astype(BF16)
                        bias = bias + fold_rows(admit_delta.astype(F32))
                    bias_out[index, :, cols] += bias
                for part in range(3):
                    cols = slice(first, first + wide)
                    slopes_acc[index, part, :, cols] += dot_nn(normed_t, deltas[index, part, :, cols])
            tall = output_grads.shape[0]
            for half in range(2):
                @pl.when(block // (blocks // 2) == half)
                def _():
                    there = pl.multiple_of(block % (blocks // 2) * tall, tall)
                    second_out[half][index, pl.ds(there, tall), channels:] = output_grads[...]

    @pl.when((phase == 1) & (block == blocks - 1))
    def _():
        for index in range(sets):
            put_blocks(slopes_acc.at[index, 0], [out.at[index] for out in first_out], me_ref[0], 0)
            put_blocks(slopes_acc.at[index, 1], [out.at[index] for out in first_out], me_ref[0], channels)
            put_blocks(slopes_acc.at[index, 2], [out.at[index] for out in second_out], me_ref[1], 0)


def mixer_backward(mixed, normed, mask, me, per_set):
    rows, width = mixed.shape
    sets = len(per_set)
    channels = mask.shape[1]
    blocks = rows // BLOCK
    back = lambda phase, block: (jnp.where(phase == 0, blocks - 1 - block, 0), 0)
    late = lambda phase, block: (jnp.where(phase == 0, 0, block), 0)
    whole = lambda phase, block: (0, 0)
    all3 = lambda phase, block: (0, 0, 0)
    set_specs = [
        pl.BlockSpec((channels, width), whole),
        pl.BlockSpec((BLOCK, channels), back),
        pl.BlockSpec((BLOCK, channels), late),
        pl.BlockSpec((BLOCK, channels), late),
        pl.BlockSpec((1, channels), whole),
        pl.BlockSpec((width // blocks, channels), late),
    ]
    results = pl.pallas_call(
        functools.partial(mixer_back_kernel, sets),
        grid=(2, blocks),
        in_specs=[
            pl.BlockSpec((BLOCK, width), back),
            pl.BlockSpec((BLOCK, width), late),
            pl.BlockSpec((8, channels), whole),
            pl.BlockSpec(memory_space=pltpu.SMEM),
        ]
        + set_specs * sets,
        out_specs=[pl.BlockSpec((BLOCK, channels), late)] * sets
        + [pl.BlockSpec((sets, width // 2, 2 * channels), all3)] * 4
        + [pl.BlockSpec((sets, 8, channels), all3)] * 2,
        out_shape=[jax.ShapeDtypeStruct((rows, channels), BF16)] * sets
        + [jax.ShapeDtypeStruct((sets, width // 2, 2 * channels), BF16)] * 4
        + [jax.ShapeDtypeStruct((sets, 8, channels), F32)] * 2,
        scratch_shapes=[
            pltpu.VMEM((sets, rows, channels), F32),
            pltpu.VMEM((sets, rows, channels), F32),
            pltpu.VMEM((sets, BLOCK, channels), F32),
            pltpu.VMEM((sets, rows, channels), BF16),
            pltpu.VMEM((sets, 3, BLOCK, channels), BF16),
            pltpu.VMEM((sets, 3, width, channels), F32),
            pltpu.VMEM((sets, 16, channels), F32),
            pltpu.VMEM((sets, 8, channels), F32),
        ],
        compiler_params=pltpu.CompilerParams(vmem_limit_bytes=VMEM_BYTES, dimension_semantics=("arbitrary", "arbitrary")),
        cost_estimate=pl.CostEstimate(flops=2 * rows * width * 4 * channels * sets, bytes_accessed=rows * channels * 12 * sets, transcendentals=0),
        name="mixer_backward",
    )(mixed, normed, mask, me, *[item for one in per_set for item in one])
    return results[:sets], results[sets : sets + 2], results[sets + 2 : sets + 4], *results[sets + 4 :]


def input_kernel(sets, *refs):
    x_ref, mixed_ref, gain_ref, *refs = refs
    factors, refs = refs[: 4 * sets], refs[4 * sets :]
    weights, refs = refs[: 3 * sets], refs[3 * sets :]
    out_ref, slope_ref, out_s = refs

    @pl.when(pl.program_id(0) == 0)
    def _():
        slope_ref[...] = jnp.zeros_like(slope_ref)

    normed_delta = None
    for index in range(sets):
        carried = factors[4 * index][...].astype(F32)
        for part in range(3):
            delta = (carried * factors[4 * index + 1 + part][...].astype(F32)).astype(BF16)
            term = dot_nt(delta, weights[3 * index + part][...])
            normed_delta = term if normed_delta is None else normed_delta + term
    rows = x_ref[...].astype(F32)
    scale = row_scale(rows)
    slope_ref[...] += fold_rows(normed_delta * rows * scale)
    scaled = normed_delta * gain_ref[...]
    inner = jnp.mean(scaled * rows, -1, keepdims=True)
    result = mixed_ref[...].astype(F32) + scale * (scaled - rows * (scale * scale * inner))
    separate(result, out_s, out_ref)


def input_backward(x_rows, mixed, gain, factors, weights):
    rows, width = x_rows.shape
    sets = len(factors) // 4
    channels = weights[0].shape[1]
    by_rows = lambda block: (block, 0)
    whole = lambda block: (0, 0)
    return pl.pallas_call(
        functools.partial(input_kernel, sets),
        grid=(rows // BLOCK,),
        in_specs=[pl.BlockSpec((BLOCK, width), by_rows)] * 2
        + [pl.BlockSpec((1, width), whole)]
        + [pl.BlockSpec((BLOCK, channels), by_rows)] * (4 * sets)
        + [pl.BlockSpec((width, channels), whole)] * (3 * sets),
        out_specs=[pl.BlockSpec((SEGMENTS, STEPS, width), lambda block: (0, block, 0)), pl.BlockSpec((8, width), whole)],
        out_shape=[jax.ShapeDtypeStruct((SEGMENTS, rows // SEGMENTS, width), F32), jax.ShapeDtypeStruct((8, width), F32)],
        scratch_shapes=[pltpu.VMEM((width // 128, BLOCK, 128), F32)],
        compiler_params=pltpu.CompilerParams(vmem_limit_bytes=VMEM_BYTES, dimension_semantics=("arbitrary",)),
        cost_estimate=pl.CostEstimate(flops=2 * rows * width * 3 * channels * sets, bytes_accessed=rows * channels * 8 * sets, transcendentals=0),
        name="input_backward",
    )(x_rows, mixed, gain, *factors, *weights)


def finish_kernel(channels, first_low, first_high, second_low, second_high, me_ref, forget_out, admit_out, value_out, output_out, scratch):
    tall = 2 * first_low.shape[0] // PLACES
    for place in range(PLACES):
        here = slice(place % (PLACES // 2) * tall, (place % (PLACES // 2) + 1) * tall)
        first_ref, second_ref = ((first_low, second_low), (first_high, second_high))[place // (PLACES // 2)]
        for index, (sums, outs) in enumerate(((first_ref, (forget_out, admit_out)), (second_ref, (value_out, scratch)))):
            there = pl.multiple_of((place ^ me_ref[index]) * tall, tall)
            outs[0][pl.ds(there, tall), :] = sums[here, :channels].astype(F32)
            outs[1][pl.ds(there, tall), :] = sums[here, channels:].astype(F32)
    output_out[...] = scratch[...].T


def finish_slopes(first, second, me):
    width, channels = 2 * first[0].shape[0], first[0].shape[1] // 2
    return pl.pallas_call(
        functools.partial(finish_kernel, channels),
        in_specs=[pl.BlockSpec(memory_space=pltpu.VMEM)] * 4 + [pl.BlockSpec(memory_space=pltpu.SMEM)],
        out_shape=[jax.ShapeDtypeStruct((width, channels), F32)] * 3 + [jax.ShapeDtypeStruct((channels, width), F32)],
        scratch_shapes=[pltpu.VMEM((width, channels), F32)],
        compiler_params=pltpu.CompilerParams(vmem_limit_bytes=VMEM_BYTES),
        name="finish_slopes",
    )(*first, *second, me)


def run_masks(seq_lengths, rows, shift, channels):
    ends = jnp.cumsum(seq_lengths[0])
    begins = ends - seq_lengths[0]
    places = shift + jnp.arange(SEGMENTS, dtype=jnp.int32) * (rows // SEGMENTS)
    fresh = jnp.any((places[:, None] == begins[None, :]) & (seq_lengths[0] > 0)[None, :], -1)
    return jnp.broadcast_to(jnp.where(fresh, 0.0, 1.0).astype(F32)[:, None], (SEGMENTS, channels))


def regroup(stacked, half):
    count, both, width = stacked.shape
    if both == 2 * half:
        return stacked
    arrays = jnp.moveaxis(stacked.reshape(count, 2, both // 2, width), 1, 0).reshape(2, -1, half, width)
    return jnp.moveaxis(arrays, 0, 1).reshape(-1, 2 * half, width)


def added(mine, theirs):
    return (mine.astype(F32) + theirs.astype(F32)).astype(mine.dtype)


def after(values, *earlier):
    return lax.optimization_barrier((values, earlier))[0]


class Links:
    TENSOR, CORE, NEAR, Z_NEAR, Z_FAR = 1, 2, 4, 8, 16
    FIRST = (CORE, TENSOR, NEAR, Z_NEAR, Z_FAR)
    SECOND = (CORE, Z_NEAR, TENSOR, NEAR, Z_FAR)

    def __init__(self):
        dp = lax.axis_index("dp")
        core, near, z_near, z_far = dp % 2, dp // 2 % 2, dp // 4 % 2, dp // 8
        self.core = core
        first = core * 8 + near * 4 + z_near * 2 + z_far
        second = core * 8 + z_near * 4 + near * 2 + z_far
        self.me = jnp.stack([first, second]).astype(jnp.int32)

    def swap(self, values, bit):
        pairs = [(device, device ^ bit) for device in range(32)]
        return lax.ppermute(values, ("dp", "tensor"), pairs)

    def begin_weights(self, own_weights):
        half = own_weights[0].shape[0] // 2
        cut = [lax.dynamic_slice_in_dim(w, self.core * half, half) for w in own_weights]
        mine = jnp.stack(cut[:3])
        first = self.swap(mine, self.TENSOR)
        return mine, first, lambda: self.swap(after(cut[3], first), self.TENSOR)

    def end_weights(self, got):
        rest = self.swap(got, self.CORE)
        lower = self.core == 0
        return jnp.concatenate([jnp.where(lower, got, rest), jnp.where(lower, rest, got)], -2)

    def bias(self, own_bias):
        return own_bias, self.swap(own_bias, self.TENSOR)

    def begin_dense(self, shard):
        return [shard] + [self.swap(shard, bits) for bits in (self.Z_NEAR, self.Z_FAR, self.Z_NEAR | self.Z_FAR)]

    def middle_dense(self, pieces):
        own = jnp.stack(pieces)
        return own, self.swap(own, self.NEAR), self.swap(own, self.TENSOR)

    def end_dense(self, own, near, other):
        own = jnp.concatenate([own, near], 0)
        other = jnp.concatenate([other, self.swap(other, self.NEAR)], 0)
        own_rest, other_rest = self.swap(own, self.CORE), self.swap(other, self.CORE)
        return jnp.concatenate([own, other, own_rest, other_rest], 0)

    def dense_begin(self, upper, lower):
        cut = lambda values: values.reshape(2, 2, 2, 2, *values.shape[1:])
        orders = ([0, 1, 3, 2], [1, 0, 3, 2])
        return [(cut(keep), cut(self.swap(send, self.CORE)), order) for (keep, send), order in zip((upper, lower), orders)]

    def dense_step(self, stream):
        bits = (self.TENSOR, self.NEAR, self.Z_FAR, self.Z_NEAR)
        kept, received, order = stream
        if not order:
            return added(kept, received)
        axis = order[0]
        part = lambda values, index: lax.index_in_dim(values, index, axis, keepdims=True)
        send = added(part(kept, 1), part(received, 1))
        return added(part(kept, 0), part(received, 0)), self.swap(send, bits[axis]), order[1:]

    def mixer_step(self, kept, received, bit, extra=None):
        if bit == self.TENSOR:
            part = lambda values, index: values[index : index + 1]
        else:
            part = lambda values, index: values[:, index * (values.shape[1] // 2) : (index + 1) * (values.shape[1] // 2)]
        send = added(part(kept, 1), part(received, 1))
        keep = added(part(kept, 0), part(received, 0))
        if extra is None:
            return keep, self.swap(send, bit)
        got = self.swap(jnp.concatenate([send, extra], 1), bit)
        return keep, got[:, : send.shape[1]], added(extra, got[:, send.shape[1] :])

    def mixer_grow(self, values, bit):
        return jnp.concatenate([values, self.swap(values, bit)], 1)

    def grow_with(self, values, extra, bit):
        got = self.swap(jnp.concatenate([values, extra], 1), bit)
        return values, got[:, : values.shape[1]], added(extra, got[:, values.shape[1] :])


class Plain:
    def __init__(self, n_tensor, own):
        self.n_tensor, self.own = n_tensor, own
        self.me = jnp.zeros((2,), jnp.int32)

    def weights(self, own_weights):
        whole = [lax.all_gather(w, "tensor", axis=1, tiled=True) for w in own_weights[:3]]
        pairs = [jnp.split(w, 2, 1) for w in whole]
        pairs.append(jnp.split(lax.all_gather(own_weights[3], "tensor", axis=0, tiled=True), 2, 0))
        return [p[0] for p in pairs], [p[1] for p in pairs]

    def bias(self, own_bias):
        return tuple(jnp.split(lax.all_gather(own_bias, "tensor", axis=0, tiled=True), 2))

    def dense(self, shard):
        return regroup(lax.all_gather(shard, ("dp", "tensor"), axis=0), 64)

    def dense_sums(self, upper, lower):
        pairs = [jnp.concatenate(halves, 0) for halves in (upper, lower)]
        return [lax.psum_scatter(g.reshape(-1, g.shape[-1]), ("dp", "tensor"), scatter_dimension=0, tiled=True) for g in pairs]

    def mixer_sums(self, grads):
        grads = jnp.concatenate(grads, 1)
        _, width, columns = grads.shape
        whole = jnp.moveaxis(grads.reshape(2, width, 2, columns // 2), 0, 2).reshape(width, 2, columns)
        part = lax.psum_scatter(whole, "tensor", scatter_dimension=2, tiled=True)
        return jnp.split(lax.psum(part, "dp").reshape(width, 2 * self.own), 2, 0)

def on_device(
    block_in,
    out_cotangent,
    seq_lengths,
    premix_gain,
    forget_weight,
    admit_weight,
    value_weight,
    admit_bias,
    output_weight,
    dense_gain,
    upper_weight,
    lower_weight,
):
    n_dp, n_tensor = lax.axis_size("dp"), lax.axis_size("tensor")
    rows, width = block_in.shape
    place = lax.axis_index("tensor")
    own = forget_weight.shape[1]
    premix = premix_gain.astype(F32)[None]
    dense = dense_gain.astype(F32)[None]
    paired = (n_dp, n_tensor) == (16, 2)
    links = Links() if paired else Plain(n_tensor, own)
    me = links.me
    own_weights = [forget_weight, admit_weight, value_weight, output_weight]
    dense_shard = jnp.concatenate([upper_weight.T, lower_weight], 0)
    if paired:
        weights = [own_weights, None]
        channels = own
        mine, got, begin_output = links.begin_weights(own_weights)
        pieces = links.begin_dense(after(dense_shard, mine))
    else:
        weights = links.weights(own_weights)
        channels = weights[0][0].shape[1]
    biases = [b.astype(F32)[None] for b in links.bias(admit_bias)]
    mask = run_masks(seq_lengths, rows, place * rows, channels)
    crossing = rows % LONGEST != 0
    nothing = jnp.zeros((1, channels), F32)

    def chained(ends, backwards):
        every = lax.all_gather(ends, "tensor", axis=0)
        entering = jnp.zeros_like(ends[0:1])
        mine = entering
        order = range(n_tensor - 1, -1, -1) if backwards else range(n_tensor)
        for index in order:
            mine = jnp.where(place == index, entering, mine)
            entering = every[index, 0:1] + every[index, 1:2] * entering
        return mine

    def forward(first, rows_in, index):
        carry = nothing
        if crossing:
            ends = mixer_forward(first, rows_in, premix, weights[index][:3], biases[index], mask, carry)[-1]
            carry = chained(ends, False)
        return mixer_forward(first, rows_in, premix, weights[index][:3], biases[index], mask, carry)

    x_rows, normed, *kept_0 = forward(True, block_in, 0)
    if paired:
        got, pieces = after((got, pieces), normed)
        got_output = begin_output()
        middle = links.middle_dense(pieces)
        other = links.end_weights(got)
        weights[1] = [other[0], other[1], other[2]]
    kept_1 = forward(False, normed, 1)
    if paired:
        got_output, middle = after((got_output, middle), kept_1[1])
        weights[1].append(links.end_weights(got_output))
        gathered = links.end_dense(*middle)
    else:
        gathered = links.dense(dense_shard)
    kept = [kept_0, kept_1]
    outputs = [w[3] for w in weights]
    block_out, mixed, *dense_grads, dense_part, grads_0, grads_1 = dense_both(
        x_rows, out_cotangent, [k[1] for k in kept], outputs, dense, gathered, me
    )
    output_grads = [grads_0, grads_1]
    if paired:
        dense_streams = links.dense_begin(dense_grads[:2], dense_grads[2:])

    carries = [nothing, nothing]
    for _ in range(2 if crossing else 1):
        per_set = [
            (outputs[index], kept[index][0], kept[index][2], kept[index][3], carries[index], output_grads[index])
            for index in range(2)
        ]
        carried, first, second, bias_parts, ends = mixer_backward(mixed, normed, mask, me, per_set)
        if crossing:
            carries = [chained(ends[index], True) for index in range(2)]
    factors = [f for index in range(2) for f in (carried[index], kept[index][2], kept[index][3], kept[index][0])]
    if paired:
        first = first[0], links.swap(first[1], Links.CORE)
        second = second[0], links.swap(second[1], Links.CORE)
        factors[0] = after(factors[0], first, second)
        first = links.mixer_step(*first, Links.FIRST[1])
        second = links.mixer_step(*second, Links.SECOND[1])
    input_slope, premix_part = input_backward(x_rows, mixed, premix, factors, weights[0][:3] + weights[1][:3])

    bias_parts = jnp.sum(bias_parts, 1)
    if paired:
        bias_parts = jnp.where(place == 0, bias_parts, bias_parts[::-1])
    small = jnp.concatenate([jnp.sum(premix_part, 0), jnp.sum(dense_part, 0), bias_parts[0], bias_parts[1]], 0)
    if paired:
        small = small.reshape(1, -1, 2 * channels).astype(BF16)
        filled = small.shape[1]
        small = jnp.pad(small, ((0, 0), (0, 16 - filled), (0, 0)))
        first, second = after((first, second), small)
        for step in (2, 3, 4):
            first = links.mixer_step(*first, Links.FIRST[step])
            *second, small = links.mixer_step(*second, Links.SECOND[step], small)
        first, second = added(*first), added(*second)
        first, second = links.mixer_grow(first, Links.Z_FAR), links.mixer_grow(second, Links.Z_FAR)
        low, high, small = links.grow_with(first, small, Links.Z_NEAR)
        first, second = jnp.concatenate([low, high], 1), links.mixer_grow(second, Links.NEAR)
        first, second = links.mixer_grow(first, Links.NEAR), links.mixer_grow(second, Links.Z_NEAR)
        first = first[0], links.swap(first, Links.CORE)[0]
        low, high, small = links.grow_with(second, small, Links.CORE)
        second = low[0], high[0]
        small = small[0, :filled].reshape(-1).astype(F32)
        for _ in range(4):
            dense_streams = [links.dense_step(d) for d in dense_streams]
        upper_sum, lower_sum = (links.dense_step(d).reshape(-1, width) for d in dense_streams)
    else:
        small = lax.psum(small, ("dp", "tensor"))
        upper_sum, lower_sum = links.dense_sums(dense_grads[:2], dense_grads[2:])
        first, second = links.mixer_sums(first), links.mixer_sums(second)
    upper_slope, lower_slope = upper_sum.astype(F32).T, lower_sum.astype(F32)
    forget_slope, admit_slope, value_slope, output_slope = finish_slopes(first, second, me)
    shard = width // (n_dp * n_tensor)
    at = (lax.axis_index("dp") * n_tensor + place) * shard
    premix_slope = lax.dynamic_slice(small, (at,), (shard,))
    dense_slope = lax.dynamic_slice(small, (width + at,), (shard,))
    bias_slope = lax.dynamic_slice(small, (2 * width + place * own,), (own,))
    return (
        block_out.reshape(rows, width),
        input_slope.reshape(rows, width),
        premix_slope,
        forget_slope,
        admit_slope,
        value_slope,
        bias_slope,
        output_slope,
        dense_slope,
        upper_slope,
        lower_slope,
    )


def solution(mesh):
    placed = (
        P(("dp", "tensor"), None),
        P(("dp", "tensor"), None),
        P("dp", None),
        P(),
        P(None, "tensor"),
        P(None, "tensor"),
        P(None, "tensor"),
        P("tensor"),
        P("tensor", None),
        P(),
        P(None, ("dp", "tensor")),
        P(("dp", "tensor"), None),
    )
    return jax.shard_map(
        on_device,
        mesh=mesh,
        in_specs=placed,
        out_specs=(
            P(("dp", "tensor"), None),
            P(("dp", "tensor"), None),
            P(("dp", "tensor")),
            P(None, "tensor"),
            P(None, "tensor"),
            P(None, "tensor"),
            P("tensor"),
            P("tensor", None),
            P(("dp", "tensor")),
            P(None, ("dp", "tensor")),
            P(("dp", "tensor"), None),
        ),
        check_vma=False,
    )
```

time: 353 us -> 233 us (0.66); the launches traced: 348 us -> 232 us
  waiting for transfers between devices: 122 us -> 32.4 us
  Pallas kernels: 142 us -> 117 us
  local copies, waits for them, and re-layouts: 16.9 us -> 9.56 us
  other arithmetic: 16.3 us -> 23.4 us
    ppermute x30 -> x41, waiting for transfers between devices: 122 us -> 32.4 us  [swap(): return lax.ppermute(values, ('dp', 'tensor'), pairs)]
    pallas_call x2 -> x1, Pallas kernels: 38.9 us -> 22.2 us  [mixer_backward(): pl.pallas_call(functools.partial(mixer_back_kernel, sets), grid=(2, block...]
    convert_element_type x8 -> x20, other arithmetic: 4.52 us -> 12.7 us  [added(): return (mine.astype(F32) + theirs.astype(F32)).astype(mine.dtype)]
    pallas_call x2, Pallas kernels: 38.4 us -> 30.7 us  [mixer_forward(): pl.pallas_call(functools.partial(mixer_kernel, first), grid=(2, blocks),...]
    slice x11 -> x3, local copies, waits for them, and re-layouts: 6.26 us -> 0.04 us  [the longest x1 0.02 us: on_device(): bias_parts[0]]
    ppermute x30 -> x41, starting transfers between devices: 49.7 us -> 48.9 us  [swap(): return lax.ppermute(values, ('dp', 'tensor'), pairs)]
  transfers between devices with their start and end apart: 30 -> 41, of which waited for: 17 -> 14; matrix products, arithmetic and copies ran while one was open for 8% -> 12% of each run, Pallas kernels for 21% -> 29%
where the time goes in v2:
time: 233 us; the launch traced here: 232 us
  Pallas kernels  117 us (50%)
  starting transfers between devices  48.9 us (21%)
  waiting for transfers between devices  32.4 us (14%)
  other arithmetic  23.4 us (10%)
  local copies, waits for them, and re-layouts  9.56 us (4%)
    ppermute x41, starting transfers between devices, swap(): return lax.ppermute(values, ('dp', 'tensor'), pairs)  48.9 us
    pallas_call x1, Pallas kernels, dense_both(): pl.pallas_call(functools.partial(dense_kernel, sets, 512), grid=(rows //...  45.3 us
    ppermute x41, waiting for transfers between devices, swap(): return lax.ppermute(values, ('dp', 'tensor'), pairs)  32.4 us
    pallas_call x2, Pallas kernels, mixer_forward(): pl.pallas_call(functools.partial(mixer_kernel, first), grid=(2, blocks),...  30.7 us
    pallas_call x1, Pallas kernels, mixer_backward(): pl.pallas_call(functools.partial(mixer_back_kernel, sets), grid=(2, block...  22.2 us
    pallas_call x1, Pallas kernels, input_backward(): pl.pallas_call(functools.partial(input_kernel, sets), grid=(rows // BLOCK...  14.8 us
    convert_element_type x20, other arithmetic, added(): return (mine.astype(F32) + theirs.astype(F32)).astype(mine.dtype)  12.7 us
  transfers between devices with their start and end apart: 41, of which 14 were waited for; matrix products, arithmetic and copies ran while one was open for 12% of the time, Pallas kernels for 29%

profile of v2, /device:TPU:1, one launch (start us, length us, event | category | flops | bytes accessed | tf_op | source)
XLA Modules:
  0.0 232.5 jit_solution(9843780429416862411)
XLA Ops:
  0.7 1.0 dynamic-slice_bitcast_fusion.2
  1.7 1.1 dynamic-slice_bitcast_fusion
  2.9 2.1 collective-permute-start
  5.0 1.4 collective-permute-start.1
  6.4 2.3 collective-permute-start.2
  8.9 0.6 broadcast_in_dim.52
  10.3 0.7 broadcast_in_dim.46.refs_6_.refs_5_.mask
  10.9 0.6 broadcast_in_dim.47.refs_7_.refs_6_.refs_4_.refs_10_
  11.5 16.1 %mixer_forward.2 = (bf16[2048,512]{1,0:T(8,128)(2,1)}, bf16[2048,512]{1,0:T(8,128)(2,1)}, bf16[2048,512]{1,0:T(8,128)(2,1)}, bf16[2048,512]{1,0:T(8,128)(2,1)}, ...) custom-call(bf16[8,256,512]{2,1,0:T(8,128)(2,1)} %bitcast.75, f32[1,512]{1,0:T(1,128)} %bitcast.69, ...), custom_call_target="tpu_custom_call" | custom-call | flops 3221225472 | bytes 16777216 | tf_op jit(solution)/shard_map/mixer_forward/pallas_call | solution.py:212
  27.7 1.8 collective-permute-start.4
  29.6 2.3 %collective-permute-done.5 = bf16[512]{0:T(512)(128)(2,1)S(1)} collective-permute-done((bf16[512]{0:T(512)(128)(2,1)S(1)}, bf16[512]{0:T(512)(128)(2,1)S(1)}, u32[]{:S(2)}, u32[]{:S(2)}) %collective-permute-start.5) | collective-permute-done | bytes 1056 | tf_op jit(solution)/shard_map/ppermute | solution.py:602
  32.6 1.3 collective-permute-start.7
  34.1 1.2 collective-permute-start.6
  35.5 1.2 fusion.4
  36.7 14.6 %mixer_forward.3 = (bf16[2048,512]{1,0:T(8,128)(2,1)}, bf16[2048,512]{1,0:T(8,128)(2,1)}, bf16[2048,512]{1,0:T(8,128)(2,1)}, bf16[2048,512]{1,0:T(8,128)(2,1)}, f32[8,512]{1,0:T(8,128)}) custom-call(bf16[2048,512]{1,0:T(8,128)(2,1)} %get-tuple-element.61.refs_0_.normed_ref, bf16[512,512]{1,0:T(8,128)(2,1)} %get-tuple-element.122.refs_1_.refs_14_, ...), custom_call_target="tpu_custom_call" | custom-call | flops 3221225472 | bytes 16777216 | tf_op jit(solution)/shard_map/mixer_forward/pallas_call | solution.py:212
  51.4 0.7 copy-done.5
  52.5 2.8 %collective-permute-start.11 = (bf16[8,128,512]{2,1,0:T(8,128)(2,1)S(1)}, bf16[8,128,512]{2,1,0:T(8,128)(2,1)S(1)}, u32[]{:S(2)}, u32[]{:S(2)}) collective-permute-start(bf16[8,128,512]{2,1,0:T(8,128)(2,1)S(1)} %pad_maximum_fusion), channel_id=1, source_target_pairs={{0,2},{1,3},{2,0},{3,1},{4,6},{5,7},{6,4},{7,5},{8,10},{9,11},{10,... | collective-permute-start | bytes 3145736 | tf_op jit(solution)/shard_map/ppermute | solution.py:602
  55.2 7.9 %collective-permute-done.10 = bf16[4,128,512]{2,1,0:T(8,128)(2,1)S(1)} collective-permute-done((bf16[4,128,512]{2,1,0:T(8,128)(2,1)S(1)}, bf16[4,128,512]{2,1,0:T(8,128)(2,1)S(1)}, u32[]{:S(2)}, u32[]{:S(2)}) %collective-permute-start.10) | collective-permute-done | bytes 524320 | tf_op jit(solution)/shard_map/ppermute | solution.py:602
  63.2 3.4 %collective-permute-start.12 = (bf16[8,128,512]{2,1,0:T(8,128)(2,1)S(1)}, bf16[8,128,512]{2,1,0:T(8,128)(2,1)S(1)}, u32[]{:S(2)}, u32[]{:S(2)}) collective-permute-start(bf16[8,128,512]{2,1,0:T(8,128)(2,1)S(1)} %pad_maximum_fusion.1), channel_id=1, source_target_pairs={{0,2},{1,3},{2,0},{3,1},{4,6},{5,7},{6,4},{7,5},{8,10},{9,11},{10,... | collective-permute-start | bytes 3145736 | tf_op jit(solution)/shard_map/ppermute | solution.py:602
  67.9 1.4 collective-permute-done.9
  69.4 0.8 pad_maximum_fusion.5.refs_5_.refs_6_
  70.5 2.0 copy-done.8
  72.5 45.3 %dense_both.1 = (bf16[8,256,512]{2,1,0:T(8,128)(2,1)}, bf16[2048,512]{1,0:T(8,128)(2,1)}, bf16[16,64,512]{2,1,0:T(8,128)(2,1)}, bf16[16,64,512]{2,1,0:T(8,128)(2...) custom-call(bf16[2048,512]{1,0:T(8,128)(2,1)} %get-tuple-element.59., ...), custom_call_target="tpu_custom_call" | custom-call | flops 25769803776 | bytes 12582912 | tf_op jit(solution)/shard_map/dense_both/pallas_call | solution.py:316
  118.3 22.2 %mixer_backward.1 = (bf16[2048,512]{1,0:T(8,128)(2,1)}, bf16[2048,512]{1,0:T(8,128)(2,1)}, bf16[2,256,1024]{2,1,0:T(8,128)(2,1)}, bf16[2,256,1024]{2,1,0:T(8,128...) custom-call(bf16[2048,512]{1,0:T(8,128)(2,1)} %get-tuple-element.75., ...), custom_call_target="tpu_custom_call" | custom-call | flops 8589934592 | bytes 25165824 | tf_op jit(solution)/shard_map/mixer_backward/pallas_call | solution.py:458
  141.1 0.8 reduce_sum.29
  142.1 2.3 add_convert_fusion.1
  144.7 2.4 %add_convert_fusion.3 = (bf16[8,64,512]{2,1,0:T(8,128)(2,1)S(1)}, bf16[8,64,512]{2,1,0:T(8,128)(2,1)}) fusion(bf16[16,64,512]{2,1,0:T(8,128)(2,1)} %collective-permute-done.31, bf16[16,64,512]{2,1,0:T(8,128)(2,1)S(1)} %copy-done.1), kind=kLoop, calls=%fused_computation.9 | loop fusion | flops 2097152 | bytes 3145728 | tf_op jit(solution)/shard_map/convert_element_type | solution.py:580
  147.3 2.5 %add_convert_fusion.4 = (bf16[2,128,1024]{2,1,0:T(8,128)(2,1)}, bf16[2,128,1024]{2,1,0:T(8,128)(2,1)S(1)}) fusion(bf16[2,256,1024]{2,1,0:T(8,128)(2,1)} %collective-permute-done.14, bf16[2,256,1024]{2,1,0:T(8,128)(2,1)S(1)} %copy-done.2), kind=kLoop, calls=%fused_computation.10 | loop fusion | flops 2097152 | bytes 3145728 | tf_op jit(solution)/shard_map/convert_element_type | solution.py:580
  150.2 2.4 %add_convert_fusion.6 = (bf16[1,256,1024]{2,1,0:T(8,128)(2,1)}, bf16[1,256,1024]{2,1,0:T(8,128)(2,1)S(1)}) fusion(bf16[2,256,1024]{2,1,0:T(8,128)(2,1)} %collective-permute-done.13, bf16[2,256,1024]{2,1,0:T(8,128)(2,1)S(1)} %copy-done), kind=kLoop, calls=%fused_computation.12 | loop fusion | flops 2097152 | bytes 3145728 | tf_op jit(solution)/shard_map/convert_element_type | solution.py:580
  152.6 1.2 collective-permute-start.15
  153.8 14.8 %input_backward.1 = (f32[8,256,512]{2,1,0:T(8,128)}, f32[8,512]{1,0:T(8,128)}) custom-call(bf16[2048,512]{1,0:T(8,128)(2,1)} %get-tuple-element.59.refs_0_, bf16[2048,512]{1,0:T(8,128)(2,1)} %get-tuple-element.75.mixed_ref.refs_1_, f32[1,512]{1,0:T(1,128)} %bitcast.70, bf16[2048,512]{1,0:T(8,128)(2,1)} %get-tuple-element.89.refs_3_, ...), custom_call_target="tpu_custom_call" | custom-call | flops 6442450944 | bytes 16777216 | tf_op jit(solution)/shard_map/input_backward/pallas_call | solution.py:523
  168.6 0.7 reduce_sum.27
  169.4 1.2 add_convert_fusion.9
  170.9 1.2 add_convert_fusion.11
  172.1 1.2 collective-permute-start.33
  173.6 1.2 collective-permute-start.17
  175.4 1.6 collective-permute-done.38
  177.1 1.1 collective-permute-start.39
  178.4 1.1 collective-permute-start.34
  179.6 4.4 %collective-permute-done.20 = bf16[1,128,1024]{2,1,0:T(8,128)(2,1)S(1)} collective-permute-done((bf16[1,128,1024]{2,1,0:T(8,128)(2,1)S(1)}, bf16[1,128,1024]{2,1,0:T(8,128)(2,1)S(1)}, u32[]{:S(2)}, u32[]{:S(2)}) %collective-permute-start.20) | collective-permute-done | bytes 262176 | tf_op jit(solution)/shard_map/ppermute | solution.py:602
  184.0 1.1 collective-permute-start.21
  185.3 1.2 collective-permute-start.18
  186.5 2.5 %collective-permute-start.40 = (bf16[1,1,1,1,64,512]{5,4,3,2,1,0:T(8,128)(2,1)S(1)}, bf16[1,1,1,1,64,512]{5,4,3,2,1,0:T(8,128)(2,1)S(1)}, u32[]{:S(2)}, u32[]{:S(2)}) collective-permute-start(bf16[1,1,1,1,64,512]{5,4,3,2,1,0:T(8,128)(2,1)S(1)} %add_convert_fusion.25), channel_id=1, source_target_pairs={{0,16},{1,17},{2,18},{3,19},{4,20},{5,21},{6,22},{7,23},{8,24},{9,... | collective-permute-start | bytes 196616 | tf_op jit(solution)/shard_map/ppermute | solution.py:602
  189.6 2.6 %collective-permute-start.19 = (bf16[1,48,1024]{2,1,0:T(8,128)(2,1)S(1)}, bf16[1,48,1024]{2,1,0:T(8,128)(2,1)S(1)}, u32[]{:S(2)}, u32[]{:S(2)}) collective-permute-start(bf16[1,48,1024]{2,1,0:T(8,128)(2,1)S(1)} %pad_maximum_fusion.14), channel_id=1, source_target_pairs={{0,16},{1,17},{2,18},{3,19},{4,20},{5,21},{6,22},{7,23},{8,24},{9,... | collective-permute-start | bytes 294920 | tf_op jit(solution)/shard_map/ppermute | solution.py:602
  192.3 8.0 %collective-permute-done.19 = bf16[1,48,1024]{2,1,0:T(8,128)(2,1)S(1)} collective-permute-done((bf16[1,48,1024]{2,1,0:T(8,128)(2,1)S(1)}, bf16[1,48,1024]{2,1,0:T(8,128)(2,1)S(1)}, u32[]{:S(2)}, u32[]{:S(2)}) %collective-permute-start.19) | collective-permute-done | bytes 98336 | tf_op jit(solution)/shard_map/ppermute | solution.py:602
  200.4 2.0 collective-permute-done.22
  202.8 1.6 collective-permute-done.25
  204.4 2.4 %collective-permute-start.26 = (bf16[1,64,1024]{2,1,0:T(8,128)(2,1)S(1)}, bf16[1,64,1024]{2,1,0:T(8,128)(2,1)S(1)}, u32[]{:S(2)}, u32[]{:S(2)}) collective-permute-start(bf16[1,64,1024]{2,1,0:T(8,128)(2,1)S(1)} %pad_maximum_fusion.13), channel_id=1, source_target_pairs={{0,4},{1,5},{2,6},{3,7},{4,0},{5,1},{6,2},{7,3},{8,12},{9,13},{10,... | collective-permute-start | bytes 393224 | tf_op jit(solution)/shard_map/ppermute | solution.py:602
  206.8 1.4 collective-permute-start.24
  208.3 1.2 collective-permute-done.26
  209.5 1.2 collective-permute-start.27
  210.6 1.1 collective-permute-done.24
  211.8 2.9 %collective-permute-start.29 = (bf16[1,128,1024]{2,1,0:T(8,128)(2,1)S(1)}, bf16[1,128,1024]{2,1,0:T(8,128)(2,1)S(1)}, u32[]{:S(2)}, u32[]{:S(2)}) collective-permute-start(bf16[1,128,1024]{2,1,0:T(8,128)(2,1)S(1)} %pad_maximum_fusion.9), channel_id=1, source_target_pairs={{0,4},{1,5},{2,6},{3,7},{4,0},{5,1},{6,2},{7,3},{8,12},{9,13},{10,... | collective-permute-start | bytes 786440 | tf_op jit(solution)/shard_map/ppermute | solution.py:602
  214.8 6.8 %collective-permute-start.28 = (bf16[1,272,1024]{2,1,0:T(8,128)(2,1)S(1)}, bf16[1,272,1024]{2,1,0:T(8,128)(2,1)S(1)}, u32[]{:S(2)}, u32[]{:S(2)}) collective-permute-start(bf16[1,272,1024]{2,1,0:T(8,128)(2,1)S(1)} %get-tuple-element.109), channel_id=1, source_target_pairs={{0,2},{1,3},{2,0},{3,1},{4,6},{5,7},{6,4},{7,5},{8,10},{9,11},{10,... | collective-permute-start | bytes 1671176 | tf_op jit(solution)/shard_map/ppermute | solution.py:602
  221.6 0.7 fusion.7
  222.3 0.7 convert_bitcast_fusion
  223.0 0.9 pad_maximum_fusion.6
  223.9 0.8 collective-permute-start.30
  224.7 0.8 maximum_bitcast_fusion.second_low
  225.6 0.7 dynamic_slice.26
  226.2 0.6 fusion.9
  226.8 0.8 slice_bitcast_fusion.second_high
  227.7 0.8 copy-done.4
  228.5 4.0 %finish_slopes.1 = (f32[512,512]{1,0:T(8,128)}, f32[512,512]{1,0:T(8,128)}, f32[512,512]{1,0:T(8,128)}, f32[512,512]{1,0:T(8,128)}) custom-call(bf16[256,1024]{1,0:T(8,128)(2,1)} %get-tuple-element.141.first_low, bf16[256,1024]{1,0:T(8,128)(2,1)} %bitcast.61, bf16[256,1024]{1,0:T(8,128)(2,1)} %maximum_bitcast_fusion.second_low, ...), custom_call_target="tpu_custom_call" | custom-call | tf_op jit(solution)/shard_map/finish_slopes/pallas_call | solution.py:553
  (139 shorter events, 9.6 us)
Async XLA Ops:
  0.6 4.4 %copy-start.10 = (bf16[512,64]{0,1:T(8,128)(2,1)S(1)}, bf16[512,64]{0,1:T(8,128)(2,1)}, u32[]{:S(2)}) copy-start(bf16[512,64]{0,1:T(8,128)(2,1)} %param.22) | copy-start | bytes 196612
  0.7 4.4 %copy-start.9 = (bf16[64,512]{1,0:T(8,128)(2,1)S(1)}, bf16[64,512]{1,0:T(8,128)(2,1)}, u32[]{:S(2)}) copy-start(bf16[64,512]{1,0:T(8,128)(2,1)} %param.23) | copy-start | bytes 196612
  0.7 8.0 %copy-start.15 = (s32[1,8]{1,0:T(1,128)S(1)}, s32[1,8]{1,0:T(1,128)}, u32[]{:S(2)}) copy-start(s32[1,8]{1,0:T(1,128)} %param.14) | copy-start | bytes 100
  0.7 8.2 %copy-start.12 = (bf16[512]{0:T(512)(128)(2,1)S(1)}, bf16[512]{0:T(512)(128)(2,1)}, u32[]{:S(2)}) copy-start(bf16[512]{0:T(512)(128)(2,1)} %param.15) | copy-start | bytes 3076
  0.7 8.8 %copy-start.13 = (bf16[512]{0:T(512)(128)(2,1)S(1)}, bf16[512]{0:T(512)(128)(2,1)}, u32[]{:S(2)}) copy-start(bf16[512]{0:T(512)(128)(2,1)} %param.19) | copy-start | bytes 3076
  2.9 24.8 %collective-permute-start = (bf16[3,256,512]{2,1,0:T(8,128)(2,1)S(1)}, bf16[3,256,512]{2,1,0:T(8,128)(2,1)S(1)}, u32[]{:S(2)}, u32[]{:S(2)}) collective-permute-start(bf16[3,256,512]{2,1,0:T(8,128)(2,1)S(1)} %pad_maximum_fusion.2), channel_id=1, source_target_pairs={{0,1},{1,0},{2,3},{3,2},{4,5},{5,4},{6,7},{7,6},{8,9},{9,8},{10,11... | collective-permute-start | bytes 2359304 | tf_op jit(solution)/shard_map/ppermute | solution.py:602
  5.0 22.6 %collective-permute-start.1 = (bf16[128,512]{1,0:T(8,128)(2,1)S(1)}, bf16[128,512]{1,0:T(8,128)(2,1)S(1)}, u32[]{:S(2)}, u32[]{:S(2)}) collective-permute-start(bf16[128,512]{1,0:T(8,128)(2,1)S(1)} %pad_maximum_fusion.12), channel_id=1, source_target_pairs={{0,8},{1,9},{2,10},{3,11},{4,12},{5,13},{6,14},{7,15},{8,0},{9,1},... | collective-permute-start | bytes 393224 | tf_op jit(solution)/shard_map/ppermute | solution.py:602
  6.4 21.3 %collective-permute-start.2 = (bf16[128,512]{1,0:T(8,128)(2,1)S(1)}, bf16[128,512]{1,0:T(8,128)(2,1)S(1)}, u32[]{:S(2)}, u32[]{:S(2)}) collective-permute-start(bf16[128,512]{1,0:T(8,128)(2,1)S(1)} %pad_maximum_fusion.12), channel_id=1, source_target_pairs={{0,16},{1,17},{2,18},{3,19},{4,20},{5,21},{6,22},{7,23},{8,24},{9,... | collective-permute-start | bytes 393224 | tf_op jit(solution)/shard_map/ppermute | solution.py:602
  8.7 19.0 %collective-permute-start.3 = (bf16[128,512]{1,0:T(8,128)(2,1)S(1)}, bf16[128,512]{1,0:T(8,128)(2,1)S(1)}, u32[]{:S(2)}, u32[]{:S(2)}) collective-permute-start(bf16[128,512]{1,0:T(8,128)(2,1)S(1)} %pad_maximum_fusion.12), channel_id=1, source_target_pairs={{0,24},{1,25},{2,26},{3,27},{4,28},{5,29},{6,30},{7,31},{8,16},{9,... | collective-permute-start | bytes 393224 | tf_op jit(solution)/shard_map/ppermute | solution.py:602
  11.5 18.0 %copy-start.7 = (bf16[512,512]{1,0:T(8,128)(2,1)S(1)}, bf16[512,512]{1,0:T(8,128)(2,1)}, u32[]{:S(2)}) copy-start(bf16[512,512]{1,0:T(8,128)(2,1)} %refs_0_.1) | copy-start | bytes 1572868
  27.7 7.7 %collective-permute-start.4 = (bf16[3,256,512]{2,1,0:T(8,128)(2,1)S(1)}, bf16[3,256,512]{2,1,0:T(8,128)(2,1)S(1)}, u32[]{:S(2)}, u32[]{:S(2)}) collective-permute-start(bf16[3,256,512]{2,1,0:T(8,128)(2,1)S(1)} %collective-permute-done), channel_id=1, source_target_pairs={{0,2},{1,3},{2,0},{3,1},{4,6},{5,7},{6,4},{7,5},{8,10},{9,11},{10,... | collective-permute-start | bytes 2359304 | tf_op jit(solution)/shard_map/ppermute | solution.py:602
  29.5 2.4 %collective-permute-start.5 = (bf16[512]{0:T(512)(128)(2,1)S(1)}, bf16[512]{0:T(512)(128)(2,1)S(1)}, u32[]{:S(2)}, u32[]{:S(2)}) collective-permute-start(bf16[512]{0:T(512)(128)(2,1)S(1)} %copy-done.13), channel_id=1, source_target_pairs={{0,1},{1,0},{2,3},{3,2},{4,5},{5,4},{6,7},{7,6},{8,9},{9,8},{10,11... | collective-permute-start | bytes 3080 | tf_op jit(solution)/shard_map/ppermute | solution.py:602
  32.6 18.8 %collective-permute-start.7 = (bf16[4,128,512]{2,1,0:T(8,128)(2,1)S(1)}, bf16[4,128,512]{2,1,0:T(8,128)(2,1)S(1)}, u32[]{:S(2)}, u32[]{:S(2)}) collective-permute-start(bf16[4,128,512]{2,1,0:T(8,128)(2,1)S(1)} %pad_maximum_fusion.4), channel_id=1, source_target_pairs={{0,4},{1,5},{2,6},{3,7},{4,0},{5,1},{6,2},{7,3},{8,12},{9,13},{10,... | collective-permute-start | bytes 1572872 | tf_op jit(solution)/shard_map/ppermute | solution.py:602
  33.9 17.5 %collective-permute-start.8 = (bf16[4,128,512]{2,1,0:T(8,128)(2,1)S(1)}, bf16[4,128,512]{2,1,0:T(8,128)(2,1)S(1)}, u32[]{:S(2)}, u32[]{:S(2)}) collective-permute-start(bf16[4,128,512]{2,1,0:T(8,128)(2,1)S(1)} %pad_maximum_fusion.4), channel_id=1, source_target_pairs={{0,1},{1,0},{2,3},{3,2},{4,5},{5,4},{6,7},{7,6},{8,9},{9,8},{10,11... | collective-permute-start | bytes 1572872 | tf_op jit(solution)/shard_map/ppermute | solution.py:602
  34.1 17.3 %collective-permute-start.6 = (bf16[256,512]{1,0:T(8,128)(2,1)S(1)}, bf16[256,512]{1,0:T(8,128)(2,1)S(1)}, u32[]{:S(2)}, u32[]{:S(2)}) collective-permute-start(bf16[256,512]{1,0:T(8,128)(2,1)S(1)} %constant_dynamic-slice_fusion), channel_id=1, source_target_pairs={{0,1},{1,0},{2,3},{3,2},{4,5},{5,4},{6,7},{7,6},{8,9},{9,8},{10,11... | collective-permute-start | bytes 786440 | tf_op jit(solution)/shard_map/ppermute | solution.py:602
  51.4 0.7 copy-start.5
  52.1 11.0 %collective-permute-start.10 = (bf16[4,128,512]{2,1,0:T(8,128)(2,1)S(1)}, bf16[4,128,512]{2,1,0:T(8,128)(2,1)S(1)}, u32[]{:S(2)}, u32[]{:S(2)}) collective-permute-start(bf16[4,128,512]{2,1,0:T(8,128)(2,1)S(1)} %collective-permute-done.8), channel_id=1, source_target_pairs={{0,4},{1,5},{2,6},{3,7},{4,0},{5,1},{6,2},{7,3},{8,12},{9,13},{10,... | collective-permute-start | bytes 1572872 | tf_op jit(solution)/shard_map/ppermute | solution.py:602
  52.4 14.8 %copy-start.14 = (bf16[512]{0:T(512)(128)(2,1)S(1)}, bf16[512]{0:T(512)(128)(2,1)}, u32[]{:S(2)}) copy-start(bf16[512]{0:T(512)(128)(2,1)} %param.21) | copy-start | bytes 3076
  52.4 15.4 %copy-start.6 = (bf16[256,512]{1,0:T(8,128)(2,1)S(1)}, bf16[256,512]{1,0:T(8,128)(2,1)}, u32[]{:S(2)}) copy-start(bf16[256,512]{1,0:T(8,128)(2,1)} %copy-done.5) | copy-start | bytes 786436
  52.5 17.8 %collective-permute-start.11 = (bf16[8,128,512]{2,1,0:T(8,128)(2,1)S(1)}, bf16[8,128,512]{2,1,0:T(8,128)(2,1)S(1)}, u32[]{:S(2)}, u32[]{:S(2)}) collective-permute-start(bf16[8,128,512]{2,1,0:T(8,128)(2,1)S(1)} %pad_maximum_fusion), channel_id=1, source_target_pairs={{0,2},{1,3},{2,0},{3,1},{4,6},{5,7},{6,4},{7,5},{8,10},{9,11},{10,... | collective-permute-start | bytes 3145736 | tf_op jit(solution)/shard_map/ppermute | solution.py:602
  63.2 7.1 %collective-permute-start.12 = (bf16[8,128,512]{2,1,0:T(8,128)(2,1)S(1)}, bf16[8,128,512]{2,1,0:T(8,128)(2,1)S(1)}, u32[]{:S(2)}, u32[]{:S(2)}) collective-permute-start(bf16[8,128,512]{2,1,0:T(8,128)(2,1)S(1)} %pad_maximum_fusion.1), channel_id=1, source_target_pairs={{0,2},{1,3},{2,0},{3,1},{4,6},{5,7},{6,4},{7,5},{8,10},{9,11},{10,... | collective-permute-start | bytes 3145736 | tf_op jit(solution)/shard_map/ppermute | solution.py:602
  67.8 1.5 collective-permute-start.9
  70.5 2.0 copy-start.8
  117.7 24.4 %collective-permute-start.36 = (bf16[16,64,512]{2,1,0:T(8,128)(2,1)}, bf16[16,64,512]{2,1,0:T(8,128)(2,1)}, u32[]{:S(2)}, u32[]{:S(2)}) collective-permute-start(bf16[16,64,512]{2,1,0:T(8,128)(2,1)} %get-tuple-element.106), channel_id=1, source_target_pairs={{0,2},{1,3},{2,0},{3,1},{4,6},{5,7},{6,4},{7,5},{8,10},{9,11},{10,... | collective-permute-start | bytes 3145736 | tf_op jit(solution)/shard_map/ppermute | solution.py:602
  118.2 26.5 %collective-permute-start.31 = (bf16[16,64,512]{2,1,0:T(8,128)(2,1)}, bf16[16,64,512]{2,1,0:T(8,128)(2,1)}, u32[]{:S(2)}, u32[]{:S(2)}) collective-permute-start(bf16[16,64,512]{2,1,0:T(8,128)(2,1)} %get-tuple-element.104), channel_id=1, source_target_pairs={{0,2},{1,3},{2,0},{3,1},{4,6},{5,7},{6,4},{7,5},{8,10},{9,11},{10,... | collective-permute-start | bytes 3145736 | tf_op jit(solution)/shard_map/ppermute | solution.py:602
  118.3 23.7 %copy-start.11 = (f32[8,512]{1,0:T(8,128)S(1)}, f32[8,512]{1,0:T(8,128)}, u32[]{:S(2)}) copy-start(f32[8,512]{1,0:T(8,128)} %get-tuple-element.93) | copy-start | bytes 49156
  118.3 23.8 %copy-start.3 = (bf16[16,64,512]{2,1,0:T(8,128)(2,1)S(1)}, bf16[16,64,512]{2,1,0:T(8,128)(2,1)}, u32[]{:S(2)}) copy-start(bf16[16,64,512]{2,1,0:T(8,128)(2,1)} %get-tuple-element.105) | copy-start | bytes 3145732
  140.5 4.2 %copy-start.1 = (bf16[16,64,512]{2,1,0:T(8,128)(2,1)S(1)}, bf16[16,64,512]{2,1,0:T(8,128)(2,1)}, u32[]{:S(2)}) copy-start(bf16[16,64,512]{2,1,0:T(8,128)(2,1)} %get-tuple-element.103) | copy-start | bytes 3145732
  140.5 6.7 %collective-permute-start.14 = (bf16[2,256,1024]{2,1,0:T(8,128)(2,1)}, bf16[2,256,1024]{2,1,0:T(8,128)(2,1)}, u32[]{:S(2)}, u32[]{:S(2)}) collective-permute-start(bf16[2,256,1024]{2,1,0:T(8,128)(2,1)} %get-tuple-element.88), channel_id=1, source_target_pairs={{0,2},{1,3},{2,0},{3,1},{4,6},{5,7},{6,4},{7,5},{8,10},{9,11},{10,... | collective-permute-start | bytes 3145736 | tf_op jit(solution)/shard_map/ppermute | solution.py:602
  141.0 9.2 %collective-permute-start.13 = (bf16[2,256,1024]{2,1,0:T(8,128)(2,1)}, bf16[2,256,1024]{2,1,0:T(8,128)(2,1)}, u32[]{:S(2)}, u32[]{:S(2)}) collective-permute-start(bf16[2,256,1024]{2,1,0:T(8,128)(2,1)} %get-tuple-element.86), channel_id=1, source_target_pairs={{0,2},{1,3},{2,0},{3,1},{4,6},{5,7},{6,4},{7,5},{8,10},{9,11},{10,... | collective-permute-start | bytes 3145736 | tf_op jit(solution)/shard_map/ppermute | solution.py:602
  144.5 2.8 %copy-start.2 = (bf16[2,256,1024]{2,1,0:T(8,128)(2,1)S(1)}, bf16[2,256,1024]{2,1,0:T(8,128)(2,1)}, u32[]{:S(2)}) copy-start(bf16[2,256,1024]{2,1,0:T(8,128)(2,1)} %get-tuple-element.87) | copy-start | bytes 3145732
  144.5 24.9 %collective-permute-start.37 = (bf16[2,1,2,2,64,512]{5,4,3,2,1,0:T(8,128)(2,1)}, bf16[2,1,2,2,64,512]{5,4,3,2,1,0:T(8,128)(2,1)}, u32[]{:S(2)}, u32[]{:S(2)}) collective-permute-start(bf16[2,1,2,2,64,512]{5,4,3,2,1,0:T(8,128)(2,1)} %get-tuple-element.114), channel_id=1, source_target_pairs={{0,4},{1,5},{2,6},{3,7},{4,0},{5,1},{6,2},{7,3},{8,12},{9,13},{10,... | collective-permute-start | bytes 1572872 | tf_op jit(solution)/shard_map/ppermute | solution.py:602
  147.1 3.1 %copy-start = (bf16[2,256,1024]{2,1,0:T(8,128)(2,1)S(1)}, bf16[2,256,1024]{2,1,0:T(8,128)(2,1)}, u32[]{:S(2)}) copy-start(bf16[2,256,1024]{2,1,0:T(8,128)(2,1)} %get-tuple-element.85) | copy-start | bytes 3145732
  147.1 23.9 %collective-permute-start.32 = (bf16[1,2,2,2,64,512]{5,4,3,2,1,0:T(8,128)(2,1)}, bf16[1,2,2,2,64,512]{5,4,3,2,1,0:T(8,128)(2,1)}, u32[]{:S(2)}, u32[]{:S(2)}) collective-permute-start(bf16[1,2,2,2,64,512]{5,4,3,2,1,0:T(8,128)(2,1)} %bitcast.28), channel_id=1, source_target_pairs={{0,1},{1,0},{2,3},{3,2},{4,5},{5,4},{6,7},{7,6},{8,9},{9,8},{10,11... | collective-permute-start | bytes 1572872 | tf_op jit(solution)/shard_map/ppermute | solution.py:602
  149.8 23.6 %collective-permute-start.16 = (bf16[2,128,1024]{2,1,0:T(8,128)(2,1)}, bf16[2,128,1024]{2,1,0:T(8,128)(2,1)S(1)}, u32[]{:S(2)}, u32[]{:S(2)}) collective-permute-start(bf16[2,128,1024]{2,1,0:T(8,128)(2,1)} %get-tuple-element.117), channel_id=1, source_target_pairs={{0,8},{1,9},{2,10},{3,11},{4,12},{5,13},{6,14},{7,15},{8,0},{9,1},... | collective-permute-start | bytes 1572872 | tf_op jit(solution)/shard_map/ppermute | solution.py:602
  152.6 20.8 %collective-permute-start.15 = (bf16[1,256,1024]{2,1,0:T(8,128)(2,1)}, bf16[1,256,1024]{2,1,0:T(8,128)(2,1)S(1)}, u32[]{:S(2)}, u32[]{:S(2)}) collective-permute-start(bf16[1,256,1024]{2,1,0:T(8,128)(2,1)} %get-tuple-element.119), channel_id=1, source_target_pairs={{0,1},{1,0},{2,3},{3,2},{4,5},{5,4},{6,7},{7,6},{8,9},{9,8},{10,11... | collective-permute-start | bytes 1572872 | tf_op jit(solution)/shard_map/ppermute | solution.py:602
  170.6 6.4 %collective-permute-start.38 = (bf16[1,1,2,2,64,512]{5,4,3,2,1,0:T(8,128)(2,1)S(1)}, bf16[1,1,2,2,64,512]{5,4,3,2,1,0:T(8,128)(2,1)S(1)}, u32[]{:S(2)}, u32[]{:S(2)}) collective-permute-start(bf16[1,1,2,2,64,512]{5,4,3,2,1,0:T(8,128)(2,1)S(1)} %get-tuple-element.127), channel_id=1, source_target_pairs={{0,1},{1,0},{2,3},{3,2},{4,5},{5,4},{6,7},{7,6},{8,9},{9,8},{10,11... | collective-permute-start | bytes 786440 | tf_op jit(solution)/shard_map/ppermute | solution.py:602
  172.1 6.2 %collective-permute-start.33 = (bf16[1,1,2,2,64,512]{5,4,3,2,1,0:T(8,128)(2,1)S(1)}, bf16[1,1,2,2,64,512]{5,4,3,2,1,0:T(8,128)(2,1)S(1)}, u32[]{:S(2)}, u32[]{:S(2)}) collective-permute-start(bf16[1,1,2,2,64,512]{5,4,3,2,1,0:T(8,128)(2,1)S(1)} %get-tuple-element.129), channel_id=1, source_target_pairs={{0,4},{1,5},{2,6},{3,7},{4,0},{5,1},{6,2},{7,3},{8,12},{9,13},{10,... | collective-permute-start | bytes 786440 | tf_op jit(solution)/shard_map/ppermute | solution.py:602
  173.6 11.6 %collective-permute-start.17 = (bf16[1,144,1024]{2,1,0:T(8,128)(2,1)S(1)}, bf16[1,144,1024]{2,1,0:T(8,128)(2,1)S(1)}, u32[]{:S(2)}, u32[]{:S(2)}) collective-permute-start(bf16[1,144,1024]{2,1,0:T(8,128)(2,1)S(1)} %pad_maximum_fusion.7), channel_id=1, source_target_pairs={{0,1},{1,0},{2,3},{3,2},{4,5},{5,4},{6,7},{7,6},{8,9},{9,8},{10,11... | collective-permute-start | bytes 884744 | tf_op jit(solution)/shard_map/ppermute | solution.py:602
  175.0 9.0 %collective-permute-start.20 = (bf16[1,128,1024]{2,1,0:T(8,128)(2,1)S(1)}, bf16[1,128,1024]{2,1,0:T(8,128)(2,1)S(1)}, u32[]{:S(2)}, u32[]{:S(2)}) collective-permute-start(bf16[1,128,1024]{2,1,0:T(8,128)(2,1)S(1)} %get-tuple-element.131), channel_id=1, source_target_pairs={{0,4},{1,5},{2,6},{3,7},{4,0},{5,1},{6,2},{7,3},{8,12},{9,13},{10,... | collective-permute-start | bytes 786440 | tf_op jit(solution)/shard_map/ppermute | solution.py:602
  177.1 9.4 %collective-permute-start.39 = (bf16[1,1,2,1,64,512]{5,4,3,2,1,0:T(8,128)(2,1)S(1)}, bf16[1,1,2,1,64,512]{5,4,3,2,1,0:T(8,128)(2,1)S(1)}, u32[]{:S(2)}, u32[]{:S(2)}) collective-permute-start(bf16[1,1,2,1,64,512]{5,4,3,2,1,0:T(8,128)(2,1)S(1)} %get-tuple-element.137), channel_id=1, source_target_pairs={{0,8},{1,9},{2,10},{3,11},{4,12},{5,13},{6,14},{7,15},{8,0},{9,1},... | collective-permute-start | bytes 393224 | tf_op jit(solution)/shard_map/ppermute | solution.py:602
  178.4 10.6 %collective-permute-start.34 = (bf16[1,1,2,1,64,512]{5,4,3,2,1,0:T(8,128)(2,1)S(1)}, bf16[1,1,2,1,64,512]{5,4,3,2,1,0:T(8,128)(2,1)S(1)}, u32[]{:S(2)}, u32[]{:S(2)}) collective-permute-start(bf16[1,1,2,1,64,512]{5,4,3,2,1,0:T(8,128)(2,1)S(1)} %get-tuple-element.139), channel_id=1, source_target_pairs={{0,8},{1,9},{2,10},{3,11},{4,12},{5,13},{6,14},{7,15},{8,0},{9,1},... | collective-permute-start | bytes 393224 | tf_op jit(solution)/shard_map/ppermute | solution.py:602
  184.0 8.1 %collective-permute-start.21 = (bf16[1,64,1024]{2,1,0:T(8,128)(2,1)S(1)}, bf16[1,64,1024]{2,1,0:T(8,128)(2,1)S(1)}, u32[]{:S(2)}, u32[]{:S(2)}) collective-permute-start(bf16[1,64,1024]{2,1,0:T(8,128)(2,1)S(1)} %get-tuple-element.143), channel_id=1, source_target_pairs={{0,8},{1,9},{2,10},{3,11},{4,12},{5,13},{6,14},{7,15},{8,0},{9,1},... | collective-permute-start | bytes 393224 | tf_op jit(solution)/shard_map/ppermute | solution.py:602
  185.3 4.2 %collective-permute-start.18 = (bf16[1,80,1024]{2,1,0:T(8,128)(2,1)S(1)}, bf16[1,80,1024]{2,1,0:T(8,128)(2,1)S(1)}, u32[]{:S(2)}, u32[]{:S(2)}) collective-permute-start(bf16[1,80,1024]{2,1,0:T(8,128)(2,1)S(1)} %pad_maximum_fusion.10), channel_id=1, source_target_pairs={{0,4},{1,5},{2,6},{3,7},{4,0},{5,1},{6,2},{7,3},{8,12},{9,13},{10,... | collective-permute-start | bytes 491528 | tf_op jit(solution)/shard_map/ppermute | solution.py:602
  186.5 35.1 %collective-permute-start.40 = (bf16[1,1,1,1,64,512]{5,4,3,2,1,0:T(8,128)(2,1)S(1)}, bf16[1,1,1,1,64,512]{5,4,3,2,1,0:T(8,128)(2,1)S(1)}, u32[]{:S(2)}, u32[]{:S(2)}) collective-permute-start(bf16[1,1,1,1,64,512]{5,4,3,2,1,0:T(8,128)(2,1)S(1)} %add_convert_fusion.25), channel_id=1, source_target_pairs={{0,16},{1,17},{2,18},{3,19},{4,20},{5,21},{6,22},{7,23},{8,24},{9,... | collective-permute-start | bytes 196616 | tf_op jit(solution)/shard_map/ppermute | solution.py:602
  189.0 33.3 %collective-permute-start.35 = (bf16[1,1,1,1,64,512]{5,4,3,2,1,0:T(8,128)(2,1)S(1)}, bf16[1,1,1,1,64,512]{5,4,3,2,1,0:T(8,128)(2,1)S(1)}, u32[]{:S(2)}, u32[]{:S(2)}) collective-permute-start(bf16[1,1,1,1,64,512]{5,4,3,2,1,0:T(8,128)(2,1)S(1)} %add_convert_fusion.28), channel_id=1, source_target_pairs={{0,16},{1,17},{2,18},{3,19},{4,20},{5,21},{6,22},{7,23},{8,24},{9,... | collective-permute-start | bytes 196616 | tf_op jit(solution)/shard_map/ppermute | solution.py:602
  189.6 10.7 %collective-permute-start.19 = (bf16[1,48,1024]{2,1,0:T(8,128)(2,1)S(1)}, bf16[1,48,1024]{2,1,0:T(8,128)(2,1)S(1)}, u32[]{:S(2)}, u32[]{:S(2)}) collective-permute-start(bf16[1,48,1024]{2,1,0:T(8,128)(2,1)S(1)} %pad_maximum_fusion.14), channel_id=1, source_target_pairs={{0,16},{1,17},{2,18},{3,19},{4,20},{5,21},{6,22},{7,23},{8,24},{9,... | collective-permute-start | bytes 294920 | tf_op jit(solution)/shard_map/ppermute | solution.py:602
  192.2 10.2 %collective-permute-start.22 = (bf16[1,32,1024]{2,1,0:T(8,128)(2,1)S(1)}, bf16[1,32,1024]{2,1,0:T(8,128)(2,1)S(1)}, u32[]{:S(2)}, u32[]{:S(2)}) collective-permute-start(bf16[1,32,1024]{2,1,0:T(8,128)(2,1)S(1)} %add_convert_fusion.33), channel_id=1, source_target_pairs={{0,16},{1,17},{2,18},{3,19},{4,20},{5,21},{6,22},{7,23},{8,24},{9,... | collective-permute-start | bytes 196616 | tf_op jit(solution)/shard_map/ppermute | solution.py:602
  200.3 4.1 %collective-permute-start.25 = (bf16[1,32,1024]{2,1,0:T(8,128)(2,1)S(1)}, bf16[1,32,1024]{2,1,0:T(8,128)(2,1)S(1)}, u32[]{:S(2)}, u32[]{:S(2)}) collective-permute-start(bf16[1,32,1024]{2,1,0:T(8,128)(2,1)S(1)} %get-tuple-element.112), channel_id=1, source_target_pairs={{0,16},{1,17},{2,18},{3,19},{4,20},{5,21},{6,22},{7,23},{8,24},{9,... | collective-permute-start | bytes 196616 | tf_op jit(solution)/shard_map/ppermute | solution.py:602
  202.4 4.4 %collective-permute-start.23 = (bf16[1,32,1024]{2,1,0:T(8,128)(2,1)S(1)}, bf16[1,32,1024]{2,1,0:T(8,128)(2,1)S(1)}, u32[]{:S(2)}, u32[]{:S(2)}) collective-permute-start(bf16[1,32,1024]{2,1,0:T(8,128)(2,1)S(1)} %add_convert_fusion.32), channel_id=1, source_target_pairs={{0,16},{1,17},{2,18},{3,19},{4,20},{5,21},{6,22},{7,23},{8,24},{9,... | collective-permute-start | bytes 196616 | tf_op jit(solution)/shard_map/ppermute | solution.py:602
  204.4 5.0 %collective-permute-start.26 = (bf16[1,64,1024]{2,1,0:T(8,128)(2,1)S(1)}, bf16[1,64,1024]{2,1,0:T(8,128)(2,1)S(1)}, u32[]{:S(2)}, u32[]{:S(2)}) collective-permute-start(bf16[1,64,1024]{2,1,0:T(8,128)(2,1)S(1)} %pad_maximum_fusion.13), channel_id=1, source_target_pairs={{0,4},{1,5},{2,6},{3,7},{4,0},{5,1},{6,2},{7,3},{8,12},{9,13},{10,... | collective-permute-start | bytes 393224 | tf_op jit(solution)/shard_map/ppermute | solution.py:602
  206.8 4.9 %collective-permute-start.24 = (bf16[1,80,1024]{2,1,0:T(8,128)(2,1)S(1)}, bf16[1,80,1024]{2,1,0:T(8,128)(2,1)S(1)}, u32[]{:S(2)}, u32[]{:S(2)}) collective-permute-start(bf16[1,80,1024]{2,1,0:T(8,128)(2,1)S(1)} %pad_maximum_fusion.11), channel_id=1, source_target_pairs={{0,8},{1,9},{2,10},{3,11},{4,12},{5,13},{6,14},{7,15},{8,0},{9,1},... | collective-permute-start | bytes 491528 | tf_op jit(solution)/shard_map/ppermute | solution.py:602
  209.5 5.3 %collective-permute-start.27 = (bf16[1,128,1024]{2,1,0:T(8,128)(2,1)S(1)}, bf16[1,128,1024]{2,1,0:T(8,128)(2,1)S(1)}, u32[]{:S(2)}, u32[]{:S(2)}) collective-permute-start(bf16[1,128,1024]{2,1,0:T(8,128)(2,1)S(1)} %pad_maximum_fusion.8), channel_id=1, source_target_pairs={{0,8},{1,9},{2,10},{3,11},{4,12},{5,13},{6,14},{7,15},{8,0},{9,1},... | collective-permute-start | bytes 786440 | tf_op jit(solution)/shard_map/ppermute | solution.py:602
  211.8 11.2 %collective-permute-start.29 = (bf16[1,128,1024]{2,1,0:T(8,128)(2,1)S(1)}, bf16[1,128,1024]{2,1,0:T(8,128)(2,1)S(1)}, u32[]{:S(2)}, u32[]{:S(2)}) collective-permute-start(bf16[1,128,1024]{2,1,0:T(8,128)(2,1)S(1)} %pad_maximum_fusion.9), channel_id=1, source_target_pairs={{0,4},{1,5},{2,6},{3,7},{4,0},{5,1},{6,2},{7,3},{8,12},{9,13},{10,... | collective-permute-start | bytes 786440 | tf_op jit(solution)/shard_map/ppermute | solution.py:602
  214.8 10.8 %collective-permute-start.28 = (bf16[1,272,1024]{2,1,0:T(8,128)(2,1)S(1)}, bf16[1,272,1024]{2,1,0:T(8,128)(2,1)S(1)}, u32[]{:S(2)}, u32[]{:S(2)}) collective-permute-start(bf16[1,272,1024]{2,1,0:T(8,128)(2,1)S(1)} %get-tuple-element.109), channel_id=1, source_target_pairs={{0,2},{1,3},{2,0},{3,1},{4,6},{5,7},{6,4},{7,5},{8,10},{9,11},{10,... | collective-permute-start | bytes 1671176 | tf_op jit(solution)/shard_map/ppermute | solution.py:602
  223.9 3.8 %collective-permute-start.30 = (bf16[1,256,1024]{2,1,0:T(8,128)(2,1)S(1)}, bf16[1,256,1024]{2,1,0:T(8,128)(2,1)S(1)}, u32[]{:S(2)}, u32[]{:S(2)}) collective-permute-start(bf16[1,256,1024]{2,1,0:T(8,128)(2,1)S(1)} %get-tuple-element.140), channel_id=1, source_target_pairs={{0,2},{1,3},{2,0},{3,1},{4,6},{5,7},{6,4},{7,5},{8,10},{9,11},{10,... | collective-permute-start | bytes 1572872 | tf_op jit(solution)/shard_map/ppermute | solution.py:602
  227.7 0.8 copy-start.4

commit v3 on v2

v3 whole, which is shorter than its diff:
```python
import functools

import jax
import jax.numpy as jnp
from jax import lax
from jax.experimental import pallas as pl
from jax.experimental.pallas import tpu as pltpu
from jax.sharding import PartitionSpec as P

EPSILON = 1e-06
LONGEST = 2048
SEGMENTS = 8
PLACES = 16
STEPS = 64
BLOCK = SEGMENTS * STEPS
GROUP = 32
GELU_SLOPE = 0.7978845608028654
GELU_CUBE = 0.044715
VMEM_BYTES = 56 * 1024 * 1024
F32 = jnp.float32
BF16 = jnp.bfloat16


def dot_nn(left, right):
    return lax.dot_general(left, right, (((1,), (0,)), ((), ())), preferred_element_type=F32)


def dot_nt(left, right):
    return lax.dot_general(left, right, (((1,), (1,)), ((), ())), preferred_element_type=F32)


def row_scale(rows):
    return lax.rsqrt(jnp.mean(rows * rows, -1, keepdims=True) + EPSILON)


def fold_rows(values):
    return jnp.sum(values.reshape(-1, 8, values.shape[-1]), 0)


def put_blocks(values, halves, me, first):
    tall = values.shape[0] // PLACES
    for place in range(PLACES):
        block = pl.multiple_of((place ^ me) * tall, tall)
        there = (place % (PLACES // 2)) * tall
        out = halves[place // (PLACES // 2)]
        out[there : there + tall, first : first + values.shape[1]] = values[pl.ds(block, tall), :].astype(out.dtype)


def interleave(block, scratch):
    lanes = scratch.shape[0]
    for lane in range(lanes):
        for run in range(SEGMENTS):
            part = block[run, :, lane * 128 : (lane + 1) * 128]
            scratch[lane, pl.ds(run, block.shape[1], stride=SEGMENTS), :] = part.astype(F32)
    return jnp.concatenate([scratch[lane] for lane in range(lanes)], -1)


def separate(values, scratch, out):
    lanes = scratch.shape[0]
    for lane in range(lanes):
        scratch[lane] = values[:, lane * 128 : (lane + 1) * 128]
    for run in range(SEGMENTS):
        parts = [scratch[lane, pl.ds(run, out.shape[1], stride=SEGMENTS), :] for lane in range(lanes)]
        out[run] = jnp.concatenate(parts, -1).astype(out.dtype)


def gates(forget_logit, admit_logit):
    top = jnp.maximum(jnp.maximum(-admit_logit, -forget_logit), 0.0)
    one = jnp.exp(-top)
    admit_exp = jnp.exp(-admit_logit - top)
    forget_exp = jnp.exp(-forget_logit - top)
    keep_part = one + admit_exp
    admit_part = one + forget_exp
    total = keep_part + admit_part
    inverse = pl.reciprocal(total, approx=True)
    inverse = inverse * (2.0 - total * inverse)
    keep = keep_part * inverse
    admit = admit_part * inverse
    return keep, admit, keep * (forget_exp * inverse), -admit * (admit_exp * inverse)


def goes_on(lengths_ref, scalars_ref, run, tall):
    place = scalars_ref[0] + run * tall
    begin = jnp.int32(0)
    fresh = False
    for entry in range(lengths_ref.shape[1]):
        length = lengths_ref[0, entry]
        fresh = fresh | ((begin == place) & (length > 0))
        begin = begin + length
    return jnp.where(fresh, 0.0, 1.0).astype(F32)


def product_of_runs(values, masks):
    result = masks[0] * values[0:1]
    for run in range(1, SEGMENTS):
        result = result * (masks[run] * values[run : run + 1])
    return result


def mixer_kernel(first, *refs):
    if first:
        x_ref, gain_ref, *refs = refs
    else:
        normed_in, *refs = refs
    wf, wa, wv, bias, lengths, scalars, carry, *refs = refs
    if first:
        x_out, normed_out, *refs = refs
    admit_out, state_out, forget_fac, admit_fac, ends_out, *refs = refs
    logits, hs, ps, vs, fs, as_, enter, *refs = refs
    phase, block = pl.program_id(0), pl.program_id(1)
    channels = wf.shape[1]
    start = pl.multiple_of(block * BLOCK, BLOCK)

    @pl.when((phase == 0) & (block == 0))
    def _():
        hs[0:8, :] = jnp.zeros((8, channels), F32)
        ps[0:8, :] = jnp.ones((8, channels), F32)

    @pl.when(phase == 0)
    def _():
        if first:
            rows = interleave(x_ref[...], refs[0])
            x_out[...] = rows.astype(BF16)
            normed = (rows * row_scale(rows) * gain_ref[...]).astype(BF16)
            normed_out[...] = normed
        else:
            normed = normed_in[...]
        wide = min(channels, 256)
        chunks = channels // wide
        weights = (wf, wa, wv)

        def project(chunk, kind):
            logits[chunk, kind] = dot_nn(normed, weights[kind][:, chunk * wide : (chunk + 1) * wide])

        def gate(chunk, lane, here, chain):
            inner, cols = slice(lane, lane + 128), slice(chunk * wide + lane, chunk * wide + lane + 128)
            rows = slice(here, here + GROUP)
            there = pl.ds(start + here, GROUP)
            value = logits[chunk, 2, rows, inner]
            keep, admit, forget_side, admit_side = gates(
                logits[chunk, 0, rows, inner], logits[chunk, 1, rows, inner] + bias[:, cols]
            )
            admit_out[rows, cols] = admit.astype(BF16)
            vs[there, cols] = value
            fs[there, cols] = forget_side
            as_[there, cols] = admit_side
            inflow = admit * value
            state, gain = chain
            for step in range(0, GROUP, 8):
                state = keep[step : step + 8] * state + inflow[step : step + 8]
                gain = gain * keep[step : step + 8]
                hs[pl.ds(start + here + step + 8, 8), cols] = state
                ps[pl.ds(start + here + step + 8, 8), cols] = gain
            return state, gain

        for kind in range(3):
            project(0, kind)
        for chunk in range(chunks):
            firsts = range(chunk * wide, (chunk + 1) * wide, 128)
            chains = [(hs[pl.ds(start, 8), c : c + 128], ps[pl.ds(start, 8), c : c + 128]) for c in firsts]
            units = [(here, lane) for here in range(0, BLOCK, GROUP) for lane in range(len(chains))]
            ahead = [(chunk + 1, kind) for kind in range(3)] if chunk + 1 < chunks else []
            for index, (here, lane) in enumerate(units):
                if ahead and index % max(1, len(units) // 3) == 0:
                    project(*ahead.pop(0))
                chains[lane] = gate(chunk, lane * 128, here, chains[lane])
            for item in ahead:
                project(*item)

    @pl.when((phase == 1) & (block == 0))
    def _():
        total = hs.shape[0]
        ends, gains = hs[total - 8 : total, :], ps[total - 8 : total, :]
        masks = [goes_on(lengths, scalars, run, (total - 8) // SEGMENTS) for run in range(SEGMENTS)]
        entering = masks[0] * carry[...]
        enter[0:1] = entering
        for run in range(1, SEGMENTS):
            entering = masks[run] * (ends[run - 1 : run] + gains[run - 1 : run] * entering)
            enter[run : run + 1] = entering
        ends_out[0:1, :] = ends[7:8] + gains[7:8] * enter[7:8, :]
        ends_out[1:2, :] = product_of_runs(gains, masks)
        ends_out[2:8, :] = jnp.zeros((6, channels), F32)

    @pl.when(phase == 1)
    def _():
        def some_rows(group, _):
            here = pl.multiple_of(group * 64, 64)
            there = pl.multiple_of(start + here, 64)
            for lane in range(0, channels, 128):
                cols = pl.ds(lane, 128)
                entering = enter[:, lane : lane + 128]
                states = hs[pl.ds(there, 72), cols].reshape(9, 8, 128) + ps[pl.ds(there, 72), cols].reshape(9, 8, 128) * entering
                states = states.reshape(72, 128)
                state_out[pl.ds(here, 64), cols] = states[8:].astype(BF16)
                change = states[:64] - vs[pl.ds(there, 64), cols]
                forget_fac[pl.ds(here, 64), cols] = (change * fs[pl.ds(there, 64), cols]).astype(BF16)
                admit_fac[pl.ds(here, 64), cols] = (change * as_[pl.ds(there, 64), cols]).astype(BF16)
            return 0

        lax.fori_loop(0, BLOCK // 64, some_rows, 0)


def mixer_forward(first, rows_in, gain, weights, bias, lengths, scalars, carry):
    width = rows_in.shape[-1]
    rows = rows_in.size // width
    channels = weights[0].shape[1]
    blocks = rows // BLOCK
    early = lambda phase, block: (jnp.where(phase == 0, block, blocks - 1), 0)
    late = lambda phase, block: (jnp.where(phase == 0, 0, block), 0)
    whole = lambda phase, block: (0, 0)
    if first:
        in_specs = [
            pl.BlockSpec((SEGMENTS, STEPS, width), lambda phase, block: (0, jnp.where(phase == 0, block, blocks - 1), 0)),
            pl.BlockSpec((1, width), whole),
        ]
        operands = [rows_in.reshape(SEGMENTS, rows // SEGMENTS, width), gain]
        out_specs = [pl.BlockSpec((BLOCK, width), early)] * 2
        out_shape = [jax.ShapeDtypeStruct((rows, width), BF16)] * 2
    else:
        in_specs, operands = [pl.BlockSpec((BLOCK, width), early)], [rows_in]
        out_specs, out_shape = [], []
    in_specs += [pl.BlockSpec((width, channels), whole)] * 3
    in_specs += [pl.BlockSpec((1, channels), whole)] + [pl.BlockSpec(memory_space=pltpu.SMEM)] * 2 + [pl.BlockSpec((1, channels), whole)]
    out_specs += [pl.BlockSpec((BLOCK, channels), early)] + [pl.BlockSpec((BLOCK, channels), late)] * 3
    out_specs += [pl.BlockSpec((8, channels), whole)]
    out_shape += [jax.ShapeDtypeStruct((rows, channels), BF16)] * 4
    out_shape += [jax.ShapeDtypeStruct((8, channels), F32)]
    wide = min(channels, 256)
    scratch = [pltpu.VMEM((channels // wide, 3, BLOCK, wide), F32)]
    scratch += [pltpu.VMEM((rows + 8, channels), F32)] * 2
    scratch += [pltpu.VMEM((rows, channels), F32)] * 3
    scratch += [pltpu.VMEM((8, channels), F32)]
    if first:
        scratch += [pltpu.VMEM((width // 128, BLOCK, 128), F32)]
    return pl.pallas_call(
        functools.partial(mixer_kernel, first),
        grid=(2, blocks),
        in_specs=in_specs,
        out_specs=out_specs,
        out_shape=out_shape,
        scratch_shapes=scratch,
        compiler_params=pltpu.CompilerParams(vmem_limit_bytes=VMEM_BYTES, dimension_semantics=("arbitrary", "arbitrary")),
        cost_estimate=pl.CostEstimate(flops=2 * rows * width * 3 * channels, bytes_accessed=rows * channels * 16, transcendentals=4 * rows * channels),
        name="mixer_forward",
    )(*operands, *weights, bias, lengths, scalars, carry)


def dense_kernel(stage, sets, pieces, *refs):
    states, refs = refs[:sets], refs[sets:]
    if stage == 0:
        x_ref, c_ref, *refs = refs
        outs_w, refs = refs[:sets], refs[sets:]
    else:
        middle_ref, sum_ref, delta_ref, dense_ref, cotangent_ref, *refs = refs
    gain_ref, scalars, *refs = refs
    pieces_w, refs = refs[:pieces], refs[pieces:]
    keep_out, send_out, *refs = refs
    if stage == 0:
        middle_out, sum_out, delta_out, dense_out, cotangent_out, upper_acc, lower_acc, cotangent_s = refs
    else:
        out_ref, mixed_ref, slope_ref, *refs = refs
        outputs_ref, refs = refs[:sets], refs[sets:]
        upper_acc, lower_acc, output_acc, out_s = refs
    step = pl.program_id(0)
    gain = gain_ref[...]
    shards, both, width = pieces_w[0].shape
    half = both // 2

    @pl.when(step == 0)
    def _():
        upper_acc[...] = jnp.zeros_like(upper_acc)
        lower_acc[...] = jnp.zeros_like(lower_acc)
        if stage == 1:
            output_acc[...] = jnp.zeros_like(output_acc)
            slope_ref[...] = jnp.zeros_like(slope_ref)

    if stage == 0:
        middle = x_ref[...].astype(F32)
        for state, weight in zip(states, outs_w):
            middle = middle + dot_nn(state[...], weight[...])
        middle_out[...] = middle
        dense_in = (middle * row_scale(middle) * gain).astype(BF16)
        dense_out[...] = dense_in
        cotangent = interleave(c_ref[...], cotangent_s).astype(BF16)
        cotangent_out[...] = cotangent
    else:
        dense_in, cotangent = dense_ref[...], cotangent_ref[...]
    dense_t, cotangent_t = dense_in.T, cotangent.T
    fed, delta = None, None
    joined = max(1, 512 // (shards * half))
    for chunk in range(0, pieces, joined):
        some = pieces_w[chunk : chunk + joined]
        upper_w = jnp.concatenate([w[:, :half, :].reshape(shards * half, width) for w in some], 0)
        lower_w = jnp.concatenate([w[:, half:, :].reshape(shards * half, width) for w in some], 0)
        cols = slice(chunk * shards * half, (chunk + joined) * shards * half)
        upper = dot_nt(dense_in, upper_w)
        square = upper * upper
        bell = 0.5 + 0.5 * jnp.tanh(upper * (GELU_SLOPE + GELU_SLOPE * GELU_CUBE * square))
        active = upper * bell
        slope = bell + active * (1.0 - bell) * (2.0 * GELU_SLOPE + 6.0 * GELU_SLOPE * GELU_CUBE * square)
        active = active.astype(BF16)
        part = dot_nn(active, lower_w)
        fed = part if fed is None else fed + part
        upper_delta = (slope * dot_nt(cotangent, lower_w)).astype(BF16)
        part = dot_nn(upper_delta, upper_w)
        delta = part if delta is None else delta + part
        lower_acc[:, cols] += dot_nn(cotangent_t, active)
        upper_acc[:, cols] += dot_nn(dense_t, upper_delta)
    if stage == 0:
        sum_out[...] = middle + fed
        delta_out[...] = delta
    else:
        separate(sum_ref[...] + fed, out_s, out_ref)
        middle = middle_ref[...]
        scale = row_scale(middle)
        delta = delta_ref[...] + delta
        slope_ref[...] += fold_rows(delta * middle * scale)
        scaled = delta * gain
        inner = jnp.mean(scaled * middle, -1, keepdims=True)
        mixed = (cotangent.astype(F32) + scale * (scaled - middle * (scale * scale * inner))).astype(BF16)
        mixed_ref[...] = mixed
        mixed_t = mixed.T
        channels = states[0].shape[1]
        for index, state in enumerate(states):
            output_acc[:, index * channels : (index + 1) * channels] += dot_nn(mixed_t, state[...])

    @pl.when(step == pl.num_programs(0) - 1)
    def _():
        for shard in range(0, pieces * shards, 2):
            cols = slice(shard * half, (shard + 2) * half)
            out = keep_out if shard < pieces * shards // 2 else send_out
            there = shard % (pieces * shards // 2)
            out[0, there : there + 2] = upper_acc[:, cols].T.astype(BF16).reshape(2, half, width)
            out[1, there : there + 2] = lower_acc[:, cols].T.astype(BF16).reshape(2, half, width)
        if stage == 1:
            tall = output_acc.shape[0] // PLACES
            for index, output in enumerate(outputs_ref):
                for place in range(PLACES):
                    there = pl.multiple_of((place ^ scalars[2]) * tall, tall)
                    output[place * tall : (place + 1) * tall, :] = output_acc[
                        pl.ds(there, tall), index * channels : (index + 1) * channels
                    ].astype(BF16)


def dense_both(stage, states, entering, output_weights, gain, scalars, pieces):
    rows, channels = states[0].shape
    width = gain.shape[1]
    shards, both, _ = pieces[0].shape
    hidden = len(pieces) * shards * both // 2
    sets = len(states)
    tall = min(rows, 512)
    by_rows = lambda block: (block, 0)
    whole = lambda block: (0, 0)
    runs_spec = pl.BlockSpec((SEGMENTS, tall // SEGMENTS, width), lambda block: (0, block, 0))
    runs_shape = (SEGMENTS, rows // SEGMENTS, width)
    row_spec = pl.BlockSpec((tall, width), by_rows)
    grads = (2, len(pieces) * shards // 2, both // 2, width)
    in_specs = [pl.BlockSpec((tall, channels), by_rows)] * sets
    out_specs = [pl.BlockSpec(grads, lambda block: (0, 0, 0, 0))] * 2
    out_shape = [jax.ShapeDtypeStruct(grads, BF16)] * 2
    scratch = [pltpu.VMEM((width, hidden), F32)] * 2
    if stage == 0:
        in_specs += [row_spec, runs_spec] + [pl.BlockSpec((channels, width), whole)] * sets
        entering = [entering[0], entering[1].reshape(runs_shape), *output_weights]
        out_specs += [row_spec] * 5
        out_shape += [jax.ShapeDtypeStruct((rows, width), d) for d in (F32, F32, F32, BF16, BF16)]
    else:
        in_specs += [row_spec] * 5
        out_specs += [runs_spec, row_spec, pl.BlockSpec((8, width), whole)] + [pl.BlockSpec((width, channels), whole)] * sets
        out_shape += [jax.ShapeDtypeStruct(runs_shape, BF16), jax.ShapeDtypeStruct((rows, width), BF16)]
        out_shape += [jax.ShapeDtypeStruct((8, width), F32)] + [jax.ShapeDtypeStruct((width, channels), BF16)] * sets
        scratch += [pltpu.VMEM((width, sets * channels), F32)]
    scratch += [pltpu.VMEM((width // 128, tall, 128), F32)]
    in_specs += [pl.BlockSpec((1, width), whole), pl.BlockSpec(memory_space=pltpu.SMEM)]
    in_specs += [pl.BlockSpec((shards, both, width), lambda block: (0, 0, 0))] * len(pieces)
    return pl.pallas_call(
        functools.partial(dense_kernel, stage, sets, len(pieces)),
        grid=(rows // tall,),
        in_specs=in_specs,
        out_specs=out_specs,
        out_shape=out_shape,
        scratch_shapes=scratch,
        compiler_params=pltpu.CompilerParams(vmem_limit_bytes=VMEM_BYTES, dimension_semantics=("arbitrary",)),
        cost_estimate=pl.CostEstimate(flops=12 * rows * width * hidden, bytes_accessed=rows * width * 24, transcendentals=rows * hidden),
        name="dense_first" if stage == 0 else "dense_second",
    )(*states, *entering, gain, scalars, *pieces)


def mixer_back_kernel(sets, mixed_ref, normed_ref, lengths, scalars, *refs):
    per_set = [refs[index * 6 : index * 6 + 6] for index in range(sets)]
    refs = refs[6 * sets :]
    carried_out, refs = refs[:sets], refs[sets:]
    first_out, second_out, refs = refs[:2], refs[2:4], refs[4:]
    bias_out, ends_out, *refs = refs
    cs, ps, state_delta, admits, deltas, slopes_acc, last, enter = refs
    phase, block = pl.program_id(0), pl.program_id(1)
    blocks = pl.num_programs(1)
    channels = per_set[0][1].shape[1]
    place = jnp.where(phase == 0, blocks - 1 - block, block)
    start = pl.multiple_of(place * BLOCK, BLOCK)

    @pl.when((phase == 0) & (block == 0))
    def _():
        last[:, 0:8, :] = jnp.zeros((sets, 8, channels), F32)
        last[:, 8:16, :] = jnp.ones((sets, 8, channels), F32)

    @pl.when(phase == 0)
    def _():
        def arrive(index):
            state_delta[index] = dot_nt(mixed_ref[...], per_set[index][0][...])

        arrive(0)
        for index in range(sets):
            admit_ref = per_set[index][1]
            for lane in range(0, channels, 128):
                if lane == 0 and index + 1 < sets:
                    arrive(index + 1)
                cols = slice(lane, lane + 128)
                kept, gain = last[index, 0:8, cols], last[index, 8:16, cols]
                for here in range(BLOCK - 16, -1, -16):
                    admit = admit_ref[here : here + 16, cols]
                    admits[index, pl.ds(start + here, 16), cols] = admit
                    keep = 1.0 - admit.astype(F32)
                    for step in (8, 0):
                        carried = state_delta[index, here + step : here + step + 8, cols] + kept
                        cs[index, pl.ds(start + here + step, 8), cols] = carried
                        ps[index, pl.ds(start + here + step, 8), cols] = gain
                        kept = keep[step : step + 8] * carried
                        gain = keep[step : step + 8] * gain
                last[index, 0:8, cols] = kept
                last[index, 8:16, cols] = gain

    @pl.when((phase == 1) & (block == 0))
    def _():
        masks = [goes_on(lengths, scalars, run, cs.shape[1] // SEGMENTS) for run in range(SEGMENTS)]
        for index in range(sets):
            kept, gain = last[index, 0:8, :], last[index, 8:16, :]
            entering = per_set[index][4][...]
            enter[index, 7:8, :] = entering
            for run in range(SEGMENTS - 1, 0, -1):
                entering = masks[run] * (kept[run : run + 1] + gain[run : run + 1] * entering)
                enter[index, run - 1 : run, :] = entering
            ends_out[index, 0:1, :] = masks[0] * (kept[0:1] + gain[0:1] * entering)
            ends_out[index, 1:2, :] = product_of_runs(gain, masks)
            ends_out[index, 2:8, :] = jnp.zeros((6, channels), F32)
        bias_out[...] = jnp.zeros_like(bias_out)
        slopes_acc[...] = jnp.zeros_like(slopes_acc)

    @pl.when(phase == 1)
    def _():
        normed_t = normed_ref[...].T
        wide = min(channels, 256)
        chunks = [(index, first) for index in range(sets) for first in range(0, channels, wide)]

        def move(index, lane, here):
            _, _, forget_fac, admit_fac, _, _ = per_set[index]
            cols = slice(lane, lane + 128)
            rows, there = slice(here, here + GROUP), pl.ds(start + here, GROUP)
            gains = ps[index, there, cols].reshape(GROUP // 8, 8, 128)
            carried = (cs[index, there, cols].reshape(GROUP // 8, 8, 128) + gains * enter[index, :, cols]).reshape(GROUP, 128)
            carried_out[index][rows, cols] = carried.astype(BF16)
            admit_delta = (carried * admit_fac[rows, cols].astype(F32)).astype(BF16)
            deltas[index, 0, rows, cols] = (carried * forget_fac[rows, cols].astype(F32)).astype(BF16)
            deltas[index, 1, rows, cols] = admit_delta
            deltas[index, 2, rows, cols] = (carried * admits[index, there, cols].astype(F32)).astype(BF16)
            return fold_rows(admit_delta.astype(F32))

        def reduce(index, first, kind):
            cols = slice(first, first + wide)
            slopes_acc[index, kind, :, cols] += dot_nn(normed_t, deltas[index, kind, :, cols])

        behind = []
        for index, first in chunks:
            lanes = range(first, first + wide, 128)
            biases = [jnp.zeros((8, 128), F32) for _ in lanes]
            units = [(here, which) for here in range(0, BLOCK, GROUP) for which in range(len(lanes))]
            for position, (here, which) in enumerate(units):
                if behind and position % max(1, len(units) // 3) == 0:
                    reduce(*behind.pop(0))
                biases[which] = biases[which] + move(index, lanes[which], here)
            for lane, bias in zip(lanes, biases):
                bias_out[index, :, lane : lane + 128] += bias
            for item in behind:
                reduce(*item)
            behind = [(index, first, kind) for kind in range(3)]
        for item in behind:
            reduce(*item)
        for index in range(sets):
            output_grads = per_set[index][5]
            tall = output_grads.shape[0]
            for half in range(2):

                @pl.when(block // (blocks // 2) == half)
                def _():
                    there = pl.multiple_of(block % (blocks // 2) * tall, tall)
                    second_out[half][index, pl.ds(there, tall), channels:] = output_grads[...]

    @pl.when((phase == 1) & (block == blocks - 1))
    def _():
        for index in range(sets):
            put_blocks(slopes_acc.at[index, 0], [out.at[index] for out in first_out], scalars[1], 0)
            put_blocks(slopes_acc.at[index, 1], [out.at[index] for out in first_out], scalars[1], channels)
            put_blocks(slopes_acc.at[index, 2], [out.at[index] for out in second_out], scalars[2], 0)


def mixer_backward(mixed, normed, lengths, scalars, per_set):
    rows, width = mixed.shape
    sets = len(per_set)
    channels = per_set[0][1].shape[1]
    blocks = rows // BLOCK
    back = lambda phase, block: (jnp.where(phase == 0, blocks - 1 - block, 0), 0)
    late = lambda phase, block: (jnp.where(phase == 0, 0, block), 0)
    whole = lambda phase, block: (0, 0)
    all3 = lambda phase, block: (0, 0, 0)
    set_specs = [
        pl.BlockSpec((channels, width), whole),
        pl.BlockSpec((BLOCK, channels), back),
        pl.BlockSpec((BLOCK, channels), late),
        pl.BlockSpec((BLOCK, channels), late),
        pl.BlockSpec((1, channels), whole),
        pl.BlockSpec((width // blocks, channels), late),
    ]
    results = pl.pallas_call(
        functools.partial(mixer_back_kernel, sets),
        grid=(2, blocks),
        in_specs=[
            pl.BlockSpec((BLOCK, width), back),
            pl.BlockSpec((BLOCK, width), late),
            pl.BlockSpec(memory_space=pltpu.SMEM),
            pl.BlockSpec(memory_space=pltpu.SMEM),
        ]
        + set_specs * sets,
        out_specs=[pl.BlockSpec((BLOCK, channels), late)] * sets
        + [pl.BlockSpec((sets, width // 2, 2 * channels), all3)] * 4
        + [pl.BlockSpec((sets, 8, channels), all3)] * 2,
        out_shape=[jax.ShapeDtypeStruct((rows, channels), BF16)] * sets
        + [jax.ShapeDtypeStruct((sets, width // 2, 2 * channels), BF16)] * 4
        + [jax.ShapeDtypeStruct((sets, 8, channels), F32)] * 2,
        scratch_shapes=[
            pltpu.VMEM((sets, rows, channels), F32),
            pltpu.VMEM((sets, rows, channels), F32),
            pltpu.VMEM((sets, BLOCK, channels), F32),
            pltpu.VMEM((sets, rows, channels), BF16),
            pltpu.VMEM((sets, 3, BLOCK, channels), BF16),
            pltpu.VMEM((sets, 3, width, channels), F32),
            pltpu.VMEM((sets, 16, channels), F32),
            pltpu.VMEM((sets, 8, channels), F32),
        ],
        compiler_params=pltpu.CompilerParams(vmem_limit_bytes=VMEM_BYTES, dimension_semantics=("arbitrary", "arbitrary")),
        cost_estimate=pl.CostEstimate(flops=2 * rows * width * 4 * channels * sets, bytes_accessed=rows * channels * 12 * sets, transcendentals=0),
        name="mixer_backward",
    )(mixed, normed, lengths, scalars, *[item for one in per_set for item in one])
    return results[:sets], results[sets : sets + 2], results[sets + 2 : sets + 4], *results[sets + 4 :]


def input_kernel(sets, *refs):
    x_ref, mixed_ref, gain_ref, *refs = refs
    factors, refs = refs[: 4 * sets], refs[4 * sets :]
    weights, refs = refs[: 3 * sets], refs[3 * sets :]
    out_ref, slope_ref, out_s = refs

    @pl.when(pl.program_id(0) == 0)
    def _():
        slope_ref[...] = jnp.zeros_like(slope_ref)

    normed_delta = None
    for index in range(sets):
        carried = factors[4 * index][...].astype(F32)
        for part in range(3):
            delta = (carried * factors[4 * index + 1 + part][...].astype(F32)).astype(BF16)
            term = dot_nt(delta, weights[3 * index + part][...])
            normed_delta = term if normed_delta is None else normed_delta + term
    rows = x_ref[...].astype(F32)
    scale = row_scale(rows)
    slope_ref[...] += fold_rows(normed_delta * rows * scale)
    scaled = normed_delta * gain_ref[...]
    inner = jnp.mean(scaled * rows, -1, keepdims=True)
    result = mixed_ref[...].astype(F32) + scale * (scaled - rows * (scale * scale * inner))
    separate(result, out_s, out_ref)


def input_backward(x_rows, mixed, gain, factors, weights):
    rows, width = x_rows.shape
    sets = len(factors) // 4
    channels = weights[0].shape[1]
    by_rows = lambda block: (block, 0)
    whole = lambda block: (0, 0)
    return pl.pallas_call(
        functools.partial(input_kernel, sets),
        grid=(rows // BLOCK,),
        in_specs=[pl.BlockSpec((BLOCK, width), by_rows)] * 2
        + [pl.BlockSpec((1, width), whole)]
        + [pl.BlockSpec((BLOCK, channels), by_rows)] * (4 * sets)
        + [pl.BlockSpec((width, channels), whole)] * (3 * sets),
        out_specs=[pl.BlockSpec((SEGMENTS, STEPS, width), lambda block: (0, block, 0)), pl.BlockSpec((8, width), whole)],
        out_shape=[jax.ShapeDtypeStruct((SEGMENTS, rows // SEGMENTS, width), F32), jax.ShapeDtypeStruct((8, width), F32)],
        scratch_shapes=[pltpu.VMEM((width // 128, BLOCK, 128), F32)],
        compiler_params=pltpu.CompilerParams(vmem_limit_bytes=VMEM_BYTES, dimension_semantics=("arbitrary",)),
        cost_estimate=pl.CostEstimate(flops=2 * rows * width * 3 * channels * sets, bytes_accessed=rows * channels * 8 * sets, transcendentals=0),
        name="input_backward",
    )(x_rows, mixed, gain, *factors, *weights)


def finish_kernel(channels, count, *refs):
    first_refs, second_refs = refs[:count], refs[count : 2 * count]
    scalars, forget_out, admit_out, value_out, output_out, scratch = refs[2 * count :]
    tall = scratch.shape[0] // PLACES
    each = PLACES // count
    for place in range(PLACES):
        here = slice(place % each * tall, (place % each + 1) * tall)
        for index, (sums, outs) in enumerate(((first_refs, (forget_out, admit_out)), (second_refs, (value_out, scratch)))):
            there = pl.multiple_of((place ^ scalars[1 + index]) * tall, tall)
            piece = sums[place // each]
            outs[0][pl.ds(there, tall), :] = piece[here, :channels].astype(F32)
            outs[1][pl.ds(there, tall), :] = piece[here, channels:].astype(F32)
    output_out[...] = scratch[...].T


def finish_slopes(first, second, scalars):
    count = len(first)
    width, channels = count * first[0].shape[0], first[0].shape[1] // 2
    return pl.pallas_call(
        functools.partial(finish_kernel, channels, count),
        in_specs=[pl.BlockSpec(memory_space=pltpu.VMEM)] * (2 * count) + [pl.BlockSpec(memory_space=pltpu.SMEM)],
        out_shape=[jax.ShapeDtypeStruct((width, channels), F32)] * 3 + [jax.ShapeDtypeStruct((channels, width), F32)],
        scratch_shapes=[pltpu.VMEM((width, channels), F32)],
        compiler_params=pltpu.CompilerParams(vmem_limit_bytes=VMEM_BYTES),
        name="finish_slopes",
    )(*first, *second, scalars)


def regroup(stacked, half):
    count, both, width = stacked.shape
    if both == 2 * half:
        return stacked
    arrays = jnp.moveaxis(stacked.reshape(count, 2, both // 2, width), 1, 0).reshape(2, -1, half, width)
    return jnp.moveaxis(arrays, 0, 1).reshape(-1, 2 * half, width)


def after(values, *earlier):
    return lax.optimization_barrier((values, earlier))[0]


def total(terms):
    result = terms[0].astype(F32)
    for term in terms[1:]:
        result = result + term.astype(F32)
    return result.astype(terms[0].dtype)


def hold(terms, *earlier):
    return terms[:-1] + [after(terms[-1], *earlier)]


def part(terms, index, axis):
    half = terms[0].shape[axis] // 2
    return [lax.slice_in_dim(t, index * half, (index + 1) * half, axis=axis) for t in terms]


class Links:
    TENSOR, CORE, NEAR, Z_NEAR, Z_FAR = 1, 2, 4, 8, 16

    def __init__(self):
        dp = lax.axis_index("dp")
        core, near, z_near, z_far = dp % 2, dp // 2 % 2, dp // 4 % 2, dp // 8
        self.core = core
        self.me = [core * 8 + z_near * 4 + near * 2 + z_far, core * 8 + near * 4 + z_near * 2 + z_far]

    def swap(self, values, bits):
        pairs = [(device, device ^ bits) for device in range(32)]
        return lax.ppermute(values, ("dp", "tensor"), pairs)

    def begin_weights(self, own_weights):
        half = own_weights[0].shape[0] // 2
        mine = jnp.stack([lax.dynamic_slice_in_dim(w, self.core * half, half) for w in own_weights])
        return mine, self.swap(mine, self.TENSOR)

    def end_weights(self, got):
        rest = self.swap(got, self.CORE)
        lower = self.core == 0
        whole = jnp.concatenate([jnp.where(lower, got, rest), jnp.where(lower, rest, got)], 1)
        return [whole[index] for index in range(4)]

    def begin_dense(self, shard):
        return [shard] + [self.swap(shard, bits) for bits in (self.Z_NEAR, self.Z_FAR, self.Z_NEAR | self.Z_FAR)]

    def dense_pieces(self, pieces):
        own = jnp.stack(pieces)
        near = self.swap(own, self.NEAR)
        other = self.swap(own, self.TENSOR)
        return own, near, other, self.swap(own, self.CORE)

    def dense_grads_cut(self, values):
        return values.reshape(2, 2, 4, *values.shape[2:])

    def dense_across(self, own_terms, other_terms):
        own = [self.dense_grads_cut(t) for t in own_terms]
        other = [self.dense_grads_cut(t) for t in other_terms]
        pick = lambda terms, index: total([t[:, index] for t in terms])
        sends = [(pick(other, 0), self.TENSOR), (pick(own, 1), self.NEAR), (pick(other, 1), self.TENSOR | self.NEAR)]
        return sends, [t[:, 0] for t in own]

    def dense_along(self, terms):
        sends = []
        for index, bits in ((1, self.Z_NEAR), (2, self.Z_FAR), (3, self.Z_NEAR | self.Z_FAR)):
            sends.append((total([t[:, index] for t in terms]), bits))
        return sends, [t[:, 0] for t in terms]

    def exchange(self, sends, kept):
        return kept + [self.swap(values, bits) for values, bits in sends]

    def halve(self, terms, bits, extra=None):
        axis = 0 if bits == self.TENSOR else 1
        send = total(part(terms, 1, axis))
        if extra is not None:
            send = jnp.concatenate([send, extra], 1)
        return [(send, bits)], part(terms, 0, axis)

    def grow(self, values, bits):
        return jnp.concatenate([values, self.swap(values, bits)], 1)


class Plain:
    def __init__(self, n_tensor, own):
        self.n_tensor, self.own = n_tensor, own
        self.me = [0, 0]

    def weights(self, own_weights):
        whole = [lax.all_gather(w, "tensor", axis=1, tiled=True) for w in own_weights[:3]]
        pairs = [jnp.split(w, 2, 1) for w in whole]
        pairs.append(jnp.split(lax.all_gather(own_weights[3], "tensor", axis=0, tiled=True), 2, 0))
        return [p[0] for p in pairs], [p[1] for p in pairs]

    def bias(self, own_bias):
        return tuple(jnp.split(lax.all_gather(own_bias, "tensor", axis=0, tiled=True), 2))

    def dense(self, shard):
        whole = regroup(lax.all_gather(shard, ("dp", "tensor"), axis=0), 64)
        pieces = [whole[first : first + 4] for first in range(0, whole.shape[0], 4)]
        return pieces[: len(pieces) // 2], pieces[len(pieces) // 2 :]

    def dense_sums(self, grads):
        whole = jnp.concatenate(grads, 1)
        whole = whole.reshape(2, -1, whole.shape[-1])
        return [lax.psum_scatter(w, ("dp", "tensor"), scatter_dimension=0, tiled=True) for w in whole]

    def mixer_sums(self, grads):
        grads = jnp.concatenate(grads, 1)
        _, width, columns = grads.shape
        whole = jnp.moveaxis(grads.reshape(2, width, 2, columns // 2), 0, 2).reshape(width, 2, columns)
        part = lax.psum_scatter(whole, "tensor", scatter_dimension=2, tiled=True)
        return jnp.split(lax.psum(part, "dp").reshape(width, 2 * self.own), 2, 0)

def on_device(
    block_in,
    out_cotangent,
    seq_lengths,
    premix_gain,
    forget_weight,
    admit_weight,
    value_weight,
    admit_bias,
    output_weight,
    dense_gain,
    upper_weight,
    lower_weight,
):
    n_dp, n_tensor = lax.axis_size("dp"), lax.axis_size("tensor")
    rows, width = block_in.shape
    place = lax.axis_index("tensor")
    own = forget_weight.shape[1]
    premix = premix_gain.astype(F32)[None]
    dense = dense_gain.astype(F32)[None]
    paired = (n_dp, n_tensor) == (16, 2)
    links = Links() if paired else Plain(n_tensor, own)
    scalars = jnp.stack([place * rows] + links.me).astype(jnp.int32)
    own_weights = [forget_weight, admit_weight, value_weight, output_weight]
    dense_shard = jnp.concatenate([upper_weight.T, lower_weight], 0)
    if paired:
        weights, biases = [own_weights], [admit_bias]
        channels = own
        mine, got = links.begin_weights(own_weights)
        pieces = links.begin_dense(after(dense_shard, mine))
        biases.append(links.swap(after(admit_bias, pieces[0]), Links.TENSOR))
    else:
        weights, biases = links.weights(own_weights), links.bias(admit_bias)
        channels = weights[0][0].shape[1]
    crossing = rows % LONGEST != 0
    nothing = jnp.zeros((1, channels), F32)

    def chained(ends, backwards):
        every = lax.all_gather(ends, "tensor", axis=0)
        entering = jnp.zeros_like(ends[0:1])
        mine = entering
        order = range(n_tensor - 1, -1, -1) if backwards else range(n_tensor)
        for index in order:
            mine = jnp.where(place == index, entering, mine)
            entering = every[index, 0:1] + every[index, 1:2] * entering
        return mine

    def forward(first, rows_in, index):
        carry = nothing
        args = (first, rows_in, premix, weights[index][:3], biases[index].astype(F32)[None], seq_lengths, scalars)
        if crossing:
            carry = chained(mixer_forward(*args, carry)[-1], False)
        return mixer_forward(*args, carry)

    x_rows, normed, *kept_0 = forward(True, block_in, 0)
    if paired:
        got, pieces, biases[1] = after((got, pieces, biases[1]), normed)
        own_four, near_four, other_four, own_rest = links.dense_pieces(pieces)
        weights.append(links.end_weights(got))
    kept_1 = forward(False, normed, 1)
    kept = [kept_0, kept_1]
    if paired:
        near_four, other_four = after((near_four, other_four), kept_1[1])
        far_four = links.swap(other_four, Links.NEAR)
        other_rest = links.swap(other_four, Links.CORE)
        pieces_0 = [own_four, near_four, own_rest, links.swap(near_four, Links.CORE)]
    else:
        pieces_0, pieces_1 = links.dense(dense_shard)
    outputs = [w[3] for w in weights]
    states = [k[1] for k in kept]
    own_keep, own_send, *rows_0 = dense_both(0, states, (x_rows, out_cotangent), outputs, dense, scalars, pieces_0)
    if paired:
        far_four, other_rest = after((far_four, other_rest), rows_0[0])
        pieces_1 = [other_four, far_four, other_rest, links.swap(far_four, Links.CORE)]
        own_terms = [own_keep, links.swap(own_send, Links.CORE)]
    other_keep, other_send, block_out, mixed, dense_part, *output_grads = dense_both(1, states, rows_0, None, dense, scalars, pieces_1)
    back_mixed = mixed
    if paired:
        other_terms = [other_keep, links.swap(other_send, Links.CORE)]
        dense_sends, dense_kept = links.dense_across(own_terms, other_terms)
        back_mixed = after(mixed, [values for values, _ in dense_sends])
        dense_terms = links.exchange(dense_sends, dense_kept)

    carries = [nothing, nothing]
    for _ in range(2 if crossing else 1):
        per_set = [
            (outputs[index], kept[index][0], kept[index][2], kept[index][3], carries[index], output_grads[index])
            for index in range(2)
        ]
        carried, first, second, bias_parts, ends = mixer_backward(back_mixed, normed, seq_lengths, scalars, per_set)
        if crossing:
            carries = [chained(ends[index], True) for index in range(2)]
    factors = [f for index in range(2) for f in (carried[index], kept[index][2], kept[index][3], kept[index][0])]
    if paired:
        dense_terms = hold(dense_terms, carried[0])
        along, along_kept = links.dense_along(dense_terms)
        core_sends = after([first[1], second[1]], dense_terms[-3:])
        first = [first[0], links.swap(core_sends[0], Links.CORE)]
        second = [second[0], links.swap(core_sends[1], Links.CORE)]
        first, second = links.halve(first, Links.TENSOR), links.halve(second, Links.NEAR)
        factors[0] = after(factors[0], first[0][0][0], second[0][0][0], [values for values, _ in along])
        first, second = links.exchange(*first), links.exchange(*second)
        dense_terms = links.exchange(along, along_kept)
    input_slope, premix_part = input_backward(x_rows, mixed, premix, factors, weights[0][:3] + weights[1][:3])

    bias_parts = jnp.sum(bias_parts, 1)
    if paired:
        bias_parts = jnp.where(place == 0, bias_parts, bias_parts[::-1])
    small = jnp.concatenate([jnp.sum(premix_part, 0), jnp.sum(dense_part, 0), bias_parts[0], bias_parts[1]], 0)
    if paired:
        small = small.reshape(1, -1, 2 * channels).astype(BF16)
        filled = small.shape[1]
        small = jnp.pad(small, ((0, 0), (0, 16 - filled), (0, 0)))
        first, second = hold(first, input_slope), hold(second, input_slope)
        dense_terms = dense_terms[:-3] + after(dense_terms[-3:], input_slope)
        small = after(small, first[-1], second[-1], dense_terms[-3:])
        small = total([small, links.swap(small, Links.CORE)])

        def halve_both(first, second, first_bits, second_bits, extra):
            first = links.halve(first, first_bits)
            second = links.halve(second, second_bits, extra)
            second_send = second[0][0][0]
            first, second = links.exchange(*first), links.exchange(*second)
            rows_sent = second_send.shape[1] - extra.shape[1]
            extra = total([extra, second[-1][:, rows_sent:]])
            return first, second[:-1] + [second[-1][:, :rows_sent]], extra

        first, second, small = halve_both(first, second, Links.Z_NEAR, Links.TENSOR, small)
        first, second, small = halve_both(first, second, Links.NEAR, Links.Z_NEAR, small)
        first, second, small = halve_both(first, second, Links.Z_FAR, Links.Z_FAR, small)
        first, second = total(first), total(second)
        first, second = links.grow(first, Links.Z_FAR), links.grow(second, Links.Z_FAR)
        count = first.shape[1]
        got = links.swap(jnp.concatenate([first, small], 1), Links.NEAR)
        first, small = jnp.concatenate([first, got[:, :count]], 1), total([small, got[:, count:]])
        second = links.grow(second, Links.Z_NEAR)
        first, second = [first, links.swap(first, Links.Z_NEAR)], [second, links.swap(second, Links.NEAR)]
        first += [links.swap(f, Links.CORE) for f in first]
        second += [links.swap(f, Links.CORE) for f in second]
        first, second = [f[0] for f in first], [f[0] for f in second]
        small = small[0, :filled].reshape(-1).astype(F32)
        upper_sum, lower_sum = total(dense_terms)
    else:
        small = lax.psum(small, ("dp", "tensor"))
        upper_sum, lower_sum = links.dense_sums([own_keep, own_send, other_keep, other_send])
        first, second = links.mixer_sums(first), links.mixer_sums(second)
    upper_slope, lower_slope = upper_sum.astype(F32).T, lower_sum.astype(F32)
    forget_slope, admit_slope, value_slope, output_slope = finish_slopes(first, second, scalars)
    shard = width // (n_dp * n_tensor)
    at = (lax.axis_index("dp") * n_tensor + place) * shard
    premix_slope = lax.dynamic_slice(small, (at,), (shard,))
    dense_slope = lax.dynamic_slice(small, (width + at,), (shard,))
    bias_slope = lax.dynamic_slice(small, (2 * width + place * own,), (own,))
    return (
        block_out.reshape(rows, width),
        input_slope.reshape(rows, width),
        premix_slope,
        forget_slope,
        admit_slope,
        value_slope,
        bias_slope,
        output_slope,
        dense_slope,
        upper_slope,
        lower_slope,
    )


def solution(mesh):
    placed = (
        P(("dp", "tensor"), None),
        P(("dp", "tensor"), None),
        P("dp", None),
        P(),
        P(None, "tensor"),
        P(None, "tensor"),
        P(None, "tensor"),
        P("tensor"),
        P("tensor", None),
        P(),
        P(None, ("dp", "tensor")),
        P(("dp", "tensor"), None),
    )
    return jax.shard_map(
        on_device,
        mesh=mesh,
        in_specs=placed,
        out_specs=(
            P(("dp", "tensor"), None),
            P(("dp", "tensor"), None),
            P(("dp", "tensor")),
            P(None, "tensor"),
            P(None, "tensor"),
            P(None, "tensor"),
            P("tensor"),
            P("tensor", None),
            P(("dp", "tensor")),
            P(None, ("dp", "tensor")),
            P(("dp", "tensor"), None),
        ),
        check_vma=False,
    )
```

time: 233 us -> 221 us (0.948)
  waiting for transfers between devices: 32.4 us -> 17.7 us
  Pallas kernels: 117 us -> 121 us
    ppermute x41 -> x42, waiting for transfers between devices: 32.4 us -> 17.7 us  [swap(): return lax.ppermute(values, ('dp', 'tensor'), pairs)]
    pallas_call x2 -> x3, Pallas kernels: 49.2 us -> 56.3 us  [the longest x2 52.3 us: dense_both(): pl.pallas_call(functools.partial(dense_kernel, stage, sets, len(pieces)),...]
    convert_element_type x20 -> x19, other arithmetic: 12.7 us -> 15.5 us  [total(): return result.astype(terms[0].dtype)]
    pallas_call x2, Pallas kernels: 30.7 us -> 28.1 us  [mixer_forward(): pl.pallas_call(functools.partial(mixer_kernel, first), grid=(2, blocks),...]
    ppermute x41 -> x42, starting transfers between devices: 48.9 us -> 48.7 us  [swap(): return lax.ppermute(values, ('dp', 'tensor'), pairs)]
  transfers between devices with their start and end apart: 41 -> 42, of which waited for: 14 -> 11; matrix products, arithmetic and copies ran while one was open for 12% -> 12% of each run, Pallas kernels for 29% -> 53%
where the time goes in v3:
time: 221 us; the launch traced here: 220 us
  Pallas kernels  121 us (55%)
  starting transfers between devices  48.7 us (22%)
  other arithmetic  23.4 us (11%)
  waiting for transfers between devices  17.7 us (8%)
  local copies, waits for them, and re-layouts  8.38 us (4%)
    pallas_call x2, Pallas kernels, dense_both(): pl.pallas_call(functools.partial(dense_kernel, stage, sets, len(pieces)),...  52.3 us
    ppermute x42, starting transfers between devices, swap(): return lax.ppermute(values, ('dp', 'tensor'), pairs)  48.7 us
    pallas_call x2, Pallas kernels, mixer_forward(): pl.pallas_call(functools.partial(mixer_kernel, first), grid=(2, blocks),...  28.1 us
    pallas_call x1, Pallas kernels, mixer_backward(): pl.pallas_call(functools.partial(mixer_back_kernel, sets), grid=(2, block...  21.5 us
    ppermute x42, waiting for transfers between devices, swap(): return lax.ppermute(values, ('dp', 'tensor'), pairs)  17.7 us
    convert_element_type x19, other arithmetic, total(): return result.astype(terms[0].dtype)  15.5 us
    pallas_call x1, Pallas kernels, input_backward(): pl.pallas_call(functools.partial(input_kernel, sets), grid=(rows // BLOCK...  14.8 us
  transfers between devices with their start and end apart: 42, of which 11 were waited for; matrix products, arithmetic and copies ran while one was open for 12% of the time, Pallas kernels for 53%

profile of v3, /device:TPU:1, one launch (start us, length us, event | category | flops | bytes accessed | tf_op | source)
XLA Modules:
  0.0 220.2 jit_solution(16110438380420360442)
XLA Ops:
  0.7 1.1 dynamic-slice_bitcast_fusion
  1.8 1.1 dynamic-slice_bitcast_fusion.2
  3.0 2.1 collective-permute-start
  5.2 1.4 collective-permute-start.1
  6.5 2.3 %collective-permute-start.2 = (bf16[128,512]{1,0:T(8,128)(2,1)S(1)}, bf16[128,512]{1,0:T(8,128)(2,1)S(1)}, u32[]{:S(2)}, u32[]{:S(2)}) collective-permute-start(bf16[128,512]{1,0:T(8,128)(2,1)S(1)} %pad_maximum_fusion.8), channel_id=1, source_target_pairs={{0,16},{1,17},{2,18},{3,19},{4,20},{5,21},{6,22},{7,23},{8,24},{9,... | collective-permute-start | bytes 393224 | tf_op jit(solution)/shard_map/ppermute | solution.py:671
  11.5 14.6 %mixer_forward.2 = (bf16[2048,512]{1,0:T(8,128)(2,1)}, bf16[2048,512]{1,0:T(8,128)(2,1)}, bf16[2048,512]{1,0:T(8,128)(2,1)}, bf16[2048,512]{1,0:T(8,128)(2,1)}, ...) custom-call(bf16[8,256,512]{2,1,0:T(8,128)(2,1)} %bitcast.117, f32[1,512]{1,0:T(1,128)} %bitcast.110, ...), custom_call_target="tpu_custom_call" | custom-call | flops 3221225472 | bytes 16777216 | tf_op jit(solution)/shard_map/mixer_forward/pallas_call | solution.py:235
  26.1 1.9 collective-permute-done.4
  28.1 1.3 collective-permute-start.5
  29.5 1.6 collective-permute-start.6
  31.0 1.2 collective-permute-start.7
  33.6 1.4 fusion.9
  35.0 13.4 %mixer_forward.3 = (bf16[2048,512]{1,0:T(8,128)(2,1)}, bf16[2048,512]{1,0:T(8,128)(2,1)}, bf16[2048,512]{1,0:T(8,128)(2,1)}, bf16[2048,512]{1,0:T(8,128)(2,1)}, f32[8,512]{1,0:T(8,128)}) custom-call(bf16[2048,512]{1,0:T(8,128)(2,1)} %get-tuple-element.72.refs_0_.normed_ref, bf16[512,512]{1,0:T(8,128)(2,1)} %get-tuple-element.137.refs_1_.refs_14_, ...), custom_call_target="tpu_custom_call" | custom-call | flops 3221225472 | bytes 16777216 | tf_op jit(solution)/shard_map/mixer_forward/pallas_call | solution.py:235
  48.5 0.7 broadcast_in_dim.35
  51.2 25.2 %dense_first.1 = (bf16[2,8,64,512]{3,2,1,0:T(8,128)(2,1)}, bf16[2,8,64,512]{3,2,1,0:T(8,128)(2,1)}, f32[2048,512]{1,0:T(8,128)}, f32[2048,512]{1,0:T(8,128)}, f3...) custom-call(bf16[2048,512]{1,0:T(8,128)(2,1)} %get-tuple-element.71.refs_0_, ...), custom_call_target="tpu_custom_call" | custom-call | flops 12884901888 | bytes 25165824 | tf_op jit(solution)/shard_map/dense_first/pallas_call | solution.py:376
  77.0 1.4 collective-permute-done.12.refs_12_
  78.4 0.8 copy-done.26
  79.2 27.2 %dense_second.1 = (bf16[2,8,64,512]{3,2,1,0:T(8,128)(2,1)}, bf16[2,8,64,512]{3,2,1,0:T(8,128)(2,1)}, bf16[8,256,512]{2,1,0:T(8,128)(2,1)}, bf16[2048,512]{1,0:T(...) custom-call(bf16[2048,512]{1,0:T(8,128)(2,1)} %get-tuple-element.71.refs_0_, ...), custom_call_target="tpu_custom_call" | custom-call | flops 12884901888 | bytes 25165824 | tf_op jit(solution)/shard_map/dense_second/pallas_call | solution.py:376
  106.7 0.9 copy-done.3
  108.0 1.2 collective-permute-start.16
  109.6 1.1 collective-permute-start.17
  110.9 1.3 collective-permute-start.15
  112.2 21.5 %mixer_backward.1 = (bf16[2048,512]{1,0:T(8,128)(2,1)}, bf16[2048,512]{1,0:T(8,128)(2,1)}, bf16[2,256,1024]{2,1,0:T(8,128)(2,1)}, bf16[2,256,1024]{2,1,0:T(8,128...) custom-call(bf16[2048,512]{1,0:T(8,128)(2,1)} %get-tuple-element.98., ...), custom_call_target="tpu_custom_call" | custom-call | flops 8589934592 | bytes 25165824 | tf_op jit(solution)/shard_map/mixer_backward/pallas_call | solution.py:523
  133.7 1.5 collective-permute-done.15
  135.1 1.0 collective-permute-start.19
  136.7 1.6 fusion.15
  138.3 1.4 collective-permute-start.22
  139.7 2.3 %collective-permute-start.23 = (bf16[2,64,512]{2,1,0:T(8,128)(2,1)S(1)}, bf16[2,64,512]{2,1,0:T(8,128)(2,1)S(1)}, u32[]{:S(2)}, u32[]{:S(2)}) collective-permute-start(bf16[2,64,512]{2,1,0:T(8,128)(2,1)S(1)} %get-tuple-element.134), channel_id=1, source_target_pairs={{0,16},{1,17},{2,18},{3,19},{4,20},{5,21},{6,22},{7,23},{8,24},{9,... | collective-permute-start | bytes 393224 | tf_op jit(solution)/shard_map/ppermute | solution.py:671
  142.0 2.0 add_convert_fusion
  144.4 2.0 add_convert_fusion.1
  146.4 0.7 collective-permute-start.20
  147.1 14.8 %input_backward.1 = (f32[8,256,512]{2,1,0:T(8,128)}, f32[8,512]{1,0:T(8,128)}) custom-call(bf16[2048,512]{1,0:T(8,128)(2,1)} %get-tuple-element.78.refs_2_.refs_0_, bf16[2048,512]{1,0:T(8,128)(2,1)} %get-tuple-element.98.mixed_ref.refs_1_, f32[1,512]{1,0:T(1,128)} %bitcast.111, bf16[2048,512]{1,0:T(8,128)(2,1)} %get-tuple-element.115.refs_3_, ...), custom_call_target="tpu_custom_call" | custom-call | flops 6442450944 | bytes 16777216 | tf_op jit(solution)/shard_map/input_backward/pallas_call | solution.py:588
  162.0 0.7 reduce_sum.27
  162.8 2.2 collective-permute-start.25
  165.0 1.2 add_convert_fusion.5
  166.6 1.2 add_convert_fusion.6
  167.8 0.8 collective-permute-start.26
  168.7 5.5 %collective-permute-done.29 = bf16[1,128,1024]{2,1,0:T(8,128)(2,1)S(1)} collective-permute-done((bf16[1,128,1024]{2,1,0:T(8,128)(2,1)S(1)}, bf16[1,128,1024]{2,1,0:T(8,128)(2,1)S(1)}, u32[]{:S(2)}, u32[]{:S(2)}) %collective-permute-start.29) | collective-permute-done | bytes 262176 | tf_op jit(solution)/shard_map/ppermute | solution.py:671
  174.1 1.0 add_convert_fusion.10
  175.2 0.7 collective-permute-start.30
  176.2 1.0 add_convert_fusion.11
  177.3 1.1 collective-permute-start.27
  178.4 1.1 collective-permute-done.30
  179.5 0.9 add_convert_fusion.14
  180.4 2.6 %collective-permute-start.31 = (bf16[1,32,1024]{2,1,0:T(8,128)(2,1)S(1)}, bf16[1,32,1024]{2,1,0:T(8,128)(2,1)S(1)}, u32[]{:S(2)}, u32[]{:S(2)}) collective-permute-start(bf16[1,32,1024]{2,1,0:T(8,128)(2,1)S(1)} %add_convert_fusion.14), channel_id=1, source_target_pairs={{0,16},{1,17},{2,18},{3,19},{4,20},{5,21},{6,22},{7,23},{8,24},{9,... | collective-permute-start | bytes 196616 | tf_op jit(solution)/shard_map/ppermute | solution.py:671
  183.0 0.9 add_convert_fusion.15
  184.0 2.2 collective-permute-start.28
  186.2 0.9 add_convert_fusion.13
  187.1 1.1 collective-permute-start.32
  188.2 1.6 collective-permute-done.28
  189.7 0.9 add_convert_fusion.12
  190.7 1.0 collective-permute-start.37
  191.7 2.2 collective-permute-done.32
  193.9 0.7 collective-permute-start.33
  194.6 1.7 collective-permute-done.37
  196.3 1.8 collective-permute-start.38
  198.2 0.8 pad_maximum_fusion.4
  198.9 2.8 %collective-permute-start.34 = (bf16[1,128,1024]{2,1,0:T(8,128)(2,1)S(1)}, bf16[1,128,1024]{2,1,0:T(8,128)(2,1)S(1)}, u32[]{:S(2)}, u32[]{:S(2)}) collective-permute-start(bf16[1,128,1024]{2,1,0:T(8,128)(2,1)S(1)} %get-tuple-element.152), channel_id=1, source_target_pairs={{0,8},{1,9},{2,10},{3,11},{4,12},{5,13},{6,14},{7,15},{8,0},{9,1},... | collective-permute-start | bytes 786440 | tf_op jit(solution)/shard_map/ppermute | solution.py:671
  201.8 0.8 pad_maximum_fusion.5
  203.2 1.2 fusion.12
  204.4 0.7 fusion.16
  205.1 5.4 %collective-permute-start.35 = (bf16[1,128,1024]{2,1,0:T(8,128)(2,1)S(1)}, bf16[1,128,1024]{2,1,0:T(8,128)(2,1)S(1)}, u32[]{:S(2)}, u32[]{:S(2)}) collective-permute-start(bf16[1,128,1024]{2,1,0:T(8,128)(2,1)S(1)} %get-tuple-element.152), channel_id=1, source_target_pairs={{0,2},{1,3},{2,0},{3,1},{4,6},{5,7},{6,4},{7,5},{8,10},{9,11},{10,... | collective-permute-start | bytes 786440 | tf_op jit(solution)/shard_map/ppermute | solution.py:671
  211.0 3.0 %collective-permute-start.41 = (bf16[1,128,1024]{2,1,0:T(8,128)(2,1)S(1)}, bf16[1,128,1024]{2,1,0:T(8,128)(2,1)S(1)}, u32[]{:S(2)}, u32[]{:S(2)}) collective-permute-start(bf16[1,128,1024]{2,1,0:T(8,128)(2,1)S(1)} %collective-permute-done.39), channel_id=1, source_target_pairs={{0,2},{1,3},{2,0},{3,1},{4,6},{5,7},{6,4},{7,5},{8,10},{9,11},{10,... | collective-permute-start | bytes 786440 | tf_op jit(solution)/shard_map/ppermute | solution.py:671
  214.0 0.7 dynamic_slice.26
  216.3 4.0 %finish_slopes.1 = (f32[512,512]{1,0:T(8,128)}, f32[512,512]{1,0:T(8,128)}, f32[512,512]{1,0:T(8,128)}, f32[512,512]{1,0:T(8,128)}) custom-call(bf16[128,1024]{1,0:T(8,128)(2,1)} %get-tuple-element.153.refs_0_, bf16[128,1024]{1,0:T(8,128)(2,1)} %bitcast.98, bf16[128,1024]{1,0:T(8,128)(2,1)} %bitcast.100, bf16[128,1024]{1,0:T(8,128)(2,1)} %bitcast.102, ...), custom_call_target="tpu_custom_call" | custom-call | tf_op jit(solution)/shard_map/finish_slopes/pallas_call | solution.py:622
  (142 shorter events, 12.6 us)
Async XLA Ops:
  0.7 4.5 %copy-start.13 = (bf16[64,512]{1,0:T(8,128)(2,1)S(1)}, bf16[64,512]{1,0:T(8,128)(2,1)}, u32[]{:S(2)}) copy-start(bf16[64,512]{1,0:T(8,128)(2,1)} %param.23) | copy-start | bytes 196612
  0.7 4.5 %copy-start.14 = (bf16[512,64]{0,1:T(8,128)(2,1)S(1)}, bf16[512,64]{0,1:T(8,128)(2,1)}, u32[]{:S(2)}) copy-start(bf16[512,64]{0,1:T(8,128)(2,1)} %param.22) | copy-start | bytes 196612
  0.7 8.2 %copy-start.18 = (bf16[512]{0:T(512)(128)(2,1)S(1)}, bf16[512]{0:T(512)(128)(2,1)}, u32[]{:S(2)}) copy-start(bf16[512]{0:T(512)(128)(2,1)} %param.19) | copy-start | bytes 3076
  0.7 9.0 %copy-start.17 = (bf16[512]{0:T(512)(128)(2,1)S(1)}, bf16[512]{0:T(512)(128)(2,1)}, u32[]{:S(2)}) copy-start(bf16[512]{0:T(512)(128)(2,1)} %param.15) | copy-start | bytes 3076
  3.0 25.0 %collective-permute-start = (bf16[4,256,512]{2,1,0:T(8,128)(2,1)S(1)}, bf16[4,256,512]{2,1,0:T(8,128)(2,1)S(1)}, u32[]{:S(2)}, u32[]{:S(2)}) collective-permute-start(bf16[4,256,512]{2,1,0:T(8,128)(2,1)S(1)} %pad_maximum_fusion), channel_id=1, source_target_pairs={{0,1},{1,0},{2,3},{3,2},{4,5},{5,4},{6,7},{7,6},{8,9},{9,8},{10,11... | collective-permute-start | bytes 3145736 | tf_op jit(solution)/shard_map/ppermute | solution.py:671
  5.2 22.9 %collective-permute-start.1 = (bf16[128,512]{1,0:T(8,128)(2,1)S(1)}, bf16[128,512]{1,0:T(8,128)(2,1)S(1)}, u32[]{:S(2)}, u32[]{:S(2)}) collective-permute-start(bf16[128,512]{1,0:T(8,128)(2,1)S(1)} %pad_maximum_fusion.8), channel_id=1, source_target_pairs={{0,8},{1,9},{2,10},{3,11},{4,12},{5,13},{6,14},{7,15},{8,0},{9,1},... | collective-permute-start | bytes 393224 | tf_op jit(solution)/shard_map/ppermute | solution.py:671
  6.5 21.5 %collective-permute-start.2 = (bf16[128,512]{1,0:T(8,128)(2,1)S(1)}, bf16[128,512]{1,0:T(8,128)(2,1)S(1)}, u32[]{:S(2)}, u32[]{:S(2)}) collective-permute-start(bf16[128,512]{1,0:T(8,128)(2,1)S(1)} %pad_maximum_fusion.8), channel_id=1, source_target_pairs={{0,16},{1,17},{2,18},{3,19},{4,20},{5,21},{6,22},{7,23},{8,24},{9,... | collective-permute-start | bytes 393224 | tf_op jit(solution)/shard_map/ppermute | solution.py:671
  8.8 19.2 %collective-permute-start.3 = (bf16[128,512]{1,0:T(8,128)(2,1)S(1)}, bf16[128,512]{1,0:T(8,128)(2,1)S(1)}, u32[]{:S(2)}, u32[]{:S(2)}) collective-permute-start(bf16[128,512]{1,0:T(8,128)(2,1)S(1)} %pad_maximum_fusion.8), channel_id=1, source_target_pairs={{0,24},{1,25},{2,26},{3,27},{4,28},{5,29},{6,30},{7,31},{8,16},{9,... | collective-permute-start | bytes 393224 | tf_op jit(solution)/shard_map/ppermute | solution.py:671
  8.8 19.2 %collective-permute-start.4 = (bf16[512]{0:T(512)(128)(2,1)S(1)}, bf16[512]{0:T(512)(128)(2,1)S(1)}, u32[]{:S(2)}, u32[]{:S(2)}) collective-permute-start(bf16[512]{0:T(512)(128)(2,1)S(1)} %copy-done.18), channel_id=1, source_target_pairs={{0,1},{1,0},{2,3},{3,2},{4,5},{5,4},{6,7},{7,6},{8,9},{9,8},{10,11... | collective-permute-start | bytes 3080 | tf_op jit(solution)/shard_map/ppermute | solution.py:671
  28.1 5.4 %collective-permute-start.5 = (bf16[4,256,512]{2,1,0:T(8,128)(2,1)S(1)}, bf16[4,256,512]{2,1,0:T(8,128)(2,1)S(1)}, u32[]{:S(2)}, u32[]{:S(2)}) collective-permute-start(bf16[4,256,512]{2,1,0:T(8,128)(2,1)S(1)} %collective-permute-done), channel_id=1, source_target_pairs={{0,2},{1,3},{2,0},{3,1},{4,6},{5,7},{6,4},{7,5},{8,10},{9,11},{10,... | collective-permute-start | bytes 3145736 | tf_op jit(solution)/shard_map/ppermute | solution.py:671
  29.5 4.1 %copy-start.6 = (bf16[4,128,512]{2,1,0:T(8,128)(2,1)}, bf16[4,128,512]{2,1,0:T(8,128)(2,1)S(1)}, u32[]{:S(2)}) copy-start(bf16[4,128,512]{2,1,0:T(8,128)(2,1)S(1)} %pad_maximum_fusion.2.refs_8_) | copy-start | bytes 1572868
  29.5 18.9 %collective-permute-start.6 = (bf16[4,128,512]{2,1,0:T(8,128)(2,1)S(1)}, bf16[4,128,512]{2,1,0:T(8,128)(2,1)S(1)}, u32[]{:S(2)}, u32[]{:S(2)}) collective-permute-start(bf16[4,128,512]{2,1,0:T(8,128)(2,1)S(1)} %pad_maximum_fusion.2.refs_8_), channel_id=1, source_target_pairs={{0,4},{1,5},{2,6},{3,7},{4,0},{5,1},{6,2},{7,3},{8,12},{9,13},{10,... | collective-permute-start | bytes 1572872 | tf_op jit(solution)/shard_map/ppermute | solution.py:671
  31.0 17.4 %collective-permute-start.7 = (bf16[4,128,512]{2,1,0:T(8,128)(2,1)S(1)}, bf16[4,128,512]{2,1,0:T(8,128)(2,1)S(1)}, u32[]{:S(2)}, u32[]{:S(2)}) collective-permute-start(bf16[4,128,512]{2,1,0:T(8,128)(2,1)S(1)} %pad_maximum_fusion.2.refs_8_), channel_id=1, source_target_pairs={{0,1},{1,0},{2,3},{3,2},{4,5},{5,4},{6,7},{7,6},{8,9},{9,8},{10,11... | collective-permute-start | bytes 1572872 | tf_op jit(solution)/shard_map/ppermute | solution.py:671
  32.3 17.9 %collective-permute-start.8 = (bf16[4,128,512]{2,1,0:T(8,128)(2,1)S(1)}, bf16[4,128,512]{2,1,0:T(8,128)(2,1)S(1)}, u32[]{:S(2)}, u32[]{:S(2)}) collective-permute-start(bf16[4,128,512]{2,1,0:T(8,128)(2,1)S(1)} %pad_maximum_fusion.2.refs_8_), channel_id=1, source_target_pairs={{0,2},{1,3},{2,0},{3,1},{4,6},{5,7},{6,4},{7,5},{8,10},{9,11},{10,... | collective-permute-start | bytes 1572872 | tf_op jit(solution)/shard_map/ppermute | solution.py:671
  35.0 13.6 %copy-start.19 = (bf16[512]{0:T(512)(128)(2,1)S(1)}, bf16[512]{0:T(512)(128)(2,1)}, u32[]{:S(2)}) copy-start(bf16[512]{0:T(512)(128)(2,1)} %param.21) | copy-start | bytes 3076
  48.4 2.0 copy-start.21
  48.4 28.0 %copy-start.20 = (bf16[4,128,512]{2,1,0:T(8,128)(2,1)}, bf16[4,128,512]{2,1,0:T(8,128)(2,1)S(1)}, u32[]{:S(2)}) copy-start(bf16[4,128,512]{2,1,0:T(8,128)(2,1)S(1)} %collective-permute-done.7.refs_9_) | copy-start | bytes 1572868
  48.4 2.0 collective-permute-start.9
  49.2 27.2 %collective-permute-start.10 = (bf16[4,128,512]{2,1,0:T(8,128)(2,1)S(1)}, bf16[4,128,512]{2,1,0:T(8,128)(2,1)S(1)}, u32[]{:S(2)}, u32[]{:S(2)}) collective-permute-start(bf16[4,128,512]{2,1,0:T(8,128)(2,1)S(1)} %collective-permute-done.7.refs_9_), channel_id=1, source_target_pairs={{0,4},{1,5},{2,6},{3,7},{4,0},{5,1},{6,2},{7,3},{8,12},{9,13},{10,... | collective-permute-start | bytes 1572872 | tf_op jit(solution)/shard_map/ppermute | solution.py:671
  49.5 27.0 %collective-permute-start.11 = (bf16[4,128,512]{2,1,0:T(8,128)(2,1)S(1)}, bf16[4,128,512]{2,1,0:T(8,128)(2,1)S(1)}, u32[]{:S(2)}, u32[]{:S(2)}) collective-permute-start(bf16[4,128,512]{2,1,0:T(8,128)(2,1)S(1)} %collective-permute-done.7.refs_9_), channel_id=1, source_target_pairs={{0,2},{1,3},{2,0},{3,1},{4,6},{5,7},{6,4},{7,5},{8,10},{9,11},{10,... | collective-permute-start | bytes 1572872 | tf_op jit(solution)/shard_map/ppermute | solution.py:671
  76.4 2.0 copy-start.23
  76.4 2.0 copy-start.24
  76.5 2.0 collective-permute-start.12
  76.6 31.1 %collective-permute-start.14 = (bf16[2,8,64,512]{3,2,1,0:T(8,128)(2,1)}, bf16[2,8,64,512]{3,2,1,0:T(8,128)(2,1)S(1)}, u32[]{:S(2)}, u32[]{:S(2)}) collective-permute-start(bf16[2,8,64,512]{3,2,1,0:T(8,128)(2,1)} %get-tuple-element.97), channel_id=1, source_target_pairs={{0,2},{1,3},{2,0},{3,1},{4,6},{5,7},{6,4},{7,5},{8,10},{9,11},{10,... | collective-permute-start | bytes 3145736 | tf_op jit(solution)/shard_map/ppermute | solution.py:671
  79.2 27.4 %copy-start.2 = (bf16[2,8,64,512]{3,2,1,0:T(8,128)(2,1)S(1)}, bf16[2,8,64,512]{3,2,1,0:T(8,128)(2,1)}, u32[]{:S(2)}) copy-start(bf16[2,8,64,512]{3,2,1,0:T(8,128)(2,1)} %get-tuple-element.96) | copy-start | bytes 3145732
  106.4 1.2 copy-start.3
  106.4 2.9 %collective-permute-start.13 = (bf16[2,8,64,512]{3,2,1,0:T(8,128)(2,1)}, bf16[2,8,64,512]{3,2,1,0:T(8,128)(2,1)S(1)}, u32[]{:S(2)}, u32[]{:S(2)}) collective-permute-start(bf16[2,8,64,512]{3,2,1,0:T(8,128)(2,1)} %get-tuple-element.95), channel_id=1, source_target_pairs={{0,2},{1,3},{2,0},{3,1},{4,6},{5,7},{6,4},{7,5},{8,10},{9,11},{10,... | collective-permute-start | bytes 3145736 | tf_op jit(solution)/shard_map/ppermute | solution.py:671
  108.0 25.7 %collective-permute-start.16 = (bf16[2,4,64,512]{3,2,0,1:T(8,128)(2,1)S(1)}, bf16[2,4,64,512]{3,2,0,1:T(8,128)(2,1)}, u32[]{:S(2)}, u32[]{:S(2)}) collective-permute-start(bf16[2,4,64,512]{3,2,0,1:T(8,128)(2,1)S(1)} %fusion.1), channel_id=1, source_target_pairs={{0,4},{1,5},{2,6},{3,7},{4,0},{5,1},{6,2},{7,3},{8,12},{9,13},{10,... | collective-permute-start | bytes 1572872 | tf_op jit(solution)/shard_map/ppermute | solution.py:671
  109.6 24.0 %collective-permute-start.17 = (bf16[2,4,64,512]{3,2,0,1:T(8,128)(2,1)S(1)}, bf16[2,4,64,512]{3,2,0,1:T(8,128)(2,1)S(1)}, u32[]{:S(2)}, u32[]{:S(2)}) collective-permute-start(bf16[2,4,64,512]{3,2,0,1:T(8,128)(2,1)S(1)} %fusion.2), channel_id=1, source_target_pairs={{0,5},{1,4},{2,7},{3,6},{4,1},{5,0},{6,3},{7,2},{8,13},{9,12},{10,... | collective-permute-start | bytes 1572872 | tf_op jit(solution)/shard_map/ppermute | solution.py:671
  110.9 24.3 %collective-permute-start.15 = (bf16[2,4,64,512]{3,2,0,1:T(8,128)(2,1)S(1)}, bf16[2,4,64,512]{3,2,0,1:T(8,128)(2,1)S(1)}, u32[]{:S(2)}, u32[]{:S(2)}) collective-permute-start(bf16[2,4,64,512]{3,2,0,1:T(8,128)(2,1)S(1)} %fusion), channel_id=1, source_target_pairs={{0,1},{1,0},{2,3},{3,2},{4,5},{5,4},{6,7},{7,6},{8,9},{9,8},{10,11... | collective-permute-start | bytes 1572872 | tf_op jit(solution)/shard_map/ppermute | solution.py:671
  112.2 24.0 %copy-start.16 = (f32[8,512]{1,0:T(8,128)S(1)}, f32[8,512]{1,0:T(8,128)}, u32[]{:S(2)}) copy-start(f32[8,512]{1,0:T(8,128)} %get-tuple-element.119) | copy-start | bytes 49156
  133.6 2.6 %copy-start.15 = (f32[2,8,512]{2,1,0:T(8,128)S(1)}, f32[2,8,512]{2,1,0:T(8,128)}, u32[]{:S(2)}) copy-start(f32[2,8,512]{2,1,0:T(8,128)} %get-tuple-element.120) | copy-start | bytes 98308
  133.6 2.5 %copy-start.4 = (bf16[2,4,64,512]{3,2,0,1:T(8,128)(2,1)}, bf16[2,4,64,512]{3,2,0,1:T(8,128)(2,1)S(1)}, u32[]{:S(2)}) copy-start(bf16[2,4,64,512]{3,2,0,1:T(8,128)(2,1)S(1)} %collective-permute-done.17) | copy-start | bytes 1572868
  135.1 1.0 copy-start.5
  135.1 6.8 %collective-permute-start.19 = (bf16[2,256,1024]{2,1,0:T(8,128)(2,1)}, bf16[2,256,1024]{2,1,0:T(8,128)(2,1)}, u32[]{:S(2)}, u32[]{:S(2)}) collective-permute-start(bf16[2,256,1024]{2,1,0:T(8,128)(2,1)} %get-tuple-element.114), channel_id=1, source_target_pairs={{0,2},{1,3},{2,0},{3,1},{4,6},{5,7},{6,4},{7,5},{8,10},{9,11},{10,... | collective-permute-start | bytes 3145736 | tf_op jit(solution)/shard_map/ppermute | solution.py:671
  136.1 8.3 %collective-permute-start.18 = (bf16[2,256,1024]{2,1,0:T(8,128)(2,1)}, bf16[2,256,1024]{2,1,0:T(8,128)(2,1)}, u32[]{:S(2)}, u32[]{:S(2)}) collective-permute-start(bf16[2,256,1024]{2,1,0:T(8,128)(2,1)} %get-tuple-element.112), channel_id=1, source_target_pairs={{0,2},{1,3},{2,0},{3,1},{4,6},{5,7},{6,4},{7,5},{8,10},{9,11},{10,... | collective-permute-start | bytes 3145736 | tf_op jit(solution)/shard_map/ppermute | solution.py:671
  136.1 5.9 %copy-start = (bf16[2,256,1024]{2,1,0:T(8,128)(2,1)S(1)}, bf16[2,256,1024]{2,1,0:T(8,128)(2,1)}, u32[]{:S(2)}) copy-start(bf16[2,256,1024]{2,1,0:T(8,128)(2,1)} %get-tuple-element.113) | copy-start | bytes 3145732
  136.2 8.2 %copy-start.1 = (bf16[2,256,1024]{2,1,0:T(8,128)(2,1)S(1)}, bf16[2,256,1024]{2,1,0:T(8,128)(2,1)}, u32[]{:S(2)}) copy-start(bf16[2,256,1024]{2,1,0:T(8,128)(2,1)} %get-tuple-element.108) | copy-start | bytes 3145732
  138.3 23.7 %collective-permute-start.22 = (bf16[2,64,512]{2,1,0:T(8,128)(2,1)S(1)}, bf16[2,64,512]{2,1,0:T(8,128)(2,1)S(1)}, u32[]{:S(2)}, u32[]{:S(2)}) collective-permute-start(bf16[2,64,512]{2,1,0:T(8,128)(2,1)S(1)} %get-tuple-element.135), channel_id=1, source_target_pairs={{0,8},{1,9},{2,10},{3,11},{4,12},{5,13},{6,14},{7,15},{8,0},{9,1},... | collective-permute-start | bytes 393224 | tf_op jit(solution)/shard_map/ppermute | solution.py:671
  139.7 22.3 %collective-permute-start.23 = (bf16[2,64,512]{2,1,0:T(8,128)(2,1)S(1)}, bf16[2,64,512]{2,1,0:T(8,128)(2,1)S(1)}, u32[]{:S(2)}, u32[]{:S(2)}) collective-permute-start(bf16[2,64,512]{2,1,0:T(8,128)(2,1)S(1)} %get-tuple-element.134), channel_id=1, source_target_pairs={{0,16},{1,17},{2,18},{3,19},{4,20},{5,21},{6,22},{7,23},{8,24},{9,... | collective-permute-start | bytes 393224 | tf_op jit(solution)/shard_map/ppermute | solution.py:671
  142.0 20.0 %collective-permute-start.24 = (bf16[2,64,512]{2,1,0:T(8,128)(2,1)S(1)}, bf16[2,64,512]{2,1,0:T(8,128)(2,1)}, u32[]{:S(2)}, u32[]{:S(2)}) collective-permute-start(bf16[2,64,512]{2,1,0:T(8,128)(2,1)S(1)} %get-tuple-element.133), channel_id=1, source_target_pairs={{0,24},{1,25},{2,26},{3,27},{4,28},{5,29},{6,30},{7,31},{8,16},{9,... | collective-permute-start | bytes 393224 | tf_op jit(solution)/shard_map/ppermute | solution.py:671
  144.0 18.8 %collective-permute-start.21 = (bf16[2,128,1024]{2,1,0:T(8,128)(2,1)}, bf16[2,128,1024]{2,1,0:T(8,128)(2,1)}, u32[]{:S(2)}, u32[]{:S(2)}) collective-permute-start(bf16[2,128,1024]{2,1,0:T(8,128)(2,1)} %add_convert_fusion), channel_id=1, source_target_pairs={{0,4},{1,5},{2,6},{3,7},{4,0},{5,1},{6,2},{7,3},{8,12},{9,13},{10,... | collective-permute-start | bytes 1572872 | tf_op jit(solution)/shard_map/ppermute | solution.py:671
  146.4 16.4 %collective-permute-start.20 = (bf16[1,256,1024]{2,1,0:T(8,128)(2,1)}, bf16[1,256,1024]{2,1,0:T(8,128)(2,1)}, u32[]{:S(2)}, u32[]{:S(2)}) collective-permute-start(bf16[1,256,1024]{2,1,0:T(8,128)(2,1)} %add_convert_fusion.1), channel_id=1, source_target_pairs={{0,1},{1,0},{2,3},{3,2},{4,5},{5,4},{6,7},{7,6},{8,9},{9,8},{10,11... | collective-permute-start | bytes 1572872 | tf_op jit(solution)/shard_map/ppermute | solution.py:671
  162.8 5.0 %collective-permute-start.25 = (bf16[1,16,1024]{2,1,0:T(8,128)(2,1)S(1)}, bf16[1,16,1024]{2,1,0:T(8,128)(2,1)S(1)}, u32[]{:S(2)}, u32[]{:S(2)}) collective-permute-start(bf16[1,16,1024]{2,1,0:T(8,128)(2,1)S(1)} %pad.4), channel_id=1, source_target_pairs={{0,2},{1,3},{2,0},{3,1},{4,6},{5,7},{6,4},{7,5},{8,10},{9,11},{10,... | collective-permute-start | bytes 98312 | tf_op jit(solution)/shard_map/ppermute | solution.py:671
  166.1 8.0 %collective-permute-start.29 = (bf16[1,128,1024]{2,1,0:T(8,128)(2,1)S(1)}, bf16[1,128,1024]{2,1,0:T(8,128)(2,1)S(1)}, u32[]{:S(2)}, u32[]{:S(2)}) collective-permute-start(bf16[1,128,1024]{2,1,0:T(8,128)(2,1)S(1)} %add_convert_fusion.5), channel_id=1, source_target_pairs={{0,8},{1,9},{2,10},{3,11},{4,12},{5,13},{6,14},{7,15},{8,0},{9,1},... | collective-permute-start | bytes 786440 | tf_op jit(solution)/shard_map/ppermute | solution.py:671
  167.8 8.4 %collective-permute-start.26 = (bf16[1,144,1024]{2,1,0:T(8,128)(2,1)S(1)}, bf16[1,144,1024]{2,1,0:T(8,128)(2,1)S(1)}, u32[]{:S(2)}, u32[]{:S(2)}) collective-permute-start(bf16[1,144,1024]{2,1,0:T(8,128)(2,1)S(1)} %pad_maximum_fusion.3), channel_id=1, source_target_pairs={{0,1},{1,0},{2,3},{3,2},{4,5},{5,4},{6,7},{7,6},{8,9},{9,8},{10,11... | collective-permute-start | bytes 884744 | tf_op jit(solution)/shard_map/ppermute | solution.py:671
  175.2 4.3 %collective-permute-start.30 = (bf16[1,64,1024]{2,1,0:T(8,128)(2,1)S(1)}, bf16[1,64,1024]{2,1,0:T(8,128)(2,1)S(1)}, u32[]{:S(2)}, u32[]{:S(2)}) collective-permute-start(bf16[1,64,1024]{2,1,0:T(8,128)(2,1)S(1)} %add_convert_fusion.10), channel_id=1, source_target_pairs={{0,4},{1,5},{2,6},{3,7},{4,0},{5,1},{6,2},{7,3},{8,12},{9,13},{10,... | collective-permute-start | bytes 393224 | tf_op jit(solution)/shard_map/ppermute | solution.py:671
  177.3 5.7 %collective-permute-start.27 = (bf16[1,80,1024]{2,1,0:T(8,128)(2,1)S(1)}, bf16[1,80,1024]{2,1,0:T(8,128)(2,1)S(1)}, u32[]{:S(2)}, u32[]{:S(2)}) collective-permute-start(bf16[1,80,1024]{2,1,0:T(8,128)(2,1)S(1)} %pad_maximum_fusion.6), channel_id=1, source_target_pairs={{0,8},{1,9},{2,10},{3,11},{4,12},{5,13},{6,14},{7,15},{8,0},{9,1},... | collective-permute-start | bytes 491528 | tf_op jit(solution)/shard_map/ppermute | solution.py:671
  180.4 5.8 %collective-permute-start.31 = (bf16[1,32,1024]{2,1,0:T(8,128)(2,1)S(1)}, bf16[1,32,1024]{2,1,0:T(8,128)(2,1)S(1)}, u32[]{:S(2)}, u32[]{:S(2)}) collective-permute-start(bf16[1,32,1024]{2,1,0:T(8,128)(2,1)S(1)} %add_convert_fusion.14), channel_id=1, source_target_pairs={{0,16},{1,17},{2,18},{3,19},{4,20},{5,21},{6,22},{7,23},{8,24},{9,... | collective-permute-start | bytes 196616 | tf_op jit(solution)/shard_map/ppermute | solution.py:671
  184.0 5.7 %collective-permute-start.28 = (bf16[1,48,1024]{2,1,0:T(8,128)(2,1)S(1)}, bf16[1,48,1024]{2,1,0:T(8,128)(2,1)S(1)}, u32[]{:S(2)}, u32[]{:S(2)}) collective-permute-start(bf16[1,48,1024]{2,1,0:T(8,128)(2,1)S(1)} %pad_maximum_fusion.10), channel_id=1, source_target_pairs={{0,16},{1,17},{2,18},{3,19},{4,20},{5,21},{6,22},{7,23},{8,24},{9,... | collective-permute-start | bytes 294920 | tf_op jit(solution)/shard_map/ppermute | solution.py:671
  187.1 6.7 %collective-permute-start.32 = (bf16[1,32,1024]{2,1,0:T(8,128)(2,1)S(1)}, bf16[1,32,1024]{2,1,0:T(8,128)(2,1)S(1)}, u32[]{:S(2)}, u32[]{:S(2)}) collective-permute-start(bf16[1,32,1024]{2,1,0:T(8,128)(2,1)S(1)} %add_convert_fusion.13), channel_id=1, source_target_pairs={{0,16},{1,17},{2,18},{3,19},{4,20},{5,21},{6,22},{7,23},{8,24},{9,... | collective-permute-start | bytes 196616 | tf_op jit(solution)/shard_map/ppermute | solution.py:671
  190.7 5.6 %collective-permute-start.37 = (bf16[1,32,1024]{2,1,0:T(8,128)(2,1)S(1)}, bf16[1,32,1024]{2,1,0:T(8,128)(2,1)S(1)}, u32[]{:S(2)}, u32[]{:S(2)}) collective-permute-start(bf16[1,32,1024]{2,1,0:T(8,128)(2,1)S(1)} %add_convert_fusion.12), channel_id=1, source_target_pairs={{0,16},{1,17},{2,18},{3,19},{4,20},{5,21},{6,22},{7,23},{8,24},{9,... | collective-permute-start | bytes 196616 | tf_op jit(solution)/shard_map/ppermute | solution.py:671
  193.9 4.3 %collective-permute-start.33 = (bf16[1,80,1024]{2,1,0:T(8,128)(2,1)S(1)}, bf16[1,80,1024]{2,1,0:T(8,128)(2,1)S(1)}, u32[]{:S(2)}, u32[]{:S(2)}) collective-permute-start(bf16[1,80,1024]{2,1,0:T(8,128)(2,1)S(1)} %pad_maximum_fusion.7), channel_id=1, source_target_pairs={{0,4},{1,5},{2,6},{3,7},{4,0},{5,1},{6,2},{7,3},{8,12},{9,13},{10,... | collective-permute-start | bytes 491528 | tf_op jit(solution)/shard_map/ppermute | solution.py:671
  196.3 5.5 %collective-permute-start.38 = (bf16[1,64,1024]{2,1,0:T(8,128)(2,1)S(1)}, bf16[1,64,1024]{2,1,0:T(8,128)(2,1)S(1)}, u32[]{:S(2)}, u32[]{:S(2)}) collective-permute-start(bf16[1,64,1024]{2,1,0:T(8,128)(2,1)S(1)} %pad_maximum_fusion.9), channel_id=1, source_target_pairs={{0,8},{1,9},{2,10},{3,11},{4,12},{5,13},{6,14},{7,15},{8,0},{9,1},... | collective-permute-start | bytes 393224 | tf_op jit(solution)/shard_map/ppermute | solution.py:671
  198.9 11.6 %collective-permute-start.34 = (bf16[1,128,1024]{2,1,0:T(8,128)(2,1)S(1)}, bf16[1,128,1024]{2,1,0:T(8,128)(2,1)S(1)}, u32[]{:S(2)}, u32[]{:S(2)}) collective-permute-start(bf16[1,128,1024]{2,1,0:T(8,128)(2,1)S(1)} %get-tuple-element.152), channel_id=1, source_target_pairs={{0,8},{1,9},{2,10},{3,11},{4,12},{5,13},{6,14},{7,15},{8,0},{9,1},... | collective-permute-start | bytes 786440 | tf_op jit(solution)/shard_map/ppermute | solution.py:671
  202.5 8.5 %collective-permute-start.39 = (bf16[1,128,1024]{2,1,0:T(8,128)(2,1)S(1)}, bf16[1,128,1024]{2,1,0:T(8,128)(2,1)S(1)}, u32[]{:S(2)}, u32[]{:S(2)}) collective-permute-start(bf16[1,128,1024]{2,1,0:T(8,128)(2,1)S(1)} %get-tuple-element.150), channel_id=1, source_target_pairs={{0,4},{1,5},{2,6},{3,7},{4,0},{5,1},{6,2},{7,3},{8,12},{9,13},{10,... | collective-permute-start | bytes 786440 | tf_op jit(solution)/shard_map/ppermute | solution.py:671
  205.1 10.1 %collective-permute-start.35 = (bf16[1,128,1024]{2,1,0:T(8,128)(2,1)S(1)}, bf16[1,128,1024]{2,1,0:T(8,128)(2,1)S(1)}, u32[]{:S(2)}, u32[]{:S(2)}) collective-permute-start(bf16[1,128,1024]{2,1,0:T(8,128)(2,1)S(1)} %get-tuple-element.152), channel_id=1, source_target_pairs={{0,2},{1,3},{2,0},{3,1},{4,6},{5,7},{6,4},{7,5},{8,10},{9,11},{10,... | collective-permute-start | bytes 786440 | tf_op jit(solution)/shard_map/ppermute | solution.py:671
  210.5 4.7 %collective-permute-start.40 = (bf16[1,128,1024]{2,1,0:T(8,128)(2,1)S(1)}, bf16[1,128,1024]{2,1,0:T(8,128)(2,1)S(1)}, u32[]{:S(2)}, u32[]{:S(2)}) collective-permute-start(bf16[1,128,1024]{2,1,0:T(8,128)(2,1)S(1)} %get-tuple-element.150), channel_id=1, source_target_pairs={{0,2},{1,3},{2,0},{3,1},{4,6},{5,7},{6,4},{7,5},{8,10},{9,11},{10,... | collective-permute-start | bytes 786440 | tf_op jit(solution)/shard_map/ppermute | solution.py:671
  210.6 4.7 %copy-start.7 = (bf16[1,128,1024]{2,1,0:T(8,128)(2,1)}, bf16[1,128,1024]{2,1,0:T(8,128)(2,1)S(1)}, u32[]{:S(2)}) copy-start(bf16[1,128,1024]{2,1,0:T(8,128)(2,1)S(1)} %collective-permute-done.34) | copy-start | bytes 786436
  210.6 4.7 %collective-permute-start.36 = (bf16[1,128,1024]{2,1,0:T(8,128)(2,1)S(1)}, bf16[1,128,1024]{2,1,0:T(8,128)(2,1)S(1)}, u32[]{:S(2)}, u32[]{:S(2)}) collective-permute-start(bf16[1,128,1024]{2,1,0:T(8,128)(2,1)S(1)} %collective-permute-done.34), channel_id=1, source_target_pairs={{0,2},{1,3},{2,0},{3,1},{4,6},{5,7},{6,4},{7,5},{8,10},{9,11},{10,... | collective-permute-start | bytes 786440 | tf_op jit(solution)/shard_map/ppermute | solution.py:671
  211.0 4.3 %copy-start.8 = (bf16[1,128,1024]{2,1,0:T(8,128)(2,1)}, bf16[1,128,1024]{2,1,0:T(8,128)(2,1)S(1)}, u32[]{:S(2)}) copy-start(bf16[1,128,1024]{2,1,0:T(8,128)(2,1)S(1)} %collective-permute-done.39) | copy-start | bytes 786436
  211.0 4.3 %collective-permute-start.41 = (bf16[1,128,1024]{2,1,0:T(8,128)(2,1)S(1)}, bf16[1,128,1024]{2,1,0:T(8,128)(2,1)S(1)}, u32[]{:S(2)}, u32[]{:S(2)}) collective-permute-start(bf16[1,128,1024]{2,1,0:T(8,128)(2,1)S(1)} %collective-permute-done.39), channel_id=1, source_target_pairs={{0,2},{1,3},{2,0},{3,1},{4,6},{5,7},{6,4},{7,5},{8,10},{9,11},{10,... | collective-permute-start | bytes 786440 | tf_op jit(solution)/shard_map/ppermute | solution.py:671
  215.3 0.9 copy-start.11
  215.3 1.0 copy-start.12
  (5 other events, 3.9 us)

commit v4 on v3

--- a/solution.py
+++ b/solution.py
@@ -19,6 +19,14 @@
 VMEM_BYTES = 56 * 1024 * 1024
 F32 = jnp.float32
 BF16 = jnp.bfloat16
+
+
+def in_hbm(values):
+    return pltpu.with_memory_space_constraint(values, pltpu.HBM)
+
+
+def hbm(shape, dtype):
+    return pltpu.HBM(shape, dtype)
 
 
 def dot_nn(left, right):
@@ -215,7 +223,7 @@
         ]
         operands = [rows_in.reshape(SEGMENTS, rows // SEGMENTS, width), gain]
         out_specs = [pl.BlockSpec((BLOCK, width), early)] * 2
-        out_shape = [jax.ShapeDtypeStruct((rows, width), BF16)] * 2
+        out_shape = [hbm((rows, width), BF16)] * 2
     else:
         in_specs, operands = [pl.BlockSpec((BLOCK, width), early)], [rows_in]
         out_specs, out_shape = [], []
@@ -223,8 +231,8 @@
     in_specs += [pl.BlockSpec((1, channels), whole)] + [pl.BlockSpec(memory_space=pltpu.SMEM)] * 2 + [pl.BlockSpec((1, channels), whole)]
     out_specs += [pl.BlockSpec((BLOCK, channels), early)] + [pl.BlockSpec((BLOCK, channels), late)] * 3
     out_specs += [pl.BlockSpec((8, channels), whole)]
-    out_shape += [jax.ShapeDtypeStruct((rows, channels), BF16)] * 4
-    out_shape += [jax.ShapeDtypeStruct((8, channels), F32)]
+    out_shape += [hbm((rows, channels), BF16)] * 4
+    out_shape += [hbm((8, channels), F32)]
     wide = min(channels, 256)
     scratch = [pltpu.VMEM((channels // wide, 3, BLOCK, wide), F32)]
     scratch += [pltpu.VMEM((rows + 8, channels), F32)] * 2
@@ -239,10 +247,10 @@
         out_specs=out_specs,
         out_shape=out_shape,
         scratch_shapes=scratch,
-        compiler_params=pltpu.CompilerParams(vmem_limit_bytes=VMEM_BYTES, dimension_semantics=("arbitrary", "arbitrary")),
+        compiler_params=pltpu.CompilerParams(vmem_limit_bytes=36 * 1024 * 1024, dimension_semantics=("arbitrary", "arbitrary")),
         cost_estimate=pl.CostEstimate(flops=2 * rows * width * 3 * channels, bytes_accessed=rows * channels * 16, transcendentals=4 * rows * channels),
         name="mixer_forward",
-    )(*operands, *weights, bias, lengths, scalars, carry)
+    )(in_hbm(operands[0]), *operands[1:], *weights, bias, lengths, scalars, carry)
 
 
 def dense_kernel(stage, sets, pieces, *refs):
@@ -278,7 +286,7 @@
         middle = x_ref[...].astype(F32)
         for state, weight in zip(states, outs_w):
             middle = middle + dot_nn(state[...], weight[...])
-        middle_out[...] = middle
+        middle_out[...] = middle.astype(BF16)
         dense_in = (middle * row_scale(middle) * gain).astype(BF16)
         dense_out[...] = dense_in
         cotangent = interleave(c_ref[...], cotangent_s).astype(BF16)
@@ -307,13 +315,13 @@
         lower_acc[:, cols] += dot_nn(cotangent_t, active)
         upper_acc[:, cols] += dot_nn(dense_t, upper_delta)
     if stage == 0:
-        sum_out[...] = middle + fed
-        delta_out[...] = delta
+        sum_out[...] = (middle + fed).astype(BF16)
+        delta_out[...] = delta.astype(BF16)
     else:
-        separate(sum_ref[...] + fed, out_s, out_ref)
-        middle = middle_ref[...]
+        separate(sum_ref[...].astype(F32) + fed, out_s, out_ref)
+        middle = middle_ref[...].astype(F32)
         scale = row_scale(middle)
-        delta = delta_ref[...] + delta
+        delta = delta_ref[...].astype(F32) + delta
         slope_ref[...] += fold_rows(delta * middle * scale)
         scaled = delta * gain
         inner = jnp.mean(scaled * middle, -1, keepdims=True)
@@ -330,8 +338,8 @@
             cols = slice(shard * half, (shard + 2) * half)
             out = keep_out if shard < pieces * shards // 2 else send_out
             there = shard % (pieces * shards // 2)
-            out[0, there : there + 2] = upper_acc[:, cols].T.astype(BF16).reshape(2, half, width)
-            out[1, there : there + 2] = lower_acc[:, cols].T.astype(BF16).reshape(2, half, width)
+            out[there : there + 2, :half, :] = upper_acc[:, cols].T.astype(BF16).reshape(2, half, width)
+            out[there : there + 2, half:, :] = lower_acc[:, cols].T.astype(BF16).reshape(2, half, width)
         if stage == 1:
             tall = output_acc.shape[0] // PLACES
             for index, output in enumerate(outputs_ref):
@@ -354,21 +362,21 @@
     runs_spec = pl.BlockSpec((SEGMENTS, tall // SEGMENTS, width), lambda block: (0, block, 0))
     runs_shape = (SEGMENTS, rows // SEGMENTS, width)
     row_spec = pl.BlockSpec((tall, width), by_rows)
-    grads = (2, len(pieces) * shards // 2, both // 2, width)
+    grads = (len(pieces) * shards // 2, both, width)
     in_specs = [pl.BlockSpec((tall, channels), by_rows)] * sets
-    out_specs = [pl.BlockSpec(grads, lambda block: (0, 0, 0, 0))] * 2
-    out_shape = [jax.ShapeDtypeStruct(grads, BF16)] * 2
+    out_specs = [pl.BlockSpec(grads, lambda block: (0, 0, 0))] * 2
+    out_shape = [hbm(grads, BF16)] * 2
     scratch = [pltpu.VMEM((width, hidden), F32)] * 2
     if stage == 0:
         in_specs += [row_spec, runs_spec] + [pl.BlockSpec((channels, width), whole)] * sets
         entering = [entering[0], entering[1].reshape(runs_shape), *output_weights]
         out_specs += [row_spec] * 5
-        out_shape += [jax.ShapeDtypeStruct((rows, width), d) for d in (F32, F32, F32, BF16, BF16)]
+        out_shape += [hbm((rows, width), BF16)] * 5
     else:
         in_specs += [row_spec] * 5
         out_specs += [runs_spec, row_spec, pl.BlockSpec((8, width), whole)] + [pl.BlockSpec((width, channels), whole)] * sets
-        out_shape += [jax.ShapeDtypeStruct(runs_shape, BF16), jax.ShapeDtypeStruct((rows, width), BF16)]
-        out_shape += [jax.ShapeDtypeStruct((8, width), F32)] + [jax.ShapeDtypeStruct((width, channels), BF16)] * sets
+        out_shape += [hbm(runs_shape, BF16), hbm((rows, width), BF16)]
+        out_shape += [hbm((8, width), F32)] + [hbm((width, channels), BF16)] * sets
         scratch += [pltpu.VMEM((width, sets * channels), F32)]
     scratch += [pltpu.VMEM((width // 128, tall, 128), F32)]
     in_specs += [pl.BlockSpec((1, width), whole), pl.BlockSpec(memory_space=pltpu.SMEM)]
@@ -380,10 +388,10 @@
         out_specs=out_specs,
         out_shape=out_shape,
         scratch_shapes=scratch,
-        compiler_params=pltpu.CompilerParams(vmem_limit_bytes=VMEM_BYTES, dimension_semantics=("arbitrary",)),
+        compiler_params=pltpu.CompilerParams(vmem_limit_bytes=44 * 1024 * 1024, dimension_semantics=("arbitrary",)),
         cost_estimate=pl.CostEstimate(flops=12 * rows * width * hidden, bytes_accessed=rows * width * 24, transcendentals=rows * hidden),
         name="dense_first" if stage == 0 else "dense_second",
-    )(*states, *entering, gain, scalars, *pieces)
+    )(*[in_hbm(v) for v in states], *[in_hbm(v) if v.shape[0] != channels else v for v in entering], gain, scalars, *pieces)
 
 
 def mixer_back_kernel(sets, mixed_ref, normed_ref, lengths, scalars, *refs):
@@ -549,7 +557,7 @@
         compiler_params=pltpu.CompilerParams(vmem_limit_bytes=VMEM_BYTES, dimension_semantics=("arbitrary", "arbitrary")),
         cost_estimate=pl.CostEstimate(flops=2 * rows * width * 4 * channels * sets, bytes_accessed=rows * channels * 12 * sets, transcendentals=0),
         name="mixer_backward",
-    )(mixed, normed, lengths, scalars, *[item for one in per_set for item in one])
+    )(in_hbm(mixed), in_hbm(normed), lengths, scalars, *[in_hbm(item) if item.shape[0] == rows else item for one in per_set for item in one])
     return results[:sets], results[sets : sets + 2], results[sets + 2 : sets + 4], *results[sets + 4 :]
 
 
@@ -578,6 +586,10 @@
     result = mixed_ref[...].astype(F32) + scale * (scaled - rows * (scale * scale * inner))
     separate(result, out_s, out_ref)
 
+    @pl.when(pl.program_id(0) == pl.num_programs(0) - 1)
+    def _():
+        slope_ref[0:1, :] = jnp.sum(slope_ref[...], 0, keepdims=True)
+
 
 def input_backward(x_rows, mixed, gain, factors, weights):
     rows, width = x_rows.shape
@@ -593,12 +605,12 @@
         + [pl.BlockSpec((BLOCK, channels), by_rows)] * (4 * sets)
         + [pl.BlockSpec((width, channels), whole)] * (3 * sets),
         out_specs=[pl.BlockSpec((SEGMENTS, STEPS, width), lambda block: (0, block, 0)), pl.BlockSpec((8, width), whole)],
-        out_shape=[jax.ShapeDtypeStruct((SEGMENTS, rows // SEGMENTS, width), F32), jax.ShapeDtypeStruct((8, width), F32)],
+        out_shape=[hbm((SEGMENTS, rows // SEGMENTS, width), F32), hbm((8, width), F32)],
         scratch_shapes=[pltpu.VMEM((width // 128, BLOCK, 128), F32)],
-        compiler_params=pltpu.CompilerParams(vmem_limit_bytes=VMEM_BYTES, dimension_semantics=("arbitrary",)),
+        compiler_params=pltpu.CompilerParams(vmem_limit_bytes=44 * 1024 * 1024, dimension_semantics=("arbitrary",)),
         cost_estimate=pl.CostEstimate(flops=2 * rows * width * 3 * channels * sets, bytes_accessed=rows * channels * 8 * sets, transcendentals=0),
         name="input_backward",
-    )(x_rows, mixed, gain, *factors, *weights)
+    )(in_hbm(x_rows), in_hbm(mixed), gain, *[in_hbm(f) for f in factors], *weights)
 
 
 def finish_kernel(channels, count, *refs):
@@ -648,6 +660,25 @@
     return result.astype(terms[0].dtype)
 
 
+def sum_kernel(*refs):
+    for index in range(len(refs) // 3):
+        left, right, out = refs[2 * index], refs[2 * index + 1], refs[2 * (len(refs) // 3) + index]
+        out[...] = (left[...].astype(F32) + right[...].astype(F32)).astype(BF16)
+
+
+def paired_sums(pairs, blocks, places):
+    specs = [pl.BlockSpec(block, functools.partial(lambda place, step: place, place)) for block, place in zip(blocks, places)]
+    return pl.pallas_call(
+        sum_kernel,
+        grid=(1,),
+        in_specs=[spec for spec in specs for _ in range(2)],
+        out_specs=[pl.BlockSpec(block, lambda step: (0, 0, 0)) for block in blocks],
+        out_shape=[jax.ShapeDtypeStruct(block, BF16) for block in blocks],
+        compiler_params=pltpu.CompilerParams(vmem_limit_bytes=VMEM_BYTES),
+        name="paired_sums",
+    )(*[item for pair in pairs for item in pair])
+
+
 def hold(terms, *earlier):
     return terms[:-1] + [after(terms[-1], *earlier)]
 
@@ -655,6 +686,28 @@
 def part(terms, index, axis):
     half = terms[0].shape[axis] // 2
     return [lax.slice_in_dim(t, index * half, (index + 1) * half, axis=axis) for t in terms]
+
+
+def pack_kernel(*refs):
+    mine_out, output_out = refs[5:]
+    for index, ref in enumerate(refs[1:4]):
+        mine_out[index] = ref[...]
+    output_out[...] = refs[4][...]
+
+
+def pack_halves(weights, half):
+    tall, wide = weights[0].shape[0] // 2, weights[0].shape[1]
+    return pl.pallas_call(
+        pack_kernel,
+        grid_spec=pltpu.PrefetchScalarGridSpec(
+            num_scalar_prefetch=1,
+            grid=(1,),
+            in_specs=[pl.BlockSpec((tall, wide), lambda step, half: (half[0], 0))] * 4,
+            out_specs=[pl.BlockSpec((3, tall, wide), lambda step, half: (0, 0, 0)), pl.BlockSpec((tall, wide), lambda step, half: (0, 0))],
+        ),
+        out_shape=[jax.ShapeDtypeStruct((3, tall, wide), BF16), jax.ShapeDtypeStruct((tall, wide), BF16)],
+        name="pack_halves",
+    )(jnp.reshape(half, (1,)).astype(jnp.int32), *weights)
 
 
 class Links:
@@ -671,40 +724,31 @@
         return lax.ppermute(values, ("dp", "tensor"), pairs)
 
     def begin_weights(self, own_weights):
-        half = own_weights[0].shape[0] // 2
-        mine = jnp.stack([lax.dynamic_slice_in_dim(w, self.core * half, half) for w in own_weights])
-        return mine, self.swap(mine, self.TENSOR)
+        mine, mine_output = pack_halves(own_weights, self.core)
+        return mine, mine_output, self.swap(mine, self.TENSOR)
 
     def end_weights(self, got):
         rest = self.swap(got, self.CORE)
         lower = self.core == 0
-        whole = jnp.concatenate([jnp.where(lower, got, rest), jnp.where(lower, rest, got)], 1)
-        return [whole[index] for index in range(4)]
+        return jnp.concatenate([jnp.where(lower, got, rest), jnp.where(lower, rest, got)], -2)
 
     def begin_dense(self, shard):
         return [shard] + [self.swap(shard, bits) for bits in (self.Z_NEAR, self.Z_FAR, self.Z_NEAR | self.Z_FAR)]
 
     def dense_pieces(self, pieces):
         own = jnp.stack(pieces)
-        near = self.swap(own, self.NEAR)
-        other = self.swap(own, self.TENSOR)
-        return own, near, other, self.swap(own, self.CORE)
-
-    def dense_grads_cut(self, values):
-        return values.reshape(2, 2, 4, *values.shape[2:])
+        return own, self.swap(own, self.NEAR), self.swap(own, self.CORE)
 
     def dense_across(self, own_terms, other_terms):
-        own = [self.dense_grads_cut(t) for t in own_terms]
-        other = [self.dense_grads_cut(t) for t in other_terms]
-        pick = lambda terms, index: total([t[:, index] for t in terms])
-        sends = [(pick(other, 0), self.TENSOR), (pick(own, 1), self.NEAR), (pick(other, 1), self.TENSOR | self.NEAR)]
-        return sends, [t[:, 0] for t in own]
+        pick = lambda terms, near: total([t[near * 4 : near * 4 + 4] for t in terms])
+        sends = [(pick(other_terms, 0), self.TENSOR), (pick(own_terms, 1), self.NEAR), (pick(other_terms, 1), self.TENSOR | self.NEAR)]
+        return sends, [t[:4] for t in own_terms]
 
     def dense_along(self, terms):
         sends = []
         for index, bits in ((1, self.Z_NEAR), (2, self.Z_FAR), (3, self.Z_NEAR | self.Z_FAR)):
-            sends.append((total([t[:, index] for t in terms]), bits))
-        return sends, [t[:, 0] for t in terms]
+            sends.append((total([t[index] for t in terms]), bits))
+        return sends, [t[0] for t in terms]
 
     def exchange(self, sends, kept):
         return kept + [self.swap(values, bits) for values, bits in sends]
@@ -721,8 +765,8 @@
 
 
 class Plain:
-    def __init__(self, n_tensor, own):
-        self.n_tensor, self.own = n_tensor, own
+    def __init__(self, n_tensor, own, hidden):
+        self.n_tensor, self.own, self.hidden = n_tensor, own, hidden
         self.me = [0, 0]
 
     def weights(self, own_weights):
@@ -740,9 +784,8 @@
         return pieces[: len(pieces) // 2], pieces[len(pieces) // 2 :]
 
     def dense_sums(self, grads):
-        whole = jnp.concatenate(grads, 1)
-        whole = whole.reshape(2, -1, whole.shape[-1])
-        return [lax.psum_scatter(w, ("dp", "tensor"), scatter_dimension=0, tiled=True) for w in whole]
+        whole = regroup(jnp.concatenate(grads, 0), self.hidden)
+        return lax.psum_scatter(whole, ("dp", "tensor"), scatter_dimension=0, tiled=True)[0]
 
     def mixer_sums(self, grads):
         grads = jnp.concatenate(grads, 1)
@@ -772,14 +815,15 @@
     premix = premix_gain.astype(F32)[None]
     dense = dense_gain.astype(F32)[None]
     paired = (n_dp, n_tensor) == (16, 2)
-    links = Links() if paired else Plain(n_tensor, own)
+    hidden = lower_weight.shape[0]
+    links = Links() if paired else Plain(n_tensor, own, hidden)
     scalars = jnp.stack([place * rows] + links.me).astype(jnp.int32)
     own_weights = [forget_weight, admit_weight, value_weight, output_weight]
     dense_shard = jnp.concatenate([upper_weight.T, lower_weight], 0)
     if paired:
         weights, biases = [own_weights], [admit_bias]
         channels = own
-        mine, got = links.begin_weights(own_weights)
+        mine, mine_output, got = links.begin_weights(own_weights)
         pieces = links.begin_dense(after(dense_shard, mine))
         biases.append(links.swap(after(admit_bias, pieces[0]), Links.TENSOR))
     else:
@@ -808,14 +852,17 @@
     x_rows, normed, *kept_0 = forward(True, block_in, 0)
     if paired:
         got, pieces, biases[1] = after((got, pieces, biases[1]), normed)
-        own_four, near_four, other_four, own_rest = links.dense_pieces(pieces)
-        weights.append(links.end_weights(got))
+        got_output = links.swap(after(mine_output, got), Links.TENSOR)
+        own_four, near_four, own_rest = links.dense_pieces(pieces)
+        other_weights = links.end_weights(got)
+        weights.append([other_weights[index] for index in range(3)])
     kept_1 = forward(False, normed, 1)
     kept = [kept_0, kept_1]
     if paired:
-        near_four, other_four = after((near_four, other_four), kept_1[1])
-        far_four = links.swap(other_four, Links.NEAR)
-        other_rest = links.swap(other_four, Links.CORE)
+        near_four, held_four = after((near_four, own_four), kept_1[1])
+        weights[1].append(links.end_weights(after(got_output, kept_1[1])))
+        other_four = links.swap(held_four, Links.TENSOR)
+        far_four = links.swap(held_four, Links.TENSOR | Links.NEAR)
         pieces_0 = [own_four, near_four, own_rest, links.swap(near_four, Links.CORE)]
     else:
         pieces_0, pieces_1 = links.dense(dense_shard)
@@ -823,8 +870,8 @@
     states = [k[1] for k in kept]
     own_keep, own_send, *rows_0 = dense_both(0, states, (x_rows, out_cotangent), outputs, dense, scalars, pieces_0)
     if paired:
-        far_four, other_rest = after((far_four, other_rest), rows_0[0])
-        pieces_1 = [other_four, far_four, other_rest, links.swap(far_four, Links.CORE)]
+        far_four, other_four = after((far_four, other_four), rows_0[0])
+        pieces_1 = [other_four, far_four, links.swap(other_four, Links.CORE), links.swap(far_four, Links.CORE)]
         own_terms = [own_keep, links.swap(own_send, Links.CORE)]
     other_keep, other_send, block_out, mixed, dense_part, *output_grads = dense_both(1, states, rows_0, None, dense, scalars, pieces_1)
     back_mixed = mixed
@@ -850,7 +897,10 @@
         core_sends = after([first[1], second[1]], dense_terms[-3:])
         first = [first[0], links.swap(core_sends[0], Links.CORE)]
         second = [second[0], links.swap(core_sends[1], Links.CORE)]
-        first, second = links.halve(first, Links.TENSOR), links.halve(second, Links.NEAR)
+        sets, tall, wide = first[0].shape
+        sends = paired_sums((first, second), ((1, tall, wide), (sets, tall // 2, wide)), ((1, 0, 0), (0, 1, 0)))
+        first = [(sends[0], Links.TENSOR)], part(first, 0, 0)
+        second = [(sends[1], Links.NEAR)], part(second, 0, 1)
         factors[0] = after(factors[0], first[0][0][0], second[0][0][0], [values for values, _ in along])
         first, second = links.exchange(*first), links.exchange(*second)
         dense_terms = links.exchange(along, along_kept)
@@ -859,7 +909,7 @@
     bias_parts = jnp.sum(bias_parts, 1)
     if paired:
         bias_parts = jnp.where(place == 0, bias_parts, bias_parts[::-1])
-    small = jnp.concatenate([jnp.sum(premix_part, 0), jnp.sum(dense_part, 0), bias_parts[0], bias_parts[1]], 0)
+    small = jnp.concatenate([premix_part[0], jnp.sum(dense_part, 0), bias_parts[0], bias_parts[1]], 0)
     if paired:
         small = small.reshape(1, -1, 2 * channels).astype(BF16)
         filled = small.shape[1]
@@ -892,12 +942,13 @@
         second += [links.swap(f, Links.CORE) for f in second]
         first, second = [f[0] for f in first], [f[0] for f in second]
         small = small[0, :filled].reshape(-1).astype(F32)
-        upper_sum, lower_sum = total(dense_terms)
+        dense_sum = total(dense_terms)
     else:
         small = lax.psum(small, ("dp", "tensor"))
-        upper_sum, lower_sum = links.dense_sums([own_keep, own_send, other_keep, other_send])
+        dense_sum = links.dense_sums([own_keep, own_send, other_keep, other_send])
         first, second = links.mixer_sums(first), links.mixer_sums(second)
-    upper_slope, lower_slope = upper_sum.astype(F32).T, lower_sum.astype(F32)
+    dense_sum = dense_sum.astype(F32)
+    upper_slope, lower_slope = dense_sum[:hidden].T, dense_sum[hidden:]
     forget_slope, admit_slope, value_slope, output_slope = finish_slopes(first, second, scalars)
     shard = width // (n_dp * n_tensor)
     at = (lax.axis_index("dp") * n_tensor + place) * shard

time: 221 us -> 212 us (0.959)
  other arithmetic: 23.4 us -> 16.8 us
  local copies, waits for them, and re-layouts: 8.38 us -> 3.88 us
    pallas_call x0 -> x2, Pallas kernels: none -> 4.91 us  [the longest x1 2.6 us: paired_sums(): pl.pallas_call(sum_kernel, grid=(1,), in_specs=[spec for spec in specs fo...]
    convert_element_type x19 -> x15, other arithmetic: 15.5 us -> 11.5 us  [total(): return result.astype(terms[0].dtype)]
    pallas_call x2, Pallas kernels: 52.3 us -> 49.1 us  [dense_both(): pl.pallas_call(functools.partial(dense_kernel, stage, sets, len(pieces)),...]
    unnamed x57 -> x49, local copies, waits for them, and re-layouts: 3.61 us -> 1 us
    ppermute x42 -> x44, starting transfers between devices: 48.7 us -> 50.2 us  [swap(): return lax.ppermute(values, ('dp', 'tensor'), pairs)]
    ppermute x42 -> x44, waiting for transfers between devices: 17.7 us -> 19.1 us  [swap(): return lax.ppermute(values, ('dp', 'tensor'), pairs)]
  transfers between devices with their start and end apart: 42 -> 44, of which waited for: 11 -> 11; matrix products, arithmetic and copies ran while one was open for 12% -> 9% of each run, Pallas kernels for 53% -> 54%
where the time goes in v4:
time: 212 us; the launch traced here: 211 us
  Pallas kernels  120 us (57%)
  starting transfers between devices  50.2 us (24%)
  waiting for transfers between devices  19.1 us (9%)
  other arithmetic  16.8 us (8%)
  local copies, waits for them, and re-layouts  3.88 us (2%)
    ppermute x44, starting transfers between devices, swap(): return lax.ppermute(values, ('dp', 'tensor'), pairs)  50.2 us
    pallas_call x2, Pallas kernels, dense_both(): pl.pallas_call(functools.partial(dense_kernel, stage, sets, len(pieces)),...  49.1 us
    pallas_call x2, Pallas kernels, mixer_forward(): pl.pallas_call(functools.partial(mixer_kernel, first), grid=(2, blocks),...  26.8 us
    pallas_call x1, Pallas kernels, mixer_backward(): pl.pallas_call(functools.partial(mixer_back_kernel, sets), grid=(2, block...  21.6 us
    ppermute x44, waiting for transfers between devices, swap(): return lax.ppermute(values, ('dp', 'tensor'), pairs)  19.1 us
    pallas_call x1, Pallas kernels, input_backward(): pl.pallas_call(functools.partial(input_kernel, sets), grid=(rows // BLOCK...  13.5 us
    convert_element_type x15, other arithmetic, total(): return result.astype(terms[0].dtype)  11.5 us
  transfers between devices with their start and end apart: 44, of which 11 were waited for; matrix products, arithmetic and copies ran while one was open for 9% of the time, Pallas kernels for 54%

profile of v4, /device:TPU:1, one launch (start us, length us, event | category | flops | bytes accessed | tf_op | source)
XLA Modules:
  0.0 211.0 jit_solution(10101672185737010526)
XLA Ops:
  0.7 2.3 %pack_halves.1 = (bf16[3,256,512]{2,1,0:T(8,128)(2,1)}, bf16[256,512]{1,0:T(8,128)(2,1)}) custom-call(s32[1]{0:T(128)} %bitcast.6.refs_0_, bf16[512,512]{1,0:T(8,128)(2,1)} %refs_11_.1, bf16[512,512]{1,0:T(8,128)(2,1)} %refs_12_.1, bf16[512,512]{1,0:T(8,128)(2,1)} %refs_13_.1, bf16[512,512]{1,0:T(8,128)(2,1)} %refs_0_.1), custom_call_target="tpu_custom_call" | custom-call | tf_op jit(solution)/shard_map/pack_halves/pallas_call | solution.py:700
  3.1 2.0 collective-permute-start
  5.1 1.4 collective-permute-start.1
  6.5 2.3 %collective-permute-start.2 = (bf16[128,512]{1,0:T(8,128)(2,1)S(1)}, bf16[128,512]{1,0:T(8,128)(2,1)S(1)}, u32[]{:S(2)}, u32[]{:S(2)}) collective-permute-start(bf16[128,512]{1,0:T(8,128)(2,1)S(1)} %pad_maximum_fusion.8), channel_id=1, source_target_pairs={{0,16},{1,17},{2,18},{3,19},{4,20},{5,21},{6,22},{7,23},{8,24},{9,... | collective-permute-start | bytes 393224 | tf_op jit(solution)/shard_map/ppermute | solution.py:724
  9.2 14.0 %mixer_forward.2 = (bf16[2048,512]{1,0:T(8,128)(2,1)}, bf16[2048,512]{1,0:T(8,128)(2,1)}, bf16[2048,512]{1,0:T(8,128)(2,1)}, bf16[2048,512]{1,0:T(8,128)(2,1)}, ...) custom-call(bf16[8,256,512]{2,1,0:T(8,128)(2,1)} %bitcast.76, f32[1,512]{1,0:T(1,128)S(1)} %bitcast.56, ...), custom_call_target="tpu_custom_call" | custom-call | flops 3221225472 | bytes 16777216 | tf_op jit(solution)/shard_map/mixer_forward/pallas_call | solution.py:243
  23.3 1.9 collective-permute-start.5
  25.1 1.4 collective-permute-start.6
  26.6 1.3 collective-permute-start.8
  28.0 1.2 broadcast_select_fusion
  29.3 12.8 %mixer_forward.3 = (bf16[2048,512]{1,0:T(8,128)(2,1)}, bf16[2048,512]{1,0:T(8,128)(2,1)}, bf16[2048,512]{1,0:T(8,128)(2,1)}, bf16[2048,512]{1,0:T(8,128)(2,1)}, f32[8,512]{1,0:T(8,128)}) custom-call(bf16[2048,512]{1,0:T(8,128)(2,1)} %get-tuple-element.78.refs_0_.normed_ref, bf16[512,512]{1,0:T(8,128)(2,1)S(1)} %get-tuple-element.151.refs_1_.refs_14_, ...), custom_call_target="tpu_custom_call" | custom-call | flops 3221225472 | bytes 16777216 | tf_op jit(solution)/shard_map/mixer_forward/pallas_call | solution.py:243
  42.1 0.7 collective-permute-start.7
  43.3 1.3 collective-permute-start.11
  45.5 23.7 %dense_first.1 = (bf16[8,128,512]{2,1,0:T(8,128)(2,1)}, bf16[8,128,512]{2,1,0:T(8,128)(2,1)}, bf16[2048,512]{1,0:T(8,128)(2,1)}, bf16[2048,512]{1,0:T(8,128)(2,1...) custom-call(bf16[2048,512]{1,0:T(8,128)(2,1)} %get-tuple-element.77.refs_0_, ...), custom_call_target="tpu_custom_call" | custom-call | flops 12884901888 | bytes 25165824 | tf_op jit(solution)/shard_map/dense_first/pallas_call | solution.py:384
  69.2 0.5 collective-permute-start.13
  70.2 1.0 collective-permute-done.13.refs_11_
  71.2 1.5 collective-permute-done.14.refs_12_
  72.7 25.4 %dense_second.1 = (bf16[8,128,512]{2,1,0:T(8,128)(2,1)}, bf16[8,128,512]{2,1,0:T(8,128)(2,1)}, bf16[8,256,512]{2,1,0:T(8,128)(2,1)}, bf16[2048,512]{1,0:T(8,128)...) custom-call(bf16[2048,512]{1,0:T(8,128)(2,1)} %get-tuple-element.77.refs_0_, ...), custom_call_target="tpu_custom_call" | custom-call | flops 12884901888 | bytes 25165824 | tf_op jit(solution)/shard_map/dense_second/pallas_call | solution.py:384
  98.7 1.1 collective-permute-start.18
  99.8 1.3 collective-permute-done.15
  101.4 1.3 collective-permute-start.17
  102.7 1.0 collective-permute-start.19
  103.7 21.6 %mixer_backward.1 = (bf16[2048,512]{1,0:T(8,128)(2,1)}, bf16[2048,512]{1,0:T(8,128)(2,1)}, bf16[2,256,1024]{2,1,0:T(8,128)(2,1)}, bf16[2,256,1024]{2,1,0:T(8,128...) custom-call(bf16[2048,512]{1,0:T(8,128)(2,1)} %get-tuple-element.108, ...), custom_call_target="tpu_custom_call" | custom-call | flops 8589934592 | bytes 25165824 | tf_op jit(solution)/shard_map/mixer_backward/pallas_call | solution.py:531
  125.3 1.4 collective-permute-done.19
  126.7 1.2 collective-permute-start.20
  128.0 0.8 reduce_sum.19
  128.9 2.5 %fusion.10 = (bf16[128,512]{1,0:T(8,128)(2,1)}, bf16[128,512]{1,0:T(8,128)(2,1)}, bf16[128,512]{1,0:T(8,128)(2,1)}) fusion(bf16[4,128,512]{2,1,0:T(8,128)(2,1)} %collective-permute-done.18, bf16[4,128,512]{2,1,0:T(8,128)(2,1)} %collective-permute-done.17, bf16[8,128,512]{2,1,0:T(8,128)(2,1)} %copy-done.9, bf16[4,128,512]{2,1,0:T(8,128)(2,1)} %collective-permute-done.19, ...), kind=kLoop, calls=%fused_computation.37 | loop fusion | flops 1966080 | bytes 2359296 | tf_op jit(solution)/shard_map/convert_element_type | solution.py:660
  131.8 3.2 %collective-permute-start.25 = (bf16[128,512]{1,0:T(8,128)(2,1)}, bf16[128,512]{1,0:T(8,128)(2,1)S(1)}, u32[]{:S(2)}, u32[]{:S(2)}) collective-permute-start(bf16[128,512]{1,0:T(8,128)(2,1)} %get-tuple-element.146), channel_id=1, source_target_pairs={{0,16},{1,17},{2,18},{3,19},{4,20},{5,21},{6,22},{7,23},{8,24},{9,... | collective-permute-start | bytes 393224 | tf_op jit(solution)/shard_map/ppermute | solution.py:724
  135.0 2.6 %paired_sums.1 = (bf16[1,256,1024]{2,1,0:T(8,128)(2,1)}, bf16[2,128,1024]{2,1,0:T(8,128)(2,1)}) custom-call(bf16[2,256,1024]{2,1,0:T(8,128)(2,1)} %get-tuple-element.118.refs_0_, bf16[2,256,1024]{2,1,0:T(8,128)(2,1)} %collective-permute-done.20.refs_1_, bf16[2,256,1024]{2,1,0:T(8,128)(2,1)} %get-tuple-element.123.refs_2_, ...), custom_call_target="tpu_custom_call" | custom-call | tf_op jit(solution)/shard_map/paired_sums/pallas_call | solution.py:671
  137.6 0.6 collective-permute-start.22
  138.2 1.1 collective-permute-start.23
  139.3 13.5 %input_backward.1 = (f32[8,256,512]{2,1,0:T(8,128)}, f32[8,512]{1,0:T(8,128)}) custom-call(bf16[2048,512]{1,0:T(8,128)(2,1)} %get-tuple-element.85.refs_2_.refs_0_, bf16[2048,512]{1,0:T(8,128)(2,1)} %get-tuple-element.108.mixed_ref.refs_1_, f32[1,512]{1,0:T(1,128)S(1)} %bitcast.57, bf16[2048,512]{1,0:T(8,128)(2,1)} %get-tuple-element.127.refs_3_, ...), custom_call_target="tpu_custom_call" | custom-call | flops 6442450944 | bytes 16777216 | tf_op jit(solution)/shard_map/input_backward/pallas_call | solution.py:600
  152.8 0.7 slice_reduce_fusion.1
  153.7 1.8 collective-permute-start.27
  155.5 1.2 add_convert_fusion.3
  156.9 1.2 add_convert_fusion.4
  158.5 6.2 %collective-permute-done.31 = bf16[1,128,1024]{2,1,0:T(8,128)(2,1)S(1)} collective-permute-done((bf16[1,128,1024]{2,1,0:T(8,128)(2,1)S(1)}, bf16[1,128,1024]{2,1,0:T(8,128)(2,1)S(1)}, u32[]{:S(2)}, u32[]{:S(2)}) %collective-permute-start.31) | collective-permute-done | bytes 262176 | tf_op jit(solution)/shard_map/ppermute | solution.py:724
  164.7 1.1 add_convert_fusion.8
  166.6 1.1 add_convert_fusion.9
  167.7 1.5 collective-permute-start.29
  169.2 1.0 collective-permute-done.32
  170.1 0.9 add_convert_fusion.12
  171.1 2.6 %collective-permute-start.33 = (bf16[1,32,1024]{2,1,0:T(8,128)(2,1)S(1)}, bf16[1,32,1024]{2,1,0:T(8,128)(2,1)S(1)}, u32[]{:S(2)}, u32[]{:S(2)}) collective-permute-start(bf16[1,32,1024]{2,1,0:T(8,128)(2,1)S(1)} %add_convert_fusion.12), channel_id=1, source_target_pairs={{0,16},{1,17},{2,18},{3,19},{4,20},{5,21},{6,22},{7,23},{8,24},{9,... | collective-permute-start | bytes 196616 | tf_op jit(solution)/shard_map/ppermute | solution.py:724
  173.8 1.0 add_convert_fusion.13
  174.7 2.2 %collective-permute-start.30 = (bf16[1,48,1024]{2,1,0:T(8,128)(2,1)S(1)}, bf16[1,48,1024]{2,1,0:T(8,128)(2,1)S(1)}, u32[]{:S(2)}, u32[]{:S(2)}) collective-permute-start(bf16[1,48,1024]{2,1,0:T(8,128)(2,1)S(1)} %pad_maximum_fusion.10), channel_id=1, source_target_pairs={{0,16},{1,17},{2,18},{3,19},{4,20},{5,21},{6,22},{7,23},{8,24},{9,... | collective-permute-start | bytes 294920 | tf_op jit(solution)/shard_map/ppermute | solution.py:724
  176.9 1.0 add_convert_fusion.11
  177.9 1.0 collective-permute-start.34
  178.9 1.6 collective-permute-done.30
  180.5 1.0 add_convert_fusion.10
  181.4 1.0 collective-permute-start.39
  182.4 2.1 %collective-permute-done.34 = bf16[1,32,1024]{2,1,0:T(8,128)(2,1)S(1)} collective-permute-done((bf16[1,32,1024]{2,1,0:T(8,128)(2,1)S(1)}, bf16[1,32,1024]{2,1,0:T(8,128)(2,1)S(1)}, u32[]{:S(2)}, u32[]{:S(2)}) %collective-permute-start.34) | collective-permute-done | bytes 65568 | tf_op jit(solution)/shard_map/ppermute | solution.py:724
  185.0 2.1 %collective-permute-done.39 = bf16[1,32,1024]{2,1,0:T(8,128)(2,1)S(1)} collective-permute-done((bf16[1,32,1024]{2,1,0:T(8,128)(2,1)S(1)}, bf16[1,32,1024]{2,1,0:T(8,128)(2,1)S(1)}, u32[]{:S(2)}, u32[]{:S(2)}) %collective-permute-start.39) | collective-permute-done | bytes 65568 | tf_op jit(solution)/shard_map/ppermute | solution.py:724
  187.1 1.8 collective-permute-start.40
  188.9 0.8 pad_maximum_fusion.4
  189.7 2.8 %collective-permute-start.36 = (bf16[1,128,1024]{2,1,0:T(8,128)(2,1)S(1)}, bf16[1,128,1024]{2,1,0:T(8,128)(2,1)S(1)}, u32[]{:S(2)}, u32[]{:S(2)}) collective-permute-start(bf16[1,128,1024]{2,1,0:T(8,128)(2,1)S(1)} %get-tuple-element.161), channel_id=1, source_target_pairs={{0,8},{1,9},{2,10},{3,11},{4,12},{5,13},{6,14},{7,15},{8,0},{9,1},... | collective-permute-start | bytes 786440 | tf_op jit(solution)/shard_map/ppermute | solution.py:724
  192.5 0.8 pad_maximum_fusion.5
  193.3 1.3 fusion.11
  194.6 0.7 fusion.15
  195.3 5.8 %collective-permute-start.37 = (bf16[1,128,1024]{2,1,0:T(8,128)(2,1)S(1)}, bf16[1,128,1024]{2,1,0:T(8,128)(2,1)S(1)}, u32[]{:S(2)}, u32[]{:S(2)}) collective-permute-start(bf16[1,128,1024]{2,1,0:T(8,128)(2,1)S(1)} %get-tuple-element.161), channel_id=1, source_target_pairs={{0,2},{1,3},{2,0},{3,1},{4,6},{5,7},{6,4},{7,5},{8,10},{9,11},{10,... | collective-permute-start | bytes 786440 | tf_op jit(solution)/shard_map/ppermute | solution.py:724
  201.2 0.5 collective-permute-start.38
  201.7 3.1 %collective-permute-start.43 = (bf16[1,128,1024]{2,1,0:T(8,128)(2,1)S(1)}, bf16[1,128,1024]{2,1,0:T(8,128)(2,1)S(1)}, u32[]{:S(2)}, u32[]{:S(2)}) collective-permute-start(bf16[1,128,1024]{2,1,0:T(8,128)(2,1)S(1)} %collective-permute-done.41), channel_id=1, source_target_pairs={{0,2},{1,3},{2,0},{3,1},{4,6},{5,7},{6,4},{7,5},{8,10},{9,11},{10,... | collective-permute-start | bytes 786440 | tf_op jit(solution)/shard_map/ppermute | solution.py:724
  204.8 0.7 dynamic_slice.10
  205.4 0.6 fusion.16
  206.1 0.6 copy-done.13
  207.0 4.0 %finish_slopes.1 = (f32[512,512]{1,0:T(8,128)}, f32[512,512]{1,0:T(8,128)}, f32[512,512]{1,0:T(8,128)}, f32[512,512]{1,0:T(8,128)}) custom-call(bf16[128,1024]{1,0:T(8,128)(2,1)} %get-tuple-element.162.refs_0_, bf16[128,1024]{1,0:T(8,128)(2,1)} %bitcast.63, bf16[128,1024]{1,0:T(8,128)(2,1)} %bitcast.65, bf16[128,1024]{1,0:T(8,128)(2,1)} %bitcast.67, ...), custom_call_target="tpu_custom_call" | custom-call | tf_op jit(solution)/shard_map/finish_slopes/pallas_call | solution.py:634
  (131 shorter events, 6.1 us)
Async XLA Ops:
  0.6 8.5 %copy-start = (bf16[512,512]{1,0:T(8,128)(2,1)S(1)}, bf16[512,512]{1,0:T(8,128)(2,1)}, u32[]{:S(2)}) copy-start(bf16[512,512]{1,0:T(8,128)(2,1)} %refs_11_.1) | copy-start | bytes 1572868
  0.7 8.5 %copy-start.1 = (bf16[512,512]{1,0:T(8,128)(2,1)S(1)}, bf16[512,512]{1,0:T(8,128)(2,1)}, u32[]{:S(2)}) copy-start(bf16[512,512]{1,0:T(8,128)(2,1)} %refs_12_.1) | copy-start | bytes 1572868
  0.7 8.5 %copy-start.2 = (bf16[512,512]{1,0:T(8,128)(2,1)S(1)}, bf16[512,512]{1,0:T(8,128)(2,1)}, u32[]{:S(2)}) copy-start(bf16[512,512]{1,0:T(8,128)(2,1)} %refs_13_.1) | copy-start | bytes 1572868
  0.7 4.4 %copy-start.17 = (bf16[64,512]{1,0:T(8,128)(2,1)S(1)}, bf16[64,512]{1,0:T(8,128)(2,1)}, u32[]{:S(2)}) copy-start(bf16[64,512]{1,0:T(8,128)(2,1)} %param.23) | copy-start | bytes 196612
  0.7 4.4 %copy-start.18 = (bf16[512,64]{0,1:T(8,128)(2,1)S(1)}, bf16[512,64]{0,1:T(8,128)(2,1)}, u32[]{:S(2)}) copy-start(bf16[512,64]{0,1:T(8,128)(2,1)} %param.22) | copy-start | bytes 196612
  0.7 8.1 %copy-start.21 = (bf16[512]{0:T(512)(128)(2,1)S(1)}, bf16[512]{0:T(512)(128)(2,1)}, u32[]{:S(2)}) copy-start(bf16[512]{0:T(512)(128)(2,1)} %param.19) | copy-start | bytes 3076
  0.7 8.3 %copy-start.20 = (bf16[512]{0:T(512)(128)(2,1)S(1)}, bf16[512]{0:T(512)(128)(2,1)}, u32[]{:S(2)}) copy-start(bf16[512]{0:T(512)(128)(2,1)} %param.15) | copy-start | bytes 3076
  0.7 8.4 %copy-start.7 = (s32[1,8]{1,0:T(1,128)S(1)}, s32[1,8]{1,0:T(1,128)}, u32[]{:S(2)}) copy-start(s32[1,8]{1,0:T(1,128)} %lengths.1) | copy-start | bytes 100
  3.1 20.2 %collective-permute-start = (bf16[3,256,512]{2,1,0:T(8,128)(2,1)}, bf16[3,256,512]{2,1,0:T(8,128)(2,1)S(1)}, u32[]{:S(2)}, u32[]{:S(2)}) collective-permute-start(bf16[3,256,512]{2,1,0:T(8,128)(2,1)} %get-tuple-element.79), channel_id=1, source_target_pairs={{0,1},{1,0},{2,3},{3,2},{4,5},{5,4},{6,7},{7,6},{8,9},{9,8},{10,11... | collective-permute-start | bytes 2359304 | tf_op jit(solution)/shard_map/ppermute | solution.py:724
  5.1 18.1 %collective-permute-start.1 = (bf16[128,512]{1,0:T(8,128)(2,1)S(1)}, bf16[128,512]{1,0:T(8,128)(2,1)S(1)}, u32[]{:S(2)}, u32[]{:S(2)}) collective-permute-start(bf16[128,512]{1,0:T(8,128)(2,1)S(1)} %pad_maximum_fusion.8), channel_id=1, source_target_pairs={{0,8},{1,9},{2,10},{3,11},{4,12},{5,13},{6,14},{7,15},{8,0},{9,1},... | collective-permute-start | bytes 393224 | tf_op jit(solution)/shard_map/ppermute | solution.py:724
  6.5 16.8 %collective-permute-start.2 = (bf16[128,512]{1,0:T(8,128)(2,1)S(1)}, bf16[128,512]{1,0:T(8,128)(2,1)S(1)}, u32[]{:S(2)}, u32[]{:S(2)}) collective-permute-start(bf16[128,512]{1,0:T(8,128)(2,1)S(1)} %pad_maximum_fusion.8), channel_id=1, source_target_pairs={{0,16},{1,17},{2,18},{3,19},{4,20},{5,21},{6,22},{7,23},{8,24},{9,... | collective-permute-start | bytes 393224 | tf_op jit(solution)/shard_map/ppermute | solution.py:724
  8.8 14.5 %collective-permute-start.3 = (bf16[128,512]{1,0:T(8,128)(2,1)S(1)}, bf16[128,512]{1,0:T(8,128)(2,1)S(1)}, u32[]{:S(2)}, u32[]{:S(2)}) collective-permute-start(bf16[128,512]{1,0:T(8,128)(2,1)S(1)} %pad_maximum_fusion.8), channel_id=1, source_target_pairs={{0,24},{1,25},{2,26},{3,27},{4,28},{5,29},{6,30},{7,31},{8,16},{9,... | collective-permute-start | bytes 393224 | tf_op jit(solution)/shard_map/ppermute | solution.py:724
  8.8 14.4 %collective-permute-start.4 = (bf16[512]{0:T(512)(128)(2,1)S(1)}, bf16[512]{0:T(512)(128)(2,1)S(1)}, u32[]{:S(2)}, u32[]{:S(2)}) collective-permute-start(bf16[512]{0:T(512)(128)(2,1)S(1)} %copy-done.21), channel_id=1, source_target_pairs={{0,1},{1,0},{2,3},{3,2},{4,5},{5,4},{6,7},{7,6},{8,9},{9,8},{10,11... | collective-permute-start | bytes 3080 | tf_op jit(solution)/shard_map/ppermute | solution.py:724
  9.1 63.6 %copy-start.5 = (s32[3]{0:T(128)}, s32[3]{0:T(128)S(1)}, u32[]{:S(2)}) copy-start(s32[3]{0:T(128)S(1)} %pad_add_fusion.refs_7_.refs_6_.refs_8_.scalars) | copy-start | bytes 40
  9.2 20.1 %copy-start.6 = (f32[1,512]{1,0:T(1,128)}, f32[1,512]{1,0:T(1,128)S(1)}, u32[]{:S(2)}) copy-start(f32[1,512]{1,0:T(1,128)S(1)} %broadcast_in_dim.27.refs_8_.refs_7_.refs_4_.refs_10_) | copy-start | bytes 6148
  9.2 15.9 %copy-start.23 = (bf16[256,512]{1,0:T(8,128)(2,1)S(1)}, bf16[256,512]{1,0:T(8,128)(2,1)}, u32[]{:S(2)}) copy-start(bf16[256,512]{1,0:T(8,128)(2,1)} %get-tuple-element.87) | copy-start | bytes 786436
  23.3 4.7 %collective-permute-start.5 = (bf16[3,256,512]{2,1,0:T(8,128)(2,1)S(1)}, bf16[3,256,512]{2,1,0:T(8,128)(2,1)}, u32[]{:S(2)}, u32[]{:S(2)}) collective-permute-start(bf16[3,256,512]{2,1,0:T(8,128)(2,1)S(1)} %collective-permute-done), channel_id=1, source_target_pairs={{0,2},{1,3},{2,0},{3,1},{4,6},{5,7},{6,4},{7,5},{8,10},{9,11},{10,... | collective-permute-start | bytes 2359304 | tf_op jit(solution)/shard_map/ppermute | solution.py:724
  25.1 17.0 %collective-permute-start.6 = (bf16[256,512]{1,0:T(8,128)(2,1)S(1)}, bf16[256,512]{1,0:T(8,128)(2,1)S(1)}, u32[]{:S(2)}, u32[]{:S(2)}) collective-permute-start(bf16[256,512]{1,0:T(8,128)(2,1)S(1)} %copy-done.23), channel_id=1, source_target_pairs={{0,1},{1,0},{2,3},{3,2},{4,5},{5,4},{6,7},{7,6},{8,9},{9,8},{10,11... | collective-permute-start | bytes 786440 | tf_op jit(solution)/shard_map/ppermute | solution.py:724
  26.6 16.3 %collective-permute-start.8 = (bf16[4,128,512]{2,1,0:T(8,128)(2,1)S(1)}, bf16[4,128,512]{2,1,0:T(8,128)(2,1)S(1)}, u32[]{:S(2)}, u32[]{:S(2)}) collective-permute-start(bf16[4,128,512]{2,1,0:T(8,128)(2,1)S(1)} %pad_maximum_fusion.2.refs_8_), channel_id=1, source_target_pairs={{0,4},{1,5},{2,6},{3,7},{4,0},{5,1},{6,2},{7,3},{8,12},{9,13},{10,... | collective-permute-start | bytes 1572872 | tf_op jit(solution)/shard_map/ppermute | solution.py:724
  29.3 14.0 %copy-start.22 = (bf16[512]{0:T(512)(128)(2,1)S(1)}, bf16[512]{0:T(512)(128)(2,1)}, u32[]{:S(2)}) copy-start(bf16[512]{0:T(512)(128)(2,1)} %param.21) | copy-start | bytes 3076
  42.1 3.4 %copy-start.3 = (bf16[512,512]{1,0:T(8,128)(2,1)S(1)}, bf16[512,512]{1,0:T(8,128)(2,1)}, u32[]{:S(2)}) copy-start(bf16[512,512]{1,0:T(8,128)(2,1)} %refs_0_.1) | copy-start | bytes 1572868
  42.1 2.8 %collective-permute-start.7 = (bf16[256,512]{1,0:T(8,128)(2,1)S(1)}, bf16[256,512]{1,0:T(8,128)(2,1)S(1)}, u32[]{:S(2)}, u32[]{:S(2)}) collective-permute-start(bf16[256,512]{1,0:T(8,128)(2,1)S(1)} %collective-permute-done.6), channel_id=1, source_target_pairs={{0,2},{1,3},{2,0},{3,1},{4,6},{5,7},{6,4},{7,5},{8,10},{9,11},{10,... | collective-permute-start | bytes 786440 | tf_op jit(solution)/shard_map/ppermute | solution.py:724
  42.8 2.2 %collective-permute-start.9 = (bf16[4,128,512]{2,1,0:T(8,128)(2,1)S(1)}, bf16[4,128,512]{2,1,0:T(8,128)(2,1)S(1)}, u32[]{:S(2)}, u32[]{:S(2)}) collective-permute-start(bf16[4,128,512]{2,1,0:T(8,128)(2,1)S(1)} %pad_maximum_fusion.2.refs_8_), channel_id=1, source_target_pairs={{0,2},{1,3},{2,0},{3,1},{4,6},{5,7},{6,4},{7,5},{8,10},{9,11},{10,... | collective-permute-start | bytes 1572872 | tf_op jit(solution)/shard_map/ppermute | solution.py:724
  42.9 2.6 %collective-permute-start.10 = (bf16[4,128,512]{2,1,0:T(8,128)(2,1)S(1)}, bf16[4,128,512]{2,1,0:T(8,128)(2,1)S(1)}, u32[]{:S(2)}, u32[]{:S(2)}) collective-permute-start(bf16[4,128,512]{2,1,0:T(8,128)(2,1)S(1)} %collective-permute-done.8.refs_9_), channel_id=1, source_target_pairs={{0,2},{1,3},{2,0},{3,1},{4,6},{5,7},{6,4},{7,5},{8,10},{9,11},{10,... | collective-permute-start | bytes 1572872 | tf_op jit(solution)/shard_map/ppermute | solution.py:724
  43.3 25.8 %collective-permute-start.11 = (bf16[4,128,512]{2,1,0:T(8,128)(2,1)S(1)}, bf16[4,128,512]{2,1,0:T(8,128)(2,1)S(1)}, u32[]{:S(2)}, u32[]{:S(2)}) collective-permute-start(bf16[4,128,512]{2,1,0:T(8,128)(2,1)S(1)} %pad_maximum_fusion.2.refs_8_), channel_id=1, source_target_pairs={{0,5},{1,4},{2,7},{3,6},{4,1},{5,0},{6,3},{7,2},{8,13},{9,12},{10,... | collective-permute-start | bytes 1572872 | tf_op jit(solution)/shard_map/ppermute | solution.py:724
  44.7 24.5 %collective-permute-start.12 = (bf16[4,128,512]{2,1,0:T(8,128)(2,1)S(1)}, bf16[4,128,512]{2,1,0:T(8,128)(2,1)S(1)}, u32[]{:S(2)}, u32[]{:S(2)}) collective-permute-start(bf16[4,128,512]{2,1,0:T(8,128)(2,1)S(1)} %pad_maximum_fusion.2.refs_8_), channel_id=1, source_target_pairs={{0,1},{1,0},{2,3},{3,2},{4,5},{5,4},{6,7},{7,6},{8,9},{9,8},{10,11... | collective-permute-start | bytes 1572872 | tf_op jit(solution)/shard_map/ppermute | solution.py:724
  45.0 24.1 %copy-start.4 = (bf16[512,512]{1,0:T(8,128)(2,1)}, bf16[512,512]{1,0:T(8,128)(2,1)S(1)}, u32[]{:S(2)}) copy-start(bf16[512,512]{1,0:T(8,128)(2,1)S(1)} %pad_maximum_fusion.1.refs_5_.refs_6_) | copy-start | bytes 1572868
  69.2 2.0 collective-permute-start.13
  69.6 3.0 %collective-permute-start.14 = (bf16[4,128,512]{2,1,0:T(8,128)(2,1)S(1)}, bf16[4,128,512]{2,1,0:T(8,128)(2,1)S(1)}, u32[]{:S(2)}, u32[]{:S(2)}) collective-permute-start(bf16[4,128,512]{2,1,0:T(8,128)(2,1)S(1)} %collective-permute-done.11.refs_10_), channel_id=1, source_target_pairs={{0,2},{1,3},{2,0},{3,1},{4,6},{5,7},{6,4},{7,5},{8,10},{9,11},{10,... | collective-permute-start | bytes 1572872 | tf_op jit(solution)/shard_map/ppermute | solution.py:724
  69.7 28.8 %collective-permute-start.16 = (bf16[8,128,512]{2,1,0:T(8,128)(2,1)}, bf16[8,128,512]{2,1,0:T(8,128)(2,1)S(1)}, u32[]{:S(2)}, u32[]{:S(2)}) collective-permute-start(bf16[8,128,512]{2,1,0:T(8,128)(2,1)} %get-tuple-element.107), channel_id=1, source_target_pairs={{0,2},{1,3},{2,0},{3,1},{4,6},{5,7},{6,4},{7,5},{8,10},{9,11},{10,... | collective-permute-start | bytes 3145736 | tf_op jit(solution)/shard_map/ppermute | solution.py:724
  72.7 25.9 %copy-start.8 = (bf16[8,128,512]{2,1,0:T(8,128)(2,1)S(1)}, bf16[8,128,512]{2,1,0:T(8,128)(2,1)}, u32[]{:S(2)}) copy-start(bf16[8,128,512]{2,1,0:T(8,128)(2,1)} %get-tuple-element.106) | copy-start | bytes 3145732
  98.1 3.0 %copy-start.10 = (bf16[8,128,512]{2,1,0:T(8,128)(2,1)S(1)}, bf16[8,128,512]{2,1,0:T(8,128)(2,1)}, u32[]{:S(2)}) copy-start(bf16[8,128,512]{2,1,0:T(8,128)(2,1)} %get-tuple-element.104) | copy-start | bytes 3145732
  98.1 2.9 %collective-permute-start.15 = (bf16[8,128,512]{2,1,0:T(8,128)(2,1)}, bf16[8,128,512]{2,1,0:T(8,128)(2,1)S(1)}, u32[]{:S(2)}, u32[]{:S(2)}) collective-permute-start(bf16[8,128,512]{2,1,0:T(8,128)(2,1)} %get-tuple-element.105), channel_id=1, source_target_pairs={{0,2},{1,3},{2,0},{3,1},{4,6},{5,7},{6,4},{7,5},{8,10},{9,11},{10,... | collective-permute-start | bytes 3145736 | tf_op jit(solution)/shard_map/ppermute | solution.py:724
  98.6 2.8 %copy-start.9 = (bf16[8,128,512]{2,1,0:T(8,128)(2,1)}, bf16[8,128,512]{2,1,0:T(8,128)(2,1)S(1)}, u32[]{:S(2)}) copy-start(bf16[8,128,512]{2,1,0:T(8,128)(2,1)S(1)} %collective-permute-done.16) | copy-start | bytes 3145732
  98.7 28.0 %collective-permute-start.18 = (bf16[4,128,512]{2,1,0:T(8,128)(2,1)S(1)}, bf16[4,128,512]{2,1,0:T(8,128)(2,1)}, u32[]{:S(2)}, u32[]{:S(2)}) collective-permute-start(bf16[4,128,512]{2,1,0:T(8,128)(2,1)S(1)} %add_convert_fusion.1), channel_id=1, source_target_pairs={{0,4},{1,5},{2,6},{3,7},{4,0},{5,1},{6,2},{7,3},{8,12},{9,13},{10,... | collective-permute-start | bytes 1572872 | tf_op jit(solution)/shard_map/ppermute | solution.py:724
  101.4 25.3 %collective-permute-start.17 = (bf16[4,128,512]{2,1,0:T(8,128)(2,1)S(1)}, bf16[4,128,512]{2,1,0:T(8,128)(2,1)}, u32[]{:S(2)}, u32[]{:S(2)}) collective-permute-start(bf16[4,128,512]{2,1,0:T(8,128)(2,1)S(1)} %get-tuple-element.149), channel_id=1, source_target_pairs={{0,1},{1,0},{2,3},{3,2},{4,5},{5,4},{6,7},{7,6},{8,9},{9,8},{10,11... | collective-permute-start | bytes 1572872 | tf_op jit(solution)/shard_map/ppermute | solution.py:724
  102.7 24.0 %collective-permute-start.19 = (bf16[4,128,512]{2,1,0:T(8,128)(2,1)S(1)}, bf16[4,128,512]{2,1,0:T(8,128)(2,1)}, u32[]{:S(2)}, u32[]{:S(2)}) collective-permute-start(bf16[4,128,512]{2,1,0:T(8,128)(2,1)S(1)} %get-tuple-element.148), channel_id=1, source_target_pairs={{0,5},{1,4},{2,7},{3,6},{4,1},{5,0},{6,3},{7,2},{8,13},{9,12},{10,... | collective-permute-start | bytes 1572872 | tf_op jit(solution)/shard_map/ppermute | solution.py:724
  103.7 24.3 %copy-start.19 = (f32[8,512]{1,0:T(8,128)S(1)}, f32[8,512]{1,0:T(8,128)}, u32[]{:S(2)}) copy-start(f32[8,512]{1,0:T(8,128)} %get-tuple-element.131) | copy-start | bytes 49156
  126.7 8.3 %collective-permute-start.20 = (bf16[2,256,1024]{2,1,0:T(8,128)(2,1)}, bf16[2,256,1024]{2,1,0:T(8,128)(2,1)}, u32[]{:S(2)}, u32[]{:S(2)}) collective-permute-start(bf16[2,256,1024]{2,1,0:T(8,128)(2,1)} %get-tuple-element.122), channel_id=1, source_target_pairs={{0,2},{1,3},{2,0},{3,1},{4,6},{5,7},{6,4},{7,5},{8,10},{9,11},{10,... | collective-permute-start | bytes 3145736 | tf_op jit(solution)/shard_map/ppermute | solution.py:724
  127.9 7.1 %collective-permute-start.21 = (bf16[2,256,1024]{2,1,0:T(8,128)(2,1)}, bf16[2,256,1024]{2,1,0:T(8,128)(2,1)}, u32[]{:S(2)}, u32[]{:S(2)}) collective-permute-start(bf16[2,256,1024]{2,1,0:T(8,128)(2,1)} %get-tuple-element.124), channel_id=1, source_target_pairs={{0,2},{1,3},{2,0},{3,1},{4,6},{5,7},{6,4},{7,5},{8,10},{9,11},{10,... | collective-permute-start | bytes 3145736 | tf_op jit(solution)/shard_map/ppermute | solution.py:724
  131.4 22.2 %collective-permute-start.24 = (bf16[128,512]{1,0:T(8,128)(2,1)}, bf16[128,512]{1,0:T(8,128)(2,1)S(1)}, u32[]{:S(2)}, u32[]{:S(2)}) collective-permute-start(bf16[128,512]{1,0:T(8,128)(2,1)} %get-tuple-element.147), channel_id=1, source_target_pairs={{0,8},{1,9},{2,10},{3,11},{4,12},{5,13},{6,14},{7,15},{8,0},{9,1},... | collective-permute-start | bytes 393224 | tf_op jit(solution)/shard_map/ppermute | solution.py:724
  131.8 21.8 %collective-permute-start.25 = (bf16[128,512]{1,0:T(8,128)(2,1)}, bf16[128,512]{1,0:T(8,128)(2,1)S(1)}, u32[]{:S(2)}, u32[]{:S(2)}) collective-permute-start(bf16[128,512]{1,0:T(8,128)(2,1)} %get-tuple-element.146), channel_id=1, source_target_pairs={{0,16},{1,17},{2,18},{3,19},{4,20},{5,21},{6,22},{7,23},{8,24},{9,... | collective-permute-start | bytes 393224 | tf_op jit(solution)/shard_map/ppermute | solution.py:724
  135.0 18.6 %collective-permute-start.26 = (bf16[128,512]{1,0:T(8,128)(2,1)}, bf16[128,512]{1,0:T(8,128)(2,1)S(1)}, u32[]{:S(2)}, u32[]{:S(2)}) collective-permute-start(bf16[128,512]{1,0:T(8,128)(2,1)} %get-tuple-element.145), channel_id=1, source_target_pairs={{0,24},{1,25},{2,26},{3,27},{4,28},{5,29},{6,30},{7,31},{8,16},{9,... | collective-permute-start | bytes 393224 | tf_op jit(solution)/shard_map/ppermute | solution.py:724
  137.6 16.0 %collective-permute-start.22 = (bf16[1,256,1024]{2,1,0:T(8,128)(2,1)}, bf16[1,256,1024]{2,1,0:T(8,128)(2,1)}, u32[]{:S(2)}, u32[]{:S(2)}) collective-permute-start(bf16[1,256,1024]{2,1,0:T(8,128)(2,1)} %get-tuple-element.125), channel_id=1, source_target_pairs={{0,1},{1,0},{2,3},{3,2},{4,5},{5,4},{6,7},{7,6},{8,9},{9,8},{10,11... | collective-permute-start | bytes 1572872 | tf_op jit(solution)/shard_map/ppermute | solution.py:724
  138.2 15.5 %collective-permute-start.23 = (bf16[2,128,1024]{2,1,0:T(8,128)(2,1)}, bf16[2,128,1024]{2,1,0:T(8,128)(2,1)}, u32[]{:S(2)}, u32[]{:S(2)}) collective-permute-start(bf16[2,128,1024]{2,1,0:T(8,128)(2,1)} %get-tuple-element.126), channel_id=1, source_target_pairs={{0,4},{1,5},{2,6},{3,7},{4,0},{5,1},{6,2},{7,3},{8,12},{9,13},{10,... | collective-permute-start | bytes 1572872 | tf_op jit(solution)/shard_map/ppermute | solution.py:724
  153.7 4.4 %collective-permute-start.27 = (bf16[1,16,1024]{2,1,0:T(8,128)(2,1)S(1)}, bf16[1,16,1024]{2,1,0:T(8,128)(2,1)S(1)}, u32[]{:S(2)}, u32[]{:S(2)}) collective-permute-start(bf16[1,16,1024]{2,1,0:T(8,128)(2,1)S(1)} %pad.4), channel_id=1, source_target_pairs={{0,2},{1,3},{2,0},{3,1},{4,6},{5,7},{6,4},{7,5},{8,10},{9,11},{10,... | collective-permute-start | bytes 98312 | tf_op jit(solution)/shard_map/ppermute | solution.py:724
  156.7 8.0 %collective-permute-start.31 = (bf16[1,128,1024]{2,1,0:T(8,128)(2,1)S(1)}, bf16[1,128,1024]{2,1,0:T(8,128)(2,1)S(1)}, u32[]{:S(2)}, u32[]{:S(2)}) collective-permute-start(bf16[1,128,1024]{2,1,0:T(8,128)(2,1)S(1)} %add_convert_fusion.3), channel_id=1, source_target_pairs={{0,8},{1,9},{2,10},{3,11},{4,12},{5,13},{6,14},{7,15},{8,0},{9,1},... | collective-permute-start | bytes 786440 | tf_op jit(solution)/shard_map/ppermute | solution.py:724
  158.2 8.4 %collective-permute-start.28 = (bf16[1,144,1024]{2,1,0:T(8,128)(2,1)S(1)}, bf16[1,144,1024]{2,1,0:T(8,128)(2,1)S(1)}, u32[]{:S(2)}, u32[]{:S(2)}) collective-permute-start(bf16[1,144,1024]{2,1,0:T(8,128)(2,1)S(1)} %pad_maximum_fusion.3), channel_id=1, source_target_pairs={{0,1},{1,0},{2,3},{3,2},{4,5},{5,4},{6,7},{7,6},{8,9},{9,8},{10,11... | collective-permute-start | bytes 884744 | tf_op jit(solution)/shard_map/ppermute | solution.py:724
  165.8 4.3 %collective-permute-start.32 = (bf16[1,64,1024]{2,1,0:T(8,128)(2,1)S(1)}, bf16[1,64,1024]{2,1,0:T(8,128)(2,1)S(1)}, u32[]{:S(2)}, u32[]{:S(2)}) collective-permute-start(bf16[1,64,1024]{2,1,0:T(8,128)(2,1)S(1)} %add_convert_fusion.8), channel_id=1, source_target_pairs={{0,4},{1,5},{2,6},{3,7},{4,0},{5,1},{6,2},{7,3},{8,12},{9,13},{10,... | collective-permute-start | bytes 393224 | tf_op jit(solution)/shard_map/ppermute | solution.py:724
  167.7 6.0 %collective-permute-start.29 = (bf16[1,80,1024]{2,1,0:T(8,128)(2,1)S(1)}, bf16[1,80,1024]{2,1,0:T(8,128)(2,1)S(1)}, u32[]{:S(2)}, u32[]{:S(2)}) collective-permute-start(bf16[1,80,1024]{2,1,0:T(8,128)(2,1)S(1)} %pad_maximum_fusion.6), channel_id=1, source_target_pairs={{0,8},{1,9},{2,10},{3,11},{4,12},{5,13},{6,14},{7,15},{8,0},{9,1},... | collective-permute-start | bytes 491528 | tf_op jit(solution)/shard_map/ppermute | solution.py:724
  171.1 5.9 %collective-permute-start.33 = (bf16[1,32,1024]{2,1,0:T(8,128)(2,1)S(1)}, bf16[1,32,1024]{2,1,0:T(8,128)(2,1)S(1)}, u32[]{:S(2)}, u32[]{:S(2)}) collective-permute-start(bf16[1,32,1024]{2,1,0:T(8,128)(2,1)S(1)} %add_convert_fusion.12), channel_id=1, source_target_pairs={{0,16},{1,17},{2,18},{3,19},{4,20},{5,21},{6,22},{7,23},{8,24},{9,... | collective-permute-start | bytes 196616 | tf_op jit(solution)/shard_map/ppermute | solution.py:724
  174.7 5.7 %collective-permute-start.30 = (bf16[1,48,1024]{2,1,0:T(8,128)(2,1)S(1)}, bf16[1,48,1024]{2,1,0:T(8,128)(2,1)S(1)}, u32[]{:S(2)}, u32[]{:S(2)}) collective-permute-start(bf16[1,48,1024]{2,1,0:T(8,128)(2,1)S(1)} %pad_maximum_fusion.10), channel_id=1, source_target_pairs={{0,16},{1,17},{2,18},{3,19},{4,20},{5,21},{6,22},{7,23},{8,24},{9,... | collective-permute-start | bytes 294920 | tf_op jit(solution)/shard_map/ppermute | solution.py:724
  177.9 6.7 %collective-permute-start.34 = (bf16[1,32,1024]{2,1,0:T(8,128)(2,1)S(1)}, bf16[1,32,1024]{2,1,0:T(8,128)(2,1)S(1)}, u32[]{:S(2)}, u32[]{:S(2)}) collective-permute-start(bf16[1,32,1024]{2,1,0:T(8,128)(2,1)S(1)} %add_convert_fusion.11), channel_id=1, source_target_pairs={{0,16},{1,17},{2,18},{3,19},{4,20},{5,21},{6,22},{7,23},{8,24},{9,... | collective-permute-start | bytes 196616 | tf_op jit(solution)/shard_map/ppermute | solution.py:724
  181.4 5.7 %collective-permute-start.39 = (bf16[1,32,1024]{2,1,0:T(8,128)(2,1)S(1)}, bf16[1,32,1024]{2,1,0:T(8,128)(2,1)S(1)}, u32[]{:S(2)}, u32[]{:S(2)}) collective-permute-start(bf16[1,32,1024]{2,1,0:T(8,128)(2,1)S(1)} %add_convert_fusion.10), channel_id=1, source_target_pairs={{0,16},{1,17},{2,18},{3,19},{4,20},{5,21},{6,22},{7,23},{8,24},{9,... | collective-permute-start | bytes 196616 | tf_op jit(solution)/shard_map/ppermute | solution.py:724
  184.6 4.3 %collective-permute-start.35 = (bf16[1,80,1024]{2,1,0:T(8,128)(2,1)S(1)}, bf16[1,80,1024]{2,1,0:T(8,128)(2,1)S(1)}, u32[]{:S(2)}, u32[]{:S(2)}) collective-permute-start(bf16[1,80,1024]{2,1,0:T(8,128)(2,1)S(1)} %pad_maximum_fusion.7), channel_id=1, source_target_pairs={{0,4},{1,5},{2,6},{3,7},{4,0},{5,1},{6,2},{7,3},{8,12},{9,13},{10,... | collective-permute-start | bytes 491528 | tf_op jit(solution)/shard_map/ppermute | solution.py:724
  187.1 5.4 %collective-permute-start.40 = (bf16[1,64,1024]{2,1,0:T(8,128)(2,1)S(1)}, bf16[1,64,1024]{2,1,0:T(8,128)(2,1)S(1)}, u32[]{:S(2)}, u32[]{:S(2)}) collective-permute-start(bf16[1,64,1024]{2,1,0:T(8,128)(2,1)S(1)} %pad_maximum_fusion.9), channel_id=1, source_target_pairs={{0,8},{1,9},{2,10},{3,11},{4,12},{5,13},{6,14},{7,15},{8,0},{9,1},... | collective-permute-start | bytes 393224 | tf_op jit(solution)/shard_map/ppermute | solution.py:724
  189.7 11.5 %collective-permute-start.36 = (bf16[1,128,1024]{2,1,0:T(8,128)(2,1)S(1)}, bf16[1,128,1024]{2,1,0:T(8,128)(2,1)S(1)}, u32[]{:S(2)}, u32[]{:S(2)}) collective-permute-start(bf16[1,128,1024]{2,1,0:T(8,128)(2,1)S(1)} %get-tuple-element.161), channel_id=1, source_target_pairs={{0,8},{1,9},{2,10},{3,11},{4,12},{5,13},{6,14},{7,15},{8,0},{9,1},... | collective-permute-start | bytes 786440 | tf_op jit(solution)/shard_map/ppermute | solution.py:724
  193.3 8.4 %collective-permute-start.41 = (bf16[1,128,1024]{2,1,0:T(8,128)(2,1)S(1)}, bf16[1,128,1024]{2,1,0:T(8,128)(2,1)S(1)}, u32[]{:S(2)}, u32[]{:S(2)}) collective-permute-start(bf16[1,128,1024]{2,1,0:T(8,128)(2,1)S(1)} %get-tuple-element.159), channel_id=1, source_target_pairs={{0,4},{1,5},{2,6},{3,7},{4,0},{5,1},{6,2},{7,3},{8,12},{9,13},{10,... | collective-permute-start | bytes 786440 | tf_op jit(solution)/shard_map/ppermute | solution.py:724
  195.3 10.7 %collective-permute-start.37 = (bf16[1,128,1024]{2,1,0:T(8,128)(2,1)S(1)}, bf16[1,128,1024]{2,1,0:T(8,128)(2,1)S(1)}, u32[]{:S(2)}, u32[]{:S(2)}) collective-permute-start(bf16[1,128,1024]{2,1,0:T(8,128)(2,1)S(1)} %get-tuple-element.161), channel_id=1, source_target_pairs={{0,2},{1,3},{2,0},{3,1},{4,6},{5,7},{6,4},{7,5},{8,10},{9,11},{10,... | collective-permute-start | bytes 786440 | tf_op jit(solution)/shard_map/ppermute | solution.py:724
  201.2 4.9 %collective-permute-start.42 = (bf16[1,128,1024]{2,1,0:T(8,128)(2,1)S(1)}, bf16[1,128,1024]{2,1,0:T(8,128)(2,1)S(1)}, u32[]{:S(2)}, u32[]{:S(2)}) collective-permute-start(bf16[1,128,1024]{2,1,0:T(8,128)(2,1)S(1)} %get-tuple-element.159), channel_id=1, source_target_pairs={{0,2},{1,3},{2,0},{3,1},{4,6},{5,7},{6,4},{7,5},{8,10},{9,11},{10,... | collective-permute-start | bytes 786440 | tf_op jit(solution)/shard_map/ppermute | solution.py:724
  201.2 4.9 %copy-start.11 = (bf16[1,128,1024]{2,1,0:T(8,128)(2,1)}, bf16[1,128,1024]{2,1,0:T(8,128)(2,1)S(1)}, u32[]{:S(2)}) copy-start(bf16[1,128,1024]{2,1,0:T(8,128)(2,1)S(1)} %collective-permute-done.36) | copy-start | bytes 786436
  201.2 4.8 %collective-permute-start.38 = (bf16[1,128,1024]{2,1,0:T(8,128)(2,1)S(1)}, bf16[1,128,1024]{2,1,0:T(8,128)(2,1)S(1)}, u32[]{:S(2)}, u32[]{:S(2)}) collective-permute-start(bf16[1,128,1024]{2,1,0:T(8,128)(2,1)S(1)} %collective-permute-done.36), channel_id=1, source_target_pairs={{0,2},{1,3},{2,0},{3,1},{4,6},{5,7},{6,4},{7,5},{8,10},{9,11},{10,... | collective-permute-start | bytes 786440 | tf_op jit(solution)/shard_map/ppermute | solution.py:724
  201.7 4.4 %copy-start.12 = (bf16[1,128,1024]{2,1,0:T(8,128)(2,1)}, bf16[1,128,1024]{2,1,0:T(8,128)(2,1)S(1)}, u32[]{:S(2)}) copy-start(bf16[1,128,1024]{2,1,0:T(8,128)(2,1)S(1)} %collective-permute-done.41) | copy-start | bytes 786436
  201.7 4.4 %collective-permute-start.43 = (bf16[1,128,1024]{2,1,0:T(8,128)(2,1)S(1)}, bf16[1,128,1024]{2,1,0:T(8,128)(2,1)S(1)}, u32[]{:S(2)}, u32[]{:S(2)}) collective-permute-start(bf16[1,128,1024]{2,1,0:T(8,128)(2,1)S(1)} %collective-permute-done.41), channel_id=1, source_target_pairs={{0,2},{1,3},{2,0},{3,1},{4,6},{5,7},{6,4},{7,5},{8,10},{9,11},{10,... | collective-permute-start | bytes 786440 | tf_op jit(solution)/shard_map/ppermute | solution.py:724
  (4 other events, 3.3 us)

commit v5 on v4

--- a/solution.py
+++ b/solution.py
@@ -341,6 +341,7 @@
             out[there : there + 2, :half, :] = upper_acc[:, cols].T.astype(BF16).reshape(2, half, width)
             out[there : there + 2, half:, :] = lower_acc[:, cols].T.astype(BF16).reshape(2, half, width)
         if stage == 1:
+            slope_ref[0:1, :] = jnp.sum(slope_ref[...], 0, keepdims=True)
             tall = output_acc.shape[0] // PLACES
             for index, output in enumerate(outputs_ref):
                 for place in range(PLACES):
@@ -506,6 +507,7 @@
     @pl.when((phase == 1) & (block == blocks - 1))
     def _():
         for index in range(sets):
+            bias_out[index, 0:1, :] = jnp.sum(bias_out[index], 0, keepdims=True)
             put_blocks(slopes_acc.at[index, 0], [out.at[index] for out in first_out], scalars[1], 0)
             put_blocks(slopes_acc.at[index, 1], [out.at[index] for out in first_out], scalars[1], channels)
             put_blocks(slopes_acc.at[index, 2], [out.at[index] for out in second_out], scalars[2], 0)
@@ -554,7 +556,7 @@
             pltpu.VMEM((sets, 16, channels), F32),
             pltpu.VMEM((sets, 8, channels), F32),
         ],
-        compiler_params=pltpu.CompilerParams(vmem_limit_bytes=VMEM_BYTES, dimension_semantics=("arbitrary", "arbitrary")),
+        compiler_params=pltpu.CompilerParams(vmem_limit_bytes=50 * 1024 * 1024, dimension_semantics=("arbitrary", "arbitrary")),
         cost_estimate=pl.CostEstimate(flops=2 * rows * width * 4 * channels * sets, bytes_accessed=rows * channels * 12 * sets, transcendentals=0),
         name="mixer_backward",
     )(in_hbm(mixed), in_hbm(normed), lengths, scalars, *[in_hbm(item) if item.shape[0] == rows else item for one in per_set for item in one])
@@ -565,7 +567,7 @@
     x_ref, mixed_ref, gain_ref, *refs = refs
     factors, refs = refs[: 4 * sets], refs[4 * sets :]
     weights, refs = refs[: 3 * sets], refs[3 * sets :]
-    out_ref, slope_ref, out_s = refs
+    dense_ref, bias_ref, scalars, out_ref, small_ref, slope_ref, out_s = refs
 
     @pl.when(pl.program_id(0) == 0)
     def _():
@@ -588,10 +590,15 @@
 
     @pl.when(pl.program_id(0) == pl.num_programs(0) - 1)
     def _():
-        slope_ref[0:1, :] = jnp.sum(slope_ref[...], 0, keepdims=True)
-
-
-def input_backward(x_rows, mixed, gain, factors, weights):
+        gains = jnp.concatenate([jnp.sum(slope_ref[...], 0, keepdims=True), dense_ref[0:1, :]], 1)
+        low = jnp.where(scalars[3] == 0, bias_ref[0, 0:1, :], bias_ref[1, 0:1, :])
+        high = jnp.where(scalars[3] == 0, bias_ref[1, 0:1, :], bias_ref[0, 0:1, :])
+        biases = jnp.concatenate([low, high], 1)
+        rest = jnp.zeros((small_ref.shape[0] - 2, biases.shape[1]), F32)
+        small_ref[...] = jnp.concatenate([gains, biases, rest], 0).astype(BF16)
+
+
+def input_backward(x_rows, mixed, gain, factors, weights, dense_part, bias_parts, scalars):
     rows, width = x_rows.shape
     sets = len(factors) // 4
     channels = weights[0].shape[1]
@@ -603,14 +610,15 @@
         in_specs=[pl.BlockSpec((BLOCK, width), by_rows)] * 2
         + [pl.BlockSpec((1, width), whole)]
         + [pl.BlockSpec((BLOCK, channels), by_rows)] * (4 * sets)
-        + [pl.BlockSpec((width, channels), whole)] * (3 * sets),
-        out_specs=[pl.BlockSpec((SEGMENTS, STEPS, width), lambda block: (0, block, 0)), pl.BlockSpec((8, width), whole)],
-        out_shape=[hbm((SEGMENTS, rows // SEGMENTS, width), F32), hbm((8, width), F32)],
-        scratch_shapes=[pltpu.VMEM((width // 128, BLOCK, 128), F32)],
+        + [pl.BlockSpec((width, channels), whole)] * (3 * sets)
+        + [pl.BlockSpec((8, width), whole), pl.BlockSpec((sets, 8, channels), lambda block: (0, 0, 0)), pl.BlockSpec(memory_space=pltpu.SMEM)],
+        out_specs=[pl.BlockSpec((SEGMENTS, STEPS, width), lambda block: (0, block, 0)), pl.BlockSpec((16, sets * channels), whole)],
+        out_shape=[hbm((SEGMENTS, rows // SEGMENTS, width), F32), jax.ShapeDtypeStruct((16, sets * channels), BF16)],
+        scratch_shapes=[pltpu.VMEM((8, width), F32), pltpu.VMEM((width // 128, BLOCK, 128), F32)],
         compiler_params=pltpu.CompilerParams(vmem_limit_bytes=44 * 1024 * 1024, dimension_semantics=("arbitrary",)),
         cost_estimate=pl.CostEstimate(flops=2 * rows * width * 3 * channels * sets, bytes_accessed=rows * channels * 8 * sets, transcendentals=0),
         name="input_backward",
-    )(in_hbm(x_rows), in_hbm(mixed), gain, *[in_hbm(f) for f in factors], *weights)
+    )(in_hbm(x_rows), in_hbm(mixed), gain, *[in_hbm(f) for f in factors], *weights, dense_part, bias_parts, scalars)
 
 
 def finish_kernel(channels, count, *refs):
@@ -661,8 +669,9 @@
 
 
 def sum_kernel(*refs):
-    for index in range(len(refs) // 3):
-        left, right, out = refs[2 * index], refs[2 * index + 1], refs[2 * (len(refs) // 3) + index]
+    count = len(refs) // 3
+    for index in range(count):
+        left, right, out = refs[2 * index], refs[2 * index + 1], refs[2 * count + index]
         out[...] = (left[...].astype(F32) + right[...].astype(F32)).astype(BF16)
 
 
@@ -715,9 +724,9 @@
 
     def __init__(self):
         dp = lax.axis_index("dp")
-        core, near, z_near, z_far = dp % 2, dp // 2 % 2, dp // 4 % 2, dp // 8
+        core, near, z_near = dp % 2, dp // 2 % 2, dp // 4 % 2
         self.core = core
-        self.me = [core * 8 + z_near * 4 + near * 2 + z_far, core * 8 + near * 4 + z_near * 2 + z_far]
+        self.me = [core * 8 + z_near * 4 + near * 2, core * 8 + near * 4 + z_near * 2]
 
     def swap(self, values, bits):
         pairs = [(device, device ^ bits) for device in range(32)]
@@ -817,7 +826,7 @@
     paired = (n_dp, n_tensor) == (16, 2)
     hidden = lower_weight.shape[0]
     links = Links() if paired else Plain(n_tensor, own, hidden)
-    scalars = jnp.stack([place * rows] + links.me).astype(jnp.int32)
+    scalars = jnp.stack([place * rows] + links.me + [place if paired else 0]).astype(jnp.int32)
     own_weights = [forget_weight, admit_weight, value_weight, output_weight]
     dense_shard = jnp.concatenate([upper_weight.T, lower_weight], 0)
     if paired:
@@ -898,42 +907,42 @@
         first = [first[0], links.swap(core_sends[0], Links.CORE)]
         second = [second[0], links.swap(core_sends[1], Links.CORE)]
         sets, tall, wide = first[0].shape
-        sends = paired_sums((first, second), ((1, tall, wide), (sets, tall // 2, wide)), ((1, 0, 0), (0, 1, 0)))
-        first = [(sends[0], Links.TENSOR)], part(first, 0, 0)
-        second = [(sends[1], Links.NEAR)], part(second, 0, 1)
+        blocks = ((1, tall, wide), (sets, tall // 2, wide))
+        sums = paired_sums((first, second) * 2, blocks * 2, ((1, 0, 0), (0, 1, 0), (0, 0, 0), (0, 0, 0)))
+        first, second = ([(sums[0], Links.TENSOR)], [sums[2]]), ([(sums[1], Links.NEAR)], [sums[3]])
         factors[0] = after(factors[0], first[0][0][0], second[0][0][0], [values for values, _ in along])
         first, second = links.exchange(*first), links.exchange(*second)
         dense_terms = links.exchange(along, along_kept)
-    input_slope, premix_part = input_backward(x_rows, mixed, premix, factors, weights[0][:3] + weights[1][:3])
-
-    bias_parts = jnp.sum(bias_parts, 1)
+    input_slope, small = input_backward(
+        x_rows, mixed, premix, factors, weights[0][:3] + weights[1][:3], dense_part, bias_parts, scalars
+    )
+
     if paired:
-        bias_parts = jnp.where(place == 0, bias_parts, bias_parts[::-1])
-    small = jnp.concatenate([premix_part[0], jnp.sum(dense_part, 0), bias_parts[0], bias_parts[1]], 0)
-    if paired:
-        small = small.reshape(1, -1, 2 * channels).astype(BF16)
-        filled = small.shape[1]
-        small = jnp.pad(small, ((0, 0), (0, 16 - filled), (0, 0)))
+        small = small[None]
         first, second = hold(first, input_slope), hold(second, input_slope)
         dense_terms = dense_terms[:-3] + after(dense_terms[-3:], input_slope)
         small = after(small, first[-1], second[-1], dense_terms[-3:])
         small = total([small, links.swap(small, Links.CORE)])
 
         def halve_both(first, second, first_bits, second_bits, extra):
-            first = links.halve(first, first_bits)
-            second = links.halve(second, second_bits, extra)
-            second_send = second[0][0][0]
-            first, second = links.exchange(*first), links.exchange(*second)
+            first, first_kept = links.halve(first, first_bits)
+            second, second_kept = links.halve(second, second_bits, extra)
+            second_send = second[0][0]
+            if first_bits == Links.Z_NEAR:
+                first_kept, second_kept = ([lax.optimization_barrier(total(kept))] for kept in (first_kept, second_kept))
+            first, second = links.exchange(first, first_kept), links.exchange(second, second_kept)
             rows_sent = second_send.shape[1] - extra.shape[1]
             extra = total([extra, second[-1][:, rows_sent:]])
             return first, second[:-1] + [second[-1][:, :rows_sent]], extra
 
         first, second, small = halve_both(first, second, Links.Z_NEAR, Links.TENSOR, small)
         first, second, small = halve_both(first, second, Links.NEAR, Links.Z_NEAR, small)
-        first, second, small = halve_both(first, second, Links.Z_FAR, Links.Z_FAR, small)
         first, second = total(first), total(second)
-        first, second = links.grow(first, Links.Z_FAR), links.grow(second, Links.Z_FAR)
         count = first.shape[1]
+        first_got = links.swap(first, Links.Z_FAR)
+        second_got = links.swap(jnp.concatenate([second, small], 1), Links.Z_FAR)
+        first, second = total([first, first_got]), total([second, second_got[:, :count]])
+        small = total([small, second_got[:, count:]])
         got = links.swap(jnp.concatenate([first, small], 1), Links.NEAR)
         first, small = jnp.concatenate([first, got[:, :count]], 1), total([small, got[:, count:]])
         second = links.grow(second, Links.Z_NEAR)
@@ -941,10 +950,10 @@
         first += [links.swap(f, Links.CORE) for f in first]
         second += [links.swap(f, Links.CORE) for f in second]
         first, second = [f[0] for f in first], [f[0] for f in second]
-        small = small[0, :filled].reshape(-1).astype(F32)
+        small = small[0].astype(F32)
         dense_sum = total(dense_terms)
     else:
-        small = lax.psum(small, ("dp", "tensor"))
+        small = lax.psum(small.astype(F32), ("dp", "tensor"))
         dense_sum = links.dense_sums([own_keep, own_send, other_keep, other_send])
         first, second = links.mixer_sums(first), links.mixer_sums(second)
     dense_sum = dense_sum.astype(F32)
@@ -952,9 +961,9 @@
     forget_slope, admit_slope, value_slope, output_slope = finish_slopes(first, second, scalars)
     shard = width // (n_dp * n_tensor)
     at = (lax.axis_index("dp") * n_tensor + place) * shard
-    premix_slope = lax.dynamic_slice(small, (at,), (shard,))
-    dense_slope = lax.dynamic_slice(small, (width + at,), (shard,))
-    bias_slope = lax.dynamic_slice(small, (2 * width + place * own,), (own,))
+    premix_slope = lax.dynamic_slice(small, (0, at), (1, shard))[0]
+    dense_slope = lax.dynamic_slice(small, (0, width + at), (1, shard))[0]
+    bias_slope = lax.dynamic_slice(small, (1, place * own), (1, own))[0]
     return (
         block_out.reshape(rows, width),
         input_slope.reshape(rows, width),

time: 212 us -> 204 us (0.962)
  other arithmetic: 16.8 us -> 6.33 us
  waiting for transfers between devices: 19.1 us -> 27.9 us
  starting transfers between devices: 50.2 us -> 43.3 us
    convert_element_type x15, other arithmetic: 11.5 us -> 2.08 us  [total(): return result.astype(terms[0].dtype)]
    ppermute x44 -> x42, waiting for transfers between devices: 19.1 us -> 27.9 us  [swap(): return lax.ppermute(values, ('dp', 'tensor'), pairs)]
    ppermute x44 -> x42, starting transfers between devices: 50.2 us -> 43.3 us  [swap(): return lax.ppermute(values, ('dp', 'tensor'), pairs)]
    unnamed x49 -> x62, local copies, waits for them, and re-layouts: 1 us -> 3.24 us
  transfers between devices with their start and end apart: 44 -> 42, of which waited for: 11 -> 11; matrix products, arithmetic and copies ran while one was open for 9% -> 4% of each run, Pallas kernels for 54% -> 56%
where the time goes in v5:
time: 204 us
  Pallas kernels  120 us (59%)
  starting transfers between devices  43.3 us (21%)
  waiting for transfers between devices  27.9 us (14%)
  other arithmetic  6.33 us (3%)
  local copies, waits for them, and re-layouts  5.22 us (3%)
    pallas_call x2, Pallas kernels, dense_both(): pl.pallas_call(functools.partial(dense_kernel, stage, sets, len(pieces)),...  49.7 us
    ppermute x42, starting transfers between devices, swap(): return lax.ppermute(values, ('dp', 'tensor'), pairs)  43.3 us
    ppermute x42, waiting for transfers between devices, swap(): return lax.ppermute(values, ('dp', 'tensor'), pairs)  27.9 us
    pallas_call x2, Pallas kernels, mixer_forward(): pl.pallas_call(functools.partial(mixer_kernel, first), grid=(2, blocks),...  26.7 us
    pallas_call x1, Pallas kernels, mixer_backward(): pl.pallas_call(functools.partial(mixer_back_kernel, sets), grid=(2, block...  20.2 us
    pallas_call x1, Pallas kernels, input_backward(): pl.pallas_call(functools.partial(input_kernel, sets), grid=(rows // BLOCK...  13.6 us
  transfers between devices with their start and end apart: 42, of which 11 were waited for; matrix products, arithmetic and copies ran while one was open for 4% of the time, Pallas kernels for 56%

profile of v5, /device:TPU:1, one launch (start us, length us, event | category | flops | bytes accessed | tf_op | source)
XLA Modules:
  0.0 204.1 jit_solution(9616870116829857995)
XLA Ops:
  0.7 2.3 %pack_halves.1 = (bf16[3,256,512]{2,1,0:T(8,128)(2,1)}, bf16[256,512]{1,0:T(8,128)(2,1)}) custom-call(s32[1]{0:T(128)} %bitcast.7.refs_0_, bf16[512,512]{1,0:T(8,128)(2,1)} %refs_11_.1, bf16[512,512]{1,0:T(8,128)(2,1)} %refs_12_.1, bf16[512,512]{1,0:T(8,128)(2,1)} %refs_13_.1, bf16[512,512]{1,0:T(8,128)(2,1)} %refs_0_.1), custom_call_target="tpu_custom_call" | custom-call | tf_op jit(solution)/shard_map/pack_halves/pallas_call | solution.py:709
  3.1 2.0 collective-permute-start
  5.1 1.4 collective-permute-start.1
  6.5 2.3 %collective-permute-start.2 = (bf16[128,512]{1,0:T(8,128)(2,1)S(1)}, bf16[128,512]{1,0:T(8,128)(2,1)}, u32[]{:S(2)}, u32[]{:S(2)}) collective-permute-start(bf16[128,512]{1,0:T(8,128)(2,1)S(1)} %pad_maximum_fusion.9), channel_id=1, source_target_pairs={{0,16},{1,17},{2,18},{3,19},{4,20},{5,21},{6,22},{7,23},{8,24},{9,... | collective-permute-start | bytes 393224 | tf_op jit(solution)/shard_map/ppermute | solution.py:733
  9.2 14.0 %mixer_forward.2 = (bf16[2048,512]{1,0:T(8,128)(2,1)}, bf16[2048,512]{1,0:T(8,128)(2,1)}, bf16[2048,512]{1,0:T(8,128)(2,1)}, bf16[2048,512]{1,0:T(8,128)(2,1)}, ...) custom-call(bf16[8,256,512]{2,1,0:T(8,128)(2,1)} %bitcast.77, f32[1,512]{1,0:T(1,128)S(1)} %bitcast.60, ...), custom_call_target="tpu_custom_call" | custom-call | flops 3221225472 | bytes 16777216 | tf_op jit(solution)/shard_map/mixer_forward/pallas_call | solution.py:243
  23.2 1.9 collective-permute-start.5
  25.1 1.4 collective-permute-start.6
  26.5 1.0 pad_maximum_fusion.2.refs_8_
  27.6 1.3 collective-permute-start.8
  29.1 12.8 %mixer_forward.3 = (bf16[2048,512]{1,0:T(8,128)(2,1)}, bf16[2048,512]{1,0:T(8,128)(2,1)}, bf16[2048,512]{1,0:T(8,128)(2,1)}, bf16[2048,512]{1,0:T(8,128)(2,1)}, f32[8,512]{1,0:T(8,128)}) custom-call(bf16[2048,512]{1,0:T(8,128)(2,1)} %get-tuple-element.80.refs_0_.normed_ref, bf16[512,512]{1,0:T(8,128)(2,1)S(1)} %get-tuple-element.153.refs_1_.refs_14_, ...), custom_call_target="tpu_custom_call" | custom-call | flops 3221225472 | bytes 16777216 | tf_op jit(solution)/shard_map/mixer_forward/pallas_call | solution.py:243
  41.9 0.7 collective-permute-start.7
  42.6 0.4 collective-permute-start.10
  43.3 1.2 collective-permute-start.12
  44.6 0.6 collective-permute-done.10.refs_11_
  45.2 24.0 %dense_first.1 = (bf16[8,128,512]{2,1,0:T(8,128)(2,1)}, bf16[8,128,512]{2,1,0:T(8,128)(2,1)}, bf16[2048,512]{1,0:T(8,128)(2,1)}, bf16[2048,512]{1,0:T(8,128)(2,1...) custom-call(bf16[2048,512]{1,0:T(8,128)(2,1)} %get-tuple-element.79.refs_0_, ...), custom_call_target="tpu_custom_call" | custom-call | flops 12884901888 | bytes 25165824 | tf_op jit(solution)/shard_map/dense_first/pallas_call | solution.py:385
  69.3 0.4 collective-permute-start.13
  69.9 0.4 collective-permute-start.16
  70.2 1.0 collective-permute-done.13.refs_11_
  71.3 1.5 collective-permute-done.14.refs_12_
  72.8 25.6 %dense_second.1 = (bf16[8,128,512]{2,1,0:T(8,128)(2,1)}, bf16[8,128,512]{2,1,0:T(8,128)(2,1)}, bf16[8,256,512]{2,1,0:T(8,128)(2,1)}, bf16[2048,512]{1,0:T(8,128)...) custom-call(bf16[2048,512]{1,0:T(8,128)(2,1)} %get-tuple-element.79.refs_0_, ...), custom_call_target="tpu_custom_call" | custom-call | flops 12884901888 | bytes 25165824 | tf_op jit(solution)/shard_map/dense_second/pallas_call | solution.py:385
  98.4 0.4 collective-permute-start.15
  99.0 1.0 collective-permute-start.18
  100.0 1.4 collective-permute-done.15
  101.7 0.3 collective-permute-start.17
  102.0 1.8 collective-permute-start.19
  103.8 20.2 %mixer_backward.1 = (bf16[2048,512]{1,0:T(8,128)(2,1)}, bf16[2048,512]{1,0:T(8,128)(2,1)}, bf16[2,256,1024]{2,1,0:T(8,128)(2,1)S(1)}, bf16[2,256,1024]{2,1,0:T(8...) custom-call(bf16[2048,512]{1,0:T(8,128)(2,1)} %get-tuple-element.110, ...), custom_call_target="tpu_custom_call" | custom-call | flops 8589934592 | bytes 25165824 | tf_op jit(solution)/shard_map/mixer_backward/pallas_call | solution.py:533
  124.0 1.0 copy-done
  125.0 1.8 collective-permute-done.19
  126.8 1.2 collective-permute-start.20
  128.1 1.0 fusion.10
  129.1 0.4 collective-permute-start.24
  129.5 3.2 %collective-permute-start.25 = (bf16[128,512]{1,0:T(8,128)(2,1)}, bf16[128,512]{1,0:T(8,128)(2,1)S(1)}, u32[]{:S(2)}, u32[]{:S(2)}) collective-permute-start(bf16[128,512]{1,0:T(8,128)(2,1)} %get-tuple-element.148), channel_id=1, source_target_pairs={{0,16},{1,17},{2,18},{3,19},{4,20},{5,21},{6,22},{7,23},{8,24},{9,... | collective-permute-start | bytes 393224 | tf_op jit(solution)/shard_map/ppermute | solution.py:733
  132.7 0.9 copy-done.10
  133.7 0.3 copy-done.11
  134.0 3.7 %paired_sums.1 = (bf16[1,256,1024]{2,1,0:T(8,128)(2,1)}, bf16[2,128,1024]{2,1,0:T(8,128)(2,1)}, bf16[1,256,1024]{2,1,0:T(8,128)(2,1)}, bf16[2,128,1024]{2,1,0:T(8,128)(2,1)}) custom-call(bf16[2,256,1024]{2,1,0:T(8,128)(2,1)} %copy-done, bf16[2,256,1024]{2,1,0:T(8,128)(2,1)} %copy-done.10, bf16[2,256,1024]{2,1,0:T(8,128)(2,1)} %get-tuple-element.125.refs_2_.refs_6_, ...), custom_call_target="tpu_custom_call" | custom-call | tf_op jit(solution)/shard_map/paired_sums/pallas_call | solution.py:680
  137.9 0.6 collective-permute-start.23
  138.5 13.6 %input_backward.1 = (f32[8,256,512]{2,1,0:T(8,128)}, bf16[16,1024]{1,0:T(8,128)(2,1)S(1)}) custom-call(bf16[2048,512]{1,0:T(8,128)(2,1)} %get-tuple-element.87.refs_2_.refs_0_, bf16[2048,512]{1,0:T(8,128)(2,1)} %get-tuple-element.110.mixed_ref.refs_1_, f32[1,512]{1,0:T(1,128)S(1)} %bitcast.61, bf16[2048,512]{1,0:T(8,128)(2,1)} %get-tuple-element.129.refs_3_, ...), custom_call_target="tpu_custom_call" | custom-call | flops 6442450944 | bytes 16777216 | tf_op jit(solution)/shard_map/input_backward/pallas_call | solution.py:607
  152.2 1.8 collective-permute-start.27
  154.5 0.3 collective-permute-done.27
  154.9 1.2 collective-permute-start.28
  156.2 6.2 %collective-permute-done.31 = bf16[1,128,1024]{2,1,0:T(8,128)(2,1)S(1)} collective-permute-done((bf16[1,128,1024]{2,1,0:T(8,128)(2,1)S(1)}, bf16[1,128,1024]{2,1,0:T(8,128)(2,1)S(1)}, u32[]{:S(2)}, u32[]{:S(2)}) %collective-permute-start.31) | collective-permute-done | bytes 262176 | tf_op jit(solution)/shard_map/ppermute | solution.py:733
  162.4 1.0 collective-permute-start.32
  163.5 1.0 collective-permute-start.29
  164.5 2.2 %collective-permute-done.32 = bf16[1,64,1024]{2,1,0:T(8,128)(2,1)S(1)} collective-permute-done((bf16[1,64,1024]{2,1,0:T(8,128)(2,1)S(1)}, bf16[1,64,1024]{2,1,0:T(8,128)(2,1)S(1)}, u32[]{:S(2)}, u32[]{:S(2)}) %collective-permute-start.32) | collective-permute-done | bytes 131104 | tf_op jit(solution)/shard_map/ppermute | solution.py:733
  166.8 2.6 %collective-permute-start.33 = (bf16[1,64,1024]{2,1,0:T(8,128)(2,1)S(1)}, bf16[1,64,1024]{2,1,0:T(8,128)(2,1)S(1)}, u32[]{:S(2)}, u32[]{:S(2)}) collective-permute-start(bf16[1,64,1024]{2,1,0:T(8,128)(2,1)S(1)} %add_convert_fusion.12), channel_id=1, source_target_pairs={{0,16},{1,17},{2,18},{3,19},{4,20},{5,21},{6,22},{7,23},{8,24},{9,... | collective-permute-start | bytes 393224 | tf_op jit(solution)/shard_map/ppermute | solution.py:733
  169.5 1.8 collective-permute-start.30
  171.4 1.4 collective-permute-done.33
  172.8 9.3 %collective-permute-done.30 = bf16[1,80,1024]{2,1,0:T(8,128)(2,1)S(1)} collective-permute-done((bf16[1,80,1024]{2,1,0:T(8,128)(2,1)S(1)}, bf16[1,80,1024]{2,1,0:T(8,128)(2,1)S(1)}, u32[]{:S(2)}, u32[]{:S(2)}) %collective-permute-start.30) | collective-permute-done | bytes 163872 | tf_op jit(solution)/shard_map/ppermute | solution.py:733
  182.2 0.8 collective-permute-start.38
  183.0 1.0 collective-permute-start.34
  184.0 2.1 %collective-permute-done.38 = bf16[1,64,1024]{2,1,0:T(8,128)(2,1)S(1)} collective-permute-done((bf16[1,64,1024]{2,1,0:T(8,128)(2,1)S(1)}, bf16[1,64,1024]{2,1,0:T(8,128)(2,1)S(1)}, u32[]{:S(2)}, u32[]{:S(2)}) %collective-permute-start.38) | collective-permute-done | bytes 131104 | tf_op jit(solution)/shard_map/ppermute | solution.py:733
  186.1 0.8 pad_maximum_fusion.5
  186.8 0.9 collective-permute-start.39
  187.8 0.8 pad_maximum_fusion.4
  188.5 0.7 collective-permute-start.35
  189.3 1.2 fusion.11
  190.5 0.7 fusion.17
  191.2 3.1 %collective-permute-start.40 = (bf16[1,128,1024]{2,1,0:T(8,128)(2,1)S(1)}, bf16[1,128,1024]{2,1,0:T(8,128)(2,1)S(1)}, u32[]{:S(2)}, u32[]{:S(2)}) collective-permute-start(bf16[1,128,1024]{2,1,0:T(8,128)(2,1)S(1)} %get-tuple-element.165), channel_id=1, source_target_pairs={{0,2},{1,3},{2,0},{3,1},{4,6},{5,7},{6,4},{7,5},{8,10},{9,11},{10,... | collective-permute-start | bytes 786440 | tf_op jit(solution)/shard_map/ppermute | solution.py:733
  194.3 1.7 collective-permute-start.41
  195.9 2.0 collective-permute-start.37
  197.9 0.6 fusion.14
  198.5 0.7 constant_dynamic-slice_fusion.1
  199.3 0.7 copy-done.21
  200.2 4.0 %finish_slopes.1 = (f32[512,512]{1,0:T(8,128)}, f32[512,512]{1,0:T(8,128)}, f32[512,512]{1,0:T(8,128)}, f32[512,512]{1,0:T(8,128)}) custom-call(bf16[128,1024]{1,0:T(8,128)(2,1)} %get-tuple-element.168.refs_0_, bf16[128,1024]{1,0:T(8,128)(2,1)} %bitcast.68, bf16[128,1024]{1,0:T(8,128)(2,1)} %bitcast.70, bf16[128,1024]{1,0:T(8,128)(2,1)} %bitcast.72, ...), custom_call_target="tpu_custom_call" | custom-call | tf_op jit(solution)/shard_map/finish_slopes/pallas_call | solution.py:642
  (130 shorter events, 3.2 us)
Async XLA Ops:
  0.6 8.5 %copy-start.1 = (bf16[512,512]{1,0:T(8,128)(2,1)S(1)}, bf16[512,512]{1,0:T(8,128)(2,1)}, u32[]{:S(2)}) copy-start(bf16[512,512]{1,0:T(8,128)(2,1)} %refs_11_.1) | copy-start | bytes 1572868
  0.7 8.5 %copy-start.2 = (bf16[512,512]{1,0:T(8,128)(2,1)S(1)}, bf16[512,512]{1,0:T(8,128)(2,1)}, u32[]{:S(2)}) copy-start(bf16[512,512]{1,0:T(8,128)(2,1)} %refs_12_.1) | copy-start | bytes 1572868
  0.7 8.5 %copy-start.3 = (bf16[512,512]{1,0:T(8,128)(2,1)S(1)}, bf16[512,512]{1,0:T(8,128)(2,1)}, u32[]{:S(2)}) copy-start(bf16[512,512]{1,0:T(8,128)(2,1)} %refs_13_.1) | copy-start | bytes 1572868
  0.7 4.4 %copy-start.26 = (bf16[64,512]{1,0:T(8,128)(2,1)S(1)}, bf16[64,512]{1,0:T(8,128)(2,1)}, u32[]{:S(2)}) copy-start(bf16[64,512]{1,0:T(8,128)(2,1)} %param.23) | copy-start | bytes 196612
  0.7 4.4 %copy-start.27 = (bf16[512,64]{0,1:T(8,128)(2,1)S(1)}, bf16[512,64]{0,1:T(8,128)(2,1)}, u32[]{:S(2)}) copy-start(bf16[512,64]{0,1:T(8,128)(2,1)} %param.22) | copy-start | bytes 196612
  0.7 8.1 %copy-start.29 = (bf16[512]{0:T(512)(128)(2,1)S(1)}, bf16[512]{0:T(512)(128)(2,1)}, u32[]{:S(2)}) copy-start(bf16[512]{0:T(512)(128)(2,1)} %param.19) | copy-start | bytes 3076
  0.7 8.3 %copy-start.28 = (bf16[512]{0:T(512)(128)(2,1)S(1)}, bf16[512]{0:T(512)(128)(2,1)}, u32[]{:S(2)}) copy-start(bf16[512]{0:T(512)(128)(2,1)} %param.15) | copy-start | bytes 3076
  0.7 8.4 %copy-start.7 = (s32[1,8]{1,0:T(1,128)S(1)}, s32[1,8]{1,0:T(1,128)}, u32[]{:S(2)}) copy-start(s32[1,8]{1,0:T(1,128)} %lengths.1) | copy-start | bytes 100
  3.1 20.1 %collective-permute-start = (bf16[3,256,512]{2,1,0:T(8,128)(2,1)}, bf16[3,256,512]{2,1,0:T(8,128)(2,1)S(1)}, u32[]{:S(2)}, u32[]{:S(2)}) collective-permute-start(bf16[3,256,512]{2,1,0:T(8,128)(2,1)} %get-tuple-element.81), channel_id=1, source_target_pairs={{0,1},{1,0},{2,3},{3,2},{4,5},{5,4},{6,7},{7,6},{8,9},{9,8},{10,11... | collective-permute-start | bytes 2359304 | tf_op jit(solution)/shard_map/ppermute | solution.py:733
  5.1 18.1 %collective-permute-start.1 = (bf16[128,512]{1,0:T(8,128)(2,1)S(1)}, bf16[128,512]{1,0:T(8,128)(2,1)S(1)}, u32[]{:S(2)}, u32[]{:S(2)}) collective-permute-start(bf16[128,512]{1,0:T(8,128)(2,1)S(1)} %pad_maximum_fusion.9), channel_id=1, source_target_pairs={{0,8},{1,9},{2,10},{3,11},{4,12},{5,13},{6,14},{7,15},{8,0},{9,1},... | collective-permute-start | bytes 393224 | tf_op jit(solution)/shard_map/ppermute | solution.py:733
  6.5 16.7 %collective-permute-start.2 = (bf16[128,512]{1,0:T(8,128)(2,1)S(1)}, bf16[128,512]{1,0:T(8,128)(2,1)}, u32[]{:S(2)}, u32[]{:S(2)}) collective-permute-start(bf16[128,512]{1,0:T(8,128)(2,1)S(1)} %pad_maximum_fusion.9), channel_id=1, source_target_pairs={{0,16},{1,17},{2,18},{3,19},{4,20},{5,21},{6,22},{7,23},{8,24},{9,... | collective-permute-start | bytes 393224 | tf_op jit(solution)/shard_map/ppermute | solution.py:733
  8.8 14.4 %collective-permute-start.3 = (bf16[128,512]{1,0:T(8,128)(2,1)S(1)}, bf16[128,512]{1,0:T(8,128)(2,1)}, u32[]{:S(2)}, u32[]{:S(2)}) collective-permute-start(bf16[128,512]{1,0:T(8,128)(2,1)S(1)} %pad_maximum_fusion.9), channel_id=1, source_target_pairs={{0,24},{1,25},{2,26},{3,27},{4,28},{5,29},{6,30},{7,31},{8,16},{9,... | collective-permute-start | bytes 393224 | tf_op jit(solution)/shard_map/ppermute | solution.py:733
  8.8 14.4 %collective-permute-start.4 = (bf16[512]{0:T(512)(128)(2,1)S(1)}, bf16[512]{0:T(512)(128)(2,1)S(1)}, u32[]{:S(2)}, u32[]{:S(2)}) collective-permute-start(bf16[512]{0:T(512)(128)(2,1)S(1)} %copy-done.29), channel_id=1, source_target_pairs={{0,1},{1,0},{2,3},{3,2},{4,5},{5,4},{6,7},{7,6},{8,9},{9,8},{10,11... | collective-permute-start | bytes 3080 | tf_op jit(solution)/shard_map/ppermute | solution.py:733
  9.1 129.3 %copy-start.6 = (s32[4]{0:T(128)}, s32[4]{0:T(128)S(1)}, u32[]{:S(2)}) copy-start(s32[4]{0:T(128)S(1)} %pad_add_fusion.refs_7_.refs_6_.refs_8_.scalars.refs_19_) | copy-start | bytes 52
  23.2 5.7 %collective-permute-start.5 = (bf16[3,256,512]{2,1,0:T(8,128)(2,1)S(1)}, bf16[3,256,512]{2,1,0:T(8,128)(2,1)S(1)}, u32[]{:S(2)}, u32[]{:S(2)}) collective-permute-start(bf16[3,256,512]{2,1,0:T(8,128)(2,1)S(1)} %collective-permute-done), channel_id=1, source_target_pairs={{0,2},{1,3},{2,0},{3,1},{4,6},{5,7},{6,4},{7,5},{8,10},{9,11},{10,... | collective-permute-start | bytes 2359304 | tf_op jit(solution)/shard_map/ppermute | solution.py:733
  25.1 16.8 %collective-permute-start.6 = (bf16[256,512]{1,0:T(8,128)(2,1)}, bf16[256,512]{1,0:T(8,128)(2,1)S(1)}, u32[]{:S(2)}, u32[]{:S(2)}) collective-permute-start(bf16[256,512]{1,0:T(8,128)(2,1)} %get-tuple-element.89), channel_id=1, source_target_pairs={{0,1},{1,0},{2,3},{3,2},{4,5},{5,4},{6,7},{7,6},{8,9},{9,8},{10,11... | collective-permute-start | bytes 786440 | tf_op jit(solution)/shard_map/ppermute | solution.py:733
  27.6 15.1 %collective-permute-start.8 = (bf16[4,128,512]{2,1,0:T(8,128)(2,1)S(1)}, bf16[4,128,512]{2,1,0:T(8,128)(2,1)S(1)}, u32[]{:S(2)}, u32[]{:S(2)}) collective-permute-start(bf16[4,128,512]{2,1,0:T(8,128)(2,1)S(1)} %pad_maximum_fusion.2.refs_8_), channel_id=1, source_target_pairs={{0,4},{1,5},{2,6},{3,7},{4,0},{5,1},{6,2},{7,3},{8,12},{9,13},{10,... | collective-permute-start | bytes 1572872 | tf_op jit(solution)/shard_map/ppermute | solution.py:733
  29.1 14.0 %copy-start.30 = (bf16[512]{0:T(512)(128)(2,1)S(1)}, bf16[512]{0:T(512)(128)(2,1)}, u32[]{:S(2)}) copy-start(bf16[512]{0:T(512)(128)(2,1)} %param.21) | copy-start | bytes 3076
  41.9 3.4 %copy-start.4 = (bf16[512,512]{1,0:T(8,128)(2,1)S(1)}, bf16[512,512]{1,0:T(8,128)(2,1)}, u32[]{:S(2)}) copy-start(bf16[512,512]{1,0:T(8,128)(2,1)} %refs_0_.1) | copy-start | bytes 1572868
  41.9 2.7 %collective-permute-start.7 = (bf16[256,512]{1,0:T(8,128)(2,1)S(1)}, bf16[256,512]{1,0:T(8,128)(2,1)S(1)}, u32[]{:S(2)}, u32[]{:S(2)}) collective-permute-start(bf16[256,512]{1,0:T(8,128)(2,1)S(1)} %collective-permute-done.6), channel_id=1, source_target_pairs={{0,2},{1,3},{2,0},{3,1},{4,6},{5,7},{6,4},{7,5},{8,10},{9,11},{10,... | collective-permute-start | bytes 786440 | tf_op jit(solution)/shard_map/ppermute | solution.py:733
  42.6 2.0 %collective-permute-start.9 = (bf16[4,128,512]{2,1,0:T(8,128)(2,1)S(1)}, bf16[4,128,512]{2,1,0:T(8,128)(2,1)S(1)}, u32[]{:S(2)}, u32[]{:S(2)}) collective-permute-start(bf16[4,128,512]{2,1,0:T(8,128)(2,1)S(1)} %pad_maximum_fusion.2.refs_8_), channel_id=1, source_target_pairs={{0,2},{1,3},{2,0},{3,1},{4,6},{5,7},{6,4},{7,5},{8,10},{9,11},{10,... | collective-permute-start | bytes 1572872 | tf_op jit(solution)/shard_map/ppermute | solution.py:733
  42.6 2.6 %collective-permute-start.10 = (bf16[4,128,512]{2,1,0:T(8,128)(2,1)S(1)}, bf16[4,128,512]{2,1,0:T(8,128)(2,1)S(1)}, u32[]{:S(2)}, u32[]{:S(2)}) collective-permute-start(bf16[4,128,512]{2,1,0:T(8,128)(2,1)S(1)} %collective-permute-done.8.refs_9_), channel_id=1, source_target_pairs={{0,2},{1,3},{2,0},{3,1},{4,6},{5,7},{6,4},{7,5},{8,10},{9,11},{10,... | collective-permute-start | bytes 1572872 | tf_op jit(solution)/shard_map/ppermute | solution.py:733
  43.1 26.2 %collective-permute-start.11 = (bf16[4,128,512]{2,1,0:T(8,128)(2,1)S(1)}, bf16[4,128,512]{2,1,0:T(8,128)(2,1)S(1)}, u32[]{:S(2)}, u32[]{:S(2)}) collective-permute-start(bf16[4,128,512]{2,1,0:T(8,128)(2,1)S(1)} %pad_maximum_fusion.2.refs_8_), channel_id=1, source_target_pairs={{0,5},{1,4},{2,7},{3,6},{4,1},{5,0},{6,3},{7,2},{8,13},{9,12},{10,... | collective-permute-start | bytes 1572872 | tf_op jit(solution)/shard_map/ppermute | solution.py:733
  43.3 26.0 %collective-permute-start.12 = (bf16[4,128,512]{2,1,0:T(8,128)(2,1)S(1)}, bf16[4,128,512]{2,1,0:T(8,128)(2,1)S(1)}, u32[]{:S(2)}, u32[]{:S(2)}) collective-permute-start(bf16[4,128,512]{2,1,0:T(8,128)(2,1)S(1)} %pad_maximum_fusion.2.refs_8_), channel_id=1, source_target_pairs={{0,1},{1,0},{2,3},{3,2},{4,5},{5,4},{6,7},{7,6},{8,9},{9,8},{10,11... | collective-permute-start | bytes 1572872 | tf_op jit(solution)/shard_map/ppermute | solution.py:733
  69.3 2.0 collective-permute-start.13
  69.7 3.1 %collective-permute-start.14 = (bf16[4,128,512]{2,1,0:T(8,128)(2,1)S(1)}, bf16[4,128,512]{2,1,0:T(8,128)(2,1)S(1)}, u32[]{:S(2)}, u32[]{:S(2)}) collective-permute-start(bf16[4,128,512]{2,1,0:T(8,128)(2,1)S(1)} %collective-permute-done.11.refs_10_), channel_id=1, source_target_pairs={{0,2},{1,3},{2,0},{3,1},{4,6},{5,7},{6,4},{7,5},{8,10},{9,11},{10,... | collective-permute-start | bytes 1572872 | tf_op jit(solution)/shard_map/ppermute | solution.py:733
  69.9 29.0 %collective-permute-start.16 = (bf16[8,128,512]{2,1,0:T(8,128)(2,1)}, bf16[8,128,512]{2,1,0:T(8,128)(2,1)S(1)}, u32[]{:S(2)}, u32[]{:S(2)}) collective-permute-start(bf16[8,128,512]{2,1,0:T(8,128)(2,1)} %get-tuple-element.109), channel_id=1, source_target_pairs={{0,2},{1,3},{2,0},{3,1},{4,6},{5,7},{6,4},{7,5},{8,10},{9,11},{10,... | collective-permute-start | bytes 3145736 | tf_op jit(solution)/shard_map/ppermute | solution.py:733
  72.8 26.1 %copy-start.12 = (bf16[8,128,512]{2,1,0:T(8,128)(2,1)S(1)}, bf16[8,128,512]{2,1,0:T(8,128)(2,1)}, u32[]{:S(2)}) copy-start(bf16[8,128,512]{2,1,0:T(8,128)(2,1)} %get-tuple-element.108) | copy-start | bytes 3145732
  98.4 2.9 %collective-permute-start.15 = (bf16[8,128,512]{2,1,0:T(8,128)(2,1)}, bf16[8,128,512]{2,1,0:T(8,128)(2,1)S(1)}, u32[]{:S(2)}, u32[]{:S(2)}) collective-permute-start(bf16[8,128,512]{2,1,0:T(8,128)(2,1)} %get-tuple-element.107), channel_id=1, source_target_pairs={{0,2},{1,3},{2,0},{3,1},{4,6},{5,7},{6,4},{7,5},{8,10},{9,11},{10,... | collective-permute-start | bytes 3145736 | tf_op jit(solution)/shard_map/ppermute | solution.py:733
  98.8 29.3 %copy-start.13 = (bf16[8,128,512]{2,1,0:T(8,128)(2,1)}, bf16[8,128,512]{2,1,0:T(8,128)(2,1)S(1)}, u32[]{:S(2)}) copy-start(bf16[8,128,512]{2,1,0:T(8,128)(2,1)S(1)} %collective-permute-done.16) | copy-start | bytes 3145732
  98.8 5.0 %copy-start.8 = (bf16[512,512]{1,0:T(8,128)(2,1)S(1)}, bf16[512,512]{1,0:T(8,128)(2,1)}, u32[]{:S(2)}) copy-start(bf16[512,512]{1,0:T(8,128)(2,1)} %get-tuple-element.114.refs_5_) | copy-start | bytes 1572868
  98.8 5.0 %copy-start.9 = (bf16[512,512]{1,0:T(8,128)(2,1)S(1)}, bf16[512,512]{1,0:T(8,128)(2,1)}, u32[]{:S(2)}) copy-start(bf16[512,512]{1,0:T(8,128)(2,1)} %get-tuple-element.118.refs_11_) | copy-start | bytes 1572868
  99.0 27.8 %collective-permute-start.18 = (bf16[4,128,512]{2,1,0:T(8,128)(2,1)S(1)}, bf16[4,128,512]{2,1,0:T(8,128)(2,1)S(1)}, u32[]{:S(2)}, u32[]{:S(2)}) collective-permute-start(bf16[4,128,512]{2,1,0:T(8,128)(2,1)S(1)} %add_convert_fusion.1), channel_id=1, source_target_pairs={{0,4},{1,5},{2,6},{3,7},{4,0},{5,1},{6,2},{7,3},{8,12},{9,13},{10,... | collective-permute-start | bytes 1572872 | tf_op jit(solution)/shard_map/ppermute | solution.py:733
  101.7 25.1 %collective-permute-start.17 = (bf16[4,128,512]{2,1,0:T(8,128)(2,1)S(1)}, bf16[4,128,512]{2,1,0:T(8,128)(2,1)S(1)}, u32[]{:S(2)}, u32[]{:S(2)}) collective-permute-start(bf16[4,128,512]{2,1,0:T(8,128)(2,1)S(1)} %get-tuple-element.151), channel_id=1, source_target_pairs={{0,1},{1,0},{2,3},{3,2},{4,5},{5,4},{6,7},{7,6},{8,9},{9,8},{10,11... | collective-permute-start | bytes 1572872 | tf_op jit(solution)/shard_map/ppermute | solution.py:733
  102.0 24.8 %collective-permute-start.19 = (bf16[4,128,512]{2,1,0:T(8,128)(2,1)S(1)}, bf16[4,128,512]{2,1,0:T(8,128)(2,1)S(1)}, u32[]{:S(2)}, u32[]{:S(2)}) collective-permute-start(bf16[4,128,512]{2,1,0:T(8,128)(2,1)S(1)} %get-tuple-element.150), channel_id=1, source_target_pairs={{0,5},{1,4},{2,7},{3,6},{4,1},{5,0},{6,3},{7,2},{8,13},{9,12},{10,... | collective-permute-start | bytes 1572872 | tf_op jit(solution)/shard_map/ppermute | solution.py:733
  126.8 5.9 %copy-start.16 = (bf16[4,128,512]{2,1,0:T(8,128)(2,1)}, bf16[4,128,512]{2,1,0:T(8,128)(2,1)S(1)}, u32[]{:S(2)}) copy-start(bf16[4,128,512]{2,1,0:T(8,128)(2,1)S(1)} %collective-permute-done.19) | copy-start | bytes 1572868
  126.8 5.9 %copy-start.15 = (bf16[4,128,512]{2,1,0:T(8,128)(2,1)}, bf16[4,128,512]{2,1,0:T(8,128)(2,1)S(1)}, u32[]{:S(2)}) copy-start(bf16[4,128,512]{2,1,0:T(8,128)(2,1)S(1)} %collective-permute-done.17) | copy-start | bytes 1572868
  126.8 5.9 %collective-permute-start.20 = (bf16[2,256,1024]{2,1,0:T(8,128)(2,1)}, bf16[2,256,1024]{2,1,0:T(8,128)(2,1)S(1)}, u32[]{:S(2)}, u32[]{:S(2)}) collective-permute-start(bf16[2,256,1024]{2,1,0:T(8,128)(2,1)} %get-tuple-element.124), channel_id=1, source_target_pairs={{0,2},{1,3},{2,0},{3,1},{4,6},{5,7},{6,4},{7,5},{8,10},{9,11},{10,... | collective-permute-start | bytes 3145736 | tf_op jit(solution)/shard_map/ppermute | solution.py:733
  128.0 4.7 %collective-permute-start.21 = (bf16[2,256,1024]{2,1,0:T(8,128)(2,1)}, bf16[2,256,1024]{2,1,0:T(8,128)(2,1)S(1)}, u32[]{:S(2)}, u32[]{:S(2)}) collective-permute-start(bf16[2,256,1024]{2,1,0:T(8,128)(2,1)} %get-tuple-element.126), channel_id=1, source_target_pairs={{0,2},{1,3},{2,0},{3,1},{4,6},{5,7},{6,4},{7,5},{8,10},{9,11},{10,... | collective-permute-start | bytes 3145736 | tf_op jit(solution)/shard_map/ppermute | solution.py:733
  129.1 23.1 %collective-permute-start.24 = (bf16[128,512]{1,0:T(8,128)(2,1)}, bf16[128,512]{1,0:T(8,128)(2,1)S(1)}, u32[]{:S(2)}, u32[]{:S(2)}) collective-permute-start(bf16[128,512]{1,0:T(8,128)(2,1)} %get-tuple-element.149), channel_id=1, source_target_pairs={{0,8},{1,9},{2,10},{3,11},{4,12},{5,13},{6,14},{7,15},{8,0},{9,1},... | collective-permute-start | bytes 393224 | tf_op jit(solution)/shard_map/ppermute | solution.py:733
  129.5 22.7 %collective-permute-start.25 = (bf16[128,512]{1,0:T(8,128)(2,1)}, bf16[128,512]{1,0:T(8,128)(2,1)S(1)}, u32[]{:S(2)}, u32[]{:S(2)}) collective-permute-start(bf16[128,512]{1,0:T(8,128)(2,1)} %get-tuple-element.148), channel_id=1, source_target_pairs={{0,16},{1,17},{2,18},{3,19},{4,20},{5,21},{6,22},{7,23},{8,24},{9,... | collective-permute-start | bytes 393224 | tf_op jit(solution)/shard_map/ppermute | solution.py:733
  132.7 19.5 %collective-permute-start.26 = (bf16[128,512]{1,0:T(8,128)(2,1)}, bf16[128,512]{1,0:T(8,128)(2,1)S(1)}, u32[]{:S(2)}, u32[]{:S(2)}) collective-permute-start(bf16[128,512]{1,0:T(8,128)(2,1)} %get-tuple-element.147), channel_id=1, source_target_pairs={{0,24},{1,25},{2,26},{3,27},{4,28},{5,29},{6,30},{7,31},{8,16},{9,... | collective-permute-start | bytes 393224 | tf_op jit(solution)/shard_map/ppermute | solution.py:733
  134.0 4.5 %copy-start.5 = (f32[8,512]{1,0:T(8,128)S(1)}, f32[8,512]{1,0:T(8,128)}, u32[]{:S(2)}) copy-start(f32[8,512]{1,0:T(8,128)} %get-tuple-element.131.refs_17_) | copy-start | bytes 49156
  137.7 14.5 %collective-permute-start.22 = (bf16[1,256,1024]{2,1,0:T(8,128)(2,1)}, bf16[1,256,1024]{2,1,0:T(8,128)(2,1)S(1)}, u32[]{:S(2)}, u32[]{:S(2)}) collective-permute-start(bf16[1,256,1024]{2,1,0:T(8,128)(2,1)} %get-tuple-element.127), channel_id=1, source_target_pairs={{0,1},{1,0},{2,3},{3,2},{4,5},{5,4},{6,7},{7,6},{8,9},{9,8},{10,11... | collective-permute-start | bytes 1572872 | tf_op jit(solution)/shard_map/ppermute | solution.py:733
  137.9 14.2 %collective-permute-start.23 = (bf16[2,128,1024]{2,1,0:T(8,128)(2,1)}, bf16[2,128,1024]{2,1,0:T(8,128)(2,1)S(1)}, u32[]{:S(2)}, u32[]{:S(2)}) collective-permute-start(bf16[2,128,1024]{2,1,0:T(8,128)(2,1)} %get-tuple-element.128), channel_id=1, source_target_pairs={{0,4},{1,5},{2,6},{3,7},{4,0},{5,1},{6,2},{7,3},{8,12},{9,13},{10,... | collective-permute-start | bytes 1572872 | tf_op jit(solution)/shard_map/ppermute | solution.py:733
  138.5 15.5 %copy-start.18 = (bf16[2,128,1024]{2,1,0:T(8,128)(2,1)S(1)}, bf16[2,128,1024]{2,1,0:T(8,128)(2,1)}, u32[]{:S(2)}) copy-start(bf16[2,128,1024]{2,1,0:T(8,128)(2,1)} %get-tuple-element.141) | copy-start | bytes 1572868
  138.5 15.7 %copy-start.17 = (bf16[1,256,1024]{2,1,0:T(8,128)(2,1)S(1)}, bf16[1,256,1024]{2,1,0:T(8,128)(2,1)}, u32[]{:S(2)}) copy-start(bf16[1,256,1024]{2,1,0:T(8,128)(2,1)} %get-tuple-element.142) | copy-start | bytes 1572868
  152.1 30.8 %copy-start.25 = (bf16[128,512]{1,0:T(8,128)(2,1)}, bf16[128,512]{1,0:T(8,128)(2,1)S(1)}, u32[]{:S(2)}) copy-start(bf16[128,512]{1,0:T(8,128)(2,1)S(1)} %collective-permute-done.26) | copy-start | bytes 393220
  152.2 2.7 %collective-permute-start.27 = (bf16[1,16,1024]{2,1,0:T(8,128)(2,1)S(1)}, bf16[1,16,1024]{2,1,0:T(8,128)(2,1)S(1)}, u32[]{:S(2)}, u32[]{:S(2)}) collective-permute-start(bf16[1,16,1024]{2,1,0:T(8,128)(2,1)S(1)} %bitcast.58), channel_id=1, source_target_pairs={{0,2},{1,3},{2,0},{3,1},{4,6},{5,7},{6,4},{7,5},{8,10},{9,11},{10,... | collective-permute-start | bytes 98312 | tf_op jit(solution)/shard_map/ppermute | solution.py:733
  154.4 8.0 %collective-permute-start.31 = (bf16[1,128,1024]{2,1,0:T(8,128)(2,1)S(1)}, bf16[1,128,1024]{2,1,0:T(8,128)(2,1)S(1)}, u32[]{:S(2)}, u32[]{:S(2)}) collective-permute-start(bf16[1,128,1024]{2,1,0:T(8,128)(2,1)S(1)} %get-tuple-element.158), channel_id=1, source_target_pairs={{0,8},{1,9},{2,10},{3,11},{4,12},{5,13},{6,14},{7,15},{8,0},{9,1},... | collective-permute-start | bytes 786440 | tf_op jit(solution)/shard_map/ppermute | solution.py:733
  154.9 8.5 %collective-permute-start.28 = (bf16[1,144,1024]{2,1,0:T(8,128)(2,1)S(1)}, bf16[1,144,1024]{2,1,0:T(8,128)(2,1)S(1)}, u32[]{:S(2)}, u32[]{:S(2)}) collective-permute-start(bf16[1,144,1024]{2,1,0:T(8,128)(2,1)S(1)} %pad_maximum_fusion.3), channel_id=1, source_target_pairs={{0,1},{1,0},{2,3},{3,2},{4,5},{5,4},{6,7},{7,6},{8,9},{9,8},{10,11... | collective-permute-start | bytes 884744 | tf_op jit(solution)/shard_map/ppermute | solution.py:733
  162.4 4.3 %collective-permute-start.32 = (bf16[1,64,1024]{2,1,0:T(8,128)(2,1)S(1)}, bf16[1,64,1024]{2,1,0:T(8,128)(2,1)S(1)}, u32[]{:S(2)}, u32[]{:S(2)}) collective-permute-start(bf16[1,64,1024]{2,1,0:T(8,128)(2,1)S(1)} %add_convert_fusion.13), channel_id=1, source_target_pairs={{0,4},{1,5},{2,6},{3,7},{4,0},{5,1},{6,2},{7,3},{8,12},{9,13},{10,... | collective-permute-start | bytes 393224 | tf_op jit(solution)/shard_map/ppermute | solution.py:733
  163.5 5.9 %collective-permute-start.29 = (bf16[1,80,1024]{2,1,0:T(8,128)(2,1)S(1)}, bf16[1,80,1024]{2,1,0:T(8,128)(2,1)S(1)}, u32[]{:S(2)}, u32[]{:S(2)}) collective-permute-start(bf16[1,80,1024]{2,1,0:T(8,128)(2,1)S(1)} %pad_maximum_fusion.6), channel_id=1, source_target_pairs={{0,8},{1,9},{2,10},{3,11},{4,12},{5,13},{6,14},{7,15},{8,0},{9,1},... | collective-permute-start | bytes 491528 | tf_op jit(solution)/shard_map/ppermute | solution.py:733
  166.8 6.0 %collective-permute-start.33 = (bf16[1,64,1024]{2,1,0:T(8,128)(2,1)S(1)}, bf16[1,64,1024]{2,1,0:T(8,128)(2,1)S(1)}, u32[]{:S(2)}, u32[]{:S(2)}) collective-permute-start(bf16[1,64,1024]{2,1,0:T(8,128)(2,1)S(1)} %add_convert_fusion.12), channel_id=1, source_target_pairs={{0,16},{1,17},{2,18},{3,19},{4,20},{5,21},{6,22},{7,23},{8,24},{9,... | collective-permute-start | bytes 393224 | tf_op jit(solution)/shard_map/ppermute | solution.py:733
  169.5 12.6 %collective-permute-start.30 = (bf16[1,80,1024]{2,1,0:T(8,128)(2,1)S(1)}, bf16[1,80,1024]{2,1,0:T(8,128)(2,1)S(1)}, u32[]{:S(2)}, u32[]{:S(2)}) collective-permute-start(bf16[1,80,1024]{2,1,0:T(8,128)(2,1)S(1)} %pad_maximum_fusion.7), channel_id=1, source_target_pairs={{0,16},{1,17},{2,18},{3,19},{4,20},{5,21},{6,22},{7,23},{8,24},{9,... | collective-permute-start | bytes 491528 | tf_op jit(solution)/shard_map/ppermute | solution.py:733
  182.2 3.9 %collective-permute-start.38 = (bf16[1,64,1024]{2,1,0:T(8,128)(2,1)S(1)}, bf16[1,64,1024]{2,1,0:T(8,128)(2,1)S(1)}, u32[]{:S(2)}, u32[]{:S(2)}) collective-permute-start(bf16[1,64,1024]{2,1,0:T(8,128)(2,1)S(1)} %add_convert_fusion.10), channel_id=1, source_target_pairs={{0,8},{1,9},{2,10},{3,11},{4,12},{5,13},{6,14},{7,15},{8,0},{9,1},... | collective-permute-start | bytes 393224 | tf_op jit(solution)/shard_map/ppermute | solution.py:733
  183.0 4.7 %collective-permute-start.34 = (bf16[1,80,1024]{2,1,0:T(8,128)(2,1)S(1)}, bf16[1,80,1024]{2,1,0:T(8,128)(2,1)S(1)}, u32[]{:S(2)}, u32[]{:S(2)}) collective-permute-start(bf16[1,80,1024]{2,1,0:T(8,128)(2,1)S(1)} %pad_maximum_fusion.8), channel_id=1, source_target_pairs={{0,4},{1,5},{2,6},{3,7},{4,0},{5,1},{6,2},{7,3},{8,12},{9,13},{10,... | collective-permute-start | bytes 491528 | tf_op jit(solution)/shard_map/ppermute | solution.py:733
  186.8 7.5 %collective-permute-start.39 = (bf16[1,128,1024]{2,1,0:T(8,128)(2,1)S(1)}, bf16[1,128,1024]{2,1,0:T(8,128)(2,1)S(1)}, u32[]{:S(2)}, u32[]{:S(2)}) collective-permute-start(bf16[1,128,1024]{2,1,0:T(8,128)(2,1)S(1)} %get-tuple-element.165), channel_id=1, source_target_pairs={{0,4},{1,5},{2,6},{3,7},{4,0},{5,1},{6,2},{7,3},{8,12},{9,13},{10,... | collective-permute-start | bytes 786440 | tf_op jit(solution)/shard_map/ppermute | solution.py:733
  188.5 7.4 %collective-permute-start.35 = (bf16[1,128,1024]{2,1,0:T(8,128)(2,1)S(1)}, bf16[1,128,1024]{2,1,0:T(8,128)(2,1)S(1)}, u32[]{:S(2)}, u32[]{:S(2)}) collective-permute-start(bf16[1,128,1024]{2,1,0:T(8,128)(2,1)S(1)} %get-tuple-element.167), channel_id=1, source_target_pairs={{0,8},{1,9},{2,10},{3,11},{4,12},{5,13},{6,14},{7,15},{8,0},{9,1},... | collective-permute-start | bytes 786440 | tf_op jit(solution)/shard_map/ppermute | solution.py:733
  191.2 8.0 %collective-permute-start.40 = (bf16[1,128,1024]{2,1,0:T(8,128)(2,1)S(1)}, bf16[1,128,1024]{2,1,0:T(8,128)(2,1)S(1)}, u32[]{:S(2)}, u32[]{:S(2)}) collective-permute-start(bf16[1,128,1024]{2,1,0:T(8,128)(2,1)S(1)} %get-tuple-element.165), channel_id=1, source_target_pairs={{0,2},{1,3},{2,0},{3,1},{4,6},{5,7},{6,4},{7,5},{8,10},{9,11},{10,... | collective-permute-start | bytes 786440 | tf_op jit(solution)/shard_map/ppermute | solution.py:733
  194.3 4.9 %collective-permute-start.36 = (bf16[1,128,1024]{2,1,0:T(8,128)(2,1)S(1)}, bf16[1,128,1024]{2,1,0:T(8,128)(2,1)S(1)}, u32[]{:S(2)}, u32[]{:S(2)}) collective-permute-start(bf16[1,128,1024]{2,1,0:T(8,128)(2,1)S(1)} %get-tuple-element.167), channel_id=1, source_target_pairs={{0,2},{1,3},{2,0},{3,1},{4,6},{5,7},{6,4},{7,5},{8,10},{9,11},{10,... | collective-permute-start | bytes 786440 | tf_op jit(solution)/shard_map/ppermute | solution.py:733
  194.3 5.0 %copy-start.19 = (bf16[1,128,1024]{2,1,0:T(8,128)(2,1)}, bf16[1,128,1024]{2,1,0:T(8,128)(2,1)S(1)}, u32[]{:S(2)}) copy-start(bf16[1,128,1024]{2,1,0:T(8,128)(2,1)S(1)} %collective-permute-done.39) | copy-start | bytes 786436
  194.3 4.9 %collective-permute-start.41 = (bf16[1,128,1024]{2,1,0:T(8,128)(2,1)S(1)}, bf16[1,128,1024]{2,1,0:T(8,128)(2,1)S(1)}, u32[]{:S(2)}, u32[]{:S(2)}) collective-permute-start(bf16[1,128,1024]{2,1,0:T(8,128)(2,1)S(1)} %collective-permute-done.39), channel_id=1, source_target_pairs={{0,2},{1,3},{2,0},{3,1},{4,6},{5,7},{6,4},{7,5},{8,10},{9,11},{10,... | collective-permute-start | bytes 786440 | tf_op jit(solution)/shard_map/ppermute | solution.py:733
  195.9 3.3 %collective-permute-start.37 = (bf16[1,128,1024]{2,1,0:T(8,128)(2,1)S(1)}, bf16[1,128,1024]{2,1,0:T(8,128)(2,1)S(1)}, u32[]{:S(2)}, u32[]{:S(2)}) collective-permute-start(bf16[1,128,1024]{2,1,0:T(8,128)(2,1)S(1)} %collective-permute-done.35), channel_id=1, source_target_pairs={{0,2},{1,3},{2,0},{3,1},{4,6},{5,7},{6,4},{7,5},{8,10},{9,11},{10,... | collective-permute-start | bytes 786440 | tf_op jit(solution)/shard_map/ppermute | solution.py:733
  (9 other events, 12.9 us)

commit v6 on v5

--- a/solution.py
+++ b/solution.py
@@ -294,26 +294,47 @@
     else:
         dense_in, cotangent = dense_ref[...], cotangent_ref[...]
     dense_t, cotangent_t = dense_in.T, cotangent.T
-    fed, delta = None, None
     joined = max(1, 512 // (shards * half))
-    for chunk in range(0, pieces, joined):
+    chunks = range(0, pieces, joined)
+
+    def weights(chunk):
         some = pieces_w[chunk : chunk + joined]
         upper_w = jnp.concatenate([w[:, :half, :].reshape(shards * half, width) for w in some], 0)
-        lower_w = jnp.concatenate([w[:, half:, :].reshape(shards * half, width) for w in some], 0)
-        cols = slice(chunk * shards * half, (chunk + joined) * shards * half)
-        upper = dot_nt(dense_in, upper_w)
+        return upper_w, jnp.concatenate([w[:, half:, :].reshape(shards * half, width) for w in some], 0)
+
+    def bend(upper):
         square = upper * upper
         bell = 0.5 + 0.5 * jnp.tanh(upper * (GELU_SLOPE + GELU_SLOPE * GELU_CUBE * square))
         active = upper * bell
         slope = bell + active * (1.0 - bell) * (2.0 * GELU_SLOPE + 6.0 * GELU_SLOPE * GELU_CUBE * square)
-        active = active.astype(BF16)
-        part = dot_nn(active, lower_w)
-        fed = part if fed is None else fed + part
-        upper_delta = (slope * dot_nt(cotangent, lower_w)).astype(BF16)
-        part = dot_nn(upper_delta, upper_w)
-        delta = part if delta is None else delta + part
+        return active.astype(BF16), slope
+
+    def gather(chunk, active, upper_delta):
+        cols = slice(chunk * shards * half, (chunk + joined) * shards * half)
         lower_acc[:, cols] += dot_nn(cotangent_t, active)
         upper_acc[:, cols] += dot_nn(dense_t, upper_delta)
+
+    fed, delta, behind = None, None, None
+    upper_w, lower_w = weights(0)
+    upper, back = dot_nt(dense_in, upper_w), dot_nt(cotangent, lower_w)
+    for chunk in chunks:
+        following = chunk + joined
+        if following < pieces:
+            next_upper_w, next_lower_w = weights(following)
+            next_upper = dot_nt(dense_in, next_upper_w)
+        active, slope = bend(upper)
+        upper_delta = (slope * back).astype(BF16)
+        if following < pieces:
+            next_back = dot_nt(cotangent, next_lower_w)
+        if behind is not None:
+            gather(*behind)
+        fed_part, delta_part = dot_nn(active, lower_w), dot_nn(upper_delta, upper_w)
+        fed = fed_part if fed is None else fed + fed_part
+        delta = delta_part if delta is None else delta + delta_part
+        behind = chunk, active, upper_delta
+        if following < pieces:
+            upper_w, lower_w, upper, back = next_upper_w, next_lower_w, next_upper, next_back
+    gather(*behind)
     if stage == 0:
         sum_out[...] = (middle + fed).astype(BF16)
         delta_out[...] = delta.astype(BF16)
@@ -497,11 +518,15 @@
         for index in range(sets):
             output_grads = per_set[index][5]
             tall = output_grads.shape[0]
+            turns = cs.shape[1] // BLOCK
             for half in range(2):
-
-                @pl.when(block // (blocks // 2) == half)
+                if turns == 1:
+                    second_out[half][index, :, channels:] = output_grads[half * (tall // 2) : (half + 1) * (tall // 2), :]
+                    continue
+
+                @pl.when(block // (turns // 2) == half)
                 def _():
-                    there = pl.multiple_of(block % (blocks // 2) * tall, tall)
+                    there = pl.multiple_of(block % (turns // 2) * tall, tall)
                     second_out[half][index, pl.ds(there, tall), channels:] = output_grads[...]
 
     @pl.when((phase == 1) & (block == blocks - 1))
@@ -615,7 +640,7 @@
         out_specs=[pl.BlockSpec((SEGMENTS, STEPS, width), lambda block: (0, block, 0)), pl.BlockSpec((16, sets * channels), whole)],
         out_shape=[hbm((SEGMENTS, rows // SEGMENTS, width), F32), jax.ShapeDtypeStruct((16, sets * channels), BF16)],
         scratch_shapes=[pltpu.VMEM((8, width), F32), pltpu.VMEM((width // 128, BLOCK, 128), F32)],
-        compiler_params=pltpu.CompilerParams(vmem_limit_bytes=44 * 1024 * 1024, dimension_semantics=("arbitrary",)),
+        compiler_params=pltpu.CompilerParams(vmem_limit_bytes=34 * 1024 * 1024, dimension_semantics=("arbitrary",)),
         cost_estimate=pl.CostEstimate(flops=2 * rows * width * 3 * channels * sets, bytes_accessed=rows * channels * 8 * sets, transcendentals=0),
         name="input_backward",
     )(in_hbm(x_rows), in_hbm(mixed), gain, *[in_hbm(f) for f in factors], *weights, dense_part, bias_parts, scalars)
@@ -881,11 +906,12 @@
     if paired:
         far_four, other_four = after((far_four, other_four), rows_0[0])
         pieces_1 = [other_four, far_four, links.swap(other_four, Links.CORE), links.swap(far_four, Links.CORE)]
-        own_terms = [own_keep, links.swap(own_send, Links.CORE)]
+        own_terms = [own_keep, links.swap(after(own_send, pieces_1), Links.CORE)]
     other_keep, other_send, block_out, mixed, dense_part, *output_grads = dense_both(1, states, rows_0, None, dense, scalars, pieces_1)
     back_mixed = mixed
     if paired:
-        other_terms = [other_keep, links.swap(other_send, Links.CORE)]
+        own_terms[1] = after(own_terms[1], mixed)
+        other_terms = [other_keep, links.swap(after(other_send, own_terms[1]), Links.CORE)]
         dense_sends, dense_kept = links.dense_across(own_terms, other_terms)
         back_mixed = after(mixed, [values for values, _ in dense_sends])
         dense_terms = links.exchange(dense_sends, dense_kept)

time: 204 us -> 203 us (level)
  no operation moved by 1% of the time
where the time goes in v6:
time: 203 us
  Pallas kernels  120 us (59%)
  starting transfers between devices  42.7 us (21%)
  waiting for transfers between devices  28 us (14%)
  other arithmetic  6.33 us (3%)
  local copies, waits for them, and re-layouts  5.21 us (3%)
    pallas_call x2, Pallas kernels, dense_both(): pl.pallas_call(functools.partial(dense_kernel, stage, sets, len(pieces)),...  49 us
    ppermute x42, starting transfers between devices, swap(): return lax.ppermute(values, ('dp', 'tensor'), pairs)  42.7 us
    ppermute x42, waiting for transfers between devices, swap(): return lax.ppermute(values, ('dp', 'tensor'), pairs)  28 us
    pallas_call x2, Pallas kernels, mixer_forward(): pl.pallas_call(functools.partial(mixer_kernel, first), grid=(2, blocks),...  26.7 us
    pallas_call x1, Pallas kernels, mixer_backward(): pl.pallas_call(functools.partial(mixer_back_kernel, sets), grid=(2, block...  20.2 us
    pallas_call x1, Pallas kernels, input_backward(): pl.pallas_call(functools.partial(input_kernel, sets), grid=(rows // BLOCK...  13.6 us
  transfers between devices with their start and end apart: 42, of which 11 were waited for; matrix products, arithmetic and copies ran while one was open for 4% of the time, Pallas kernels for 56%

profile of v6, /device:TPU:1, one launch (start us, length us, event | category | flops | bytes accessed | tf_op | source)
XLA Modules:
  0.0 203.0 jit_solution(8182972850777734354)
XLA Ops:
  0.7 2.3 %pack_halves.1 = (bf16[3,256,512]{2,1,0:T(8,128)(2,1)}, bf16[256,512]{1,0:T(8,128)(2,1)}) custom-call(s32[1]{0:T(128)} %bitcast.7.refs_0_, bf16[512,512]{1,0:T(8,128)(2,1)} %refs_11_.1, bf16[512,512]{1,0:T(8,128)(2,1)} %refs_12_.1, bf16[512,512]{1,0:T(8,128)(2,1)} %refs_13_.1, bf16[512,512]{1,0:T(8,128)(2,1)} %refs_0_.1), custom_call_target="tpu_custom_call" | custom-call | tf_op jit(solution)/shard_map/pack_halves/pallas_call | solution.py:734
  3.1 2.0 %collective-permute-start = (bf16[3,256,512]{2,1,0:T(8,128)(2,1)}, bf16[3,256,512]{2,1,0:T(8,128)(2,1)S(1)}, u32[]{:S(2)}, u32[]{:S(2)}) collective-permute-start(bf16[3,256,512]{2,1,0:T(8,128)(2,1)} %get-tuple-element.84), channel_id=1, source_target_pairs={{0,1},{1,0},{2,3},{3,2},{4,5},{5,4},{6,7},{7,6},{8,9},{9,8},{10,11... | collective-permute-start | bytes 2359304 | tf_op jit(solution)/shard_map/ppermute | solution.py:758
  5.1 1.4 collective-permute-start.1
  6.5 2.3 %collective-permute-start.2 = (bf16[128,512]{1,0:T(8,128)(2,1)S(1)}, bf16[128,512]{1,0:T(8,128)(2,1)}, u32[]{:S(2)}, u32[]{:S(2)}) collective-permute-start(bf16[128,512]{1,0:T(8,128)(2,1)S(1)} %pad_maximum_fusion.9), channel_id=1, source_target_pairs={{0,16},{1,17},{2,18},{3,19},{4,20},{5,21},{6,22},{7,23},{8,24},{9,... | collective-permute-start | bytes 393224 | tf_op jit(solution)/shard_map/ppermute | solution.py:758
  9.2 14.0 %mixer_forward.2 = (bf16[2048,512]{1,0:T(8,128)(2,1)}, bf16[2048,512]{1,0:T(8,128)(2,1)}, bf16[2048,512]{1,0:T(8,128)(2,1)}, bf16[2048,512]{1,0:T(8,128)(2,1)}, ...) custom-call(bf16[8,256,512]{2,1,0:T(8,128)(2,1)} %bitcast.77, f32[1,512]{1,0:T(1,128)S(1)} %bitcast.60, ...), custom_call_target="tpu_custom_call" | custom-call | flops 3221225472 | bytes 16777216 | tf_op jit(solution)/shard_map/mixer_forward/pallas_call | solution.py:243
  23.2 1.9 collective-permute-start.5
  25.1 1.0 pad_maximum_fusion.2.refs_8_
  26.1 1.5 collective-permute-start.8
  27.6 1.2 collective-permute-start.6
  29.1 12.8 %mixer_forward.3 = (bf16[2048,512]{1,0:T(8,128)(2,1)}, bf16[2048,512]{1,0:T(8,128)(2,1)}, bf16[2048,512]{1,0:T(8,128)(2,1)}, bf16[2048,512]{1,0:T(8,128)(2,1)}, f32[8,512]{1,0:T(8,128)}) custom-call(bf16[2048,512]{1,0:T(8,128)(2,1)} %get-tuple-element.83.refs_0_.normed_ref, bf16[512,512]{1,0:T(8,128)(2,1)S(1)} %get-tuple-element.159.refs_1_.refs_14_, ...), custom_call_target="tpu_custom_call" | custom-call | flops 3221225472 | bytes 16777216 | tf_op jit(solution)/shard_map/mixer_forward/pallas_call | solution.py:243
  41.8 0.7 collective-permute-start.7
  42.6 0.4 collective-permute-start.10
  43.0 0.3 collective-permute-start.11
  43.3 1.1 collective-permute-start.12
  44.5 0.6 collective-permute-done.10.refs_11_
  45.2 23.9 %dense_first.1 = (bf16[8,128,512]{2,1,0:T(8,128)(2,1)}, bf16[8,128,512]{2,1,0:T(8,128)(2,1)}, bf16[2048,512]{1,0:T(8,128)(2,1)}, bf16[2048,512]{1,0:T(8,128)(2,1...) custom-call(bf16[2048,512]{1,0:T(8,128)(2,1)} %get-tuple-element.82.refs_0_, ...), custom_call_target="tpu_custom_call" | custom-call | flops 12884901888 | bytes 25165824 | tf_op jit(solution)/shard_map/dense_first/pallas_call | solution.py:406
  69.1 0.4 collective-permute-start.13
  69.6 1.4 collective-permute-done.13.refs_11_
  71.0 0.7 collective-permute-done.14.refs_12_
  71.8 0.4 collective-permute-start.15
  72.2 25.1 %dense_second.1 = (bf16[8,128,512]{2,1,0:T(8,128)(2,1)}, bf16[8,128,512]{2,1,0:T(8,128)(2,1)}, bf16[8,256,512]{2,1,0:T(8,128)(2,1)}, bf16[2048,512]{1,0:T(8,128)...) custom-call(bf16[2048,512]{1,0:T(8,128)(2,1)} %get-tuple-element.82.refs_0_, ...), custom_call_target="tpu_custom_call" | custom-call | flops 12884901888 | bytes 25165824 | tf_op jit(solution)/shard_map/dense_second/pallas_call | solution.py:406
  97.7 0.9 collective-permute-start.18
  98.6 1.6 collective-permute-done.16
  100.6 1.0 collective-permute-start.19
  101.6 1.2 collective-permute-start.17
  102.8 20.2 %mixer_backward.1 = (bf16[2048,512]{1,0:T(8,128)(2,1)}, bf16[2048,512]{1,0:T(8,128)(2,1)}, bf16[2,256,1024]{2,1,0:T(8,128)(2,1)S(1)}, bf16[2,256,1024]{2,1,0:T(8...) custom-call(bf16[2048,512]{1,0:T(8,128)(2,1)} %get-tuple-element.116, ...), custom_call_target="tpu_custom_call" | custom-call | flops 8589934592 | bytes 25165824 | tf_op jit(solution)/shard_map/mixer_backward/pallas_call | solution.py:558
  123.0 1.0 copy-done
  123.9 2.0 collective-permute-done.17
  126.0 1.0 collective-permute-start.20
  126.9 1.0 fusion.10
  127.9 0.4 collective-permute-start.24
  128.3 3.2 %collective-permute-start.25 = (bf16[128,512]{1,0:T(8,128)(2,1)}, bf16[128,512]{1,0:T(8,128)(2,1)S(1)}, u32[]{:S(2)}, u32[]{:S(2)}) collective-permute-start(bf16[128,512]{1,0:T(8,128)(2,1)} %get-tuple-element.154), channel_id=1, source_target_pairs={{0,16},{1,17},{2,18},{3,19},{4,20},{5,21},{6,22},{7,23},{8,24},{9,... | collective-permute-start | bytes 393224 | tf_op jit(solution)/shard_map/ppermute | solution.py:758
  131.5 0.9 copy-done.10
  132.5 0.3 copy-done.11
  132.8 3.7 %paired_sums.1 = (bf16[1,256,1024]{2,1,0:T(8,128)(2,1)}, bf16[2,128,1024]{2,1,0:T(8,128)(2,1)}, bf16[1,256,1024]{2,1,0:T(8,128)(2,1)}, bf16[2,128,1024]{2,1,0:T(8,128)(2,1)}) custom-call(bf16[2,256,1024]{2,1,0:T(8,128)(2,1)} %copy-done, bf16[2,256,1024]{2,1,0:T(8,128)(2,1)} %copy-done.10, bf16[2,256,1024]{2,1,0:T(8,128)(2,1)} %get-tuple-element.131.refs_2_.refs_6_, ...), custom_call_target="tpu_custom_call" | custom-call | tf_op jit(solution)/shard_map/paired_sums/pallas_call | solution.py:705
  136.5 0.5 collective-permute-start.23
  137.3 13.6 %input_backward.1 = (f32[8,256,512]{2,1,0:T(8,128)}, bf16[16,1024]{1,0:T(8,128)(2,1)S(1)}) custom-call(bf16[2048,512]{1,0:T(8,128)(2,1)} %get-tuple-element.90.refs_2_.refs_0_, bf16[2048,512]{1,0:T(8,128)(2,1)} %get-tuple-element.116.mixed_ref.refs_1_, f32[1,512]{1,0:T(1,128)S(1)} %bitcast.61, bf16[2048,512]{1,0:T(8,128)(2,1)} %get-tuple-element.135.refs_3_, ...), custom_call_target="tpu_custom_call" | custom-call | flops 6442450944 | bytes 16777216 | tf_op jit(solution)/shard_map/input_backward/pallas_call | solution.py:632
  151.2 1.9 collective-permute-start.27
  153.4 0.5 collective-permute-done.27
  154.0 1.3 collective-permute-start.28
  155.3 6.0 %collective-permute-done.31 = bf16[1,128,1024]{2,1,0:T(8,128)(2,1)S(1)} collective-permute-done((bf16[1,128,1024]{2,1,0:T(8,128)(2,1)S(1)}, bf16[1,128,1024]{2,1,0:T(8,128)(2,1)S(1)}, u32[]{:S(2)}, u32[]{:S(2)}) %collective-permute-start.31) | collective-permute-done | bytes 262176 | tf_op jit(solution)/shard_map/ppermute | solution.py:758
  161.3 1.0 collective-permute-start.32
  162.4 1.0 collective-permute-start.29
  163.4 2.2 %collective-permute-done.32 = bf16[1,64,1024]{2,1,0:T(8,128)(2,1)S(1)} collective-permute-done((bf16[1,64,1024]{2,1,0:T(8,128)(2,1)S(1)}, bf16[1,64,1024]{2,1,0:T(8,128)(2,1)S(1)}, u32[]{:S(2)}, u32[]{:S(2)}) %collective-permute-start.32) | collective-permute-done | bytes 131104 | tf_op jit(solution)/shard_map/ppermute | solution.py:758
  165.7 2.6 %collective-permute-start.33 = (bf16[1,64,1024]{2,1,0:T(8,128)(2,1)S(1)}, bf16[1,64,1024]{2,1,0:T(8,128)(2,1)S(1)}, u32[]{:S(2)}, u32[]{:S(2)}) collective-permute-start(bf16[1,64,1024]{2,1,0:T(8,128)(2,1)S(1)} %add_convert_fusion.12), channel_id=1, source_target_pairs={{0,16},{1,17},{2,18},{3,19},{4,20},{5,21},{6,22},{7,23},{8,24},{9,... | collective-permute-start | bytes 393224 | tf_op jit(solution)/shard_map/ppermute | solution.py:758
  168.4 1.8 collective-permute-start.30
  170.3 1.4 collective-permute-done.33
  171.7 9.3 %collective-permute-done.30 = bf16[1,80,1024]{2,1,0:T(8,128)(2,1)S(1)} collective-permute-done((bf16[1,80,1024]{2,1,0:T(8,128)(2,1)S(1)}, bf16[1,80,1024]{2,1,0:T(8,128)(2,1)S(1)}, u32[]{:S(2)}, u32[]{:S(2)}) %collective-permute-start.30) | collective-permute-done | bytes 163872 | tf_op jit(solution)/shard_map/ppermute | solution.py:758
  181.1 0.8 collective-permute-start.38
  181.9 1.0 collective-permute-start.34
  182.9 2.1 %collective-permute-done.38 = bf16[1,64,1024]{2,1,0:T(8,128)(2,1)S(1)} collective-permute-done((bf16[1,64,1024]{2,1,0:T(8,128)(2,1)S(1)}, bf16[1,64,1024]{2,1,0:T(8,128)(2,1)S(1)}, u32[]{:S(2)}, u32[]{:S(2)}) %collective-permute-start.38) | collective-permute-done | bytes 131104 | tf_op jit(solution)/shard_map/ppermute | solution.py:758
  184.9 0.8 pad_maximum_fusion.5
  185.7 0.9 collective-permute-start.39
  186.7 0.8 pad_maximum_fusion.4
  187.4 0.7 collective-permute-start.35
  188.2 1.2 fusion.11
  189.4 0.7 fusion.17
  190.1 3.1 %collective-permute-start.40 = (bf16[1,128,1024]{2,1,0:T(8,128)(2,1)S(1)}, bf16[1,128,1024]{2,1,0:T(8,128)(2,1)S(1)}, u32[]{:S(2)}, u32[]{:S(2)}) collective-permute-start(bf16[1,128,1024]{2,1,0:T(8,128)(2,1)S(1)} %get-tuple-element.171), channel_id=1, source_target_pairs={{0,2},{1,3},{2,0},{3,1},{4,6},{5,7},{6,4},{7,5},{8,10},{9,11},{10,... | collective-permute-start | bytes 786440 | tf_op jit(solution)/shard_map/ppermute | solution.py:758
  193.2 1.7 collective-permute-start.41
  194.8 2.0 collective-permute-start.37
  196.8 0.6 fusion.14
  197.4 0.7 constant_dynamic-slice_fusion.1
  198.2 0.7 copy-done.21
  199.1 4.0 %finish_slopes.1 = (f32[512,512]{1,0:T(8,128)}, f32[512,512]{1,0:T(8,128)}, f32[512,512]{1,0:T(8,128)}, f32[512,512]{1,0:T(8,128)}) custom-call(bf16[128,1024]{1,0:T(8,128)(2,1)} %get-tuple-element.174.refs_0_, bf16[128,1024]{1,0:T(8,128)(2,1)} %bitcast.68, bf16[128,1024]{1,0:T(8,128)(2,1)} %bitcast.70, bf16[128,1024]{1,0:T(8,128)(2,1)} %bitcast.72, ...), custom_call_target="tpu_custom_call" | custom-call | tf_op jit(solution)/shard_map/finish_slopes/pallas_call | solution.py:667
  (130 shorter events, 3.1 us)
Async XLA Ops:
  0.6 8.5 %copy-start.1 = (bf16[512,512]{1,0:T(8,128)(2,1)S(1)}, bf16[512,512]{1,0:T(8,128)(2,1)}, u32[]{:S(2)}) copy-start(bf16[512,512]{1,0:T(8,128)(2,1)} %refs_11_.1) | copy-start | bytes 1572868
  0.7 8.5 %copy-start.2 = (bf16[512,512]{1,0:T(8,128)(2,1)S(1)}, bf16[512,512]{1,0:T(8,128)(2,1)}, u32[]{:S(2)}) copy-start(bf16[512,512]{1,0:T(8,128)(2,1)} %refs_12_.1) | copy-start | bytes 1572868
  0.7 8.5 %copy-start.3 = (bf16[512,512]{1,0:T(8,128)(2,1)S(1)}, bf16[512,512]{1,0:T(8,128)(2,1)}, u32[]{:S(2)}) copy-start(bf16[512,512]{1,0:T(8,128)(2,1)} %refs_13_.1) | copy-start | bytes 1572868
  0.7 4.4 %copy-start.27 = (bf16[512,64]{0,1:T(8,128)(2,1)S(1)}, bf16[512,64]{0,1:T(8,128)(2,1)}, u32[]{:S(2)}) copy-start(bf16[512,64]{0,1:T(8,128)(2,1)} %param.22) | copy-start | bytes 196612
  0.7 4.4 %copy-start.26 = (bf16[64,512]{1,0:T(8,128)(2,1)S(1)}, bf16[64,512]{1,0:T(8,128)(2,1)}, u32[]{:S(2)}) copy-start(bf16[64,512]{1,0:T(8,128)(2,1)} %param.23) | copy-start | bytes 196612
  0.7 8.1 %copy-start.29 = (bf16[512]{0:T(512)(128)(2,1)S(1)}, bf16[512]{0:T(512)(128)(2,1)}, u32[]{:S(2)}) copy-start(bf16[512]{0:T(512)(128)(2,1)} %param.19) | copy-start | bytes 3076
  0.7 8.3 %copy-start.28 = (bf16[512]{0:T(512)(128)(2,1)S(1)}, bf16[512]{0:T(512)(128)(2,1)}, u32[]{:S(2)}) copy-start(bf16[512]{0:T(512)(128)(2,1)} %param.15) | copy-start | bytes 3076
  0.7 8.4 %copy-start.7 = (s32[1,8]{1,0:T(1,128)S(1)}, s32[1,8]{1,0:T(1,128)}, u32[]{:S(2)}) copy-start(s32[1,8]{1,0:T(1,128)} %lengths.1) | copy-start | bytes 100
  3.1 20.1 %collective-permute-start = (bf16[3,256,512]{2,1,0:T(8,128)(2,1)}, bf16[3,256,512]{2,1,0:T(8,128)(2,1)S(1)}, u32[]{:S(2)}, u32[]{:S(2)}) collective-permute-start(bf16[3,256,512]{2,1,0:T(8,128)(2,1)} %get-tuple-element.84), channel_id=1, source_target_pairs={{0,1},{1,0},{2,3},{3,2},{4,5},{5,4},{6,7},{7,6},{8,9},{9,8},{10,11... | collective-permute-start | bytes 2359304 | tf_op jit(solution)/shard_map/ppermute | solution.py:758
  5.1 18.1 %collective-permute-start.1 = (bf16[128,512]{1,0:T(8,128)(2,1)S(1)}, bf16[128,512]{1,0:T(8,128)(2,1)S(1)}, u32[]{:S(2)}, u32[]{:S(2)}) collective-permute-start(bf16[128,512]{1,0:T(8,128)(2,1)S(1)} %pad_maximum_fusion.9), channel_id=1, source_target_pairs={{0,8},{1,9},{2,10},{3,11},{4,12},{5,13},{6,14},{7,15},{8,0},{9,1},... | collective-permute-start | bytes 393224 | tf_op jit(solution)/shard_map/ppermute | solution.py:758
  6.5 16.7 %collective-permute-start.2 = (bf16[128,512]{1,0:T(8,128)(2,1)S(1)}, bf16[128,512]{1,0:T(8,128)(2,1)}, u32[]{:S(2)}, u32[]{:S(2)}) collective-permute-start(bf16[128,512]{1,0:T(8,128)(2,1)S(1)} %pad_maximum_fusion.9), channel_id=1, source_target_pairs={{0,16},{1,17},{2,18},{3,19},{4,20},{5,21},{6,22},{7,23},{8,24},{9,... | collective-permute-start | bytes 393224 | tf_op jit(solution)/shard_map/ppermute | solution.py:758
  8.8 14.4 %collective-permute-start.3 = (bf16[128,512]{1,0:T(8,128)(2,1)S(1)}, bf16[128,512]{1,0:T(8,128)(2,1)}, u32[]{:S(2)}, u32[]{:S(2)}) collective-permute-start(bf16[128,512]{1,0:T(8,128)(2,1)S(1)} %pad_maximum_fusion.9), channel_id=1, source_target_pairs={{0,24},{1,25},{2,26},{3,27},{4,28},{5,29},{6,30},{7,31},{8,16},{9,... | collective-permute-start | bytes 393224 | tf_op jit(solution)/shard_map/ppermute | solution.py:758
  8.8 14.4 %collective-permute-start.4 = (bf16[512]{0:T(512)(128)(2,1)S(1)}, bf16[512]{0:T(512)(128)(2,1)S(1)}, u32[]{:S(2)}, u32[]{:S(2)}) collective-permute-start(bf16[512]{0:T(512)(128)(2,1)S(1)} %copy-done.29), channel_id=1, source_target_pairs={{0,1},{1,0},{2,3},{3,2},{4,5},{5,4},{6,7},{7,6},{8,9},{9,8},{10,11... | collective-permute-start | bytes 3080 | tf_op jit(solution)/shard_map/ppermute | solution.py:758
  9.1 128.2 %copy-start.6 = (s32[4]{0:T(128)}, s32[4]{0:T(128)S(1)}, u32[]{:S(2)}) copy-start(s32[4]{0:T(128)S(1)} %pad_add_fusion.refs_7_.refs_6_.refs_8_.scalars.refs_19_) | copy-start | bytes 52
  23.2 5.6 %collective-permute-start.5 = (bf16[3,256,512]{2,1,0:T(8,128)(2,1)S(1)}, bf16[3,256,512]{2,1,0:T(8,128)(2,1)S(1)}, u32[]{:S(2)}, u32[]{:S(2)}) collective-permute-start(bf16[3,256,512]{2,1,0:T(8,128)(2,1)S(1)} %collective-permute-done), channel_id=1, source_target_pairs={{0,2},{1,3},{2,0},{3,1},{4,6},{5,7},{6,4},{7,5},{8,10},{9,11},{10,... | collective-permute-start | bytes 2359304 | tf_op jit(solution)/shard_map/ppermute | solution.py:758
  26.1 16.5 %collective-permute-start.8 = (bf16[4,128,512]{2,1,0:T(8,128)(2,1)S(1)}, bf16[4,128,512]{2,1,0:T(8,128)(2,1)S(1)}, u32[]{:S(2)}, u32[]{:S(2)}) collective-permute-start(bf16[4,128,512]{2,1,0:T(8,128)(2,1)S(1)} %pad_maximum_fusion.2.refs_8_), channel_id=1, source_target_pairs={{0,4},{1,5},{2,6},{3,7},{4,0},{5,1},{6,2},{7,3},{8,12},{9,13},{10,... | collective-permute-start | bytes 1572872 | tf_op jit(solution)/shard_map/ppermute | solution.py:758
  27.6 14.2 %collective-permute-start.6 = (bf16[256,512]{1,0:T(8,128)(2,1)}, bf16[256,512]{1,0:T(8,128)(2,1)S(1)}, u32[]{:S(2)}, u32[]{:S(2)}) collective-permute-start(bf16[256,512]{1,0:T(8,128)(2,1)} %get-tuple-element.92), channel_id=1, source_target_pairs={{0,1},{1,0},{2,3},{3,2},{4,5},{5,4},{6,7},{7,6},{8,9},{9,8},{10,11... | collective-permute-start | bytes 786440 | tf_op jit(solution)/shard_map/ppermute | solution.py:758
  29.1 13.9 %copy-start.30 = (bf16[512]{0:T(512)(128)(2,1)S(1)}, bf16[512]{0:T(512)(128)(2,1)}, u32[]{:S(2)}) copy-start(bf16[512]{0:T(512)(128)(2,1)} %param.21) | copy-start | bytes 3076
  41.8 3.3 %copy-start.4 = (bf16[512,512]{1,0:T(8,128)(2,1)S(1)}, bf16[512,512]{1,0:T(8,128)(2,1)}, u32[]{:S(2)}) copy-start(bf16[512,512]{1,0:T(8,128)(2,1)} %refs_0_.1) | copy-start | bytes 1572868
  41.8 2.6 %collective-permute-start.7 = (bf16[256,512]{1,0:T(8,128)(2,1)S(1)}, bf16[256,512]{1,0:T(8,128)(2,1)S(1)}, u32[]{:S(2)}, u32[]{:S(2)}) collective-permute-start(bf16[256,512]{1,0:T(8,128)(2,1)S(1)} %collective-permute-done.6), channel_id=1, source_target_pairs={{0,2},{1,3},{2,0},{3,1},{4,6},{5,7},{6,4},{7,5},{8,10},{9,11},{10,... | collective-permute-start | bytes 786440 | tf_op jit(solution)/shard_map/ppermute | solution.py:758
  42.5 2.0 %collective-permute-start.9 = (bf16[4,128,512]{2,1,0:T(8,128)(2,1)S(1)}, bf16[4,128,512]{2,1,0:T(8,128)(2,1)S(1)}, u32[]{:S(2)}, u32[]{:S(2)}) collective-permute-start(bf16[4,128,512]{2,1,0:T(8,128)(2,1)S(1)} %pad_maximum_fusion.2.refs_8_), channel_id=1, source_target_pairs={{0,2},{1,3},{2,0},{3,1},{4,6},{5,7},{6,4},{7,5},{8,10},{9,11},{10,... | collective-permute-start | bytes 1572872 | tf_op jit(solution)/shard_map/ppermute | solution.py:758
  42.6 2.6 %collective-permute-start.10 = (bf16[4,128,512]{2,1,0:T(8,128)(2,1)S(1)}, bf16[4,128,512]{2,1,0:T(8,128)(2,1)S(1)}, u32[]{:S(2)}, u32[]{:S(2)}) collective-permute-start(bf16[4,128,512]{2,1,0:T(8,128)(2,1)S(1)} %collective-permute-done.8.refs_9_), channel_id=1, source_target_pairs={{0,2},{1,3},{2,0},{3,1},{4,6},{5,7},{6,4},{7,5},{8,10},{9,11},{10,... | collective-permute-start | bytes 1572872 | tf_op jit(solution)/shard_map/ppermute | solution.py:758
  43.0 26.0 %collective-permute-start.11 = (bf16[4,128,512]{2,1,0:T(8,128)(2,1)S(1)}, bf16[4,128,512]{2,1,0:T(8,128)(2,1)S(1)}, u32[]{:S(2)}, u32[]{:S(2)}) collective-permute-start(bf16[4,128,512]{2,1,0:T(8,128)(2,1)S(1)} %pad_maximum_fusion.2.refs_8_), channel_id=1, source_target_pairs={{0,5},{1,4},{2,7},{3,6},{4,1},{5,0},{6,3},{7,2},{8,13},{9,12},{10,... | collective-permute-start | bytes 1572872 | tf_op jit(solution)/shard_map/ppermute | solution.py:758
  43.3 25.7 %collective-permute-start.12 = (bf16[4,128,512]{2,1,0:T(8,128)(2,1)S(1)}, bf16[4,128,512]{2,1,0:T(8,128)(2,1)S(1)}, u32[]{:S(2)}, u32[]{:S(2)}) collective-permute-start(bf16[4,128,512]{2,1,0:T(8,128)(2,1)S(1)} %pad_maximum_fusion.2.refs_8_), channel_id=1, source_target_pairs={{0,1},{1,0},{2,3},{3,2},{4,5},{5,4},{6,7},{7,6},{8,9},{9,8},{10,11... | collective-permute-start | bytes 1572872 | tf_op jit(solution)/shard_map/ppermute | solution.py:758
  69.1 2.0 collective-permute-start.13
  69.5 2.3 %collective-permute-start.14 = (bf16[4,128,512]{2,1,0:T(8,128)(2,1)S(1)}, bf16[4,128,512]{2,1,0:T(8,128)(2,1)S(1)}, u32[]{:S(2)}, u32[]{:S(2)}) collective-permute-start(bf16[4,128,512]{2,1,0:T(8,128)(2,1)S(1)} %collective-permute-done.11.refs_10_), channel_id=1, source_target_pairs={{0,2},{1,3},{2,0},{3,1},{4,6},{5,7},{6,4},{7,5},{8,10},{9,11},{10,... | collective-permute-start | bytes 1572872 | tf_op jit(solution)/shard_map/ppermute | solution.py:758
  71.8 25.5 %collective-permute-start.15 = (bf16[8,128,512]{2,1,0:T(8,128)(2,1)}, bf16[8,128,512]{2,1,0:T(8,128)(2,1)S(1)}, u32[]{:S(2)}, u32[]{:S(2)}) collective-permute-start(bf16[8,128,512]{2,1,0:T(8,128)(2,1)} %get-tuple-element.112), channel_id=1, source_target_pairs={{0,2},{1,3},{2,0},{3,1},{4,6},{5,7},{6,4},{7,5},{8,10},{9,11},{10,... | collective-permute-start | bytes 3145736 | tf_op jit(solution)/shard_map/ppermute | solution.py:758
  72.2 25.4 %copy-start.12 = (bf16[8,128,512]{2,1,0:T(8,128)(2,1)S(1)}, bf16[8,128,512]{2,1,0:T(8,128)(2,1)}, u32[]{:S(2)}) copy-start(bf16[8,128,512]{2,1,0:T(8,128)(2,1)} %get-tuple-element.115) | copy-start | bytes 3145732
  97.3 29.6 %copy-start.13 = (bf16[8,128,512]{2,1,0:T(8,128)(2,1)}, bf16[8,128,512]{2,1,0:T(8,128)(2,1)S(1)}, u32[]{:S(2)}) copy-start(bf16[8,128,512]{2,1,0:T(8,128)(2,1)S(1)} %collective-permute-done.15) | copy-start | bytes 3145732
  97.3 2.9 %collective-permute-start.16 = (bf16[8,128,512]{2,1,0:T(8,128)(2,1)}, bf16[8,128,512]{2,1,0:T(8,128)(2,1)S(1)}, u32[]{:S(2)}, u32[]{:S(2)}) collective-permute-start(bf16[8,128,512]{2,1,0:T(8,128)(2,1)} %get-tuple-element.114), channel_id=1, source_target_pairs={{0,2},{1,3},{2,0},{3,1},{4,6},{5,7},{6,4},{7,5},{8,10},{9,11},{10,... | collective-permute-start | bytes 3145736 | tf_op jit(solution)/shard_map/ppermute | solution.py:758
  97.6 5.2 %copy-start.8 = (bf16[512,512]{1,0:T(8,128)(2,1)S(1)}, bf16[512,512]{1,0:T(8,128)(2,1)}, u32[]{:S(2)}) copy-start(bf16[512,512]{1,0:T(8,128)(2,1)} %get-tuple-element.120.refs_5_) | copy-start | bytes 1572868
  97.6 5.2 %copy-start.9 = (bf16[512,512]{1,0:T(8,128)(2,1)S(1)}, bf16[512,512]{1,0:T(8,128)(2,1)}, u32[]{:S(2)}) copy-start(bf16[512,512]{1,0:T(8,128)(2,1)} %get-tuple-element.124.refs_11_) | copy-start | bytes 1572868
  97.7 26.2 %collective-permute-start.18 = (bf16[4,128,512]{2,1,0:T(8,128)(2,1)S(1)}, bf16[4,128,512]{2,1,0:T(8,128)(2,1)S(1)}, u32[]{:S(2)}, u32[]{:S(2)}) collective-permute-start(bf16[4,128,512]{2,1,0:T(8,128)(2,1)S(1)} %add_convert_fusion.1), channel_id=1, source_target_pairs={{0,4},{1,5},{2,6},{3,7},{4,0},{5,1},{6,2},{7,3},{8,12},{9,13},{10,... | collective-permute-start | bytes 1572872 | tf_op jit(solution)/shard_map/ppermute | solution.py:758
  100.6 23.3 %collective-permute-start.19 = (bf16[4,128,512]{2,1,0:T(8,128)(2,1)S(1)}, bf16[4,128,512]{2,1,0:T(8,128)(2,1)S(1)}, u32[]{:S(2)}, u32[]{:S(2)}) collective-permute-start(bf16[4,128,512]{2,1,0:T(8,128)(2,1)S(1)} %get-tuple-element.156), channel_id=1, source_target_pairs={{0,5},{1,4},{2,7},{3,6},{4,1},{5,0},{6,3},{7,2},{8,13},{9,12},{10,... | collective-permute-start | bytes 1572872 | tf_op jit(solution)/shard_map/ppermute | solution.py:758
  101.6 24.4 %collective-permute-start.17 = (bf16[4,128,512]{2,1,0:T(8,128)(2,1)S(1)}, bf16[4,128,512]{2,1,0:T(8,128)(2,1)S(1)}, u32[]{:S(2)}, u32[]{:S(2)}) collective-permute-start(bf16[4,128,512]{2,1,0:T(8,128)(2,1)S(1)} %get-tuple-element.157), channel_id=1, source_target_pairs={{0,1},{1,0},{2,3},{3,2},{4,5},{5,4},{6,7},{7,6},{8,9},{9,8},{10,11... | collective-permute-start | bytes 1572872 | tf_op jit(solution)/shard_map/ppermute | solution.py:758
  123.9 7.6 %copy-start.15 = (bf16[4,128,512]{2,1,0:T(8,128)(2,1)}, bf16[4,128,512]{2,1,0:T(8,128)(2,1)S(1)}, u32[]{:S(2)}) copy-start(bf16[4,128,512]{2,1,0:T(8,128)(2,1)S(1)} %collective-permute-done.19) | copy-start | bytes 1572868
  126.0 5.6 %copy-start.16 = (bf16[4,128,512]{2,1,0:T(8,128)(2,1)}, bf16[4,128,512]{2,1,0:T(8,128)(2,1)S(1)}, u32[]{:S(2)}) copy-start(bf16[4,128,512]{2,1,0:T(8,128)(2,1)S(1)} %collective-permute-done.17) | copy-start | bytes 1572868
  126.0 5.5 %collective-permute-start.20 = (bf16[2,256,1024]{2,1,0:T(8,128)(2,1)}, bf16[2,256,1024]{2,1,0:T(8,128)(2,1)S(1)}, u32[]{:S(2)}, u32[]{:S(2)}) collective-permute-start(bf16[2,256,1024]{2,1,0:T(8,128)(2,1)} %get-tuple-element.130), channel_id=1, source_target_pairs={{0,2},{1,3},{2,0},{3,1},{4,6},{5,7},{6,4},{7,5},{8,10},{9,11},{10,... | collective-permute-start | bytes 3145736 | tf_op jit(solution)/shard_map/ppermute | solution.py:758
  126.9 4.6 %collective-permute-start.21 = (bf16[2,256,1024]{2,1,0:T(8,128)(2,1)}, bf16[2,256,1024]{2,1,0:T(8,128)(2,1)S(1)}, u32[]{:S(2)}, u32[]{:S(2)}) collective-permute-start(bf16[2,256,1024]{2,1,0:T(8,128)(2,1)} %get-tuple-element.132), channel_id=1, source_target_pairs={{0,2},{1,3},{2,0},{3,1},{4,6},{5,7},{6,4},{7,5},{8,10},{9,11},{10,... | collective-permute-start | bytes 3145736 | tf_op jit(solution)/shard_map/ppermute | solution.py:758
  127.9 23.0 %collective-permute-start.24 = (bf16[128,512]{1,0:T(8,128)(2,1)}, bf16[128,512]{1,0:T(8,128)(2,1)S(1)}, u32[]{:S(2)}, u32[]{:S(2)}) collective-permute-start(bf16[128,512]{1,0:T(8,128)(2,1)} %get-tuple-element.155), channel_id=1, source_target_pairs={{0,8},{1,9},{2,10},{3,11},{4,12},{5,13},{6,14},{7,15},{8,0},{9,1},... | collective-permute-start | bytes 393224 | tf_op jit(solution)/shard_map/ppermute | solution.py:758
  128.3 22.7 %collective-permute-start.25 = (bf16[128,512]{1,0:T(8,128)(2,1)}, bf16[128,512]{1,0:T(8,128)(2,1)S(1)}, u32[]{:S(2)}, u32[]{:S(2)}) collective-permute-start(bf16[128,512]{1,0:T(8,128)(2,1)} %get-tuple-element.154), channel_id=1, source_target_pairs={{0,16},{1,17},{2,18},{3,19},{4,20},{5,21},{6,22},{7,23},{8,24},{9,... | collective-permute-start | bytes 393224 | tf_op jit(solution)/shard_map/ppermute | solution.py:758
  131.5 19.5 %collective-permute-start.26 = (bf16[128,512]{1,0:T(8,128)(2,1)}, bf16[128,512]{1,0:T(8,128)(2,1)S(1)}, u32[]{:S(2)}, u32[]{:S(2)}) collective-permute-start(bf16[128,512]{1,0:T(8,128)(2,1)} %get-tuple-element.153), channel_id=1, source_target_pairs={{0,24},{1,25},{2,26},{3,27},{4,28},{5,29},{6,30},{7,31},{8,16},{9,... | collective-permute-start | bytes 393224 | tf_op jit(solution)/shard_map/ppermute | solution.py:758
  132.8 4.5 %copy-start.5 = (f32[8,512]{1,0:T(8,128)S(1)}, f32[8,512]{1,0:T(8,128)}, u32[]{:S(2)}) copy-start(f32[8,512]{1,0:T(8,128)} %get-tuple-element.137.refs_17_) | copy-start | bytes 49156
  136.5 14.5 %collective-permute-start.23 = (bf16[2,128,1024]{2,1,0:T(8,128)(2,1)}, bf16[2,128,1024]{2,1,0:T(8,128)(2,1)S(1)}, u32[]{:S(2)}, u32[]{:S(2)}) collective-permute-start(bf16[2,128,1024]{2,1,0:T(8,128)(2,1)} %get-tuple-element.134), channel_id=1, source_target_pairs={{0,4},{1,5},{2,6},{3,7},{4,0},{5,1},{6,2},{7,3},{8,12},{9,13},{10,... | collective-permute-start | bytes 1572872 | tf_op jit(solution)/shard_map/ppermute | solution.py:758
  137.0 13.9 %collective-permute-start.22 = (bf16[1,256,1024]{2,1,0:T(8,128)(2,1)}, bf16[1,256,1024]{2,1,0:T(8,128)(2,1)S(1)}, u32[]{:S(2)}, u32[]{:S(2)}) collective-permute-start(bf16[1,256,1024]{2,1,0:T(8,128)(2,1)} %get-tuple-element.133), channel_id=1, source_target_pairs={{0,1},{1,0},{2,3},{3,2},{4,5},{5,4},{6,7},{7,6},{8,9},{9,8},{10,11... | collective-permute-start | bytes 1572872 | tf_op jit(solution)/shard_map/ppermute | solution.py:758
  137.3 13.7 %copy-start.18 = (bf16[2,128,1024]{2,1,0:T(8,128)(2,1)S(1)}, bf16[2,128,1024]{2,1,0:T(8,128)(2,1)}, u32[]{:S(2)}) copy-start(bf16[2,128,1024]{2,1,0:T(8,128)(2,1)} %get-tuple-element.147) | copy-start | bytes 1572868
  137.3 15.8 %copy-start.17 = (bf16[1,256,1024]{2,1,0:T(8,128)(2,1)S(1)}, bf16[1,256,1024]{2,1,0:T(8,128)(2,1)}, u32[]{:S(2)}) copy-start(bf16[1,256,1024]{2,1,0:T(8,128)(2,1)} %get-tuple-element.148) | copy-start | bytes 1572868
  151.0 30.9 %copy-start.25 = (bf16[128,512]{1,0:T(8,128)(2,1)}, bf16[128,512]{1,0:T(8,128)(2,1)S(1)}, u32[]{:S(2)}) copy-start(bf16[128,512]{1,0:T(8,128)(2,1)S(1)} %collective-permute-done.26) | copy-start | bytes 393220
  151.2 2.8 %collective-permute-start.27 = (bf16[1,16,1024]{2,1,0:T(8,128)(2,1)S(1)}, bf16[1,16,1024]{2,1,0:T(8,128)(2,1)S(1)}, u32[]{:S(2)}, u32[]{:S(2)}) collective-permute-start(bf16[1,16,1024]{2,1,0:T(8,128)(2,1)S(1)} %bitcast.58), channel_id=1, source_target_pairs={{0,2},{1,3},{2,0},{3,1},{4,6},{5,7},{6,4},{7,5},{8,10},{9,11},{10,... | collective-permute-start | bytes 98312 | tf_op jit(solution)/shard_map/ppermute | solution.py:758
  153.3 8.0 %collective-permute-start.31 = (bf16[1,128,1024]{2,1,0:T(8,128)(2,1)S(1)}, bf16[1,128,1024]{2,1,0:T(8,128)(2,1)S(1)}, u32[]{:S(2)}, u32[]{:S(2)}) collective-permute-start(bf16[1,128,1024]{2,1,0:T(8,128)(2,1)S(1)} %get-tuple-element.164), channel_id=1, source_target_pairs={{0,8},{1,9},{2,10},{3,11},{4,12},{5,13},{6,14},{7,15},{8,0},{9,1},... | collective-permute-start | bytes 786440 | tf_op jit(solution)/shard_map/ppermute | solution.py:758
  154.0 8.3 %collective-permute-start.28 = (bf16[1,144,1024]{2,1,0:T(8,128)(2,1)S(1)}, bf16[1,144,1024]{2,1,0:T(8,128)(2,1)S(1)}, u32[]{:S(2)}, u32[]{:S(2)}) collective-permute-start(bf16[1,144,1024]{2,1,0:T(8,128)(2,1)S(1)} %pad_maximum_fusion.3), channel_id=1, source_target_pairs={{0,1},{1,0},{2,3},{3,2},{4,5},{5,4},{6,7},{7,6},{8,9},{9,8},{10,11... | collective-permute-start | bytes 884744 | tf_op jit(solution)/shard_map/ppermute | solution.py:758
  161.3 4.3 %collective-permute-start.32 = (bf16[1,64,1024]{2,1,0:T(8,128)(2,1)S(1)}, bf16[1,64,1024]{2,1,0:T(8,128)(2,1)S(1)}, u32[]{:S(2)}, u32[]{:S(2)}) collective-permute-start(bf16[1,64,1024]{2,1,0:T(8,128)(2,1)S(1)} %add_convert_fusion.13), channel_id=1, source_target_pairs={{0,4},{1,5},{2,6},{3,7},{4,0},{5,1},{6,2},{7,3},{8,12},{9,13},{10,... | collective-permute-start | bytes 393224 | tf_op jit(solution)/shard_map/ppermute | solution.py:758
  162.4 5.9 %collective-permute-start.29 = (bf16[1,80,1024]{2,1,0:T(8,128)(2,1)S(1)}, bf16[1,80,1024]{2,1,0:T(8,128)(2,1)S(1)}, u32[]{:S(2)}, u32[]{:S(2)}) collective-permute-start(bf16[1,80,1024]{2,1,0:T(8,128)(2,1)S(1)} %pad_maximum_fusion.6), channel_id=1, source_target_pairs={{0,8},{1,9},{2,10},{3,11},{4,12},{5,13},{6,14},{7,15},{8,0},{9,1},... | collective-permute-start | bytes 491528 | tf_op jit(solution)/shard_map/ppermute | solution.py:758
  165.7 6.0 %collective-permute-start.33 = (bf16[1,64,1024]{2,1,0:T(8,128)(2,1)S(1)}, bf16[1,64,1024]{2,1,0:T(8,128)(2,1)S(1)}, u32[]{:S(2)}, u32[]{:S(2)}) collective-permute-start(bf16[1,64,1024]{2,1,0:T(8,128)(2,1)S(1)} %add_convert_fusion.12), channel_id=1, source_target_pairs={{0,16},{1,17},{2,18},{3,19},{4,20},{5,21},{6,22},{7,23},{8,24},{9,... | collective-permute-start | bytes 393224 | tf_op jit(solution)/shard_map/ppermute | solution.py:758
  168.4 12.6 %collective-permute-start.30 = (bf16[1,80,1024]{2,1,0:T(8,128)(2,1)S(1)}, bf16[1,80,1024]{2,1,0:T(8,128)(2,1)S(1)}, u32[]{:S(2)}, u32[]{:S(2)}) collective-permute-start(bf16[1,80,1024]{2,1,0:T(8,128)(2,1)S(1)} %pad_maximum_fusion.7), channel_id=1, source_target_pairs={{0,16},{1,17},{2,18},{3,19},{4,20},{5,21},{6,22},{7,23},{8,24},{9,... | collective-permute-start | bytes 491528 | tf_op jit(solution)/shard_map/ppermute | solution.py:758
  181.1 3.9 %collective-permute-start.38 = (bf16[1,64,1024]{2,1,0:T(8,128)(2,1)S(1)}, bf16[1,64,1024]{2,1,0:T(8,128)(2,1)S(1)}, u32[]{:S(2)}, u32[]{:S(2)}) collective-permute-start(bf16[1,64,1024]{2,1,0:T(8,128)(2,1)S(1)} %add_convert_fusion.10), channel_id=1, source_target_pairs={{0,8},{1,9},{2,10},{3,11},{4,12},{5,13},{6,14},{7,15},{8,0},{9,1},... | collective-permute-start | bytes 393224 | tf_op jit(solution)/shard_map/ppermute | solution.py:758
  181.9 4.7 %collective-permute-start.34 = (bf16[1,80,1024]{2,1,0:T(8,128)(2,1)S(1)}, bf16[1,80,1024]{2,1,0:T(8,128)(2,1)S(1)}, u32[]{:S(2)}, u32[]{:S(2)}) collective-permute-start(bf16[1,80,1024]{2,1,0:T(8,128)(2,1)S(1)} %pad_maximum_fusion.8), channel_id=1, source_target_pairs={{0,4},{1,5},{2,6},{3,7},{4,0},{5,1},{6,2},{7,3},{8,12},{9,13},{10,... | collective-permute-start | bytes 491528 | tf_op jit(solution)/shard_map/ppermute | solution.py:758
  185.7 7.5 %collective-permute-start.39 = (bf16[1,128,1024]{2,1,0:T(8,128)(2,1)S(1)}, bf16[1,128,1024]{2,1,0:T(8,128)(2,1)S(1)}, u32[]{:S(2)}, u32[]{:S(2)}) collective-permute-start(bf16[1,128,1024]{2,1,0:T(8,128)(2,1)S(1)} %get-tuple-element.171), channel_id=1, source_target_pairs={{0,4},{1,5},{2,6},{3,7},{4,0},{5,1},{6,2},{7,3},{8,12},{9,13},{10,... | collective-permute-start | bytes 786440 | tf_op jit(solution)/shard_map/ppermute | solution.py:758
  187.4 7.4 %collective-permute-start.35 = (bf16[1,128,1024]{2,1,0:T(8,128)(2,1)S(1)}, bf16[1,128,1024]{2,1,0:T(8,128)(2,1)S(1)}, u32[]{:S(2)}, u32[]{:S(2)}) collective-permute-start(bf16[1,128,1024]{2,1,0:T(8,128)(2,1)S(1)} %get-tuple-element.173), channel_id=1, source_target_pairs={{0,8},{1,9},{2,10},{3,11},{4,12},{5,13},{6,14},{7,15},{8,0},{9,1},... | collective-permute-start | bytes 786440 | tf_op jit(solution)/shard_map/ppermute | solution.py:758
  190.1 8.0 %collective-permute-start.40 = (bf16[1,128,1024]{2,1,0:T(8,128)(2,1)S(1)}, bf16[1,128,1024]{2,1,0:T(8,128)(2,1)S(1)}, u32[]{:S(2)}, u32[]{:S(2)}) collective-permute-start(bf16[1,128,1024]{2,1,0:T(8,128)(2,1)S(1)} %get-tuple-element.171), channel_id=1, source_target_pairs={{0,2},{1,3},{2,0},{3,1},{4,6},{5,7},{6,4},{7,5},{8,10},{9,11},{10,... | collective-permute-start | bytes 786440 | tf_op jit(solution)/shard_map/ppermute | solution.py:758
  193.2 4.9 %collective-permute-start.36 = (bf16[1,128,1024]{2,1,0:T(8,128)(2,1)S(1)}, bf16[1,128,1024]{2,1,0:T(8,128)(2,1)S(1)}, u32[]{:S(2)}, u32[]{:S(2)}) collective-permute-start(bf16[1,128,1024]{2,1,0:T(8,128)(2,1)S(1)} %get-tuple-element.173), channel_id=1, source_target_pairs={{0,2},{1,3},{2,0},{3,1},{4,6},{5,7},{6,4},{7,5},{8,10},{9,11},{10,... | collective-permute-start | bytes 786440 | tf_op jit(solution)/shard_map/ppermute | solution.py:758
  193.2 5.0 %copy-start.19 = (bf16[1,128,1024]{2,1,0:T(8,128)(2,1)}, bf16[1,128,1024]{2,1,0:T(8,128)(2,1)S(1)}, u32[]{:S(2)}) copy-start(bf16[1,128,1024]{2,1,0:T(8,128)(2,1)S(1)} %collective-permute-done.39) | copy-start | bytes 786436
  193.2 4.9 %collective-permute-start.41 = (bf16[1,128,1024]{2,1,0:T(8,128)(2,1)S(1)}, bf16[1,128,1024]{2,1,0:T(8,128)(2,1)S(1)}, u32[]{:S(2)}, u32[]{:S(2)}) collective-permute-start(bf16[1,128,1024]{2,1,0:T(8,128)(2,1)S(1)} %collective-permute-done.39), channel_id=1, source_target_pairs={{0,2},{1,3},{2,0},{3,1},{4,6},{5,7},{6,4},{7,5},{8,10},{9,11},{10,... | collective-permute-start | bytes 786440 | tf_op jit(solution)/shard_map/ppermute | solution.py:758
  194.8 3.3 %collective-permute-start.37 = (bf16[1,128,1024]{2,1,0:T(8,128)(2,1)S(1)}, bf16[1,128,1024]{2,1,0:T(8,128)(2,1)S(1)}, u32[]{:S(2)}, u32[]{:S(2)}) collective-permute-start(bf16[1,128,1024]{2,1,0:T(8,128)(2,1)S(1)} %collective-permute-done.35), channel_id=1, source_target_pairs={{0,2},{1,3},{2,0},{3,1},{4,6},{5,7},{6,4},{7,5},{8,10},{9,11},{10,... | collective-permute-start | bytes 786440 | tf_op jit(solution)/shard_map/ppermute | solution.py:758
  (9 other events, 12.9 us)

commit v7 on v6

--- a/solution.py
+++ b/solution.py
@@ -294,7 +294,7 @@
     else:
         dense_in, cotangent = dense_ref[...], cotangent_ref[...]
     dense_t, cotangent_t = dense_in.T, cotangent.T
-    joined = max(1, 512 // (shards * half))
+    joined = max(1, 256 // (shards * half))
     chunks = range(0, pieces, joined)
 
     def weights(chunk):

time: 203 us -> 203 us (level)
  no operation moved by 1% of the time
where the time goes in v7:
time: 203 us
  Pallas kernels  119 us (59%)
  starting transfers between devices  43.3 us (21%)
  waiting for transfers between devices  27.6 us (14%)
  other arithmetic  6.33 us (3%)
  local copies, waits for them, and re-layouts  5.21 us (3%)
    pallas_call x2, Pallas kernels, dense_both(): pl.pallas_call(functools.partial(dense_kernel, stage, sets, len(pieces)),...  48.5 us
    ppermute x42, starting transfers between devices, swap(): return lax.ppermute(values, ('dp', 'tensor'), pairs)  43.3 us
    ppermute x42, waiting for transfers between devices, swap(): return lax.ppermute(values, ('dp', 'tensor'), pairs)  27.6 us
    pallas_call x2, Pallas kernels, mixer_forward(): pl.pallas_call(functools.partial(mixer_kernel, first), grid=(2, blocks),...  26.7 us
    pallas_call x1, Pallas kernels, mixer_backward(): pl.pallas_call(functools.partial(mixer_back_kernel, sets), grid=(2, block...  20.2 us
    pallas_call x1, Pallas kernels, input_backward(): pl.pallas_call(functools.partial(input_kernel, sets), grid=(rows // BLOCK...  13.6 us
  transfers between devices with their start and end apart: 42, of which 11 were waited for; matrix products, arithmetic and copies ran while one was open for 4% of the time, Pallas kernels for 56%

profile of v7, /device:TPU:1, one launch (start us, length us, event | category | flops | bytes accessed | tf_op | source)
XLA Modules:
  0.0 202.7 jit_solution(9980177380367128306)
XLA Ops:
  0.7 2.3 %pack_halves.1 = (bf16[3,256,512]{2,1,0:T(8,128)(2,1)}, bf16[256,512]{1,0:T(8,128)(2,1)}) custom-call(s32[1]{0:T(128)} %bitcast.7.refs_0_, bf16[512,512]{1,0:T(8,128)(2,1)} %refs_11_.1, bf16[512,512]{1,0:T(8,128)(2,1)} %refs_12_.1, bf16[512,512]{1,0:T(8,128)(2,1)} %refs_13_.1, bf16[512,512]{1,0:T(8,128)(2,1)} %refs_0_.1), custom_call_target="tpu_custom_call" | custom-call | tf_op jit(solution)/shard_map/pack_halves/pallas_call | solution.py:734
  3.1 2.0 %collective-permute-start = (bf16[3,256,512]{2,1,0:T(8,128)(2,1)}, bf16[3,256,512]{2,1,0:T(8,128)(2,1)S(1)}, u32[]{:S(2)}, u32[]{:S(2)}) collective-permute-start(bf16[3,256,512]{2,1,0:T(8,128)(2,1)} %get-tuple-element.84), channel_id=1, source_target_pairs={{0,1},{1,0},{2,3},{3,2},{4,5},{5,4},{6,7},{7,6},{8,9},{9,8},{10,11... | collective-permute-start | bytes 2359304 | tf_op jit(solution)/shard_map/ppermute | solution.py:758
  5.1 1.4 collective-permute-start.1
  6.5 2.3 %collective-permute-start.2 = (bf16[128,512]{1,0:T(8,128)(2,1)S(1)}, bf16[128,512]{1,0:T(8,128)(2,1)}, u32[]{:S(2)}, u32[]{:S(2)}) collective-permute-start(bf16[128,512]{1,0:T(8,128)(2,1)S(1)} %pad_maximum_fusion.9), channel_id=1, source_target_pairs={{0,16},{1,17},{2,18},{3,19},{4,20},{5,21},{6,22},{7,23},{8,24},{9,... | collective-permute-start | bytes 393224 | tf_op jit(solution)/shard_map/ppermute | solution.py:758
  9.2 14.0 %mixer_forward.2 = (bf16[2048,512]{1,0:T(8,128)(2,1)}, bf16[2048,512]{1,0:T(8,128)(2,1)}, bf16[2048,512]{1,0:T(8,128)(2,1)}, bf16[2048,512]{1,0:T(8,128)(2,1)}, ...) custom-call(bf16[8,256,512]{2,1,0:T(8,128)(2,1)} %bitcast.77, f32[1,512]{1,0:T(1,128)S(1)} %bitcast.60, ...), custom_call_target="tpu_custom_call" | custom-call | flops 3221225472 | bytes 16777216 | tf_op jit(solution)/shard_map/mixer_forward/pallas_call | solution.py:243
  23.2 1.9 collective-permute-start.5
  25.1 1.0 pad_maximum_fusion.2.refs_8_
  26.1 1.5 collective-permute-start.8
  27.6 1.2 collective-permute-start.6
  29.1 12.8 %mixer_forward.3 = (bf16[2048,512]{1,0:T(8,128)(2,1)}, bf16[2048,512]{1,0:T(8,128)(2,1)}, bf16[2048,512]{1,0:T(8,128)(2,1)}, bf16[2048,512]{1,0:T(8,128)(2,1)}, f32[8,512]{1,0:T(8,128)}) custom-call(bf16[2048,512]{1,0:T(8,128)(2,1)} %get-tuple-element.83.refs_0_.normed_ref, bf16[512,512]{1,0:T(8,128)(2,1)S(1)} %get-tuple-element.159.refs_1_.refs_14_, ...), custom_call_target="tpu_custom_call" | custom-call | flops 3221225472 | bytes 16777216 | tf_op jit(solution)/shard_map/mixer_forward/pallas_call | solution.py:243
  41.8 0.7 collective-permute-start.7
  42.6 0.4 collective-permute-start.10
  43.0 0.3 collective-permute-start.11
  43.3 1.1 collective-permute-start.12
  44.5 0.6 collective-permute-done.10.refs_11_
  45.2 23.0 %dense_first.1 = (bf16[8,128,512]{2,1,0:T(8,128)(2,1)}, bf16[8,128,512]{2,1,0:T(8,128)(2,1)}, bf16[2048,512]{1,0:T(8,128)(2,1)}, bf16[2048,512]{1,0:T(8,128)(2,1...) custom-call(bf16[2048,512]{1,0:T(8,128)(2,1)} %get-tuple-element.82.refs_0_, ...), custom_call_target="tpu_custom_call" | custom-call | flops 12884901888 | bytes 25165824 | tf_op jit(solution)/shard_map/dense_first/pallas_call | solution.py:406
  68.2 0.4 collective-permute-start.13
  68.8 1.4 collective-permute-done.13.refs_11_
  70.2 0.7 collective-permute-done.14.refs_12_
  71.0 0.4 collective-permute-start.15
  71.3 25.5 %dense_second.1 = (bf16[8,128,512]{2,1,0:T(8,128)(2,1)}, bf16[8,128,512]{2,1,0:T(8,128)(2,1)}, bf16[8,256,512]{2,1,0:T(8,128)(2,1)}, bf16[2048,512]{1,0:T(8,128)...) custom-call(bf16[2048,512]{1,0:T(8,128)(2,1)} %get-tuple-element.82.refs_0_, ...), custom_call_target="tpu_custom_call" | custom-call | flops 12884901888 | bytes 25165824 | tf_op jit(solution)/shard_map/dense_second/pallas_call | solution.py:406
  97.2 1.2 collective-permute-start.18
  98.4 1.4 collective-permute-done.16
  100.1 1.2 collective-permute-start.19
  101.3 1.2 collective-permute-start.17
  102.5 20.2 %mixer_backward.1 = (bf16[2048,512]{1,0:T(8,128)(2,1)}, bf16[2048,512]{1,0:T(8,128)(2,1)}, bf16[2,256,1024]{2,1,0:T(8,128)(2,1)S(1)}, bf16[2,256,1024]{2,1,0:T(8...) custom-call(bf16[2048,512]{1,0:T(8,128)(2,1)} %get-tuple-element.116, ...), custom_call_target="tpu_custom_call" | custom-call | flops 8589934592 | bytes 25165824 | tf_op jit(solution)/shard_map/mixer_backward/pallas_call | solution.py:558
  122.7 1.0 copy-done
  123.7 2.0 collective-permute-done.17
  125.7 1.0 collective-permute-start.20
  126.6 1.0 fusion.10
  127.6 0.4 collective-permute-start.24
  128.0 3.2 %collective-permute-start.25 = (bf16[128,512]{1,0:T(8,128)(2,1)}, bf16[128,512]{1,0:T(8,128)(2,1)S(1)}, u32[]{:S(2)}, u32[]{:S(2)}) collective-permute-start(bf16[128,512]{1,0:T(8,128)(2,1)} %get-tuple-element.154), channel_id=1, source_target_pairs={{0,16},{1,17},{2,18},{3,19},{4,20},{5,21},{6,22},{7,23},{8,24},{9,... | collective-permute-start | bytes 393224 | tf_op jit(solution)/shard_map/ppermute | solution.py:758
  131.3 0.9 copy-done.10
  132.2 0.3 copy-done.11
  132.5 3.7 %paired_sums.1 = (bf16[1,256,1024]{2,1,0:T(8,128)(2,1)}, bf16[2,128,1024]{2,1,0:T(8,128)(2,1)}, bf16[1,256,1024]{2,1,0:T(8,128)(2,1)}, bf16[2,128,1024]{2,1,0:T(8,128)(2,1)}) custom-call(bf16[2,256,1024]{2,1,0:T(8,128)(2,1)} %copy-done, bf16[2,256,1024]{2,1,0:T(8,128)(2,1)} %copy-done.10, bf16[2,256,1024]{2,1,0:T(8,128)(2,1)} %get-tuple-element.131.refs_2_.refs_6_, ...), custom_call_target="tpu_custom_call" | custom-call | tf_op jit(solution)/shard_map/paired_sums/pallas_call | solution.py:705
  136.2 0.3 collective-permute-start.23
  136.8 13.6 %input_backward.1 = (f32[8,256,512]{2,1,0:T(8,128)}, bf16[16,1024]{1,0:T(8,128)(2,1)S(1)}) custom-call(bf16[2048,512]{1,0:T(8,128)(2,1)} %get-tuple-element.90.refs_2_.refs_0_, bf16[2048,512]{1,0:T(8,128)(2,1)} %get-tuple-element.116.mixed_ref.refs_1_, f32[1,512]{1,0:T(1,128)S(1)} %bitcast.61, bf16[2048,512]{1,0:T(8,128)(2,1)} %get-tuple-element.135.refs_3_, ...), custom_call_target="tpu_custom_call" | custom-call | flops 6442450944 | bytes 16777216 | tf_op jit(solution)/shard_map/input_backward/pallas_call | solution.py:632
  150.7 1.9 collective-permute-start.27
  152.9 0.5 collective-permute-done.27
  153.5 1.3 collective-permute-start.28
  154.8 6.0 %collective-permute-done.31 = bf16[1,128,1024]{2,1,0:T(8,128)(2,1)S(1)} collective-permute-done((bf16[1,128,1024]{2,1,0:T(8,128)(2,1)S(1)}, bf16[1,128,1024]{2,1,0:T(8,128)(2,1)S(1)}, u32[]{:S(2)}, u32[]{:S(2)}) %collective-permute-start.31) | collective-permute-done | bytes 262176 | tf_op jit(solution)/shard_map/ppermute | solution.py:758
  160.8 1.2 collective-permute-start.32
  162.1 0.8 collective-permute-start.29
  162.9 2.2 %collective-permute-done.32 = bf16[1,64,1024]{2,1,0:T(8,128)(2,1)S(1)} collective-permute-done((bf16[1,64,1024]{2,1,0:T(8,128)(2,1)S(1)}, bf16[1,64,1024]{2,1,0:T(8,128)(2,1)S(1)}, u32[]{:S(2)}, u32[]{:S(2)}) %collective-permute-start.32) | collective-permute-done | bytes 131104 | tf_op jit(solution)/shard_map/ppermute | solution.py:758
  165.2 2.6 %collective-permute-start.33 = (bf16[1,64,1024]{2,1,0:T(8,128)(2,1)S(1)}, bf16[1,64,1024]{2,1,0:T(8,128)(2,1)S(1)}, u32[]{:S(2)}, u32[]{:S(2)}) collective-permute-start(bf16[1,64,1024]{2,1,0:T(8,128)(2,1)S(1)} %add_convert_fusion.12), channel_id=1, source_target_pairs={{0,16},{1,17},{2,18},{3,19},{4,20},{5,21},{6,22},{7,23},{8,24},{9,... | collective-permute-start | bytes 393224 | tf_op jit(solution)/shard_map/ppermute | solution.py:758
  167.9 1.8 collective-permute-start.30
  169.8 1.4 collective-permute-done.33
  171.2 9.3 %collective-permute-done.30 = bf16[1,80,1024]{2,1,0:T(8,128)(2,1)S(1)} collective-permute-done((bf16[1,80,1024]{2,1,0:T(8,128)(2,1)S(1)}, bf16[1,80,1024]{2,1,0:T(8,128)(2,1)S(1)}, u32[]{:S(2)}, u32[]{:S(2)}) %collective-permute-start.30) | collective-permute-done | bytes 163872 | tf_op jit(solution)/shard_map/ppermute | solution.py:758
  180.6 0.8 collective-permute-start.38
  181.4 1.2 collective-permute-start.34
  182.6 1.9 collective-permute-done.38
  184.5 0.8 pad_maximum_fusion.5
  185.2 1.1 collective-permute-start.39
  186.4 0.8 pad_maximum_fusion.4
  187.1 0.7 collective-permute-start.35
  187.9 1.2 fusion.11
  189.1 0.7 fusion.17
  189.8 2.9 %collective-permute-start.40 = (bf16[1,128,1024]{2,1,0:T(8,128)(2,1)S(1)}, bf16[1,128,1024]{2,1,0:T(8,128)(2,1)S(1)}, u32[]{:S(2)}, u32[]{:S(2)}) collective-permute-start(bf16[1,128,1024]{2,1,0:T(8,128)(2,1)S(1)} %get-tuple-element.171), channel_id=1, source_target_pairs={{0,2},{1,3},{2,0},{3,1},{4,6},{5,7},{6,4},{7,5},{8,10},{9,11},{10,... | collective-permute-start | bytes 786440 | tf_op jit(solution)/shard_map/ppermute | solution.py:758
  192.7 1.7 collective-permute-start.41
  194.3 2.2 %collective-permute-start.37 = (bf16[1,128,1024]{2,1,0:T(8,128)(2,1)S(1)}, bf16[1,128,1024]{2,1,0:T(8,128)(2,1)S(1)}, u32[]{:S(2)}, u32[]{:S(2)}) collective-permute-start(bf16[1,128,1024]{2,1,0:T(8,128)(2,1)S(1)} %collective-permute-done.35), channel_id=1, source_target_pairs={{0,2},{1,3},{2,0},{3,1},{4,6},{5,7},{6,4},{7,5},{8,10},{9,11},{10,... | collective-permute-start | bytes 786440 | tf_op jit(solution)/shard_map/ppermute | solution.py:758
  196.5 0.6 fusion.14
  197.1 0.7 constant_dynamic-slice_fusion.1
  197.9 0.7 copy-done.21
  198.8 4.0 %finish_slopes.1 = (f32[512,512]{1,0:T(8,128)}, f32[512,512]{1,0:T(8,128)}, f32[512,512]{1,0:T(8,128)}, f32[512,512]{1,0:T(8,128)}) custom-call(bf16[128,1024]{1,0:T(8,128)(2,1)} %get-tuple-element.174.refs_0_, bf16[128,1024]{1,0:T(8,128)(2,1)} %bitcast.68, bf16[128,1024]{1,0:T(8,128)(2,1)} %bitcast.70, bf16[128,1024]{1,0:T(8,128)(2,1)} %bitcast.72, ...), custom_call_target="tpu_custom_call" | custom-call | tf_op jit(solution)/shard_map/finish_slopes/pallas_call | solution.py:667
  (130 shorter events, 3.1 us)
Async XLA Ops:
  0.6 8.5 %copy-start.1 = (bf16[512,512]{1,0:T(8,128)(2,1)S(1)}, bf16[512,512]{1,0:T(8,128)(2,1)}, u32[]{:S(2)}) copy-start(bf16[512,512]{1,0:T(8,128)(2,1)} %refs_11_.1) | copy-start | bytes 1572868
  0.7 8.5 %copy-start.2 = (bf16[512,512]{1,0:T(8,128)(2,1)S(1)}, bf16[512,512]{1,0:T(8,128)(2,1)}, u32[]{:S(2)}) copy-start(bf16[512,512]{1,0:T(8,128)(2,1)} %refs_12_.1) | copy-start | bytes 1572868
  0.7 8.5 %copy-start.3 = (bf16[512,512]{1,0:T(8,128)(2,1)S(1)}, bf16[512,512]{1,0:T(8,128)(2,1)}, u32[]{:S(2)}) copy-start(bf16[512,512]{1,0:T(8,128)(2,1)} %refs_13_.1) | copy-start | bytes 1572868
  0.7 4.4 %copy-start.27 = (bf16[512,64]{0,1:T(8,128)(2,1)S(1)}, bf16[512,64]{0,1:T(8,128)(2,1)}, u32[]{:S(2)}) copy-start(bf16[512,64]{0,1:T(8,128)(2,1)} %param.22) | copy-start | bytes 196612
  0.7 4.4 %copy-start.26 = (bf16[64,512]{1,0:T(8,128)(2,1)S(1)}, bf16[64,512]{1,0:T(8,128)(2,1)}, u32[]{:S(2)}) copy-start(bf16[64,512]{1,0:T(8,128)(2,1)} %param.23) | copy-start | bytes 196612
  0.7 8.1 %copy-start.29 = (bf16[512]{0:T(512)(128)(2,1)S(1)}, bf16[512]{0:T(512)(128)(2,1)}, u32[]{:S(2)}) copy-start(bf16[512]{0:T(512)(128)(2,1)} %param.19) | copy-start | bytes 3076
  0.7 8.3 %copy-start.28 = (bf16[512]{0:T(512)(128)(2,1)S(1)}, bf16[512]{0:T(512)(128)(2,1)}, u32[]{:S(2)}) copy-start(bf16[512]{0:T(512)(128)(2,1)} %param.15) | copy-start | bytes 3076
  0.7 8.4 %copy-start.7 = (s32[1,8]{1,0:T(1,128)S(1)}, s32[1,8]{1,0:T(1,128)}, u32[]{:S(2)}) copy-start(s32[1,8]{1,0:T(1,128)} %lengths.1) | copy-start | bytes 100
  3.1 20.1 %collective-permute-start = (bf16[3,256,512]{2,1,0:T(8,128)(2,1)}, bf16[3,256,512]{2,1,0:T(8,128)(2,1)S(1)}, u32[]{:S(2)}, u32[]{:S(2)}) collective-permute-start(bf16[3,256,512]{2,1,0:T(8,128)(2,1)} %get-tuple-element.84), channel_id=1, source_target_pairs={{0,1},{1,0},{2,3},{3,2},{4,5},{5,4},{6,7},{7,6},{8,9},{9,8},{10,11... | collective-permute-start | bytes 2359304 | tf_op jit(solution)/shard_map/ppermute | solution.py:758
  5.1 18.1 %collective-permute-start.1 = (bf16[128,512]{1,0:T(8,128)(2,1)S(1)}, bf16[128,512]{1,0:T(8,128)(2,1)S(1)}, u32[]{:S(2)}, u32[]{:S(2)}) collective-permute-start(bf16[128,512]{1,0:T(8,128)(2,1)S(1)} %pad_maximum_fusion.9), channel_id=1, source_target_pairs={{0,8},{1,9},{2,10},{3,11},{4,12},{5,13},{6,14},{7,15},{8,0},{9,1},... | collective-permute-start | bytes 393224 | tf_op jit(solution)/shard_map/ppermute | solution.py:758
  6.5 16.7 %collective-permute-start.2 = (bf16[128,512]{1,0:T(8,128)(2,1)S(1)}, bf16[128,512]{1,0:T(8,128)(2,1)}, u32[]{:S(2)}, u32[]{:S(2)}) collective-permute-start(bf16[128,512]{1,0:T(8,128)(2,1)S(1)} %pad_maximum_fusion.9), channel_id=1, source_target_pairs={{0,16},{1,17},{2,18},{3,19},{4,20},{5,21},{6,22},{7,23},{8,24},{9,... | collective-permute-start | bytes 393224 | tf_op jit(solution)/shard_map/ppermute | solution.py:758
  8.8 14.4 %collective-permute-start.3 = (bf16[128,512]{1,0:T(8,128)(2,1)S(1)}, bf16[128,512]{1,0:T(8,128)(2,1)}, u32[]{:S(2)}, u32[]{:S(2)}) collective-permute-start(bf16[128,512]{1,0:T(8,128)(2,1)S(1)} %pad_maximum_fusion.9), channel_id=1, source_target_pairs={{0,24},{1,25},{2,26},{3,27},{4,28},{5,29},{6,30},{7,31},{8,16},{9,... | collective-permute-start | bytes 393224 | tf_op jit(solution)/shard_map/ppermute | solution.py:758
  8.8 14.4 %collective-permute-start.4 = (bf16[512]{0:T(512)(128)(2,1)S(1)}, bf16[512]{0:T(512)(128)(2,1)S(1)}, u32[]{:S(2)}, u32[]{:S(2)}) collective-permute-start(bf16[512]{0:T(512)(128)(2,1)S(1)} %copy-done.29), channel_id=1, source_target_pairs={{0,1},{1,0},{2,3},{3,2},{4,5},{5,4},{6,7},{7,6},{8,9},{9,8},{10,11... | collective-permute-start | bytes 3080 | tf_op jit(solution)/shard_map/ppermute | solution.py:758
  9.1 127.7 %copy-start.6 = (s32[4]{0:T(128)}, s32[4]{0:T(128)S(1)}, u32[]{:S(2)}) copy-start(s32[4]{0:T(128)S(1)} %pad_add_fusion.refs_7_.refs_6_.refs_8_.scalars.refs_19_) | copy-start | bytes 52
  23.2 5.6 %collective-permute-start.5 = (bf16[3,256,512]{2,1,0:T(8,128)(2,1)S(1)}, bf16[3,256,512]{2,1,0:T(8,128)(2,1)S(1)}, u32[]{:S(2)}, u32[]{:S(2)}) collective-permute-start(bf16[3,256,512]{2,1,0:T(8,128)(2,1)S(1)} %collective-permute-done), channel_id=1, source_target_pairs={{0,2},{1,3},{2,0},{3,1},{4,6},{5,7},{6,4},{7,5},{8,10},{9,11},{10,... | collective-permute-start | bytes 2359304 | tf_op jit(solution)/shard_map/ppermute | solution.py:758
  26.1 16.5 %collective-permute-start.8 = (bf16[4,128,512]{2,1,0:T(8,128)(2,1)S(1)}, bf16[4,128,512]{2,1,0:T(8,128)(2,1)S(1)}, u32[]{:S(2)}, u32[]{:S(2)}) collective-permute-start(bf16[4,128,512]{2,1,0:T(8,128)(2,1)S(1)} %pad_maximum_fusion.2.refs_8_), channel_id=1, source_target_pairs={{0,4},{1,5},{2,6},{3,7},{4,0},{5,1},{6,2},{7,3},{8,12},{9,13},{10,... | collective-permute-start | bytes 1572872 | tf_op jit(solution)/shard_map/ppermute | solution.py:758
  27.6 14.2 %collective-permute-start.6 = (bf16[256,512]{1,0:T(8,128)(2,1)}, bf16[256,512]{1,0:T(8,128)(2,1)S(1)}, u32[]{:S(2)}, u32[]{:S(2)}) collective-permute-start(bf16[256,512]{1,0:T(8,128)(2,1)} %get-tuple-element.92), channel_id=1, source_target_pairs={{0,1},{1,0},{2,3},{3,2},{4,5},{5,4},{6,7},{7,6},{8,9},{9,8},{10,11... | collective-permute-start | bytes 786440 | tf_op jit(solution)/shard_map/ppermute | solution.py:758
  29.1 13.9 %copy-start.30 = (bf16[512]{0:T(512)(128)(2,1)S(1)}, bf16[512]{0:T(512)(128)(2,1)}, u32[]{:S(2)}) copy-start(bf16[512]{0:T(512)(128)(2,1)} %param.21) | copy-start | bytes 3076
  41.8 2.6 %collective-permute-start.7 = (bf16[256,512]{1,0:T(8,128)(2,1)S(1)}, bf16[256,512]{1,0:T(8,128)(2,1)S(1)}, u32[]{:S(2)}, u32[]{:S(2)}) collective-permute-start(bf16[256,512]{1,0:T(8,128)(2,1)S(1)} %collective-permute-done.6), channel_id=1, source_target_pairs={{0,2},{1,3},{2,0},{3,1},{4,6},{5,7},{6,4},{7,5},{8,10},{9,11},{10,... | collective-permute-start | bytes 786440 | tf_op jit(solution)/shard_map/ppermute | solution.py:758
  42.5 2.0 %collective-permute-start.9 = (bf16[4,128,512]{2,1,0:T(8,128)(2,1)S(1)}, bf16[4,128,512]{2,1,0:T(8,128)(2,1)S(1)}, u32[]{:S(2)}, u32[]{:S(2)}) collective-permute-start(bf16[4,128,512]{2,1,0:T(8,128)(2,1)S(1)} %pad_maximum_fusion.2.refs_8_), channel_id=1, source_target_pairs={{0,2},{1,3},{2,0},{3,1},{4,6},{5,7},{6,4},{7,5},{8,10},{9,11},{10,... | collective-permute-start | bytes 1572872 | tf_op jit(solution)/shard_map/ppermute | solution.py:758
  42.6 2.6 %collective-permute-start.10 = (bf16[4,128,512]{2,1,0:T(8,128)(2,1)S(1)}, bf16[4,128,512]{2,1,0:T(8,128)(2,1)S(1)}, u32[]{:S(2)}, u32[]{:S(2)}) collective-permute-start(bf16[4,128,512]{2,1,0:T(8,128)(2,1)S(1)} %collective-permute-done.8.refs_9_), channel_id=1, source_target_pairs={{0,2},{1,3},{2,0},{3,1},{4,6},{5,7},{6,4},{7,5},{8,10},{9,11},{10,... | collective-permute-start | bytes 1572872 | tf_op jit(solution)/shard_map/ppermute | solution.py:758
  43.0 25.2 %collective-permute-start.11 = (bf16[4,128,512]{2,1,0:T(8,128)(2,1)S(1)}, bf16[4,128,512]{2,1,0:T(8,128)(2,1)S(1)}, u32[]{:S(2)}, u32[]{:S(2)}) collective-permute-start(bf16[4,128,512]{2,1,0:T(8,128)(2,1)S(1)} %pad_maximum_fusion.2.refs_8_), channel_id=1, source_target_pairs={{0,5},{1,4},{2,7},{3,6},{4,1},{5,0},{6,3},{7,2},{8,13},{9,12},{10,... | collective-permute-start | bytes 1572872 | tf_op jit(solution)/shard_map/ppermute | solution.py:758
  43.3 24.9 %collective-permute-start.12 = (bf16[4,128,512]{2,1,0:T(8,128)(2,1)S(1)}, bf16[4,128,512]{2,1,0:T(8,128)(2,1)S(1)}, u32[]{:S(2)}, u32[]{:S(2)}) collective-permute-start(bf16[4,128,512]{2,1,0:T(8,128)(2,1)S(1)} %pad_maximum_fusion.2.refs_8_), channel_id=1, source_target_pairs={{0,1},{1,0},{2,3},{3,2},{4,5},{5,4},{6,7},{7,6},{8,9},{9,8},{10,11... | collective-permute-start | bytes 1572872 | tf_op jit(solution)/shard_map/ppermute | solution.py:758
  68.2 2.0 collective-permute-start.13
  68.7 2.3 %collective-permute-start.14 = (bf16[4,128,512]{2,1,0:T(8,128)(2,1)S(1)}, bf16[4,128,512]{2,1,0:T(8,128)(2,1)S(1)}, u32[]{:S(2)}, u32[]{:S(2)}) collective-permute-start(bf16[4,128,512]{2,1,0:T(8,128)(2,1)S(1)} %collective-permute-done.11.refs_10_), channel_id=1, source_target_pairs={{0,2},{1,3},{2,0},{3,1},{4,6},{5,7},{6,4},{7,5},{8,10},{9,11},{10,... | collective-permute-start | bytes 1572872 | tf_op jit(solution)/shard_map/ppermute | solution.py:758
  71.0 25.9 %collective-permute-start.15 = (bf16[8,128,512]{2,1,0:T(8,128)(2,1)}, bf16[8,128,512]{2,1,0:T(8,128)(2,1)S(1)}, u32[]{:S(2)}, u32[]{:S(2)}) collective-permute-start(bf16[8,128,512]{2,1,0:T(8,128)(2,1)} %get-tuple-element.112), channel_id=1, source_target_pairs={{0,2},{1,3},{2,0},{3,1},{4,6},{5,7},{6,4},{7,5},{8,10},{9,11},{10,... | collective-permute-start | bytes 3145736 | tf_op jit(solution)/shard_map/ppermute | solution.py:758
  71.3 25.7 %copy-start.12 = (bf16[8,128,512]{2,1,0:T(8,128)(2,1)S(1)}, bf16[8,128,512]{2,1,0:T(8,128)(2,1)}, u32[]{:S(2)}) copy-start(bf16[8,128,512]{2,1,0:T(8,128)(2,1)} %get-tuple-element.115) | copy-start | bytes 3145732
  96.8 29.8 %copy-start.13 = (bf16[8,128,512]{2,1,0:T(8,128)(2,1)}, bf16[8,128,512]{2,1,0:T(8,128)(2,1)S(1)}, u32[]{:S(2)}) copy-start(bf16[8,128,512]{2,1,0:T(8,128)(2,1)S(1)} %collective-permute-done.15) | copy-start | bytes 3145732
  96.9 2.9 %collective-permute-start.16 = (bf16[8,128,512]{2,1,0:T(8,128)(2,1)}, bf16[8,128,512]{2,1,0:T(8,128)(2,1)S(1)}, u32[]{:S(2)}, u32[]{:S(2)}) collective-permute-start(bf16[8,128,512]{2,1,0:T(8,128)(2,1)} %get-tuple-element.114), channel_id=1, source_target_pairs={{0,2},{1,3},{2,0},{3,1},{4,6},{5,7},{6,4},{7,5},{8,10},{9,11},{10,... | collective-permute-start | bytes 3145736 | tf_op jit(solution)/shard_map/ppermute | solution.py:758
  97.1 5.4 %copy-start.8 = (bf16[512,512]{1,0:T(8,128)(2,1)S(1)}, bf16[512,512]{1,0:T(8,128)(2,1)}, u32[]{:S(2)}) copy-start(bf16[512,512]{1,0:T(8,128)(2,1)} %get-tuple-element.120.refs_5_) | copy-start | bytes 1572868
  97.1 5.4 %copy-start.9 = (bf16[512,512]{1,0:T(8,128)(2,1)S(1)}, bf16[512,512]{1,0:T(8,128)(2,1)}, u32[]{:S(2)}) copy-start(bf16[512,512]{1,0:T(8,128)(2,1)} %get-tuple-element.124.refs_11_) | copy-start | bytes 1572868
  97.2 26.4 %collective-permute-start.18 = (bf16[4,128,512]{2,1,0:T(8,128)(2,1)S(1)}, bf16[4,128,512]{2,1,0:T(8,128)(2,1)S(1)}, u32[]{:S(2)}, u32[]{:S(2)}) collective-permute-start(bf16[4,128,512]{2,1,0:T(8,128)(2,1)S(1)} %add_convert_fusion.1), channel_id=1, source_target_pairs={{0,4},{1,5},{2,6},{3,7},{4,0},{5,1},{6,2},{7,3},{8,12},{9,13},{10,... | collective-permute-start | bytes 1572872 | tf_op jit(solution)/shard_map/ppermute | solution.py:758
  100.1 23.5 %collective-permute-start.19 = (bf16[4,128,512]{2,1,0:T(8,128)(2,1)S(1)}, bf16[4,128,512]{2,1,0:T(8,128)(2,1)S(1)}, u32[]{:S(2)}, u32[]{:S(2)}) collective-permute-start(bf16[4,128,512]{2,1,0:T(8,128)(2,1)S(1)} %get-tuple-element.156), channel_id=1, source_target_pairs={{0,5},{1,4},{2,7},{3,6},{4,1},{5,0},{6,3},{7,2},{8,13},{9,12},{10,... | collective-permute-start | bytes 1572872 | tf_op jit(solution)/shard_map/ppermute | solution.py:758
  101.3 24.4 %collective-permute-start.17 = (bf16[4,128,512]{2,1,0:T(8,128)(2,1)S(1)}, bf16[4,128,512]{2,1,0:T(8,128)(2,1)S(1)}, u32[]{:S(2)}, u32[]{:S(2)}) collective-permute-start(bf16[4,128,512]{2,1,0:T(8,128)(2,1)S(1)} %get-tuple-element.157), channel_id=1, source_target_pairs={{0,1},{1,0},{2,3},{3,2},{4,5},{5,4},{6,7},{7,6},{8,9},{9,8},{10,11... | collective-permute-start | bytes 1572872 | tf_op jit(solution)/shard_map/ppermute | solution.py:758
  123.7 7.6 %copy-start.15 = (bf16[4,128,512]{2,1,0:T(8,128)(2,1)}, bf16[4,128,512]{2,1,0:T(8,128)(2,1)S(1)}, u32[]{:S(2)}) copy-start(bf16[4,128,512]{2,1,0:T(8,128)(2,1)S(1)} %collective-permute-done.19) | copy-start | bytes 1572868
  125.7 5.6 %copy-start.16 = (bf16[4,128,512]{2,1,0:T(8,128)(2,1)}, bf16[4,128,512]{2,1,0:T(8,128)(2,1)S(1)}, u32[]{:S(2)}) copy-start(bf16[4,128,512]{2,1,0:T(8,128)(2,1)S(1)} %collective-permute-done.17) | copy-start | bytes 1572868
  125.7 5.5 %collective-permute-start.20 = (bf16[2,256,1024]{2,1,0:T(8,128)(2,1)}, bf16[2,256,1024]{2,1,0:T(8,128)(2,1)S(1)}, u32[]{:S(2)}, u32[]{:S(2)}) collective-permute-start(bf16[2,256,1024]{2,1,0:T(8,128)(2,1)} %get-tuple-element.130), channel_id=1, source_target_pairs={{0,2},{1,3},{2,0},{3,1},{4,6},{5,7},{6,4},{7,5},{8,10},{9,11},{10,... | collective-permute-start | bytes 3145736 | tf_op jit(solution)/shard_map/ppermute | solution.py:758
  126.6 4.6 %collective-permute-start.21 = (bf16[2,256,1024]{2,1,0:T(8,128)(2,1)}, bf16[2,256,1024]{2,1,0:T(8,128)(2,1)S(1)}, u32[]{:S(2)}, u32[]{:S(2)}) collective-permute-start(bf16[2,256,1024]{2,1,0:T(8,128)(2,1)} %get-tuple-element.132), channel_id=1, source_target_pairs={{0,2},{1,3},{2,0},{3,1},{4,6},{5,7},{6,4},{7,5},{8,10},{9,11},{10,... | collective-permute-start | bytes 3145736 | tf_op jit(solution)/shard_map/ppermute | solution.py:758
  127.6 22.8 %collective-permute-start.24 = (bf16[128,512]{1,0:T(8,128)(2,1)}, bf16[128,512]{1,0:T(8,128)(2,1)S(1)}, u32[]{:S(2)}, u32[]{:S(2)}) collective-permute-start(bf16[128,512]{1,0:T(8,128)(2,1)} %get-tuple-element.155), channel_id=1, source_target_pairs={{0,8},{1,9},{2,10},{3,11},{4,12},{5,13},{6,14},{7,15},{8,0},{9,1},... | collective-permute-start | bytes 393224 | tf_op jit(solution)/shard_map/ppermute | solution.py:758
  128.0 22.4 %collective-permute-start.25 = (bf16[128,512]{1,0:T(8,128)(2,1)}, bf16[128,512]{1,0:T(8,128)(2,1)S(1)}, u32[]{:S(2)}, u32[]{:S(2)}) collective-permute-start(bf16[128,512]{1,0:T(8,128)(2,1)} %get-tuple-element.154), channel_id=1, source_target_pairs={{0,16},{1,17},{2,18},{3,19},{4,20},{5,21},{6,22},{7,23},{8,24},{9,... | collective-permute-start | bytes 393224 | tf_op jit(solution)/shard_map/ppermute | solution.py:758
  131.2 19.2 %collective-permute-start.26 = (bf16[128,512]{1,0:T(8,128)(2,1)}, bf16[128,512]{1,0:T(8,128)(2,1)S(1)}, u32[]{:S(2)}, u32[]{:S(2)}) collective-permute-start(bf16[128,512]{1,0:T(8,128)(2,1)} %get-tuple-element.153), channel_id=1, source_target_pairs={{0,24},{1,25},{2,26},{3,27},{4,28},{5,29},{6,30},{7,31},{8,16},{9,... | collective-permute-start | bytes 393224 | tf_op jit(solution)/shard_map/ppermute | solution.py:758
  132.5 4.3 %copy-start.5 = (f32[8,512]{1,0:T(8,128)S(1)}, f32[8,512]{1,0:T(8,128)}, u32[]{:S(2)}) copy-start(f32[8,512]{1,0:T(8,128)} %get-tuple-element.137.refs_17_) | copy-start | bytes 49156
  136.2 14.3 %collective-permute-start.23 = (bf16[2,128,1024]{2,1,0:T(8,128)(2,1)}, bf16[2,128,1024]{2,1,0:T(8,128)(2,1)S(1)}, u32[]{:S(2)}, u32[]{:S(2)}) collective-permute-start(bf16[2,128,1024]{2,1,0:T(8,128)(2,1)} %get-tuple-element.134), channel_id=1, source_target_pairs={{0,4},{1,5},{2,6},{3,7},{4,0},{5,1},{6,2},{7,3},{8,12},{9,13},{10,... | collective-permute-start | bytes 1572872 | tf_op jit(solution)/shard_map/ppermute | solution.py:758
  136.5 13.9 %collective-permute-start.22 = (bf16[1,256,1024]{2,1,0:T(8,128)(2,1)}, bf16[1,256,1024]{2,1,0:T(8,128)(2,1)S(1)}, u32[]{:S(2)}, u32[]{:S(2)}) collective-permute-start(bf16[1,256,1024]{2,1,0:T(8,128)(2,1)} %get-tuple-element.133), channel_id=1, source_target_pairs={{0,1},{1,0},{2,3},{3,2},{4,5},{5,4},{6,7},{7,6},{8,9},{9,8},{10,11... | collective-permute-start | bytes 1572872 | tf_op jit(solution)/shard_map/ppermute | solution.py:758
  136.8 13.7 %copy-start.18 = (bf16[2,128,1024]{2,1,0:T(8,128)(2,1)S(1)}, bf16[2,128,1024]{2,1,0:T(8,128)(2,1)}, u32[]{:S(2)}) copy-start(bf16[2,128,1024]{2,1,0:T(8,128)(2,1)} %get-tuple-element.147) | copy-start | bytes 1572868
  136.8 15.8 %copy-start.17 = (bf16[1,256,1024]{2,1,0:T(8,128)(2,1)S(1)}, bf16[1,256,1024]{2,1,0:T(8,128)(2,1)}, u32[]{:S(2)}) copy-start(bf16[1,256,1024]{2,1,0:T(8,128)(2,1)} %get-tuple-element.148) | copy-start | bytes 1572868
  150.5 30.9 %copy-start.25 = (bf16[128,512]{1,0:T(8,128)(2,1)}, bf16[128,512]{1,0:T(8,128)(2,1)S(1)}, u32[]{:S(2)}) copy-start(bf16[128,512]{1,0:T(8,128)(2,1)S(1)} %collective-permute-done.26) | copy-start | bytes 393220
  150.7 2.8 %collective-permute-start.27 = (bf16[1,16,1024]{2,1,0:T(8,128)(2,1)S(1)}, bf16[1,16,1024]{2,1,0:T(8,128)(2,1)S(1)}, u32[]{:S(2)}, u32[]{:S(2)}) collective-permute-start(bf16[1,16,1024]{2,1,0:T(8,128)(2,1)S(1)} %bitcast.58), channel_id=1, source_target_pairs={{0,2},{1,3},{2,0},{3,1},{4,6},{5,7},{6,4},{7,5},{8,10},{9,11},{10,... | collective-permute-start | bytes 98312 | tf_op jit(solution)/shard_map/ppermute | solution.py:758
  152.8 8.0 %collective-permute-start.31 = (bf16[1,128,1024]{2,1,0:T(8,128)(2,1)S(1)}, bf16[1,128,1024]{2,1,0:T(8,128)(2,1)S(1)}, u32[]{:S(2)}, u32[]{:S(2)}) collective-permute-start(bf16[1,128,1024]{2,1,0:T(8,128)(2,1)S(1)} %get-tuple-element.164), channel_id=1, source_target_pairs={{0,8},{1,9},{2,10},{3,11},{4,12},{5,13},{6,14},{7,15},{8,0},{9,1},... | collective-permute-start | bytes 786440 | tf_op jit(solution)/shard_map/ppermute | solution.py:758
  153.5 8.5 %collective-permute-start.28 = (bf16[1,144,1024]{2,1,0:T(8,128)(2,1)S(1)}, bf16[1,144,1024]{2,1,0:T(8,128)(2,1)S(1)}, u32[]{:S(2)}, u32[]{:S(2)}) collective-permute-start(bf16[1,144,1024]{2,1,0:T(8,128)(2,1)S(1)} %pad_maximum_fusion.3), channel_id=1, source_target_pairs={{0,1},{1,0},{2,3},{3,2},{4,5},{5,4},{6,7},{7,6},{8,9},{9,8},{10,11... | collective-permute-start | bytes 884744 | tf_op jit(solution)/shard_map/ppermute | solution.py:758
  160.8 4.3 %collective-permute-start.32 = (bf16[1,64,1024]{2,1,0:T(8,128)(2,1)S(1)}, bf16[1,64,1024]{2,1,0:T(8,128)(2,1)S(1)}, u32[]{:S(2)}, u32[]{:S(2)}) collective-permute-start(bf16[1,64,1024]{2,1,0:T(8,128)(2,1)S(1)} %add_convert_fusion.13), channel_id=1, source_target_pairs={{0,4},{1,5},{2,6},{3,7},{4,0},{5,1},{6,2},{7,3},{8,12},{9,13},{10,... | collective-permute-start | bytes 393224 | tf_op jit(solution)/shard_map/ppermute | solution.py:758
  162.1 5.7 %collective-permute-start.29 = (bf16[1,80,1024]{2,1,0:T(8,128)(2,1)S(1)}, bf16[1,80,1024]{2,1,0:T(8,128)(2,1)S(1)}, u32[]{:S(2)}, u32[]{:S(2)}) collective-permute-start(bf16[1,80,1024]{2,1,0:T(8,128)(2,1)S(1)} %pad_maximum_fusion.6), channel_id=1, source_target_pairs={{0,8},{1,9},{2,10},{3,11},{4,12},{5,13},{6,14},{7,15},{8,0},{9,1},... | collective-permute-start | bytes 491528 | tf_op jit(solution)/shard_map/ppermute | solution.py:758
  165.2 6.0 %collective-permute-start.33 = (bf16[1,64,1024]{2,1,0:T(8,128)(2,1)S(1)}, bf16[1,64,1024]{2,1,0:T(8,128)(2,1)S(1)}, u32[]{:S(2)}, u32[]{:S(2)}) collective-permute-start(bf16[1,64,1024]{2,1,0:T(8,128)(2,1)S(1)} %add_convert_fusion.12), channel_id=1, source_target_pairs={{0,16},{1,17},{2,18},{3,19},{4,20},{5,21},{6,22},{7,23},{8,24},{9,... | collective-permute-start | bytes 393224 | tf_op jit(solution)/shard_map/ppermute | solution.py:758
  167.9 12.6 %collective-permute-start.30 = (bf16[1,80,1024]{2,1,0:T(8,128)(2,1)S(1)}, bf16[1,80,1024]{2,1,0:T(8,128)(2,1)S(1)}, u32[]{:S(2)}, u32[]{:S(2)}) collective-permute-start(bf16[1,80,1024]{2,1,0:T(8,128)(2,1)S(1)} %pad_maximum_fusion.7), channel_id=1, source_target_pairs={{0,16},{1,17},{2,18},{3,19},{4,20},{5,21},{6,22},{7,23},{8,24},{9,... | collective-permute-start | bytes 491528 | tf_op jit(solution)/shard_map/ppermute | solution.py:758
  180.6 3.9 %collective-permute-start.38 = (bf16[1,64,1024]{2,1,0:T(8,128)(2,1)S(1)}, bf16[1,64,1024]{2,1,0:T(8,128)(2,1)S(1)}, u32[]{:S(2)}, u32[]{:S(2)}) collective-permute-start(bf16[1,64,1024]{2,1,0:T(8,128)(2,1)S(1)} %add_convert_fusion.10), channel_id=1, source_target_pairs={{0,8},{1,9},{2,10},{3,11},{4,12},{5,13},{6,14},{7,15},{8,0},{9,1},... | collective-permute-start | bytes 393224 | tf_op jit(solution)/shard_map/ppermute | solution.py:758
  181.4 4.9 %collective-permute-start.34 = (bf16[1,80,1024]{2,1,0:T(8,128)(2,1)S(1)}, bf16[1,80,1024]{2,1,0:T(8,128)(2,1)S(1)}, u32[]{:S(2)}, u32[]{:S(2)}) collective-permute-start(bf16[1,80,1024]{2,1,0:T(8,128)(2,1)S(1)} %pad_maximum_fusion.8), channel_id=1, source_target_pairs={{0,4},{1,5},{2,6},{3,7},{4,0},{5,1},{6,2},{7,3},{8,12},{9,13},{10,... | collective-permute-start | bytes 491528 | tf_op jit(solution)/shard_map/ppermute | solution.py:758
  185.2 7.5 %collective-permute-start.39 = (bf16[1,128,1024]{2,1,0:T(8,128)(2,1)S(1)}, bf16[1,128,1024]{2,1,0:T(8,128)(2,1)S(1)}, u32[]{:S(2)}, u32[]{:S(2)}) collective-permute-start(bf16[1,128,1024]{2,1,0:T(8,128)(2,1)S(1)} %get-tuple-element.171), channel_id=1, source_target_pairs={{0,4},{1,5},{2,6},{3,7},{4,0},{5,1},{6,2},{7,3},{8,12},{9,13},{10,... | collective-permute-start | bytes 786440 | tf_op jit(solution)/shard_map/ppermute | solution.py:758
  187.1 7.2 %collective-permute-start.35 = (bf16[1,128,1024]{2,1,0:T(8,128)(2,1)S(1)}, bf16[1,128,1024]{2,1,0:T(8,128)(2,1)S(1)}, u32[]{:S(2)}, u32[]{:S(2)}) collective-permute-start(bf16[1,128,1024]{2,1,0:T(8,128)(2,1)S(1)} %get-tuple-element.173), channel_id=1, source_target_pairs={{0,8},{1,9},{2,10},{3,11},{4,12},{5,13},{6,14},{7,15},{8,0},{9,1},... | collective-permute-start | bytes 786440 | tf_op jit(solution)/shard_map/ppermute | solution.py:758
  189.8 8.0 %collective-permute-start.40 = (bf16[1,128,1024]{2,1,0:T(8,128)(2,1)S(1)}, bf16[1,128,1024]{2,1,0:T(8,128)(2,1)S(1)}, u32[]{:S(2)}, u32[]{:S(2)}) collective-permute-start(bf16[1,128,1024]{2,1,0:T(8,128)(2,1)S(1)} %get-tuple-element.171), channel_id=1, source_target_pairs={{0,2},{1,3},{2,0},{3,1},{4,6},{5,7},{6,4},{7,5},{8,10},{9,11},{10,... | collective-permute-start | bytes 786440 | tf_op jit(solution)/shard_map/ppermute | solution.py:758
  192.7 5.1 %collective-permute-start.36 = (bf16[1,128,1024]{2,1,0:T(8,128)(2,1)S(1)}, bf16[1,128,1024]{2,1,0:T(8,128)(2,1)S(1)}, u32[]{:S(2)}, u32[]{:S(2)}) collective-permute-start(bf16[1,128,1024]{2,1,0:T(8,128)(2,1)S(1)} %get-tuple-element.173), channel_id=1, source_target_pairs={{0,2},{1,3},{2,0},{3,1},{4,6},{5,7},{6,4},{7,5},{8,10},{9,11},{10,... | collective-permute-start | bytes 786440 | tf_op jit(solution)/shard_map/ppermute | solution.py:758
  192.7 5.2 %copy-start.19 = (bf16[1,128,1024]{2,1,0:T(8,128)(2,1)}, bf16[1,128,1024]{2,1,0:T(8,128)(2,1)S(1)}, u32[]{:S(2)}) copy-start(bf16[1,128,1024]{2,1,0:T(8,128)(2,1)S(1)} %collective-permute-done.39) | copy-start | bytes 786436
  192.7 5.1 %collective-permute-start.41 = (bf16[1,128,1024]{2,1,0:T(8,128)(2,1)S(1)}, bf16[1,128,1024]{2,1,0:T(8,128)(2,1)S(1)}, u32[]{:S(2)}, u32[]{:S(2)}) collective-permute-start(bf16[1,128,1024]{2,1,0:T(8,128)(2,1)S(1)} %collective-permute-done.39), channel_id=1, source_target_pairs={{0,2},{1,3},{2,0},{3,1},{4,6},{5,7},{6,4},{7,5},{8,10},{9,11},{10,... | collective-permute-start | bytes 786440 | tf_op jit(solution)/shard_map/ppermute | solution.py:758
  194.3 3.5 %copy-start.20 = (bf16[1,128,1024]{2,1,0:T(8,128)(2,1)}, bf16[1,128,1024]{2,1,0:T(8,128)(2,1)S(1)}, u32[]{:S(2)}) copy-start(bf16[1,128,1024]{2,1,0:T(8,128)(2,1)S(1)} %collective-permute-done.35) | copy-start | bytes 786436
  194.3 3.5 %collective-permute-start.37 = (bf16[1,128,1024]{2,1,0:T(8,128)(2,1)S(1)}, bf16[1,128,1024]{2,1,0:T(8,128)(2,1)S(1)}, u32[]{:S(2)}, u32[]{:S(2)}) collective-permute-start(bf16[1,128,1024]{2,1,0:T(8,128)(2,1)S(1)} %collective-permute-done.35), channel_id=1, source_target_pairs={{0,2},{1,3},{2,0},{3,1},{4,6},{5,7},{6,4},{7,5},{8,10},{9,11},{10,... | collective-permute-start | bytes 786440 | tf_op jit(solution)/shard_map/ppermute | solution.py:758
  (9 other events, 12.9 us)
